TPU v7x, 32 devices: a whole 2x2x4 slice. The times are simulated.
32 devices in a mesh: groups: 2 (over y), lon: 8 (over z, x), dom: 2 (over core).
Axes of the slice: x: 2, y: 2, z: 4, core: 2. Of those that a mesh axis runs over, the one named last changes fastest.
Arguments:
- ensemble_state: float32 [32, 4, 256, 256], P(('groups', 'dom'), None, 'lon'), parts along dimension 0, may hold values from -6 to 6
- proposal_noise: bfloat16 [2, 32, 4, 256, 256], P(None, ('groups', 'dom'), None, 'lon'), parts along dimension 1, may hold values from -1.1953125 to 1.1953125
- courant: float32 [2, 512, 256], P(None, ('groups', 'lon')), parts along dimension 1, may hold values from -0.4 to 0.4
- diffusion: float32 [4], replicated, may hold values from 0.02 to 0.1
- mixing: float32 [4, 4], replicated, may hold values from -3 to 3
- prior_weight: float32 [32], P(('groups', 'dom')), parts along dimension 0, may hold values from -2 to 0
- obs_cell: int32 [4096], P(('groups', 'lon')), parts along dimension 0, may hold values from 0 to 65535, as said below
- obs_value: float32 [4096], P(('groups', 'lon')), parts along dimension 0, may hold values from -6 to 6
- source: int32 [32], P('groups'), parts along dimension 0, may hold values from 0 to 15, as said below
Outputs:
- new_state: float32 [32, 4, 256, 256], P(('groups', 'dom'), None, 'lon'), parts along dimension 0
- log_weight: float32 [32], P(('groups', 'dom')), parts along dimension 0
There are 2 independent parts, one for each index of `groups`. A program takes and returns all parts, laid end to end along the dimension named above; an argument that names none is the same for every part. Nothing has to cross between parts.
Inputs may be any that keep to these rules, and one draw needn't show every extreme that they name: `obs_cell`: entries j * 256 to (j + 1) * 256 - 1 name distinct cells of longitude strip j, that is cells with longitude from j * 32 to (j + 1) * 32 - 1. `source`: the list is nondecreasing.
All inputs are finite; a program needn't handle non-finite values.
Results may differ from a plain program's by a relative error of at most 0.0003.
Values sent between devices are 32-bit elements; how exact they have to be, the bound alone decides.
No kernel may reach another device: no remote copies, remote signals or barrier semaphores. Data moves between devices by JAX's collectives and lax.ppermute only.
A program may use at most 64 MiB of HBM per device.

v0:
```python
import jax
import jax.numpy as jnp
from jax import lax
from jax.sharding import PartitionSpec as P

noise_var = 0.04


def padded_2(block, sides, width):
    for axis, dim in sides:
        count = lax.axis_size(axis)
        forward = [(i, i + 1) for i in range(count - 1)]
        forward.append((count - 1, 0))
        backward = [(target, source) for source, target in forward]
        low = lax.ppermute(
            lax.slice_in_dim(block, block.shape[dim] - width, None, axis=dim), axis, forward
        )
        high = lax.ppermute(lax.slice_in_dim(block, 0, width, axis=dim), axis, backward)
        block = jnp.concatenate([low, block, high], axis=dim)
    return block


def stencil(padded, courant, diffusion, mixing):
    current = padded[:, :, 1:-1]
    eastward = padded[:, :, 2:]
    westward = padded[:, :, :-2]
    northward = jnp.concatenate([current[..., 1:], current[..., -1:]], axis=3)
    southward = jnp.concatenate([current[..., :1], current[..., :-1]], axis=3)
    zonal_courant = courant[0][None, None]
    merid_courant = courant[1][None, None]
    diffusion_rate = diffusion[None, :, None, None]
    mixing_term = sum(
        (
            mixing[:, other][None, :, None, None] * current[:, other : other + 1]
            for other in range(current.shape[1])
        )
    )
    result = (
        current
        - 0.5 * zonal_courant * (eastward - westward)
        - 0.5 * merid_courant * (northward - southward)
    )
    result = result + (0.5 * zonal_courant * zonal_courant + diffusion_rate) * (
        eastward - 2.0 * current + westward
    )
    result = result + (0.5 * merid_courant * merid_courant + diffusion_rate) * (
        northward - 2.0 * current + southward
    )
    return result + mixing_term


def advance(current, courant, diffusion, mixing):
    padded = padded_2(current, (("lon", 2),), 1)
    return stencil(padded, courant, diffusion, mixing)


def nudge(moved, noise_now, cells, nudge_gain, obs_value, push_mask, count_mask):
    particles, field_count, strip_width, lat_rows = moved.shape
    plane = moved[:, 0].reshape(particles, strip_width * lat_rows)
    observed_model = plane[:, cells]
    push_value = push_mask[None] * (nudge_gain[None] * (obs_value[None] - observed_model))
    noise_cells = noise_now[:, 0].reshape(particles, strip_width * lat_rows)[:, cells]
    proposal_term = jnp.sum(
        count_mask[None] * (push_value * push_value + 2.0 * push_value * noise_cells), axis=1
    )
    plane = plane.at[:, cells].add(push_value)
    moved = moved.at[:, 0].set(plane.reshape(particles, strip_width, lat_rows))
    return (moved + noise_now, proposal_term)


def local(
    ensemble_state,
    proposal_noise,
    courant,
    diffusion,
    mixing,
    prior_weight,
    obs_cell,
    obs_value,
    source,
):
    particles, field_count, strip_width, lat_rows = ensemble_state.shape
    strip_cells = strip_width * lat_rows
    lon_index = lax.axis_index("lon")
    local_cells = obs_cell - lon_index * strip_cells
    longitudes = strip_width * lax.axis_size("lon")
    precision = 1.0 + 2.0 * (obs_cell // lat_rows).astype(jnp.float32) / longitudes
    nudge_gain = 0.25 * precision
    all_ones = jnp.ones(obs_value.shape, jnp.float32)
    moved = advance(ensemble_state, courant, diffusion, mixing)
    current, first_term = nudge(
        moved,
        proposal_noise[0].astype(jnp.float32),
        local_cells,
        nudge_gain,
        obs_value,
        all_ones,
        all_ones,
    )
    first_sum = 0.0
    later_term = first_term
    moved = advance(current, courant, diffusion, mixing)
    current, proposal_term = nudge(
        moved,
        proposal_noise[1].astype(jnp.float32),
        local_cells,
        nudge_gain,
        obs_value,
        all_ones,
        all_ones,
    )
    later_term = later_term + proposal_term
    observed_model = current[:, 0].reshape(particles, strip_cells)[:, local_cells]
    difference = obs_value[None] - observed_model
    misfit = jnp.sum(precision[None] * difference * difference, axis=1)
    local_sum = 0.5 * misfit + later_term / (2.0 * noise_var)
    weight_sum = first_sum + lax.psum(local_sum, "lon")
    log_weight = prior_weight - weight_sum / (256.0 * obs_cell.shape[0])
    dom_index = lax.axis_index("dom")
    my_sources = lax.dynamic_slice_in_dim(source, dom_index * particles, particles)
    ensemble = lax.all_gather(current, "dom", axis=0, tiled=True)
    new_state = ensemble[my_sources]
    return (new_state, log_weight)


def solution(mesh):
    placed = (
        P(("groups", "dom"), None, "lon", None),
        P(None, ("groups", "dom"), None, "lon", None),
        P(None, ("groups", "lon"), None),
        P(),
        P(),
        P(("groups", "dom")),
        P(("groups", "lon")),
        P(("groups", "lon")),
        P("groups"),
    )
    return jax.shard_map(
        local,
        mesh=mesh,
        in_specs=placed,
        out_specs=(P(("groups", "dom"), None, "lon", None), P(("groups", "dom"))),
        check_vma=False,
    )
```

profile of v0, /device:TPU:0, one launch (start us, length us, event | category | flops | bytes accessed | tf_op | source)
XLA Modules:
  0.0 119.5 jit_solution(5036676032682434971)
XLA Ops:
  7.2 1.8 %fusion.6 = (f32[8,4,1,256]{3,2,1,0:T(1,128)}, f32[8,4,1,256]{3,2,1,0:T(1,128)}) fusion(f32[8,4,32,256]{3,2,1,0:T(8,128)} %param.13), kind=kLoop, calls=%fused_computation.63 | loop fusion | bytes 131072 | tf_op jit(solution)/shard_map/slice | solution.py:16
  9.0 2.9 %collective-permute-start.1 = (f32[8,4,1,256]{3,2,1,0:T(1,128)}, f32[8,4,1,256]{3,2,1,0:T(1,128)S(1)}, u32[]{:S(2)}, u32[]{:S(2)}) collective-permute-start(f32[8,4,1,256]{3,2,1,0:T(1,128)} %get-tuple-element.52), channel_id=1, source_target_pairs={{0,2},{2,4},{4,6},{6,8},{8,10},{10,12},{12,14},{14,0},{1,3},{3,5},... | collective-permute-start | bytes 98312 | tf_op jit(solution)/shard_map/ppermute | solution.py:15
  11.9 3.0 %collective-permute-start = (f32[8,4,1,256]{3,2,1,0:T(1,128)}, f32[8,4,1,256]{3,2,1,0:T(1,128)S(1)}, u32[]{:S(2)}, u32[]{:S(2)}) collective-permute-start(f32[8,4,1,256]{3,2,1,0:T(1,128)} %get-tuple-element.53), channel_id=1, source_target_pairs={{2,0},{4,2},{6,4},{8,6},{10,8},{12,10},{14,12},{0,14},{3,1},{5,3},... | collective-permute-start | bytes 98312 | tf_op jit(solution)/shard_map/ppermute | solution.py:18
  15.0 2.3 %slice_bitcast_fusion.7 = (f32[8,32,256]{2,1,0:T(8,128)}, f32[8,32,256]{2,1,0:T(8,128)}, f32[8,32,256]{2,1,0:T(8,128)}, f32[8,32,256]{2,1,0:T(8,128)}) fusion(f32[8,4,32,256]{3,2,1,0:T(8,128)} %param.13), kind=kLoop, calls=%fused_computation.27 | loop fusion | bytes 2097152 | tf_op jit(solution)/shard_map/mul | solution.py:34
  17.3 2.4 %fusion.8 = (f32[8,4,32,1]{3,2,1,0:T(8,128)}, f32[8,4,32,1]{3,2,1,0:T(8,128)}) fusion(f32[8,4,32,256]{3,2,1,0:T(8,128)} %param.13), kind=kLoop, calls=%fused_computation.65 | loop fusion | bytes 16384 | tf_op jit(solution)/shard_map/slice | solution.py:27
  19.7 1.7 %fusion.7 = (f32[8,4,32,255]{3,2,1,0:T(8,128)}, f32[8,4,32,255]{3,2,1,0:T(8,128)}) fusion(f32[8,4,32,256]{3,2,1,0:T(8,128)S(1)} %copy-done), kind=kLoop, calls=%fused_computation.64 | loop fusion | bytes 4177920 | tf_op jit(solution)/shard_map/slice | solution.py:27
  21.4 0.5 broadcast_multiply_fusion
  21.9 0.8 slice_reduce_fusion.3
  22.7 0.3 bitcast_convert_fusion
  23.0 0.1 broadcast_add_fusion.1
  23.1 0.7 slice.234
  23.8 0.7 slice.233
  24.6 3.5 %copy.42 = f32[8,1,32,256]{0,3,2,1:T(8,128)} copy(f32[8,1,32,256]{3,2,1,0:T(8,128)} %slice.233) | data formatting | bytes 524288 | tf_op jit(solution)/shard_map/slice | solution.py:62
  28.1 2.9 %gather_fusion.4 = f32[256,8]{1,0:T(8,128)S(1)} fusion(f32[8,8192]{0,1:T(8,128)} %bitcast.52, s32[1024]{0:T(1024)S(1)} %pad_clamp_fusion.1), kind=kCustom, calls=%fused_computation.4 | custom fusion | bytes 17408 | tf_op jit(solution)/shard_map/gather | solution.py:62
  31.0 0.1 copy.43
  31.1 2.6 %copy.44 = f32[8,1,32,256]{0,3,2,1:T(8,128)} copy(f32[8,1,32,256]{3,2,1,0:T(8,128)S(1)} %copy-done.2) | data formatting | bytes 524288 | tf_op jit(solution)/shard_map/slice | solution.py:62
  33.7 2.9 %gather_fusion.5 = f32[256,8]{1,0:T(8,128)S(1)} fusion(f32[8,8192]{0,1:T(8,128)} %bitcast.53, s32[1024]{0:T(1024)S(1)} %pad_clamp_fusion.1), kind=kCustom, calls=%fused_computation.5 | custom fusion | bytes 17408 | tf_op jit(solution)/shard_map/gather | solution.py:62
  36.6 0.1 copy.45
  36.7 3.4 %add_add_fusion.1 = f32[8,4,32,256]{3,2,1,0:T(8,128)S(1)} fusion(f32[8,4,32,256]{3,2,1,0:T(8,128)S(1)} %copy-done, f32[8,4,32,255]{3,2,1,0:T(8,128)} %get-tuple-element.55, f32[8,4,32,1]{3,2,1,0:T(8,128)} %get-tuple-element.57, f32[8,4,32,1]{3,2,1,0:T(8,128)} %get-tuple-element.56, f32[8,4,32,255]{3,2,1,0:T(8,128)} %get-tuple-element.54, ...), kind=kLoop, calls=%fused_computation.17 | loop fusion | flops 7077888 | bytes 5636160 | tf_op jit(solution)/shard_map/add | solution.py:49
  40.2 2.6 %copy.32 = f32[8,1,32,256]{0,3,2,1:T(8,128)} copy(f32[8,1,32,256]{3,2,1,0:T(8,128)S(1)} %slice.220) | data formatting | bytes 524288 | tf_op jit(solution)/shard_map/slice | solution.py:59
  42.8 3.0 %gather_fusion = f32[256,8]{1,0:T(8,128)S(1)} fusion(f32[8,8192]{0,1:T(8,128)} %bitcast.48, s32[1024]{0:T(1024)} %copy-done.5), kind=kCustom, calls=%fused_computation | custom fusion | bytes 17408 | tf_op jit(solution)/shard_map/gather | solution.py:60
  45.9 0.7 add_reduce_fusion.1
  46.6 0.1 copy.34
  46.7 5.9 %scatter_fusion = f32[8,8192]{0,1:T(8,128)} fusion(f32[8,8192]{0,1:T(8,128)} %bitcast.49, s32[256]{0:T(256)S(1)} %copy-done.8, f32[256,8]{1,0:T(8,128)S(1)} %copy.34), kind=kCustom, calls=%fused_computation.6 | custom fusion | flops 2048 | bytes 25600 | tf_op jit(solution)/shard_map/scatter-add | solution.py:66
  52.7 2.8 %copy.35 = f32[8,1,32,256]{3,2,1,0:T(8,128)S(1)} copy(f32[8,1,32,256]{0,3,2,1:T(8,128)} %bitcast.50) | data formatting | bytes 524288 | tf_op jit(solution)/shard_map/reshape.46
  55.5 0.2 fusion
  55.8 0.2 fusion.5
  56.0 0.4 fusion.4
  56.4 0.1 collective-permute-start.3
  56.4 4.7 %collective-permute-start.2 = (f32[8,4,1,256]{3,2,1,0:T(1,128)S(1)}, f32[8,4,1,256]{3,2,1,0:T(1,128)S(1)}, u32[]{:S(2)}, u32[]{:S(2)}) collective-permute-start(f32[8,4,1,256]{3,2,1,0:T(1,128)S(1)} %get-tuple-element.43), channel_id=1, source_target_pairs={{2,0},{4,2},{6,4},{8,6},{10,8},{12,10},{14,12},{0,14},{3,1},{5,3},... | collective-permute-start | bytes 98312 | tf_op jit(solution)/shard_map/ppermute | solution.py:18
  61.2 0.1 slice_bitcast_fusion.3
  61.3 1.8 %collective-permute-done.3 = f32[8,4,1,256]{3,2,1,0:T(1,128)S(1)} collective-permute-done((f32[8,4,1,256]{3,2,1,0:T(1,128)S(1)}, f32[8,4,1,256]{3,2,1,0:T(1,128)S(1)}, u32[]{:S(2)}, u32[]{:S(2)}) %collective-permute-start.3) | collective-permute-done | bytes 32800 | tf_op jit(solution)/shard_map/ppermute | solution.py:15
  63.1 1.4 %add_add_fusion = f32[8,4,32,256]{3,2,1,0:T(8,128)S(1)} fusion(f32[8,4,32,256]{3,2,1,0:T(8,128)S(1)} %fusion, f32[8,4,32,255]{3,2,1,0:T(8,128)S(1)} %get-tuple-element.45, f32[8,4,32,1]{3,2,1,0:T(8,128)S(1)} %get-tuple-element.47, f32[8,4,32,1]{3,2,1,0:T(8,128)S(1)} %get-tuple-element.46, f32[8,4,32,255]{3,2,1,0:T(8,128)S(1)} %get-tuple-element.44, ...), kind=kLoop, calls=%fused_computation.16 | loop fusion | flops 7077888 | bytes 5636160 | tf_op jit(solution)/shard_map/add | solution.py:49
  64.5 2.6 %copy.36 = f32[8,1,32,256]{0,3,2,1:T(8,128)} copy(f32[8,1,32,256]{3,2,1,0:T(8,128)S(1)} %slice.231) | data formatting | bytes 524288 | tf_op jit(solution)/shard_map/slice | solution.py:59
  67.1 2.9 %gather_fusion.1 = f32[256,8]{1,0:T(8,128)S(1)} fusion(f32[8,8192]{0,1:T(8,128)} %bitcast.45, s32[1024]{0:T(1024)S(1)} %copy-done.6), kind=kCustom, calls=%fused_computation.1 | custom fusion | bytes 17408 | tf_op jit(solution)/shard_map/gather | solution.py:60
  70.1 0.1 add_reduce_fusion
  70.2 0.1 copy.38
  70.4 5.9 %scatter_fusion.1 = f32[8,8192]{0,1:T(8,128)} fusion(f32[8,8192]{0,1:T(8,128)} %bitcast.46, s32[256]{0:T(256)S(1)} %copy-done.9, f32[256,8]{1,0:T(8,128)S(1)} %copy.38), kind=kCustom, calls=%fused_computation.7 | custom fusion | flops 2048 | bytes 25600 | tf_op jit(solution)/shard_map/scatter-add | solution.py:66
  76.3 2.8 %copy.39 = f32[8,1,32,256]{3,2,1,0:T(8,128)S(1)} copy(f32[8,1,32,256]{0,3,2,1:T(8,128)} %bitcast.47) | data formatting | bytes 524288 | tf_op jit(solution)/shard_map/reshape.57
  79.2 1.1 fusion.1
  80.3 0.1 compare_select_fusion.1
  80.4 1.0 slice.232
  81.4 2.6 %copy.40 = f32[8,1,32,256]{0,3,2,1:T(8,128)} copy(f32[8,1,32,256]{3,2,1,0:T(8,128)S(1)} %slice.232) | data formatting | bytes 524288 | tf_op jit(solution)/shard_map/slice | solution.py:113
  84.0 2.9 %gather_fusion.3 = f32[256,8]{1,0:T(8,128)S(1)} fusion(f32[8,8192]{0,1:T(8,128)} %bitcast.51, s32[1024]{0:T(1024)S(1)} %copy-done.6), kind=kCustom, calls=%fused_computation.3 | custom fusion | bytes 17408 | tf_op jit(solution)/shard_map/gather | solution.py:113
  87.0 0.1 fusion.2
  87.2 21.8 %psum.7 = f32[8]{0:T(128)S(1)} all-reduce(f32[8]{0:T(128)S(1)} %multiply_add_fusion.1), channel_id=1, replica_groups=mesh['groups'=2,'lon'=8,'dom'=2] {'lon'}, use_global_device_ids=true, to_apply=%region_5.6 | all-reduce | flops 8 | bytes 64 | tf_op jit(solution)/shard_map/psum | solution.py:117
  109.0 0.5 multiply_subtract_fusion
  109.5 3.2 %gather_fusion.2 = f32[8,4,32,256]{3,2,1,0:T(8,128)} fusion(f32[16,4,32,256]{3,2,1,0:T(8,128)} %all-gather.2.cloned.1.call-done, s32[1024]{0:T(1024)S(1)} %pad_clamp_fusion), kind=kCustom, calls=%fused_computation.2 | custom fusion | bytes 2097184 | tf_op jit(solution)/shard_map/gather | solution.py:122
  (67 shorter events, 0.5 us)
Async XLA Ops:
  7.2 12.5 %copy-start = (f32[8,4,32,256]{3,2,1,0:T(8,128)S(1)}, f32[8,4,32,256]{3,2,1,0:T(8,128)}, u32[]{:S(2)}) copy-start(f32[8,4,32,256]{3,2,1,0:T(8,128)} %param.13) | copy-start | bytes 3145732
  7.2 102.3 %all-gather.2.cloned.1.call-start = ((), (), s32[]{:S(2)}) async-start(), calls=%async_computation | async-start | bytes 3145728 | tf_op jit(solution)/shard_map/all_gather | solution.py:121
  9.0 27.7 %collective-permute-start.1 = (f32[8,4,1,256]{3,2,1,0:T(1,128)}, f32[8,4,1,256]{3,2,1,0:T(1,128)S(1)}, u32[]{:S(2)}, u32[]{:S(2)}) collective-permute-start(f32[8,4,1,256]{3,2,1,0:T(1,128)} %get-tuple-element.52), channel_id=1, source_target_pairs={{0,2},{2,4},{4,6},{6,8},{8,10},{10,12},{12,14},{14,0},{1,3},{3,5},... | collective-permute-start | bytes 98312 | tf_op jit(solution)/shard_map/ppermute | solution.py:15
  11.9 24.7 %collective-permute-start = (f32[8,4,1,256]{3,2,1,0:T(1,128)}, f32[8,4,1,256]{3,2,1,0:T(1,128)S(1)}, u32[]{:S(2)}, u32[]{:S(2)}) collective-permute-start(f32[8,4,1,256]{3,2,1,0:T(1,128)} %get-tuple-element.53), channel_id=1, source_target_pairs={{2,0},{4,2},{6,4},{8,6},{10,8},{12,10},{14,12},{0,14},{3,1},{5,3},... | collective-permute-start | bytes 98312 | tf_op jit(solution)/shard_map/ppermute | solution.py:18
  15.0 6.4 %copy-start.18 = (s32[256]{0:T(256)S(1)}, s32[256]{0:T(256)}, u32[]{:S(2)}) copy-start(s32[256]{0:T(256)} %param.19) | copy-start | bytes 3076
  15.0 6.9 %copy-start.4 = (f32[4,4]{1,0:T(4,128)S(1)}, f32[4,4]{1,0:T(4,128)}, u32[]{:S(2)}) copy-start(f32[4,4]{1,0:T(4,128)} %param.17) | copy-start | bytes 196
  15.0 7.7 %copy-start.3 = (f32[2,32,256]{2,1,0:T(8,128)S(1)}, f32[2,32,256]{2,1,0:T(8,128)}, u32[]{:S(2)}) copy-start(f32[2,32,256]{2,1,0:T(8,128)} %param.15) | copy-start | bytes 196612
  15.0 7.7 %copy-start.1 = (bf16[2,8,4,32,256]{4,3,2,1,0:T(8,128)(2,1)S(1)}, bf16[2,8,4,32,256]{4,3,2,1,0:T(8,128)(2,1)}, u32[]{:S(2)}) copy-start(bf16[2,8,4,32,256]{4,3,2,1,0:T(8,128)(2,1)} %param.14) | copy-start | bytes 3145732
  19.7 3.3 %copy-start.21 = (f32[4]{0:T(128)S(1)}, f32[4]{0:T(128)}, u32[]{:S(2)}) copy-start(f32[4]{0:T(128)} %param.16) | copy-start | bytes 52
  21.9 1.9 %copy-start.7 = (s32[256]{0:T(256)}, s32[256]{0:T(256)S(1)}, u32[]{:S(2)}) copy-start(s32[256]{0:T(256)S(1)} %compare_select_fusion) | copy-start | bytes 3076
  23.1 10.6 %copy-start.5 = (s32[1024]{0:T(1024)}, s32[1024]{0:T(1024)S(1)}, u32[]{:S(2)}) copy-start(s32[1024]{0:T(1024)S(1)} %pad_clamp_fusion.1) | copy-start | bytes 12292
  24.6 6.5 %copy-start.2 = (f32[8,1,32,256]{3,2,1,0:T(8,128)S(1)}, f32[8,1,32,256]{3,2,1,0:T(8,128)}, u32[]{:S(2)}) copy-start(f32[8,1,32,256]{3,2,1,0:T(8,128)} %slice.234) | copy-start | bytes 786436
  40.1 5.8 %copy-start.10 = (f32[256]{0:T(256)S(1)}, f32[256]{0:T(256)}, u32[]{:S(2)}) copy-start(f32[256]{0:T(256)} %get-tuple-element.34) | copy-start | bytes 3076
  40.1 5.8 %copy-start.12 = (f32[256]{0:T(256)S(1)}, f32[256]{0:T(256)}, u32[]{:S(2)}) copy-start(f32[256]{0:T(256)} %param.20) | copy-start | bytes 3076
  40.1 6.6 %copy-start.8 = (s32[256]{0:T(256)S(1)}, s32[256]{0:T(256)}, u32[]{:S(2)}) copy-start(s32[256]{0:T(256)} %copy-done.7) | copy-start | bytes 3076
  55.7 7.3 %copy-start.14 = (f32[4]{0:T(128)S(1)}, f32[4]{0:T(128)}, u32[]{:S(2)}) copy-start(f32[4]{0:T(128)} %get-tuple-element.26) | copy-start | bytes 52
  55.7 7.3 %copy-start.15 = (f32[4]{0:T(128)S(1)}, f32[4]{0:T(128)}, u32[]{:S(2)}) copy-start(f32[4]{0:T(128)} %get-tuple-element.27) | copy-start | bytes 52
  55.8 7.3 %copy-start.16 = (f32[4]{0:T(128)S(1)}, f32[4]{0:T(128)}, u32[]{:S(2)}) copy-start(f32[4]{0:T(128)} %get-tuple-element.28) | copy-start | bytes 52
  55.8 7.3 %copy-start.17 = (f32[4]{0:T(128)S(1)}, f32[4]{0:T(128)}, u32[]{:S(2)}) copy-start(f32[4]{0:T(128)} %get-tuple-element.29) | copy-start | bytes 52
  56.4 6.7 %collective-permute-start.3 = (f32[8,4,1,256]{3,2,1,0:T(1,128)S(1)}, f32[8,4,1,256]{3,2,1,0:T(1,128)S(1)}, u32[]{:S(2)}, u32[]{:S(2)}) collective-permute-start(f32[8,4,1,256]{3,2,1,0:T(1,128)S(1)} %get-tuple-element.42), channel_id=1, source_target_pairs={{0,2},{2,4},{4,6},{6,8},{8,10},{10,12},{12,14},{14,0},{1,3},{3,5},... | collective-permute-start | bytes 98312 | tf_op jit(solution)/shard_map/ppermute | solution.py:15
  56.4 6.6 %collective-permute-start.2 = (f32[8,4,1,256]{3,2,1,0:T(1,128)S(1)}, f32[8,4,1,256]{3,2,1,0:T(1,128)S(1)}, u32[]{:S(2)}, u32[]{:S(2)}) collective-permute-start(f32[8,4,1,256]{3,2,1,0:T(1,128)S(1)} %get-tuple-element.43), channel_id=1, source_target_pairs={{2,0},{4,2},{6,4},{8,6},{10,8},{12,10},{14,12},{0,14},{3,1},{5,3},... | collective-permute-start | bytes 98312 | tf_op jit(solution)/shard_map/ppermute | solution.py:18
  63.1 4.1 %copy-start.6 = (s32[1024]{0:T(1024)S(1)}, s32[1024]{0:T(1024)}, u32[]{:S(2)}) copy-start(s32[1024]{0:T(1024)} %copy-done.5) | copy-start | bytes 12292
  64.4 5.7 %copy-start.11 = (f32[256]{0:T(256)S(1)}, f32[256]{0:T(256)}, u32[]{:S(2)}) copy-start(f32[256]{0:T(256)} %get-tuple-element.34) | copy-start | bytes 3076
  64.5 5.6 %copy-start.13 = (f32[256]{0:T(256)S(1)}, f32[256]{0:T(256)}, u32[]{:S(2)}) copy-start(f32[256]{0:T(256)} %param.20) | copy-start | bytes 3076
  64.5 5.9 %copy-start.9 = (s32[256]{0:T(256)S(1)}, s32[256]{0:T(256)}, u32[]{:S(2)}) copy-start(s32[256]{0:T(256)} %copy-done.7) | copy-start | bytes 3076
  76.3 4.1 %copy-start.22 = (s32[16]{0:T(128)S(1)}, s32[16]{0:T(128)}, u32[]{:S(2)}) copy-start(s32[16]{0:T(128)} %param.21) | copy-start | bytes 196
  79.2 7.8 %copy-start.19 = (f32[256]{0:T(256)S(1)}, f32[256]{0:T(256)}, u32[]{:S(2)}) copy-start(f32[256]{0:T(256)} %get-tuple-element.35) | copy-start | bytes 3076
  79.2 8.0 %copy-start.20 = (f32[8]{0:T(128)S(1)}, f32[8]{0:T(128)}, u32[]{:S(2)}) copy-start(f32[8]{0:T(128)} %get-tuple-element.32) | copy-start | bytes 100
  79.2 29.8 %copy-start.23 = (f32[8]{0:T(128)S(1)}, f32[8]{0:T(128)}, u32[]{:S(2)}) copy-start(f32[8]{0:T(128)} %param.18) | copy-start | bytes 100
Sparse Core Ops, SparseCore 0:
  80.5 12.1 all-gather.1
where the time goes:
time: 120 us
  local copies, waits for them, and re-layouts  50.4 us (42%)
  blocking collectives  21.8 us (18%)
  other arithmetic  20.3 us (17%)
  between operations  14.4 us (12%)
  starting transfers between devices  10.8 us (9%)
  waiting for transfers between devices  1.8 us (2%)
    psum x1, blocking collectives, local(): weight_sum = first_sum + lax.psum(local_sum, 'lon')  21.8 us
    scatter-add x2, other arithmetic, nudge(): plane = plane.at[:, cells].add(push_value)  11.8 us
    ppermute x2, starting transfers between devices, padded_2(): lax.ppermute(lax.slice_in_dim(block, 0, width, axis=dim), axis, backward)  7.75 us
    slice x4, local copies, waits for them, and re-layouts, nudge(): noise_now[:, 0].reshape(particles, strip_width * lat_rows)[:, cells]  7.6 us
    gather x4, local copies, waits for them, and re-layouts, nudge(): observed_model = plane[:, cells]  6.07 us
    gather x4, local copies, waits for them, and re-layouts, nudge(): noise_now[:, 0].reshape(particles, strip_width * lat_rows)[:, cells]  5.93 us
    another operation x2, local copies, waits for them, and re-layouts  5.66 us
    slice x4, local copies, waits for them, and re-layouts, nudge(): plane = moved[:, 0].reshape(particles, strip_width * lat_rows)  5.29 us
  transfers between devices with their start and end apart: 5, of which 1 were waited for; matrix products, arithmetic and copies ran while one was open for 24% of the time, Pallas kernels for 0%

commit v1 on v0

v1 whole, which is shorter than its diff:
```python
import functools

import jax
import jax.numpy as jnp
from jax import lax
from jax.experimental import pallas as pl
from jax.experimental.pallas import tpu as pltpu
from jax.sharding import PartitionSpec as P

noise_var = 0.04
VMEM = pl.BlockSpec(memory_space=pltpu.VMEM)
SMEM = pl.BlockSpec(memory_space=pltpu.SMEM)
ANY = pl.BlockSpec(memory_space=pl.ANY)
BF16 = jnp.bfloat16
F32 = jnp.float32


def north(v):
    return pltpu.roll(v, v.shape[1] - 1, 1)


def south(v):
    return pltpu.roll(v, 1, 1)


def coefficients(zonal, merid, rate, self_mix):
    lat = lax.broadcasted_iota(jnp.int32, zonal.shape, 1)
    zonal_half, zonal_rate = 0.5 * zonal, 0.5 * zonal * zonal + rate
    merid_half, merid_rate = 0.5 * merid, 0.5 * merid * merid + rate
    east, west = zonal_rate - zonal_half, zonal_rate + zonal_half
    to_north, to_south = merid_rate - merid_half, merid_rate + merid_half
    centre = 1.0 + self_mix - 2.0 * zonal_rate - 2.0 * merid_rate
    last, first = lat == zonal.shape[1] - 1, lat == 0
    centre = centre + jnp.where(last, to_north, 0.0) + jnp.where(first, to_south, 0.0)
    to_north = jnp.where(last, 0.0, to_north)
    to_south = jnp.where(first, 0.0, to_south)
    return centre, east, west, to_north, to_south


def mixed(mixing, field, values):
    total = None
    for other, value in enumerate(values):
        if other != field:
            term = mixing[field, other] * value
            total = term if total is None else total + term
    return total


def pick_rows(kinds, particles, fields, strip, rows, columns):
    out = lax.broadcasted_iota(jnp.int32, (rows, columns), 0)
    col = lax.broadcasted_iota(jnp.int32, (rows, columns), 1)
    want = jnp.full((rows, columns), -1, jnp.int32)
    for place, (field, x) in enumerate(kinds):
        inside = (out >= place * particles) & (out < (place + 1) * particles)
        target = (out - place * particles) * (fields * strip) + field * strip + x
        want = jnp.where(inside, target, want)
    return (col == want).astype(BF16)


def gather_rows(ref, first, stride, count):
    sub = lax.broadcasted_iota(jnp.int32, (count, ref.shape[1]), 0)
    out = None
    for p in range(count):
        row = jnp.broadcast_to(ref[pl.ds(first + p * stride, 1), :], sub.shape)
        out = row if out is None else jnp.where(sub == p, row, out)
    return out


def prepare(sizes, state, noise, courant, diffusion, mixing, cell, value,
            send_east, send_west, maps, noise_rows):
    particles, fields, strip, lats, strips = sizes
    x0 = lax.axis_index("lon") * strip
    shift = lats.bit_length() - 1
    local_cell = cell[...] - x0 * lats
    obs_lon = lax.shift_right_arithmetic(local_cell, shift)
    obs_lat = local_cell & (lats - 1)
    count = cell.shape[1]
    here = lax.broadcasted_iota(jnp.int32, (strip, count), 0) == obs_lon
    val = value[...]
    high = val.astype(BF16)
    rest = val - high.astype(F32)
    mid = rest.astype(BF16)
    low = (rest - mid.astype(F32)).astype(BF16)
    zero = jnp.zeros((strip, count), F32)
    parts = [jnp.where(here, 1.0, zero)]
    parts += [jnp.where(here, p.astype(F32), zero) for p in (high, mid, low)]
    left = jnp.concatenate(parts, 0).astype(BF16)
    right = (lax.broadcasted_iota(jnp.int32, (lats, count), 0) == obs_lat).astype(F32).astype(BF16)
    dense = lax.dot_general(left, right, (((1,), (1,)), ((), ())), preferred_element_type=F32)
    seen = dense[:strip]
    lon = (lax.broadcasted_iota(jnp.int32, (strip, lats), 0) + x0).astype(F32)
    precision = 1.0 + 2.0 * lon / (strip * strips)
    gain = seen * (0.25 * precision)
    weight = seen * precision
    target = dense[strip:2 * strip] + (dense[2 * strip:3 * strip] + dense[3 * strip:])
    maps[0] = gain
    maps[1] = weight
    maps[2] = target

    kinds = [(f, x) for x in (0, strip - 1) for f in range(fields)]
    pick = pick_rows(kinds, particles, fields, strip, len(kinds) * particles, noise.shape[1])
    rows = jnp.dot(pick, noise[0], preferred_element_type=F32)
    noise_rows[0] = rows[:particles]
    noise_rows[1] = rows[fields * particles:(fields + 1) * particles]

    def edge(x, inner, out, base):
        here = [gather_rows(state, f * strip + x, fields * strip, particles) for f in range(fields)]
        beside = [gather_rows(state, f * strip + inner, fields * strip, particles) for f in range(fields)]
        for f in range(fields):
            centre, east, west, to_north, to_south = coefficients(
                courant[0, x:x + 1], courant[1, x:x + 1], diffusion[f], mixing[f, f])
            known, missing = (east, west) if inner > x else (west, east)
            moved = (centre * here[f] + known * beside[f] + to_north * north(here[f])
                     + to_south * south(here[f]) + mixed(mixing, f, here))
            if f == 0:
                g = gain[x:x + 1]
                moved = moved + g * (target[x:x + 1] - moved)
                missing = (1.0 - g) * missing
            moved = moved + rows[base + f * particles:base + (f + 1) * particles]
            out[f * particles:(f + 1) * particles] = here[f]
            out[(fields + f) * particles:(fields + f + 1) * particles] = moved
            out[2 * fields * particles + f:2 * fields * particles + f + 1] = missing
        out[2 * fields * particles + fields:] = jnp.zeros((8 - fields, lats), F32)

    edge(strip - 1, strip - 2, send_east, fields * particles)
    edge(0, 1, send_west, 0)


def bulk(sizes, state, noise, courant, diffusion, mixing, maps,
         out, partial, noise_rows, coefs, middle):
    particles, fields, strip, lats, strips = sizes
    lon = lax.broadcasted_iota(jnp.int32, (strip, lats), 0)
    for f in range(fields):
        centre, east, west, to_north, to_south = coefficients(
            courant[0], courant[1], diffusion[f], mixing[f, f])
        coefs[f, 0] = centre
        coefs[f, 1] = jnp.where(lon == strip - 1, 0.0, east)
        coefs[f, 2] = jnp.where(lon == 0, 0.0, west)
        coefs[f, 3] = to_north
        coefs[f, 4] = to_south
    kinds = [(0, x) for x in (0, 1, strip - 2, strip - 1)]
    pick = pick_rows(kinds, particles, fields, strip, len(kinds) * particles, noise.shape[1])
    noise_rows[...] = jnp.dot(pick, noise[1], preferred_element_type=F32)

    def rows_of(p, f):
        return pl.ds(pl.multiple_of(p * (fields * strip) + f * strip, strip), strip)

    def moved(values, f):
        v = values[f]
        return (coefs[f, 0] * v + coefs[f, 1] * pltpu.roll(v, strip - 1, 0) + coefs[f, 2] * pltpu.roll(v, 1, 0)
                + coefs[f, 3] * north(v) + coefs[f, 4] * south(v) + mixed(mixing, f, values))

    def body(p, carry):
        values = [state[rows_of(p, f), :] for f in range(fields)]
        total = None
        for f in range(fields):
            new = moved(values, f)
            add = noise[0, rows_of(p, f), :].astype(F32)
            if f == 0:
                push = maps[0] * (maps[2] - new)
                new = new + push
                total = jnp.where((lon > 0) & (lon < strip - 1), push * (push + 2.0 * add), 0.0)
            middle[f] = new + add
        values = [middle[f] for f in range(fields)]
        for f in range(fields):
            new = moved(values, f)
            add = noise[1, rows_of(p, f), :].astype(F32)
            if f == 0:
                push = maps[0] * (maps[2] - new)
                new = new + push + add
                miss = maps[2] - new
                term = ((0.5 / noise_var) * (push * (push + 2.0 * add)) + (0.5 * maps[1]) * (miss * miss))
                total = (0.5 / noise_var) * total + jnp.where((lon > 1) & (lon < strip - 2), term, 0.0)
            else:
                new = new + add
            out[rows_of(p, f), :] = new
        total = jnp.sum(total, axis=0, keepdims=True)
        partial[pl.ds(p, 1), :] = total[:, :128] + total[:, 128:]
        return carry

    lax.fori_loop(0, particles, body, 0)


def correct(sizes, own_east, own_west, from_west, from_east, courant, diffusion, mixing, maps,
            noise0, noise1, current, partial, out, weight):
    particles, fields, strip, lats, strips = sizes
    n = fields * particles

    def split(ref, start):
        return [ref[start + f * particles:start + (f + 1) * particles] for f in range(fields)]

    def wide(v):
        return v[:, :128] + v[:, 128:]

    def push_terms(push, add):
        return (0.5 / noise_var) * (push * (push + 2.0 * add))

    for block in range(n):
        spot = pl.ds(block * strip + 8, strip - 16)
        out[spot, :] = current[spot, :]
    total = partial[...]
    for x, inner, own, other, at in ((0, 1, own_west, from_west, 0), (strip - 1, strip - 2, own_east, from_east, 1)):
        own_state, own_first = split(own, 0), split(own, n)
        other_state, other_first = split(other, 0), split(other, n)
        gain, observed, seen = maps[0, x:x + 1], maps[2, x:x + 1], maps[1, x:x + 1]
        first, outside, edge_coefs, inner_out = [], [], [], []
        for f in range(fields):
            coefs = coefficients(courant[0, x:x + 1], courant[1, x:x + 1], diffusion[f], mixing[f, f])
            outer = coefs[2] if inner > x else coefs[1]
            edge_coefs.append((coefs[0], outer, coefs[3], coefs[4]))
            coefs = coefficients(courant[0, inner:inner + 1], courant[1, inner:inner + 1], diffusion[f], mixing[f, f])
            inner_out.append(coefs[2] if inner > x else coefs[1])
            row = 2 * n + f
            outside.append(other_first[f] + other[row:row + 1] * own_state[f])
            step = outer * other_state[f]
            if f == 0:
                step = (1.0 - gain) * step
                result = own_first[0] + step
                add = noise0[at]
                push = (gain / (1.0 - gain)) * (observed - (result - add))
                total = total + wide(push_terms(push, add))
            first.append(step)
        for f in range(fields):
            centre, outer, to_north, to_south = edge_coefs[f]
            step = (centre * first[f] + outer * outside[f] + to_north * north(first[f])
                    + to_south * south(first[f]) + mixed(mixing, f, first))
            beside = inner_out[f] * first[f]
            if f == 0:
                g_in = maps[0, inner:inner + 1]
                step = (1.0 - gain) * step
                beside = (1.0 - g_in) * beside
            tile = min(x, inner) // 8 * 8
            sub = lax.broadcasted_iota(jnp.int32, (8, lats), 0)
            for p in range(particles):
                spot = pl.ds(p * fields * strip + f * strip + tile, 8)
                change = jnp.where(sub == x - tile, jnp.broadcast_to(step[p:p + 1], sub.shape),
                                   jnp.where(sub == inner - tile, jnp.broadcast_to(beside[p:p + 1], sub.shape), 0.0))
                out[spot, :] = current[spot, :] + change
            if f == 0:
                for place in (x, inner):
                    result = gather_rows(out, place, fields * strip, particles)
                    g, v, s = maps[0, place:place + 1], maps[2, place:place + 1], maps[1, place:place + 1]
                    k = (0, 1, strip - 2, strip - 1).index(place) * particles
                    add = noise1[k:k + particles]
                    push = (g / (1.0 - g)) * (v - (result - add))
                    miss = v - result
                    total = total + wide(push_terms(push, add) + (0.5 * s) * (miss * miss))
    weight[...] = total


def assemble(sizes, source, current, received, out, sems):
    particles = sizes[0]
    dom = lax.axis_index("dom")

    def copy(j, ref, at):
        return pltpu.make_async_copy(ref.at[at], out.at[j], sems.at[j])

    for j in range(particles):
        wanted = source[dom * particles + j]
        mine = wanted // particles == dom
        at = wanted % particles

        @pl.when(mine)
        def _():
            copy(j, current, at).start()

        @pl.when(jnp.logical_not(mine))
        def _():
            copy(j, received, at).start()

    for j in range(particles):
        copy(j, current, 0).wait()


def local(ensemble_state, proposal_noise, courant, diffusion, mixing, prior_weight, obs_cell, obs_value, source):
    particles, fields, strip, lats = ensemble_state.shape
    strips = lax.axis_size("lon")
    sizes = (particles, fields, strip, lats, strips)
    rows = particles * fields * strip
    state = ensemble_state.reshape(rows, lats)
    noise = proposal_noise.reshape(2, rows, lats)
    packet = jax.ShapeDtypeStruct((2 * particles * fields + 8, lats), F32)
    shape = jax.ShapeDtypeStruct

    send_east, send_west, maps, noise0 = pl.pallas_call(
        functools.partial(prepare, sizes),
        out_shape=(packet, packet, shape((3, strip, lats), F32), shape((2, particles, lats), F32)),
        in_specs=[VMEM, VMEM, VMEM, SMEM, SMEM, VMEM, VMEM],
        out_specs=(VMEM,) * 4,
        cost_estimate=pl.CostEstimate(flops=1000000, bytes_accessed=2000000, transcendentals=0),
    )(state, noise, courant, diffusion, mixing, obs_cell[None], obs_value[None])

    eastward = [(i, (i + 1) % strips) for i in range(strips)]
    westward = [(i, (i - 1) % strips) for i in range(strips)]
    from_west = lax.ppermute(send_east, "lon", eastward)
    from_east = lax.ppermute(send_west, "lon", westward)

    current, partial, noise1 = pl.pallas_call(
        functools.partial(bulk, sizes),
        out_shape=(shape((rows, lats), F32), shape((particles, 128), F32), shape((4 * particles, lats), F32)),
        in_specs=[VMEM, VMEM, VMEM, SMEM, SMEM, VMEM],
        out_specs=(VMEM,) * 3,
        scratch_shapes=[pltpu.VMEM((fields, 5, strip, lats), F32), pltpu.VMEM((fields, strip, lats), F32)],
        compiler_params=pltpu.CompilerParams(vmem_limit_bytes=32 * 1024 * 1024),
        cost_estimate=pl.CostEstimate(flops=30000000, bytes_accessed=4000000, transcendentals=0),
    )(state, noise, courant, diffusion, mixing, maps)

    current, weight = pl.pallas_call(
        functools.partial(correct, sizes),
        out_shape=(shape((rows, lats), F32), shape((particles, 128), F32)),
        in_specs=[VMEM] * 5 + [SMEM, SMEM] + [VMEM] * 5,
        out_specs=(VMEM,) * 2,
        cost_estimate=pl.CostEstimate(flops=1000000, bytes_accessed=1000000, transcendentals=0),
    )(send_east, send_west, from_west, from_east, courant, diffusion, mixing, maps, noise0, noise1, current, partial)

    current = current.reshape(particles, fields, strip, lats)
    received = lax.ppermute(current, "dom", [(0, 1), (1, 0)])
    bit = 1
    while bit < strips:
        weight = weight + lax.ppermute(weight, "lon", [(i, i ^ bit) for i in range(strips)])
        bit *= 2

    new_state = pl.pallas_call(
        functools.partial(assemble, sizes),
        out_shape=shape((particles, fields, strip, lats), F32),
        in_specs=[SMEM, ANY, ANY],
        out_specs=ANY,
        scratch_shapes=[pltpu.SemaphoreType.DMA((particles,))],
        cost_estimate=pl.CostEstimate(flops=0, bytes_accessed=2000000, transcendentals=0),
    )(source, current, received)

    log_weight = prior_weight - jnp.sum(weight, axis=1) / (256.0 * obs_cell.shape[0])
    return new_state, log_weight


def solution(mesh):
    placed = (
        P(("groups", "dom"), None, "lon", None),
        P(None, ("groups", "dom"), None, "lon", None),
        P(None, ("groups", "lon"), None),
        P(),
        P(),
        P(("groups", "dom")),
        P(("groups", "lon")),
        P(("groups", "lon")),
        P("groups"),
    )
    return jax.shard_map(
        local,
        mesh=mesh,
        in_specs=placed,
        out_specs=(P(("groups", "dom"), None, "lon", None), P(("groups", "dom"))),
        check_vma=False,
    )
```

time: 120 us -> 66.6 us (0.55)
  local copies, waits for them, and re-layouts: 50.4 us -> 5.3 us
  Pallas kernels: 0 us -> 41.9 us
  blocking collectives: 21.8 us -> 0 us
  other arithmetic: 20.3 us -> 0.64 us
  between operations: 14.4 us -> 0.73 us
  waiting for transfers between devices: 1.8 us -> 10.8 us
  starting transfers between devices: 10.8 us -> 7.07 us
    pallas_call x0 -> x4, Pallas kernels: none -> 41.9 us  [the longest x1 33.6 us: local(): pl.pallas_call(functools.partial(assemble, sizes), out_shape=shape((parti...]
    slice x17 -> x0, local copies, waits for them, and re-layouts: 23.8 us -> none  [the longest x4 7.6 us: nudge(): noise_now[:, 0].reshape(particles, strip_width * lat_rows)[:, cells]]
    psum x1 -> x0, blocking collectives: 21.8 us -> none  [local(): weight_sum = first_sum + lax.psum(local_sum, 'lon')]
    gather x11 -> x0, local copies, waits for them, and re-layouts: 18.1 us -> none  [the longest x4 6.07 us: nudge(): observed_model = plane[:, cells]]
    scatter-add x2 -> x0, other arithmetic: 11.8 us -> none  [nudge(): plane = plane.at[:, cells].add(push_value)]
    ppermute x4 -> x6, waiting for transfers between devices: 1.79 us -> 10.8 us  [the longest x3 10.8 us: local(): lax.ppermute(weight, 'lon', [(i, i ^ bit) for i in range(strips)])]
    add x6 -> x2, other arithmetic: 6.16 us -> 0.01 us  [local(): weight + lax.ppermute(weight, 'lon', [(i, i ^ bit) for i in range(strips)])]
    another operation x2 -> x0, local copies, waits for them, and re-layouts: 5.66 us -> none
  transfers between devices with their start and end apart: 5 -> 6, of which waited for: 1 -> 3; matrix products, arithmetic and copies ran while one was open for 24% -> 1% of each run, Pallas kernels for 0% -> 4%
where the time goes in v1:
time: 66.6 us; the launch traced here: 66.4 us
  Pallas kernels  41.9 us (63%)
  waiting for transfers between devices  10.8 us (16%)
  starting transfers between devices  7.07 us (11%)
  local copies, waits for them, and re-layouts  5.3 us (8%)
  between operations  0.73 us (1%)
    pallas_call x1, Pallas kernels, local(): pl.pallas_call(functools.partial(assemble, sizes), out_shape=shape((parti...  33.6 us
    ppermute x3, waiting for transfers between devices, local(): lax.ppermute(weight, 'lon', [(i, i ^ bit) for i in range(strips)])  10.8 us
    unnamed x28, local copies, waits for them, and re-layouts  5.3 us
    ppermute x1, starting transfers between devices, local(): from_east = lax.ppermute(send_west, 'lon', westward)  3.11 us
    ppermute x1, starting transfers between devices, local(): from_west = lax.ppermute(send_east, 'lon', eastward)  2.99 us
    pallas_call x1, Pallas kernels, local(): pl.pallas_call(functools.partial(bulk, sizes), out_shape=(shape((rows, la...  2.84 us
    pallas_call x1, Pallas kernels, local(): pl.pallas_call(functools.partial(correct, sizes), out_shape=(shape((rows,...  2.73 us
    pallas_call x1, Pallas kernels, local(): pl.pallas_call(functools.partial(prepare, sizes), out_shape=(packet, pack...  2.7 us
  transfers between devices with their start and end apart: 6, of which 3 were waited for; matrix products, arithmetic and copies ran while one was open for 1% of the time, Pallas kernels for 4%

profile of v1, /device:TPU:0, one launch (start us, length us, event | category | flops | bytes accessed | tf_op | source)
XLA Modules:
  0.0 66.4 jit_solution(12949691237160697237)
XLA Ops:
  0.6 0.0 copy-start
  0.6 0.0 copy-start.1
  0.7 0.0 copy-start.3
  0.7 2.7 %shard_map.104 = (f32[72,256]{1,0:T(8,128)}, f32[72,256]{1,0:T(8,128)}, f32[3,32,256]{2,1,0:T(8,128)}, f32[2,8,256]{2,1,0:T(8,128)}) custom-call(f32[1024,256]{1,0:T(8,128)} %bitcast.5, bf16[2,1024,256]{2,1,0:T(8,128)(2,1)} %bitcast.7, f32[2,32,256]{2,1,0:T(8,128)} %courant.5, f32[4]{0:T(128)} %diffusion.5, f32[4,4]{1,0:T(4,128)} %mixing.5, ...), custom_call_target="tpu_custom_call" | custom-call | flops 1000000 | bytes 2000000 | tf_op jit(solution)/shard_map/pallas_call | solution.py:285
  3.4 0.0 copy-start.6
  3.4 3.0 %collective-permute-start = (f32[72,256]{1,0:T(8,128)}, f32[72,256]{1,0:T(8,128)S(1)}, u32[]{:S(2)}, u32[]{:S(2)}) collective-permute-start(f32[72,256]{1,0:T(8,128)} %get-tuple-element.11.own_east), channel_id=1, source_target_pairs={{0,2},{2,4},{4,6},{6,8},{8,10},{10,12},{12,14},{14,0},{1,3},{3,5},... | collective-permute-start | bytes 221192 | tf_op jit(solution)/shard_map/ppermute | solution.py:295
  6.4 0.0 copy-start.7
  6.4 3.1 %collective-permute-start.1 = (f32[72,256]{1,0:T(8,128)}, f32[72,256]{1,0:T(8,128)S(1)}, u32[]{:S(2)}, u32[]{:S(2)}) collective-permute-start(f32[72,256]{1,0:T(8,128)} %get-tuple-element.12.own_west), channel_id=1, source_target_pairs={{0,14},{2,0},{4,2},{6,4},{8,6},{10,8},{12,10},{14,12},{1,15},{3,1}... | collective-permute-start | bytes 221192 | tf_op jit(solution)/shard_map/ppermute | solution.py:296
  9.5 0.0 copy-done
  9.5 0.0 copy-done.1
  9.5 0.0 copy-done.3
  9.5 0.0 copy-done.6
  9.5 0.0 copy-done.7
  9.5 0.0 copy-start.4
  9.5 0.9 %copy-done.4 = f32[3,32,256]{2,1,0:T(8,128)S(1)} copy-done((f32[3,32,256]{2,1,0:T(8,128)S(1)}, f32[3,32,256]{2,1,0:T(8,128)}, u32[]{:S(2)}) %copy-start.4) | copy-done | bytes 98328
  10.4 2.8 %shard_map.105 = (f32[1024,256]{1,0:T(8,128)S(1)}, f32[8,128]{1,0:T(8,128)S(1)}, f32[32,256]{1,0:T(8,128)S(1)}) custom-call(f32[1024,256]{1,0:T(8,128)S(1)} %bitcast.6, bf16[2,1024,256]{2,1,0:T(8,128)(2,1)S(1)} %bitcast.8, f32[2,32,256]{2,1,0:T(8,128)S(1)} %copy-done.3, f32[4]{0:T(128)S(1)} %copy-done.7, f32[4,4]{1,0:T(4,128)S(1)} %copy-done.6, ...), custom_call_target="tpu_custom_call" | custom-call | flops 30000000 | bytes 4000000 | tf_op jit(solution)/shard_map/pallas_call | solution.py:298
  13.2 0.0 copy-start.2
  13.2 1.0 %copy-done.2 = f32[1024,256]{1,0:T(8,128)} copy-done((f32[1024,256]{1,0:T(8,128)}, f32[1024,256]{1,0:T(8,128)S(1)}, u32[]{:S(2)}) %copy-start.2) | copy-done | bytes 1048600
  14.2 0.0 copy-start.5
  14.2 0.6 copy-done.5
  14.8 0.0 copy-start.8
  14.8 0.6 copy-done.8
  15.4 0.0 collective-permute-done.from_west
  15.4 0.0 copy-start.10
  15.4 0.0 collective-permute-done.1.from_east
  15.4 0.0 copy-start.11
  15.4 0.6 copy-done.10
  16.0 0.0 copy-done.11
  16.1 2.7 %shard_map.106 = (f32[1024,256]{1,0:T(8,128)}, f32[8,128]{1,0:T(8,128)}) custom-call(f32[72,256]{1,0:T(8,128)} %get-tuple-element.11.own_east, f32[72,256]{1,0:T(8,128)} %get-tuple-element.12.own_west, f32[72,256]{1,0:T(8,128)} %copy-done.10, f32[72,256]{1,0:T(8,128)} %copy-done.11, f32[2,32,256]{2,1,0:T(8,128)} %courant.5, f32[4]{0:T(128)} %diffusion.5, ...), custom_call_target="tpu_custom_call" | custom-call | flops 1000000 | bytes 1000000 | tf_op jit(solution)/shard_map/pallas_call | solution.py:308
  18.8 0.0 copy-start.12
  18.8 0.1 collective-permute-start.2
  18.9 0.6 copy-done.12
  19.5 0.0 collective-permute-start.3
  19.5 3.6 %collective-permute-done.3 = f32[8,128]{1,0:T(8,128)S(1)} collective-permute-done((f32[8,128]{1,0:T(8,128)S(1)}, f32[8,128]{1,0:T(8,128)S(1)}, u32[]{:S(2)}, u32[]{:S(2)}) %collective-permute-start.3) | collective-permute-done | bytes 4128 | tf_op jit(solution)/shard_map/ppermute | solution.py:320
  23.1 0.0 collective-permute-start.4
  23.1 3.6 %collective-permute-done.4 = f32[8,128]{1,0:T(8,128)S(1)} collective-permute-done((f32[8,128]{1,0:T(8,128)S(1)}, f32[8,128]{1,0:T(8,128)S(1)}, u32[]{:S(2)}, u32[]{:S(2)}) %collective-permute-start.4) | collective-permute-done | bytes 4128 | tf_op jit(solution)/shard_map/ppermute | solution.py:320
  26.7 0.0 copy-start.13
  26.7 0.9 %collective-permute-start.5 = (f32[8,128]{1,0:T(8,128)S(1)}, f32[8,128]{1,0:T(8,128)S(1)}, u32[]{:S(2)}, u32[]{:S(2)}) collective-permute-start(f32[8,128]{1,0:T(8,128)S(1)} %add.10), channel_id=1, source_target_pairs={{0,8},{2,10},{4,12},{6,14},{8,0},{10,2},{12,4},{14,6},{1,9},{3,11}... | collective-permute-start | bytes 12296 | tf_op jit(solution)/shard_map/ppermute | solution.py:320
  27.6 3.6 %collective-permute-done.5 = f32[8,128]{1,0:T(8,128)S(1)} collective-permute-done((f32[8,128]{1,0:T(8,128)S(1)}, f32[8,128]{1,0:T(8,128)S(1)}, u32[]{:S(2)}, u32[]{:S(2)}) %collective-permute-start.5) | collective-permute-done | bytes 4128 | tf_op jit(solution)/shard_map/ppermute | solution.py:320
  31.2 0.1 add_reduce_fusion
  31.3 0.0 copy-done.13
  31.3 0.5 multiply_subtract_fusion
  31.8 0.0 collective-permute-done.2.received
  31.8 0.0 copy-start.9
  31.8 1.0 %copy-done.9 = f32[8,4,32,256]{3,2,1,0:T(8,128)} copy-done((f32[8,4,32,256]{3,2,1,0:T(8,128)}, f32[8,4,32,256]{3,2,1,0:T(8,128)S(1)}, u32[]{:S(2)}) %copy-start.9) | copy-done | bytes 1048600
  32.8 33.6 %shard_map.107 = f32[8,4,32,256]{3,2,1,0:T(8,128)} custom-call(s32[16]{0:T(128)} %source.1, f32[8,4,32,256]{3,2,1,0:T(8,128)} %bitcast.10, f32[8,4,32,256]{3,2,1,0:T(8,128)} %copy-done.9), custom_call_target="tpu_custom_call" | custom-call | bytes 2000000 | tf_op jit(solution)/shard_map/pallas_call | solution.py:323
  (2 shorter events, 0.0 us)
Async XLA Ops:
  0.6 8.8 %copy-start = (f32[8,4,32,256]{3,2,1,0:T(8,128)S(1)}, f32[8,4,32,256]{3,2,1,0:T(8,128)}, u32[]{:S(2)}) copy-start(f32[8,4,32,256]{3,2,1,0:T(8,128)} %param.9) | copy-start | bytes 3145732
  0.6 8.8 %copy-start.1 = (bf16[2,8,4,32,256]{4,3,2,1,0:T(8,128)(2,1)S(1)}, bf16[2,8,4,32,256]{4,3,2,1,0:T(8,128)(2,1)}, u32[]{:S(2)}) copy-start(bf16[2,8,4,32,256]{4,3,2,1,0:T(8,128)(2,1)} %param.10) | copy-start | bytes 3145732
  0.7 8.8 %copy-start.3 = (f32[2,32,256]{2,1,0:T(8,128)S(1)}, f32[2,32,256]{2,1,0:T(8,128)}, u32[]{:S(2)}) copy-start(f32[2,32,256]{2,1,0:T(8,128)} %courant.5) | copy-start | bytes 196612
  3.4 6.1 %copy-start.6 = (f32[4,4]{1,0:T(4,128)S(1)}, f32[4,4]{1,0:T(4,128)}, u32[]{:S(2)}) copy-start(f32[4,4]{1,0:T(4,128)} %mixing.5) | copy-start | bytes 196
  3.4 12.0 %collective-permute-start = (f32[72,256]{1,0:T(8,128)}, f32[72,256]{1,0:T(8,128)S(1)}, u32[]{:S(2)}, u32[]{:S(2)}) collective-permute-start(f32[72,256]{1,0:T(8,128)} %get-tuple-element.11.own_east), channel_id=1, source_target_pairs={{0,2},{2,4},{4,6},{6,8},{8,10},{10,12},{12,14},{14,0},{1,3},{3,5},... | collective-permute-start | bytes 221192 | tf_op jit(solution)/shard_map/ppermute | solution.py:295
  6.4 3.1 %copy-start.7 = (f32[4]{0:T(128)S(1)}, f32[4]{0:T(128)}, u32[]{:S(2)}) copy-start(f32[4]{0:T(128)} %diffusion.5) | copy-start | bytes 52
  6.4 9.1 %collective-permute-start.1 = (f32[72,256]{1,0:T(8,128)}, f32[72,256]{1,0:T(8,128)S(1)}, u32[]{:S(2)}, u32[]{:S(2)}) collective-permute-start(f32[72,256]{1,0:T(8,128)} %get-tuple-element.12.own_west), channel_id=1, source_target_pairs={{0,14},{2,0},{4,2},{6,4},{8,6},{10,8},{12,10},{14,12},{1,15},{3,1}... | collective-permute-start | bytes 221192 | tf_op jit(solution)/shard_map/ppermute | solution.py:296
  9.5 0.9 %copy-start.4 = (f32[3,32,256]{2,1,0:T(8,128)S(1)}, f32[3,32,256]{2,1,0:T(8,128)}, u32[]{:S(2)}) copy-start(f32[3,32,256]{2,1,0:T(8,128)} %get-tuple-element.13.maps) | copy-start | bytes 294916
  13.2 1.0 %copy-start.2 = (f32[1024,256]{1,0:T(8,128)}, f32[1024,256]{1,0:T(8,128)S(1)}, u32[]{:S(2)}) copy-start(f32[1024,256]{1,0:T(8,128)S(1)} %get-tuple-element.16.current) | copy-start | bytes 3145732
  14.2 0.6 copy-start.5
  14.8 0.6 copy-start.8
  15.4 0.6 copy-start.10
  15.4 0.6 copy-start.11
  18.8 0.7 %copy-start.12 = (f32[8,128]{1,0:T(8,128)S(1)}, f32[8,128]{1,0:T(8,128)}, u32[]{:S(2)}) copy-start(f32[8,128]{1,0:T(8,128)} %get-tuple-element.19) | copy-start | bytes 12292
  18.8 13.0 %collective-permute-start.2 = (f32[8,4,32,256]{3,2,1,0:T(8,128)}, f32[8,4,32,256]{3,2,1,0:T(8,128)S(1)}, u32[]{:S(2)}, u32[]{:S(2)}) collective-permute-start(f32[8,4,32,256]{3,2,1,0:T(8,128)} %bitcast.9), channel_id=1, source_target_pairs={{0,1},{1,0},{2,3},{3,2},{4,5},{5,4},{6,7},{7,6},{8,9},{9,8},{10,11... | collective-permute-start | bytes 3145736 | tf_op jit(solution)/shard_map/ppermute | solution.py:317
  19.5 3.6 %collective-permute-start.3 = (f32[8,128]{1,0:T(8,128)S(1)}, f32[8,128]{1,0:T(8,128)S(1)}, u32[]{:S(2)}, u32[]{:S(2)}) collective-permute-start(f32[8,128]{1,0:T(8,128)S(1)} %copy-done.12), channel_id=1, source_target_pairs={{0,2},{2,0},{4,6},{6,4},{8,10},{10,8},{12,14},{14,12},{1,3},{3,1},... | collective-permute-start | bytes 12296 | tf_op jit(solution)/shard_map/ppermute | solution.py:320
  23.1 3.6 %collective-permute-start.4 = (f32[8,128]{1,0:T(8,128)S(1)}, f32[8,128]{1,0:T(8,128)S(1)}, u32[]{:S(2)}, u32[]{:S(2)}) collective-permute-start(f32[8,128]{1,0:T(8,128)S(1)} %add.9), channel_id=1, source_target_pairs={{0,4},{2,6},{4,0},{6,2},{8,12},{10,14},{12,8},{14,10},{1,5},{3,7},... | collective-permute-start | bytes 12296 | tf_op jit(solution)/shard_map/ppermute | solution.py:320
  26.7 4.6 %copy-start.13 = (f32[8]{0:T(128)S(1)}, f32[8]{0:T(128)}, u32[]{:S(2)}) copy-start(f32[8]{0:T(128)} %param.14) | copy-start | bytes 100
  26.7 4.5 %collective-permute-start.5 = (f32[8,128]{1,0:T(8,128)S(1)}, f32[8,128]{1,0:T(8,128)S(1)}, u32[]{:S(2)}, u32[]{:S(2)}) collective-permute-start(f32[8,128]{1,0:T(8,128)S(1)} %add.10), channel_id=1, source_target_pairs={{0,8},{2,10},{4,12},{6,14},{8,0},{10,2},{12,4},{14,6},{1,9},{3,11}... | collective-permute-start | bytes 12296 | tf_op jit(solution)/shard_map/ppermute | solution.py:320
  31.8 1.0 %copy-start.9 = (f32[8,4,32,256]{3,2,1,0:T(8,128)}, f32[8,4,32,256]{3,2,1,0:T(8,128)S(1)}, u32[]{:S(2)}) copy-start(f32[8,4,32,256]{3,2,1,0:T(8,128)S(1)} %collective-permute-done.2.received) | copy-start | bytes 3145732

commit v2 on v1

--- a/solution.py
+++ b/solution.py
@@ -11,6 +11,7 @@
 VMEM = pl.BlockSpec(memory_space=pltpu.VMEM)
 SMEM = pl.BlockSpec(memory_space=pltpu.SMEM)
 ANY = pl.BlockSpec(memory_space=pl.ANY)
+LIMIT = pltpu.CompilerParams(vmem_limit_bytes=16 * 1024 * 1024)
 BF16 = jnp.bfloat16
 F32 = jnp.float32
 
@@ -287,6 +288,7 @@
         out_shape=(packet, packet, shape((3, strip, lats), F32), shape((2, particles, lats), F32)),
         in_specs=[VMEM, VMEM, VMEM, SMEM, SMEM, VMEM, VMEM],
         out_specs=(VMEM,) * 4,
+        compiler_params=LIMIT,
         cost_estimate=pl.CostEstimate(flops=1000000, bytes_accessed=2000000, transcendentals=0),
     )(state, noise, courant, diffusion, mixing, obs_cell[None], obs_value[None])
 
@@ -301,7 +303,7 @@
         in_specs=[VMEM, VMEM, VMEM, SMEM, SMEM, VMEM],
         out_specs=(VMEM,) * 3,
         scratch_shapes=[pltpu.VMEM((fields, 5, strip, lats), F32), pltpu.VMEM((fields, strip, lats), F32)],
-        compiler_params=pltpu.CompilerParams(vmem_limit_bytes=32 * 1024 * 1024),
+        compiler_params=LIMIT,
         cost_estimate=pl.CostEstimate(flops=30000000, bytes_accessed=4000000, transcendentals=0),
     )(state, noise, courant, diffusion, mixing, maps)
 
@@ -310,22 +312,27 @@
         out_shape=(shape((rows, lats), F32), shape((particles, 128), F32)),
         in_specs=[VMEM] * 5 + [SMEM, SMEM] + [VMEM] * 5,
         out_specs=(VMEM,) * 2,
+        compiler_params=LIMIT,
         cost_estimate=pl.CostEstimate(flops=1000000, bytes_accessed=1000000, transcendentals=0),
     )(send_east, send_west, from_west, from_east, courant, diffusion, mixing, maps, noise0, noise1, current, partial)
 
     current = current.reshape(particles, fields, strip, lats)
     received = lax.ppermute(current, "dom", [(0, 1), (1, 0)])
-    bit = 1
-    while bit < strips:
-        weight = weight + lax.ppermute(weight, "lon", [(i, i ^ bit) for i in range(strips)])
-        bit *= 2
+    done = 1
+    while done < strips:
+        radix = min(8, strips // done)
+        others = [lax.ppermute(weight, "lon", [(i, i ^ (done * step)) for i in range(strips)])
+                  for step in range(1, radix)]
+        weight = sum(others, weight)
+        done *= radix
 
     new_state = pl.pallas_call(
         functools.partial(assemble, sizes),
         out_shape=shape((particles, fields, strip, lats), F32),
-        in_specs=[SMEM, ANY, ANY],
+        in_specs=[SMEM, VMEM, VMEM],
         out_specs=ANY,
         scratch_shapes=[pltpu.SemaphoreType.DMA((particles,))],
+        compiler_params=LIMIT,
         cost_estimate=pl.CostEstimate(flops=0, bytes_accessed=2000000, transcendentals=0),
     )(source, current, received)
 

time: 66.6 us -> 31.7 us (0.48)
  Pallas kernels: 41.9 us -> 6.03 us
  starting transfers between devices: 7.07 us -> 17.3 us
  waiting for transfers between devices: 10.8 us -> 2.67 us
  local copies, waits for them, and re-layouts: 5.3 us -> 4.12 us
    pallas_call x1, Pallas kernels: 33.6 us -> 1.58 us  [local(): pl.pallas_call(functools.partial(assemble, sizes), out_shape=shape((parti...]
    ppermute x3 -> x7, starting transfers between devices: 0.91 us -> 11.1 us  [local(): lax.ppermute(weight, 'lon', [(i, i ^ done * step) for i in range(strips)])]
    ppermute x3 -> x7, waiting for transfers between devices: 10.8 us -> 2.66 us  [local(): lax.ppermute(weight, 'lon', [(i, i ^ done * step) for i in range(strips)])]
    pallas_call x1, Pallas kernels: 2.73 us -> 0.82 us  [local(): pl.pallas_call(functools.partial(correct, sizes), out_shape=(shape((rows,...]
    pallas_call x1, Pallas kernels: 2.7 us -> 0.83 us  [local(): pl.pallas_call(functools.partial(prepare, sizes), out_shape=(packet, pack...]
    unnamed x28 -> x18, local copies, waits for them, and re-layouts: 5.3 us -> 4.12 us
  transfers between devices with their start and end apart: 6 -> 10, of which waited for: 3 -> 4; matrix products, arithmetic and copies ran while one was open for 1% -> 2% of each run, Pallas kernels for 4% -> 9%
where the time goes in v2:
time: 31.7 us; the launch traced here: 31.4 us
  starting transfers between devices  17.3 us (55%)
  Pallas kernels  6.03 us (19%)
  local copies, waits for them, and re-layouts  4.12 us (13%)
  waiting for transfers between devices  2.67 us (8%)
  between operations  0.73 us (2%)
  other arithmetic  0.63 us (2%)
    ppermute x7, starting transfers between devices, local(): lax.ppermute(weight, 'lon', [(i, i ^ done * step) for i in range(strips)])  11.1 us
    unnamed x18, local copies, waits for them, and re-layouts  4.12 us
    ppermute x1, starting transfers between devices, local(): from_east = lax.ppermute(send_west, 'lon', westward)  3.11 us
    ppermute x1, starting transfers between devices, local(): from_west = lax.ppermute(send_east, 'lon', eastward)  2.99 us
    pallas_call x1, Pallas kernels, local(): pl.pallas_call(functools.partial(bulk, sizes), out_shape=(shape((rows, la...  2.8 us
    ppermute x7, waiting for transfers between devices, local(): lax.ppermute(weight, 'lon', [(i, i ^ done * step) for i in range(strips)])  2.66 us
    pallas_call x1, Pallas kernels, local(): pl.pallas_call(functools.partial(assemble, sizes), out_shape=shape((parti...  1.58 us
    pallas_call x1, Pallas kernels, local(): pl.pallas_call(functools.partial(prepare, sizes), out_shape=(packet, pack...  0.83 us
  transfers between devices with their start and end apart: 10, of which 4 were waited for; matrix products, arithmetic and copies ran while one was open for 2% of the time, Pallas kernels for 9%

profile of v2, /device:TPU:0, one launch (start us, length us, event | category | flops | bytes accessed | tf_op | source)
XLA Modules:
  0.0 31.4 jit_solution(17593752906375646699)
XLA Ops:
  0.6 0.0 copy-start.6
  0.6 0.0 copy-start.3
  0.7 0.0 copy-start.4
  0.7 0.0 copy-start.5
  0.7 0.6 %copy-done.6 = f32[256]{0:T(256)S(1)} copy-done((f32[256]{0:T(256)S(1)}, f32[256]{0:T(256)}, u32[]{:S(2)}) %copy-start.6) | copy-done | bytes 1048
  1.3 0.0 copy-done.3
  1.3 0.0 copy-done.4
  1.3 0.0 copy-done.5
  1.4 0.0 copy-start
  1.4 1.2 %copy-done = f32[8,4,32,256]{3,2,1,0:T(8,128)S(1)} copy-done((f32[8,4,32,256]{3,2,1,0:T(8,128)S(1)}, f32[8,4,32,256]{3,2,1,0:T(8,128)}, u32[]{:S(2)}) %copy-start) | copy-done | bytes 1048600
  2.6 0.0 copy-start.1
  2.6 1.2 %copy-done.1 = bf16[2,8,4,32,256]{4,3,2,1,0:T(8,128)(2,1)S(1)} copy-done((bf16[2,8,4,32,256]{4,3,2,1,0:T(8,128)(2,1)S(1)}, bf16[2,8,4,32,256]{4,3,2,1,0:T(8,128)(2,1)}, u32[]{:S(2)}) %copy-start.1) | copy-done | bytes 1048600
  3.8 0.0 copy-start.2
  3.8 0.8 %copy-done.2 = f32[2,32,256]{2,1,0:T(8,128)S(1)} copy-done((f32[2,32,256]{2,1,0:T(8,128)S(1)}, f32[2,32,256]{2,1,0:T(8,128)}, u32[]{:S(2)}) %copy-start.2) | copy-done | bytes 65560
  4.7 0.8 %shard_map.104 = (f32[72,256]{1,0:T(8,128)S(1)}, f32[72,256]{1,0:T(8,128)S(1)}, f32[3,32,256]{2,1,0:T(8,128)S(1)}, f32[2,8,256]{2,1,0:T(8,128)S(1)}) custom-call(f32[1024,256]{1,0:T(8,128)S(1)} %bitcast.5, bf16[2,1024,256]{2,1,0:T(8,128)(2,1)S(1)} %bitcast.7, f32[2,32,256]{2,1,0:T(8,128)S(1)} %copy-done.2, f32[4]{0:T(128)S(1)} %copy-done.4, ...), custom_call_target="tpu_custom_call" | custom-call | flops 1000000 | bytes 2000000 | tf_op jit(solution)/shard_map/pallas_call | solution.py:286
  5.5 3.0 %collective-permute-start = (f32[72,256]{1,0:T(8,128)S(1)}, f32[72,256]{1,0:T(8,128)S(1)}, u32[]{:S(2)}, u32[]{:S(2)}) collective-permute-start(f32[72,256]{1,0:T(8,128)S(1)} %get-tuple-element.11.own_east), channel_id=1, source_target_pairs={{0,2},{2,4},{4,6},{6,8},{8,10},{10,12},{12,14},{14,0},{1,3},{3,5},... | collective-permute-start | bytes 221192 | tf_op jit(solution)/shard_map/ppermute | solution.py:297
  8.5 3.1 %collective-permute-start.1 = (f32[72,256]{1,0:T(8,128)S(1)}, f32[72,256]{1,0:T(8,128)S(1)}, u32[]{:S(2)}, u32[]{:S(2)}) collective-permute-start(f32[72,256]{1,0:T(8,128)S(1)} %get-tuple-element.12.own_west), channel_id=1, source_target_pairs={{0,14},{2,0},{4,2},{6,4},{8,6},{10,8},{12,10},{14,12},{1,15},{3,1}... | collective-permute-start | bytes 221192 | tf_op jit(solution)/shard_map/ppermute | solution.py:298
  11.6 2.8 %shard_map.105 = (f32[1024,256]{1,0:T(8,128)S(1)}, f32[8,128]{1,0:T(8,128)S(1)}, f32[32,256]{1,0:T(8,128)S(1)}) custom-call(f32[1024,256]{1,0:T(8,128)S(1)} %bitcast.6, bf16[2,1024,256]{2,1,0:T(8,128)(2,1)S(1)} %bitcast.8, f32[2,32,256]{2,1,0:T(8,128)S(1)} %copy-done.2, f32[4]{0:T(128)S(1)} %copy-done.4, f32[4,4]{1,0:T(4,128)S(1)} %copy-done.3, ...), custom_call_target="tpu_custom_call" | custom-call | flops 30000000 | bytes 4000000 | tf_op jit(solution)/shard_map/pallas_call | solution.py:300
  14.4 0.0 collective-permute-done.from_west
  14.4 0.0 collective-permute-done.1.from_east
  14.4 0.8 %shard_map.106 = (f32[1024,256]{1,0:T(8,128)S(1)}, f32[8,128]{1,0:T(8,128)S(1)}) custom-call(f32[72,256]{1,0:T(8,128)S(1)} %get-tuple-element.11.own_east, f32[72,256]{1,0:T(8,128)S(1)} %get-tuple-element.12.own_west, f32[72,256]{1,0:T(8,128)S(1)} %collective-permute-done.from_west, f32[72,256]{1,0:T(8,128)S(1)} %collective-permute-done.1.from_east, ...), custom_call_target="tpu_custom_call" | custom-call | flops 1000000 | bytes 1000000 | tf_op jit(solution)/shard_map/pallas_call | solution.py:310
  15.2 0.1 collective-permute-start.2
  15.3 0.0 copy-start.8
  15.3 4.3 %collective-permute-start.9 = (f32[8,128]{1,0:T(8,128)S(1)}, f32[8,128]{1,0:T(8,128)S(1)}, u32[]{:S(2)}, u32[]{:S(2)}) collective-permute-start(f32[8,128]{1,0:T(8,128)S(1)} %get-tuple-element.19), channel_id=1, source_target_pairs={{0,14},{2,12},{4,10},{6,8},{8,6},{10,4},{12,2},{14,0},{1,15},{3,13... | collective-permute-start | bytes 12296 | tf_op jit(solution)/shard_map/ppermute | solution.py:324
  19.6 0.0 collective-permute-start.8
  19.6 0.4 %collective-permute-start.7 = (f32[8,128]{1,0:T(8,128)S(1)}, f32[8,128]{1,0:T(8,128)S(1)}, u32[]{:S(2)}, u32[]{:S(2)}) collective-permute-start(f32[8,128]{1,0:T(8,128)S(1)} %get-tuple-element.19), channel_id=1, source_target_pairs={{0,10},{2,8},{4,14},{6,12},{8,2},{10,0},{12,6},{14,4},{1,11},{3,9}... | collective-permute-start | bytes 12296 | tf_op jit(solution)/shard_map/ppermute | solution.py:324
  20.0 3.1 %collective-permute-start.6 = (f32[8,128]{1,0:T(8,128)S(1)}, f32[8,128]{1,0:T(8,128)S(1)}, u32[]{:S(2)}, u32[]{:S(2)}) collective-permute-start(f32[8,128]{1,0:T(8,128)S(1)} %get-tuple-element.19), channel_id=1, source_target_pairs={{0,8},{2,10},{4,12},{6,14},{8,0},{10,2},{12,4},{14,6},{1,9},{3,11}... | collective-permute-start | bytes 12296 | tf_op jit(solution)/shard_map/ppermute | solution.py:324
  23.0 0.0 collective-permute-done.9
  23.0 1.9 %collective-permute-start.5 = (f32[8,128]{1,0:T(8,128)S(1)}, f32[8,128]{1,0:T(8,128)S(1)}, u32[]{:S(2)}, u32[]{:S(2)}) collective-permute-start(f32[8,128]{1,0:T(8,128)S(1)} %get-tuple-element.19), channel_id=1, source_target_pairs={{0,6},{2,4},{4,2},{6,0},{8,14},{10,12},{12,10},{14,8},{1,7},{3,5},... | collective-permute-start | bytes 12296 | tf_op jit(solution)/shard_map/ppermute | solution.py:324
  24.9 0.1 collective-permute-done.8
  25.0 0.5 %collective-permute-start.4 = (f32[8,128]{1,0:T(8,128)S(1)}, f32[8,128]{1,0:T(8,128)S(1)}, u32[]{:S(2)}, u32[]{:S(2)}) collective-permute-start(f32[8,128]{1,0:T(8,128)S(1)} %get-tuple-element.19), channel_id=1, source_target_pairs={{0,4},{2,6},{4,0},{6,2},{8,12},{10,14},{12,8},{14,10},{1,5},{3,7},... | collective-permute-start | bytes 12296 | tf_op jit(solution)/shard_map/ppermute | solution.py:324
  25.5 0.0 collective-permute-done.7
  25.5 1.1 %collective-permute-start.3 = (f32[8,128]{1,0:T(8,128)S(1)}, f32[8,128]{1,0:T(8,128)S(1)}, u32[]{:S(2)}, u32[]{:S(2)}) collective-permute-start(f32[8,128]{1,0:T(8,128)S(1)} %get-tuple-element.19), channel_id=1, source_target_pairs={{0,2},{2,0},{4,6},{6,4},{8,10},{10,8},{12,14},{14,12},{1,3},{3,1},... | collective-permute-start | bytes 12296 | tf_op jit(solution)/shard_map/ppermute | solution.py:324
  26.5 0.0 collective-permute-done.6
  26.5 1.0 %collective-permute-done.5 = f32[8,128]{1,0:T(8,128)S(1)} collective-permute-done((f32[8,128]{1,0:T(8,128)S(1)}, f32[8,128]{1,0:T(8,128)S(1)}, u32[]{:S(2)}, u32[]{:S(2)}) %collective-permute-start.5) | collective-permute-done | bytes 4128 | tf_op jit(solution)/shard_map/ppermute | solution.py:324
  27.5 1.1 %collective-permute-done.4 = f32[8,128]{1,0:T(8,128)S(1)} collective-permute-done((f32[8,128]{1,0:T(8,128)S(1)}, f32[8,128]{1,0:T(8,128)S(1)}, u32[]{:S(2)}, u32[]{:S(2)}) %collective-permute-start.4) | collective-permute-done | bytes 4128 | tf_op jit(solution)/shard_map/ppermute | solution.py:324
  28.6 0.5 %collective-permute-done.3 = f32[8,128]{1,0:T(8,128)S(1)} collective-permute-done((f32[8,128]{1,0:T(8,128)S(1)}, f32[8,128]{1,0:T(8,128)S(1)}, u32[]{:S(2)}, u32[]{:S(2)}) %collective-permute-start.3) | collective-permute-done | bytes 4128 | tf_op jit(solution)/shard_map/ppermute | solution.py:324
  29.1 0.1 add_reduce_fusion
  29.2 0.0 copy-done.8
  29.2 0.0 copy-start.7
  29.2 0.5 %multiply_subtract_fusion = f32[8]{0:T(128)} fusion(f32[8]{0:T(128)S(1)} %copy-done.8, f32[8]{0:T(128)S(1)} %add_reduce_fusion), kind=kLoop, calls=%fused_computation.1 | loop fusion | flops 16 | bytes 96 | tf_op jit(solution)/shard_map/sub | solution.py:339
  29.7 0.0 collective-permute-done.2.received
  29.7 0.1 copy-done.7
  29.9 1.6 %shard_map.107 = f32[8,4,32,256]{3,2,1,0:T(8,128)} custom-call(s32[16]{0:T(128)S(1)} %copy-done.7, f32[8,4,32,256]{3,2,1,0:T(8,128)S(1)} %bitcast.10, f32[8,4,32,256]{3,2,1,0:T(8,128)S(1)} %collective-permute-done.2.received), custom_call_target="tpu_custom_call" | custom-call | bytes 2000000 | tf_op jit(solution)/shard_map/pallas_call | solution.py:329
Async XLA Ops:
  0.6 0.7 %copy-start.6 = (f32[256]{0:T(256)S(1)}, f32[256]{0:T(256)}, u32[]{:S(2)}) copy-start(f32[256]{0:T(256)} %param.16) | copy-start | bytes 3076
  0.6 0.7 %copy-start.3 = (f32[4,4]{1,0:T(4,128)S(1)}, f32[4,4]{1,0:T(4,128)}, u32[]{:S(2)}) copy-start(f32[4,4]{1,0:T(4,128)} %mixing.5) | copy-start | bytes 196
  0.7 0.7 %copy-start.4 = (f32[4]{0:T(128)S(1)}, f32[4]{0:T(128)}, u32[]{:S(2)}) copy-start(f32[4]{0:T(128)} %diffusion.5) | copy-start | bytes 52
  0.7 0.7 %copy-start.5 = (s32[256]{0:T(256)S(1)}, s32[256]{0:T(256)}, u32[]{:S(2)}) copy-start(s32[256]{0:T(256)} %param.15) | copy-start | bytes 3076
  1.4 1.2 %copy-start = (f32[8,4,32,256]{3,2,1,0:T(8,128)S(1)}, f32[8,4,32,256]{3,2,1,0:T(8,128)}, u32[]{:S(2)}) copy-start(f32[8,4,32,256]{3,2,1,0:T(8,128)} %param.9) | copy-start | bytes 3145732
  2.6 1.2 %copy-start.1 = (bf16[2,8,4,32,256]{4,3,2,1,0:T(8,128)(2,1)S(1)}, bf16[2,8,4,32,256]{4,3,2,1,0:T(8,128)(2,1)}, u32[]{:S(2)}) copy-start(bf16[2,8,4,32,256]{4,3,2,1,0:T(8,128)(2,1)} %param.10) | copy-start | bytes 3145732
  3.8 0.8 %copy-start.2 = (f32[2,32,256]{2,1,0:T(8,128)S(1)}, f32[2,32,256]{2,1,0:T(8,128)}, u32[]{:S(2)}) copy-start(f32[2,32,256]{2,1,0:T(8,128)} %courant.5) | copy-start | bytes 196612
  5.5 8.9 %collective-permute-start = (f32[72,256]{1,0:T(8,128)S(1)}, f32[72,256]{1,0:T(8,128)S(1)}, u32[]{:S(2)}, u32[]{:S(2)}) collective-permute-start(f32[72,256]{1,0:T(8,128)S(1)} %get-tuple-element.11.own_east), channel_id=1, source_target_pairs={{0,2},{2,4},{4,6},{6,8},{8,10},{10,12},{12,14},{14,0},{1,3},{3,5},... | collective-permute-start | bytes 221192 | tf_op jit(solution)/shard_map/ppermute | solution.py:297
  8.5 5.9 %collective-permute-start.1 = (f32[72,256]{1,0:T(8,128)S(1)}, f32[72,256]{1,0:T(8,128)S(1)}, u32[]{:S(2)}, u32[]{:S(2)}) collective-permute-start(f32[72,256]{1,0:T(8,128)S(1)} %get-tuple-element.12.own_west), channel_id=1, source_target_pairs={{0,14},{2,0},{4,2},{6,4},{8,6},{10,8},{12,10},{14,12},{1,15},{3,1}... | collective-permute-start | bytes 221192 | tf_op jit(solution)/shard_map/ppermute | solution.py:298
  15.2 14.5 %collective-permute-start.2 = (f32[8,4,32,256]{3,2,1,0:T(8,128)S(1)}, f32[8,4,32,256]{3,2,1,0:T(8,128)S(1)}, u32[]{:S(2)}, u32[]{:S(2)}) collective-permute-start(f32[8,4,32,256]{3,2,1,0:T(8,128)S(1)} %bitcast.9), channel_id=1, source_target_pairs={{0,1},{1,0},{2,3},{3,2},{4,5},{5,4},{6,7},{7,6},{8,9},{9,8},{10,11... | collective-permute-start | bytes 3145736 | tf_op jit(solution)/shard_map/ppermute | solution.py:320
  15.3 13.9 %copy-start.8 = (f32[8]{0:T(128)S(1)}, f32[8]{0:T(128)}, u32[]{:S(2)}) copy-start(f32[8]{0:T(128)} %param.14) | copy-start | bytes 100
  15.3 7.7 %collective-permute-start.9 = (f32[8,128]{1,0:T(8,128)S(1)}, f32[8,128]{1,0:T(8,128)S(1)}, u32[]{:S(2)}, u32[]{:S(2)}) collective-permute-start(f32[8,128]{1,0:T(8,128)S(1)} %get-tuple-element.19), channel_id=1, source_target_pairs={{0,14},{2,12},{4,10},{6,8},{8,6},{10,4},{12,2},{14,0},{1,15},{3,13... | collective-permute-start | bytes 12296 | tf_op jit(solution)/shard_map/ppermute | solution.py:324
  19.6 5.4 %collective-permute-start.8 = (f32[8,128]{1,0:T(8,128)S(1)}, f32[8,128]{1,0:T(8,128)S(1)}, u32[]{:S(2)}, u32[]{:S(2)}) collective-permute-start(f32[8,128]{1,0:T(8,128)S(1)} %get-tuple-element.19), channel_id=1, source_target_pairs={{0,12},{2,14},{4,8},{6,10},{8,4},{10,6},{12,0},{14,2},{1,13},{3,15... | collective-permute-start | bytes 12296 | tf_op jit(solution)/shard_map/ppermute | solution.py:324
  19.6 5.9 %collective-permute-start.7 = (f32[8,128]{1,0:T(8,128)S(1)}, f32[8,128]{1,0:T(8,128)S(1)}, u32[]{:S(2)}, u32[]{:S(2)}) collective-permute-start(f32[8,128]{1,0:T(8,128)S(1)} %get-tuple-element.19), channel_id=1, source_target_pairs={{0,10},{2,8},{4,14},{6,12},{8,2},{10,0},{12,6},{14,4},{1,11},{3,9}... | collective-permute-start | bytes 12296 | tf_op jit(solution)/shard_map/ppermute | solution.py:324
  20.0 6.6 %collective-permute-start.6 = (f32[8,128]{1,0:T(8,128)S(1)}, f32[8,128]{1,0:T(8,128)S(1)}, u32[]{:S(2)}, u32[]{:S(2)}) collective-permute-start(f32[8,128]{1,0:T(8,128)S(1)} %get-tuple-element.19), channel_id=1, source_target_pairs={{0,8},{2,10},{4,12},{6,14},{8,0},{10,2},{12,4},{14,6},{1,9},{3,11}... | collective-permute-start | bytes 12296 | tf_op jit(solution)/shard_map/ppermute | solution.py:324
  23.0 4.5 %collective-permute-start.5 = (f32[8,128]{1,0:T(8,128)S(1)}, f32[8,128]{1,0:T(8,128)S(1)}, u32[]{:S(2)}, u32[]{:S(2)}) collective-permute-start(f32[8,128]{1,0:T(8,128)S(1)} %get-tuple-element.19), channel_id=1, source_target_pairs={{0,6},{2,4},{4,2},{6,0},{8,14},{10,12},{12,10},{14,8},{1,7},{3,5},... | collective-permute-start | bytes 12296 | tf_op jit(solution)/shard_map/ppermute | solution.py:324
  25.0 3.6 %collective-permute-start.4 = (f32[8,128]{1,0:T(8,128)S(1)}, f32[8,128]{1,0:T(8,128)S(1)}, u32[]{:S(2)}, u32[]{:S(2)}) collective-permute-start(f32[8,128]{1,0:T(8,128)S(1)} %get-tuple-element.19), channel_id=1, source_target_pairs={{0,4},{2,6},{4,0},{6,2},{8,12},{10,14},{12,8},{14,10},{1,5},{3,7},... | collective-permute-start | bytes 12296 | tf_op jit(solution)/shard_map/ppermute | solution.py:324
  25.5 3.6 %collective-permute-start.3 = (f32[8,128]{1,0:T(8,128)S(1)}, f32[8,128]{1,0:T(8,128)S(1)}, u32[]{:S(2)}, u32[]{:S(2)}) collective-permute-start(f32[8,128]{1,0:T(8,128)S(1)} %get-tuple-element.19), channel_id=1, source_target_pairs={{0,2},{2,0},{4,6},{6,4},{8,10},{10,8},{12,14},{14,12},{1,3},{3,1},... | collective-permute-start | bytes 12296 | tf_op jit(solution)/shard_map/ppermute | solution.py:324
  29.2 0.7 %copy-start.7 = (s32[16]{0:T(128)S(1)}, s32[16]{0:T(128)}, u32[]{:S(2)}) copy-start(s32[16]{0:T(128)} %source.1) | copy-start | bytes 196

commit v3 on v2

--- a/solution.py
+++ b/solution.py
@@ -11,6 +11,7 @@
 VMEM = pl.BlockSpec(memory_space=pltpu.VMEM)
 SMEM = pl.BlockSpec(memory_space=pltpu.SMEM)
 ANY = pl.BlockSpec(memory_space=pl.ANY)
+HBM = pl.BlockSpec(memory_space=pltpu.HBM)
 LIMIT = pltpu.CompilerParams(vmem_limit_bytes=16 * 1024 * 1024)
 BF16 = jnp.bfloat16
 F32 = jnp.float32
@@ -59,17 +60,30 @@
 
 
 def gather_rows(ref, first, stride, count):
-    sub = lax.broadcasted_iota(jnp.int32, (count, ref.shape[1]), 0)
+    return stack_rows([ref[pl.ds(first + p * stride, 1), :] for p in range(count)])
+
+
+def stack_rows(rows):
+    sub = lax.broadcasted_iota(jnp.int32, (len(rows), rows[0].shape[1]), 0)
     out = None
-    for p in range(count):
-        row = jnp.broadcast_to(ref[pl.ds(first + p * stride, 1), :], sub.shape)
+    for p, row in enumerate(rows):
+        row = jnp.broadcast_to(row, sub.shape)
         out = row if out is None else jnp.where(sub == p, row, out)
     return out
 
 
-def prepare(sizes, state, noise, courant, diffusion, mixing, cell, value,
-            send_east, send_west, maps, noise_rows):
+def prepare(sizes, state_hbm, noise_hbm, courant_hbm, diffusion_hbm, mixing_hbm, cell_hbm, value_hbm,
+            send_east, send_west, maps, noise_rows,
+            low, high, noise, courant, diffusion, mixing, cell, value, sems):
     particles, fields, strip, lats, strips = sizes
+    copies = [pltpu.make_async_copy(source, target, sems.at[k]) for k, (source, target) in enumerate((
+        (cell_hbm, cell), (value_hbm, value), (noise_hbm.at[0], noise), (state_hbm.at[:, :8], low),
+        (state_hbm.at[:, strip - 8:], high), (courant_hbm, courant), (diffusion_hbm, diffusion),
+        (mixing_hbm, mixing)))]
+    for copy in copies:
+        copy.start()
+    copies[0].wait()
+    copies[1].wait()
     x0 = lax.axis_index("lon") * strip
     shift = lats.bit_length() - 1
     local_cell = cell[...] - x0 * lats
@@ -78,13 +92,13 @@
     count = cell.shape[1]
     here = lax.broadcasted_iota(jnp.int32, (strip, count), 0) == obs_lon
     val = value[...]
-    high = val.astype(BF16)
-    rest = val - high.astype(F32)
-    mid = rest.astype(BF16)
-    low = (rest - mid.astype(F32)).astype(BF16)
+    val_high = val.astype(BF16)
+    rest = val - val_high.astype(F32)
+    val_mid = rest.astype(BF16)
+    val_low = (rest - val_mid.astype(F32)).astype(BF16)
     zero = jnp.zeros((strip, count), F32)
     parts = [jnp.where(here, 1.0, zero)]
-    parts += [jnp.where(here, p.astype(F32), zero) for p in (high, mid, low)]
+    parts += [jnp.where(here, p.astype(F32), zero) for p in (val_high, val_mid, val_low)]
     left = jnp.concatenate(parts, 0).astype(BF16)
     right = (lax.broadcasted_iota(jnp.int32, (lats, count), 0) == obs_lat).astype(F32).astype(BF16)
     dense = lax.dot_general(left, right, (((1,), (1,)), ((), ())), preferred_element_type=F32)
@@ -99,14 +113,23 @@
     maps[2] = target
 
     kinds = [(f, x) for x in (0, strip - 1) for f in range(fields)]
-    pick = pick_rows(kinds, particles, fields, strip, len(kinds) * particles, noise.shape[1])
-    rows = jnp.dot(pick, noise[0], preferred_element_type=F32)
+    pick = pick_rows(kinds, particles, fields, strip, len(kinds) * particles, noise.shape[0])
+    copies[2].wait()
+    rows = jnp.dot(pick, noise[...], preferred_element_type=F32)
     noise_rows[0] = rows[:particles]
     noise_rows[1] = rows[fields * particles:(fields + 1) * particles]
 
+    for copy in copies[3:]:
+        copy.wait()
+
     def edge(x, inner, out, base):
-        here = [gather_rows(state, f * strip + x, fields * strip, particles) for f in range(fields)]
-        beside = [gather_rows(state, f * strip + inner, fields * strip, particles) for f in range(fields)]
+        tile, first = (low, 0) if x < 8 else (high, strip - 8)
+
+        def rows_at(f, place):
+            return stack_rows([tile[p * fields + f, place:place + 1] for p in range(particles)])
+
+        here = [rows_at(f, x - first) for f in range(fields)]
+        beside = [rows_at(f, inner - first) for f in range(fields)]
         for f in range(fields):
             centre, east, west, to_north, to_south = coefficients(
                 courant[0, x:x + 1], courant[1, x:x + 1], diffusion[f], mixing[f, f])
@@ -286,11 +309,22 @@
     send_east, send_west, maps, noise0 = pl.pallas_call(
         functools.partial(prepare, sizes),
         out_shape=(packet, packet, shape((3, strip, lats), F32), shape((2, particles, lats), F32)),
-        in_specs=[VMEM, VMEM, VMEM, SMEM, SMEM, VMEM, VMEM],
+        in_specs=[HBM] * 7,
         out_specs=(VMEM,) * 4,
+        scratch_shapes=[
+            pltpu.VMEM((particles * fields, 8, lats), F32),
+            pltpu.VMEM((particles * fields, 8, lats), F32),
+            pltpu.VMEM((rows, lats), BF16),
+            pltpu.VMEM(courant.shape, F32),
+            pltpu.SMEM(diffusion.shape, F32),
+            pltpu.SMEM(mixing.shape, F32),
+            pltpu.VMEM((1,) + obs_cell.shape, jnp.int32),
+            pltpu.VMEM((1,) + obs_value.shape, F32),
+            pltpu.SemaphoreType.DMA((8,)),
+        ],
         compiler_params=LIMIT,
         cost_estimate=pl.CostEstimate(flops=1000000, bytes_accessed=2000000, transcendentals=0),
-    )(state, noise, courant, diffusion, mixing, obs_cell[None], obs_value[None])
+    )(state.reshape(particles * fields, strip, lats), noise, courant, diffusion, mixing, obs_cell[None], obs_value[None])
 
     eastward = [(i, (i + 1) % strips) for i in range(strips)]
     westward = [(i, (i - 1) % strips) for i in range(strips)]
@@ -318,13 +352,7 @@
 
     current = current.reshape(particles, fields, strip, lats)
     received = lax.ppermute(current, "dom", [(0, 1), (1, 0)])
-    done = 1
-    while done < strips:
-        radix = min(8, strips // done)
-        others = [lax.ppermute(weight, "lon", [(i, i ^ (done * step)) for i in range(strips)])
-                  for step in range(1, radix)]
-        weight = sum(others, weight)
-        done *= radix
+    weights = lax.all_to_all(jnp.broadcast_to(weight[None], (strips, particles, 128)), "lon", 0, 0)
 
     new_state = pl.pallas_call(
         functools.partial(assemble, sizes),
@@ -336,7 +364,7 @@
         cost_estimate=pl.CostEstimate(flops=0, bytes_accessed=2000000, transcendentals=0),
     )(source, current, received)
 
-    log_weight = prior_weight - jnp.sum(weight, axis=1) / (256.0 * obs_cell.shape[0])
+    log_weight = prior_weight - jnp.sum(weights, axis=(0, 2)) / (256.0 * obs_cell.shape[0])
     return new_state, log_weight
 
 

time: 31.7 us -> 30.6 us (0.965)
  blocking collectives: 0 us -> 12 us
  starting transfers between devices: 17.3 us -> 6.17 us
  waiting for transfers between devices: 2.67 us -> 0.02 us
  local copies, waits for them, and re-layouts: 4.12 us -> 4.66 us
    all_to_all x0 -> x1, blocking collectives: none -> 12 us  [local(): lax.all_to_all(jnp.broadcast_to(weight[None], (strips, particles, 128)),...]
    ppermute x7 -> x0, starting transfers between devices: 11.1 us -> none  [local(): lax.ppermute(weight, 'lon', [(i, i ^ done * step) for i in range(strips)])]
    ppermute x7 -> x0, waiting for transfers between devices: 2.66 us -> none  [local(): lax.ppermute(weight, 'lon', [(i, i ^ done * step) for i in range(strips)])]
    unnamed x18, local copies, waits for them, and re-layouts: 4.12 us -> 4.65 us
  transfers between devices with their start and end apart: 10 -> 3, of which waited for: 4 -> 0; matrix products, arithmetic and copies ran while one was open for 2% -> 2% of each run, Pallas kernels for 9% -> 9%
where the time goes in v3:
time: 30.6 us; the launch traced here: 30.3 us
  blocking collectives  12 us (39%)
  starting transfers between devices  6.17 us (20%)
  Pallas kernels  6.14 us (20%)
  local copies, waits for them, and re-layouts  4.66 us (15%)
  between operations  0.72 us (2%)
  other arithmetic  0.64 us (2%)
    all_to_all x1, blocking collectives, local(): lax.all_to_all(jnp.broadcast_to(weight[None], (strips, particles, 128)),...  12 us
    unnamed x18, local copies, waits for them, and re-layouts  4.65 us
    ppermute x1, starting transfers between devices, local(): from_east = lax.ppermute(send_west, 'lon', westward)  3.1 us
    ppermute x1, starting transfers between devices, local(): from_west = lax.ppermute(send_east, 'lon', eastward)  2.99 us
    pallas_call x1, Pallas kernels, local(): pl.pallas_call(functools.partial(bulk, sizes), out_shape=(shape((rows, la...  2.8 us
    pallas_call x1, Pallas kernels, local(): pl.pallas_call(functools.partial(assemble, sizes), out_shape=shape((parti...  1.58 us
    pallas_call x1, Pallas kernels, local(): pl.pallas_call(functools.partial(prepare, sizes), out_shape=(packet, pack...  0.94 us
    pallas_call x1, Pallas kernels, local(): pl.pallas_call(functools.partial(correct, sizes), out_shape=(shape((rows,...  0.83 us
  transfers between devices with their start and end apart: 3, of which 0 were waited for; matrix products, arithmetic and copies ran while one was open for 2% of the time, Pallas kernels for 9%

profile of v3, /device:TPU:0, one launch (start us, length us, event | category | flops | bytes accessed | tf_op | source)
XLA Modules:
  0.0 30.3 jit_solution(15658891661772885312)
XLA Ops:
  0.6 0.0 copy-start.6
  0.6 0.0 copy-start.3
  0.7 0.0 copy-start.4
  0.7 0.0 copy-start.5
  0.7 0.6 %copy-done.6 = f32[256]{0:T(256)S(1)} copy-done((f32[256]{0:T(256)S(1)}, f32[256]{0:T(256)}, u32[]{:S(2)}) %copy-start.6) | copy-done | bytes 1048
  1.3 0.0 copy-done.3
  1.3 0.0 copy-done.4
  1.3 0.0 copy-done.5
  1.4 0.0 copy-start
  1.4 1.2 %copy-done = f32[8,4,32,256]{3,2,1,0:T(8,128)S(1)} copy-done((f32[8,4,32,256]{3,2,1,0:T(8,128)S(1)}, f32[8,4,32,256]{3,2,1,0:T(8,128)}, u32[]{:S(2)}) %copy-start) | copy-done | bytes 1048600
  2.6 0.0 copy-start.1
  2.6 1.2 %copy-done.1 = bf16[2,8,4,32,256]{4,3,2,1,0:T(8,128)(2,1)S(1)} copy-done((bf16[2,8,4,32,256]{4,3,2,1,0:T(8,128)(2,1)S(1)}, bf16[2,8,4,32,256]{4,3,2,1,0:T(8,128)(2,1)}, u32[]{:S(2)}) %copy-start.1) | copy-done | bytes 1048600
  3.8 0.0 copy-start.2
  3.8 0.8 %copy-done.2 = f32[2,32,256]{2,1,0:T(8,128)S(1)} copy-done((f32[2,32,256]{2,1,0:T(8,128)S(1)}, f32[2,32,256]{2,1,0:T(8,128)}, u32[]{:S(2)}) %copy-start.2) | copy-done | bytes 65560
  4.7 0.9 %shard_map.104 = (f32[72,256]{1,0:T(8,128)S(1)}, f32[72,256]{1,0:T(8,128)S(1)}, f32[3,32,256]{2,1,0:T(8,128)S(1)}, f32[2,8,256]{2,1,0:T(8,128)S(1)}) custom-call(f32[32,32,256]{2,1,0:T(8,128)S(1)} %bitcast.6, bf16[2,1024,256]{2,1,0:T(8,128)(2,1)S(1)} %bitcast.8, f32[2,32,256]{2,1,0:T(8,128)S(1)} %copy-done.2, f32[4]{0:T(128)S(1)} %copy-done.4, ...), custom_call_target="tpu_custom_call" | custom-call | flops 1000000 | bytes 2000000 | tf_op jit(solution)/shard_map/pallas_call | solution.py:309
  5.6 3.0 %collective-permute-start = (f32[72,256]{1,0:T(8,128)S(1)}, f32[72,256]{1,0:T(8,128)S(1)}, u32[]{:S(2)}, u32[]{:S(2)}) collective-permute-start(f32[72,256]{1,0:T(8,128)S(1)} %get-tuple-element.11.own_east), channel_id=1, source_target_pairs={{0,2},{2,4},{4,6},{6,8},{8,10},{10,12},{12,14},{14,0},{1,3},{3,5},... | collective-permute-start | bytes 221192 | tf_op jit(solution)/shard_map/ppermute | solution.py:331
  8.6 3.1 %collective-permute-start.1 = (f32[72,256]{1,0:T(8,128)S(1)}, f32[72,256]{1,0:T(8,128)S(1)}, u32[]{:S(2)}, u32[]{:S(2)}) collective-permute-start(f32[72,256]{1,0:T(8,128)S(1)} %get-tuple-element.12.own_west), channel_id=1, source_target_pairs={{0,14},{2,0},{4,2},{6,4},{8,6},{10,8},{12,10},{14,12},{1,15},{3,1}... | collective-permute-start | bytes 221192 | tf_op jit(solution)/shard_map/ppermute | solution.py:332
  11.7 2.8 %shard_map.105 = (f32[1024,256]{1,0:T(8,128)S(1)}, f32[8,128]{1,0:T(8,128)S(1)}, f32[32,256]{1,0:T(8,128)S(1)}) custom-call(f32[1024,256]{1,0:T(8,128)S(1)} %bitcast.7, bf16[2,1024,256]{2,1,0:T(8,128)(2,1)S(1)} %bitcast.9, f32[2,32,256]{2,1,0:T(8,128)S(1)} %copy-done.2, f32[4]{0:T(128)S(1)} %copy-done.4, f32[4,4]{1,0:T(4,128)S(1)} %copy-done.3, ...), custom_call_target="tpu_custom_call" | custom-call | flops 30000000 | bytes 4000000 | tf_op jit(solution)/shard_map/pallas_call | solution.py:334
  14.5 0.0 collective-permute-done.from_west
  14.5 0.0 collective-permute-done.1.from_east
  14.5 0.8 %shard_map.106 = (f32[1024,256]{1,0:T(8,128)S(1)}, f32[8,128]{1,0:T(8,128)S(1)}) custom-call(f32[72,256]{1,0:T(8,128)S(1)} %get-tuple-element.11.own_east, f32[72,256]{1,0:T(8,128)S(1)} %get-tuple-element.12.own_west, f32[72,256]{1,0:T(8,128)S(1)} %collective-permute-done.from_west, f32[72,256]{1,0:T(8,128)S(1)} %collective-permute-done.1.from_east, ...), custom_call_target="tpu_custom_call" | custom-call | flops 1000000 | bytes 1000000 | tf_op jit(solution)/shard_map/pallas_call | solution.py:344
  15.3 0.1 collective-permute-start.2
  15.4 12.0 %all_to_all.5 = f32[8,8,128]{2,1,0:T(8,128)S(1)} all-to-all(f32[8,8,128]{2,1,0:T(8,128)S(1)} %broadcast_in_dim.14), channel_id=1, replica_groups=mesh['groups'=2,'lon'=8,'dom'=2] {'lon'}, dimensions={0} | all-to-all | bytes 65536 | tf_op jit(solution)/shard_map/all_to_all | solution.py:355
  27.4 0.0 copy-start.8
  27.4 0.1 reduce_sum.9
  27.5 0.5 %copy-done.8 = f32[8]{0:T(128)S(1)} copy-done((f32[8]{0:T(128)S(1)}, f32[8]{0:T(128)}, u32[]{:S(2)}) %copy-start.8) | copy-done | bytes 56
  28.1 0.0 copy-start.7
  28.1 0.5 %multiply_subtract_fusion = f32[8]{0:T(128)} fusion(f32[8]{0:T(128)S(1)} %copy-done.8, f32[8]{0:T(128)S(1)} %reduce_sum.9), kind=kLoop, calls=%fused_computation | loop fusion | flops 16 | bytes 96 | tf_op jit(solution)/shard_map/sub | solution.py:367
  28.6 0.0 collective-permute-done.2.received
  28.6 0.1 copy-done.7
  28.7 1.6 %shard_map.107 = f32[8,4,32,256]{3,2,1,0:T(8,128)} custom-call(s32[16]{0:T(128)S(1)} %copy-done.7, f32[8,4,32,256]{3,2,1,0:T(8,128)S(1)} %bitcast.11, f32[8,4,32,256]{3,2,1,0:T(8,128)S(1)} %collective-permute-done.2.received), custom_call_target="tpu_custom_call" | custom-call | bytes 2000000 | tf_op jit(solution)/shard_map/pallas_call | solution.py:357
  (1 shorter events, 0.0 us)
Async XLA Ops:
  0.6 0.7 %copy-start.6 = (f32[256]{0:T(256)S(1)}, f32[256]{0:T(256)}, u32[]{:S(2)}) copy-start(f32[256]{0:T(256)} %param.16) | copy-start | bytes 3076
  0.6 0.7 %copy-start.3 = (f32[4,4]{1,0:T(4,128)S(1)}, f32[4,4]{1,0:T(4,128)}, u32[]{:S(2)}) copy-start(f32[4,4]{1,0:T(4,128)} %mixing.3) | copy-start | bytes 196
  0.7 0.7 %copy-start.4 = (f32[4]{0:T(128)S(1)}, f32[4]{0:T(128)}, u32[]{:S(2)}) copy-start(f32[4]{0:T(128)} %diffusion.3) | copy-start | bytes 52
  0.7 0.7 %copy-start.5 = (s32[256]{0:T(256)S(1)}, s32[256]{0:T(256)}, u32[]{:S(2)}) copy-start(s32[256]{0:T(256)} %param.15) | copy-start | bytes 3076
  1.4 1.2 %copy-start = (f32[8,4,32,256]{3,2,1,0:T(8,128)S(1)}, f32[8,4,32,256]{3,2,1,0:T(8,128)}, u32[]{:S(2)}) copy-start(f32[8,4,32,256]{3,2,1,0:T(8,128)} %param.9) | copy-start | bytes 3145732
  2.6 1.2 %copy-start.1 = (bf16[2,8,4,32,256]{4,3,2,1,0:T(8,128)(2,1)S(1)}, bf16[2,8,4,32,256]{4,3,2,1,0:T(8,128)(2,1)}, u32[]{:S(2)}) copy-start(bf16[2,8,4,32,256]{4,3,2,1,0:T(8,128)(2,1)} %param.10) | copy-start | bytes 3145732
  3.8 0.8 %copy-start.2 = (f32[2,32,256]{2,1,0:T(8,128)S(1)}, f32[2,32,256]{2,1,0:T(8,128)}, u32[]{:S(2)}) copy-start(f32[2,32,256]{2,1,0:T(8,128)} %courant.3) | copy-start | bytes 196612
  5.6 8.9 %collective-permute-start = (f32[72,256]{1,0:T(8,128)S(1)}, f32[72,256]{1,0:T(8,128)S(1)}, u32[]{:S(2)}, u32[]{:S(2)}) collective-permute-start(f32[72,256]{1,0:T(8,128)S(1)} %get-tuple-element.11.own_east), channel_id=1, source_target_pairs={{0,2},{2,4},{4,6},{6,8},{8,10},{10,12},{12,14},{14,0},{1,3},{3,5},... | collective-permute-start | bytes 221192 | tf_op jit(solution)/shard_map/ppermute | solution.py:331
  8.6 5.9 %collective-permute-start.1 = (f32[72,256]{1,0:T(8,128)S(1)}, f32[72,256]{1,0:T(8,128)S(1)}, u32[]{:S(2)}, u32[]{:S(2)}) collective-permute-start(f32[72,256]{1,0:T(8,128)S(1)} %get-tuple-element.12.own_west), channel_id=1, source_target_pairs={{0,14},{2,0},{4,2},{6,4},{8,6},{10,8},{12,10},{14,12},{1,15},{3,1}... | collective-permute-start | bytes 221192 | tf_op jit(solution)/shard_map/ppermute | solution.py:332
  15.3 13.2 %collective-permute-start.2 = (f32[8,4,32,256]{3,2,1,0:T(8,128)S(1)}, f32[8,4,32,256]{3,2,1,0:T(8,128)S(1)}, u32[]{:S(2)}, u32[]{:S(2)}) collective-permute-start(f32[8,4,32,256]{3,2,1,0:T(8,128)S(1)} %bitcast.10), channel_id=1, source_target_pairs={{0,1},{1,0},{2,3},{3,2},{4,5},{5,4},{6,7},{7,6},{8,9},{9,8},{10,11... | collective-permute-start | bytes 3145736 | tf_op jit(solution)/shard_map/ppermute | solution.py:354
  27.4 0.7 %copy-start.8 = (f32[8]{0:T(128)S(1)}, f32[8]{0:T(128)}, u32[]{:S(2)}) copy-start(f32[8]{0:T(128)} %param.14) | copy-start | bytes 100
  28.1 0.7 %copy-start.7 = (s32[16]{0:T(128)S(1)}, s32[16]{0:T(128)}, u32[]{:S(2)}) copy-start(s32[16]{0:T(128)} %source.1) | copy-start | bytes 196

commit v4 on v3

v4 whole, which is shorter than its diff:
```python
import functools

import jax
import jax.numpy as jnp
from jax import lax
from jax.experimental import pallas as pl
from jax.experimental.pallas import tpu as pltpu
from jax.sharding import PartitionSpec as P

noise_var = 0.04
VMEM = pl.BlockSpec(memory_space=pltpu.VMEM)
SMEM = pl.BlockSpec(memory_space=pltpu.SMEM)
HBM = pl.BlockSpec(memory_space=pltpu.HBM)
LIMIT = pltpu.CompilerParams(vmem_limit_bytes=16 * 1024 * 1024)
BF16 = jnp.bfloat16
F32 = jnp.float32


def north(v):
    return pltpu.roll(v, v.shape[1] - 1, 1)


def south(v):
    return pltpu.roll(v, 1, 1)


def coefficients(zonal, merid, rate, self_mix):
    lat = lax.broadcasted_iota(jnp.int32, zonal.shape, 1)
    zonal_half, zonal_rate = 0.5 * zonal, 0.5 * zonal * zonal + rate
    merid_half, merid_rate = 0.5 * merid, 0.5 * merid * merid + rate
    east, west = zonal_rate - zonal_half, zonal_rate + zonal_half
    to_north, to_south = merid_rate - merid_half, merid_rate + merid_half
    centre = 1.0 + self_mix - 2.0 * zonal_rate - 2.0 * merid_rate
    last, first = lat == zonal.shape[1] - 1, lat == 0
    centre = centre + jnp.where(last, to_north, 0.0) + jnp.where(first, to_south, 0.0)
    to_north = jnp.where(last, 0.0, to_north)
    to_south = jnp.where(first, 0.0, to_south)
    return centre, east, west, to_north, to_south


def mixed(mixing, field, values):
    total = None
    for other, value in enumerate(values):
        if other != field:
            term = mixing[field, other] * value
            total = term if total is None else total + term
    return total


def pick_rows(kinds, particles, fields, strip, columns):
    rows = len(kinds) * particles
    out = lax.broadcasted_iota(jnp.int32, (rows, columns), 0)
    col = lax.broadcasted_iota(jnp.int32, (rows, columns), 1)
    want = jnp.full((rows, columns), -1, jnp.int32)
    for place, (field, x) in enumerate(kinds):
        inside = (out >= place * particles) & (out < (place + 1) * particles)
        target = (out - place * particles) * (fields * strip) + field * strip + x
        want = jnp.where(inside, target, want)
    return (col == want).astype(BF16)


def stack_rows(rows):
    sub = lax.broadcasted_iota(jnp.int32, (len(rows), rows[0].shape[1]), 0)
    out = None
    for p, row in enumerate(rows):
        row = jnp.broadcast_to(row, sub.shape)
        out = row if out is None else jnp.where(sub == p, row, out)
    return out


def observation_maps(sizes, cell, value):
    particles, fields, strip, lats, strips = sizes
    x0 = lax.axis_index("lon") * strip
    shift = lats.bit_length() - 1
    local_cell = cell - x0 * lats
    obs_lon = lax.shift_right_arithmetic(local_cell, shift)
    obs_lat = local_cell & (lats - 1)
    count = cell.shape[1]
    here = lax.broadcasted_iota(jnp.int32, (strip, count), 0) == obs_lon
    high = value.astype(BF16)
    rest = value - high.astype(F32)
    mid = rest.astype(BF16)
    low = (rest - mid.astype(F32)).astype(BF16)
    zero = jnp.zeros((strip, count), F32)
    parts = [jnp.where(here, 1.0, zero)]
    parts += [jnp.where(here, p.astype(F32), zero) for p in (high, mid, low)]
    left = jnp.concatenate(parts, 0).astype(BF16)
    right = (lax.broadcasted_iota(jnp.int32, (lats, count), 0) == obs_lat).astype(F32).astype(BF16)
    dense = lax.dot_general(left, right, (((1,), (1,)), ((), ())), preferred_element_type=F32)
    seen = dense[:strip]
    lon = (lax.broadcasted_iota(jnp.int32, (strip, lats), 0) + x0).astype(F32)
    precision = 1.0 + 2.0 * lon / (strip * strips)
    target = dense[strip:2 * strip] + (dense[2 * strip:3 * strip] + dense[3 * strip:])
    return seen * (0.25 * precision), seen * precision, target


def prepare(sizes, state_hbm, noise_hbm, courant_hbm, diffusion_hbm, mixing_hbm, cell_hbm, value_hbm,
            send_east, send_west,
            low, high, noise, courant, diffusion, mixing, cell, value, sems):
    particles, fields, strip, lats, strips = sizes
    copies = [pltpu.make_async_copy(source, target, sems.at[k]) for k, (source, target) in enumerate((
        (cell_hbm, cell), (value_hbm, value), (noise_hbm.at[0], noise), (state_hbm.at[:, :8], low),
        (state_hbm.at[:, strip - 8:], high), (courant_hbm, courant), (diffusion_hbm, diffusion),
        (mixing_hbm, mixing)))]
    for copy in copies:
        copy.start()
    copies[0].wait()
    copies[1].wait()
    gain, _, target = observation_maps(sizes, cell[...], value[...])

    kinds = [(f, x) for x in (0, strip - 1) for f in range(fields)]
    pick = pick_rows(kinds, particles, fields, strip, noise.shape[0])
    copies[2].wait()
    rows = jnp.dot(pick, noise[...], preferred_element_type=F32)
    for copy in copies[3:]:
        copy.wait()

    def edge(x, inner, out, base):
        tile, first = (low, 0) if x < 8 else (high, strip - 8)

        def rows_at(f, place):
            return stack_rows([tile[p * fields + f, place:place + 1] for p in range(particles)])

        here = [rows_at(f, x - first) for f in range(fields)]
        beside = [rows_at(f, inner - first) for f in range(fields)]
        for f in range(fields):
            centre, east, west, to_north, to_south = coefficients(
                courant[0, x:x + 1], courant[1, x:x + 1], diffusion[f], mixing[f, f])
            known, missing = (east, west) if inner > x else (west, east)
            moved = (centre * here[f] + known * beside[f] + to_north * north(here[f])
                     + to_south * south(here[f]) + mixed(mixing, f, here))
            if f == 0:
                g = gain[x:x + 1]
                moved = moved + g * (target[x:x + 1] - moved)
                missing = (1.0 - g) * missing
            moved = moved + rows[base + f * particles:base + (f + 1) * particles]
            out[f * particles:(f + 1) * particles] = here[f]
            out[(fields + f) * particles:(fields + f + 1) * particles] = moved
            out[2 * fields * particles + f:2 * fields * particles + f + 1] = missing
        out[2 * fields * particles + fields:] = jnp.zeros((8 - fields, lats), F32)

    edge(strip - 1, strip - 2, send_east, fields * particles)
    edge(0, 1, send_west, 0)


def bulk(sizes, state, noise, courant, diffusion, mixing, cell, value,
         out, partial, noise_rows, first_rows, edge_coefs, edge_maps, coefs, maps, middle):
    particles, fields, strip, lats, strips = sizes
    maps[0], maps[1], maps[2] = observation_maps(sizes, cell[...], value[...])
    places = (0, 1, strip - 2, strip - 1)
    for k, x in enumerate(places):
        for m in range(3):
            edge_maps[m * 4 + k:m * 4 + k + 1] = maps[m, x:x + 1]
    lon = lax.broadcasted_iota(jnp.int32, (strip, lats), 0)
    for f in range(fields):
        centre, east, west, to_north, to_south = coefficients(
            courant[0], courant[1], diffusion[f], mixing[f, f])
        coefs[f, 0] = centre
        coefs[f, 1] = jnp.where(lon == strip - 1, 0.0, east)
        coefs[f, 2] = jnp.where(lon == 0, 0.0, west)
        coefs[f, 3] = to_north
        coefs[f, 4] = to_south
        for side, (x, inner, outward) in enumerate(((0, 1, west), (strip - 1, strip - 2, east))):
            row = (side * fields + f) * 5
            for k, (values, at) in enumerate(((centre, x), (outward, x), (to_north, x), (to_south, x), (outward, inner))):
                edge_coefs[row + k:row + k + 1] = values[at:at + 1]
    kinds = [(0, x) for x in places]
    pick = pick_rows(kinds, particles, fields, strip, noise.shape[1])
    noise_rows[:4 * particles] = jnp.dot(pick, noise[1], preferred_element_type=F32)
    noise_rows[4 * particles:] = jnp.dot(pick, noise[0], preferred_element_type=F32)

    def rows_of(p, f):
        return pl.ds(pl.multiple_of(p * (fields * strip) + f * strip, strip), strip)

    def moved(values, f):
        v = values[f]
        return (coefs[f, 0] * v + coefs[f, 1] * pltpu.roll(v, strip - 1, 0) + coefs[f, 2] * pltpu.roll(v, 1, 0)
                + coefs[f, 3] * north(v) + coefs[f, 4] * south(v) + mixed(mixing, f, values))

    def body(p, carry):
        values = [state[rows_of(p, f), :] for f in range(fields)]
        total = None
        for f in range(fields):
            new = moved(values, f)
            add = noise[0, rows_of(p, f), :].astype(F32)
            if f == 0:
                push = maps[0] * (maps[2] - new)
                new = new + push
                total = jnp.where((lon > 0) & (lon < strip - 1), push * (push + 2.0 * add), 0.0)
            middle[f] = new + add
        values = [middle[f] for f in range(fields)]
        for f in range(fields):
            new = moved(values, f)
            add = noise[1, rows_of(p, f), :].astype(F32)
            if f == 0:
                push = maps[0] * (maps[2] - new)
                new = new + push + add
                miss = maps[2] - new
                term = ((0.5 / noise_var) * (push * (push + 2.0 * add)) + (0.5 * maps[1]) * (miss * miss))
                total = (0.5 / noise_var) * total + jnp.where((lon > 1) & (lon < strip - 2), term, 0.0)
            else:
                new = new + add
            out[rows_of(p, f), :] = new
        total = jnp.sum(total, axis=0, keepdims=True)
        partial[pl.ds(p, 1), :] = total[:, :128] + total[:, 128:]
        return carry

    lax.fori_loop(0, particles, body, 0)
    for k, x in enumerate(places):
        first_rows[k * particles:(k + 1) * particles] = stack_rows(
            [out[p * fields * strip + x:p * fields * strip + x + 1] for p in range(particles)])


def correct(sizes, own_east, own_west, from_west, from_east, mixing, edge_coefs, edge_maps, noise_rows, first_rows,
            partial, weight, changes):
    particles, fields, strip, lats, strips = sizes
    n = fields * particles

    def split(ref, start):
        return [ref[start + f * particles:start + (f + 1) * particles] for f in range(fields)]

    def wide(v):
        return v[:, :128] + v[:, 128:]

    def push_terms(push, add):
        return (0.5 / noise_var) * (push * (push + 2.0 * add))

    total = partial[...]
    for side, (k_edge, k_in, own, other) in enumerate(((0, 1, own_west, from_west), (3, 2, own_east, from_east))):
        own_state, other_state, other_first = split(own, 0), split(other, 0), split(other, n)

        def maps_at(k):
            return [edge_maps[m * 4 + k:m * 4 + k + 1] for m in range(3)]

        gain, seen, observed = maps_at(k_edge)
        coefs = [[edge_coefs[(side * fields + f) * 5 + k:(side * fields + f) * 5 + k + 1] for k in range(5)]
                 for f in range(fields)]
        first, outside = [], []
        for f in range(fields):
            row = 2 * n + f
            outside.append(other_first[f] + other[row:row + 1] * own_state[f])
            step = coefs[f][1] * other_state[f]
            if f == 0:
                step = (1.0 - gain) * step
                result = own[n:n + particles] + step
                add = noise_rows[(4 + k_edge) * particles:(5 + k_edge) * particles]
                push = (gain / (1.0 - gain)) * (observed - (result - add))
                total = total + wide(push_terms(push, add))
            first.append(step)
        for f in range(fields):
            centre, outward, to_north, to_south, outward_in = coefs[f]
            step = (centre * first[f] + outward * outside[f] + to_north * north(first[f])
                    + to_south * south(first[f]) + mixed(mixing, f, first))
            beside = outward_in * first[f]
            if f == 0:
                step = (1.0 - gain) * step
                beside = (1.0 - maps_at(k_in)[0]) * beside
                for k, change in ((k_edge, step), (k_in, beside)):
                    g, s, v = maps_at(k)
                    result = first_rows[k * particles:(k + 1) * particles] + change
                    add = noise_rows[k * particles:(k + 1) * particles]
                    push = (g / (1.0 - g)) * (v - (result - add))
                    miss = v - result
                    total = total + wide(push_terms(push, add) + (0.5 * s) * (miss * miss))
            changes[k_edge, f * particles:(f + 1) * particles] = step
            changes[k_in, f * particles:(f + 1) * particles] = beside
    total = jnp.broadcast_to(jnp.sum(total, axis=1, keepdims=True), total.shape)
    diagonal = lax.broadcasted_iota(jnp.int32, total.shape, 0) == lax.broadcasted_iota(jnp.int32, total.shape, 1)
    weight[...] = jnp.sum(jnp.where(diagonal, total, 0.0), axis=0, keepdims=True)


def apply_changes(sizes, current, changes, out):
    particles, fields, strip, lats, strips = sizes
    sub = lax.broadcasted_iota(jnp.int32, (8, lats), 0)
    for p in range(particles):
        for f in range(fields):
            start = (p * fields + f) * strip
            row = f * particles + p
            rows = [jnp.broadcast_to(changes[k, row:row + 1], sub.shape) for k in range(4)]
            out[start:start + 8] = current[start:start + 8] + jnp.where(
                sub == 0, rows[0], jnp.where(sub == 1, rows[1], 0.0))
            out[start + 8:start + strip - 8] = current[start + 8:start + strip - 8]
            out[start + strip - 8:start + strip] = current[start + strip - 8:start + strip] + jnp.where(
                sub == 7, rows[3], jnp.where(sub == 6, rows[2], 0.0))


def assemble(sizes, source, current, received, out, sems):
    particles = sizes[0]
    dom = lax.axis_index("dom")

    def copy(j, ref, at):
        return pltpu.make_async_copy(ref.at[at], out.at[j], sems.at[j])

    for j in range(particles):
        wanted = source[dom * particles + j]
        mine = wanted // particles == dom
        at = wanted % particles

        @pl.when(mine)
        def _():
            copy(j, current, at).start()

        @pl.when(jnp.logical_not(mine))
        def _():
            copy(j, received, at).start()

    for j in range(particles):
        copy(j, current, 0).wait()


def local(ensemble_state, proposal_noise, courant, diffusion, mixing, prior_weight, obs_cell, obs_value, source):
    particles, fields, strip, lats = ensemble_state.shape
    strips = lax.axis_size("lon")
    sizes = (particles, fields, strip, lats, strips)
    rows = particles * fields * strip
    state = ensemble_state.reshape(rows, lats)
    noise = proposal_noise.reshape(2, rows, lats)
    packet = jax.ShapeDtypeStruct((2 * particles * fields + 8, lats), F32)
    cell, value = obs_cell[None], obs_value[None]

    def shape(*dims):
        return jax.ShapeDtypeStruct(dims, F32)

    send_east, send_west = pl.pallas_call(
        functools.partial(prepare, sizes),
        out_shape=(packet, packet),
        in_specs=[HBM] * 7,
        out_specs=(VMEM,) * 2,
        scratch_shapes=[
            pltpu.VMEM((particles * fields, 8, lats), F32),
            pltpu.VMEM((particles * fields, 8, lats), F32),
            pltpu.VMEM((rows, lats), BF16),
            pltpu.VMEM(courant.shape, F32),
            pltpu.SMEM(diffusion.shape, F32),
            pltpu.SMEM(mixing.shape, F32),
            pltpu.VMEM(cell.shape, jnp.int32),
            pltpu.VMEM(value.shape, F32),
            pltpu.SemaphoreType.DMA((8,)),
        ],
        compiler_params=pltpu.CompilerParams(vmem_limit_bytes=60 * 1024 * 1024),
        cost_estimate=pl.CostEstimate(flops=1000000, bytes_accessed=2000000, transcendentals=0),
    )(state.reshape(particles * fields, strip, lats), noise, courant, diffusion, mixing, cell, value)

    eastward = [(i, (i + 1) % strips) for i in range(strips)]
    westward = [(i, (i - 1) % strips) for i in range(strips)]
    from_west = lax.ppermute(send_east, "lon", eastward)
    from_east = lax.ppermute(send_west, "lon", westward)

    current, partial, noise_rows, first_rows, edge_coefs, edge_maps = pl.pallas_call(
        functools.partial(bulk, sizes),
        out_shape=(shape(rows, lats), shape(particles, 128), shape(8 * particles, lats), shape(4 * particles, lats),
                   shape(2 * fields * 5, lats), shape(12, lats)),
        in_specs=[VMEM, VMEM, VMEM, SMEM, SMEM, VMEM, VMEM],
        out_specs=(VMEM,) * 6,
        scratch_shapes=[pltpu.VMEM((fields, 5, strip, lats), F32), pltpu.VMEM((3, strip, lats), F32),
                        pltpu.VMEM((fields, strip, lats), F32)],
        compiler_params=LIMIT,
        cost_estimate=pl.CostEstimate(flops=30000000, bytes_accessed=4000000, transcendentals=0),
    )(state, noise, courant, diffusion, mixing, cell, value)

    weight, changes = pl.pallas_call(
        functools.partial(correct, sizes),
        out_shape=(shape(1, 128), shape(4, particles * fields, lats)),
        in_specs=[VMEM] * 4 + [SMEM] + [VMEM] * 5,
        out_specs=(VMEM,) * 2,
        compiler_params=LIMIT,
        cost_estimate=pl.CostEstimate(flops=1000000, bytes_accessed=1000000, transcendentals=0),
    )(send_east, send_west, from_west, from_east, mixing, edge_coefs, edge_maps, noise_rows, first_rows, partial)

    current = pl.pallas_call(
        functools.partial(apply_changes, sizes),
        out_shape=shape(rows, lats),
        in_specs=[VMEM] * 2,
        out_specs=VMEM,
        compiler_params=LIMIT,
        cost_estimate=pl.CostEstimate(flops=1000000, bytes_accessed=2000000, transcendentals=0),
    )(current, changes).reshape(particles, fields, strip, lats)

    received = lax.ppermute(current, "dom", [(0, 1), (1, 0)])
    bit = 1
    while bit < strips:
        if 2 * bit >= strips:
            weight, received = lax.optimization_barrier((weight, received))
        weight = weight + lax.ppermute(weight, "lon", [(i, i ^ bit) for i in range(strips)])
        bit *= 2

    new_state = pl.pallas_call(
        functools.partial(assemble, sizes),
        out_shape=shape(particles, fields, strip, lats),
        in_specs=[SMEM, VMEM, VMEM],
        out_specs=HBM,
        scratch_shapes=[pltpu.SemaphoreType.DMA((particles,))],
        compiler_params=LIMIT,
        cost_estimate=pl.CostEstimate(flops=0, bytes_accessed=2000000, transcendentals=0),
    )(source, current, received)

    log_weight = prior_weight - weight[0, :particles] / (256.0 * obs_cell.shape[0])
    return new_state, log_weight


def solution(mesh):
    placed = (
        P(("groups", "dom"), None, "lon", None),
        P(None, ("groups", "dom"), None, "lon", None),
        P(None, ("groups", "lon"), None),
        P(),
        P(),
        P(("groups", "dom")),
        P(("groups", "lon")),
        P(("groups", "lon")),
        P("groups"),
    )
    return jax.shard_map(
        local,
        mesh=mesh,
        in_specs=placed,
        out_specs=(P(("groups", "dom"), None, "lon", None), P(("groups", "dom"))),
        check_vma=False,
    )
```

time: 30.6 us -> 25.5 us (0.83)
  blocking collectives: 12 us -> 0 us
  waiting for transfers between devices: 0.02 us -> 7 us
  local copies, waits for them, and re-layouts: 4.66 us -> 0.05 us
  starting transfers between devices: 6.17 us -> 9.17 us
  Pallas kernels: 6.14 us -> 7.8 us
    all_to_all x1 -> x0, blocking collectives: 12 us -> none  [local(): lax.all_to_all(jnp.broadcast_to(weight[None], (strips, particles, 128)),...]
    ppermute x0 -> x3, waiting for transfers between devices: none -> 6.99 us  [local(): lax.ppermute(weight, 'lon', [(i, i ^ bit) for i in range(strips)])]
    unnamed x18 -> x22, local copies, waits for them, and re-layouts: 4.65 us -> 0.05 us
    ppermute x0 -> x3, starting transfers between devices: none -> 2.99 us  [local(): lax.ppermute(weight, 'lon', [(i, i ^ bit) for i in range(strips)])]
    pallas_call x1, Pallas kernels: 0.94 us -> 2.33 us  [local(): pl.pallas_call(functools.partial(prepare, sizes), out_shape=(packet, pack...]
    pallas_call x3 -> x4, Pallas kernels: 5.21 us -> 5.47 us  [the longest x1 2.99 us: local(): pl.pallas_call(functools.partial(bulk, sizes), out_shape=(shape(rows, lat...]
  transfers between devices with their start and end apart: 3 -> 6, of which waited for: 0 -> 3; matrix products, arithmetic and copies ran while one was open for 2% -> 0% of each run, Pallas kernels for 9% -> 18%
where the time goes in v4:
time: 25.5 us; the launch traced here: 25.4 us
  starting transfers between devices  9.17 us (36%)
  Pallas kernels  7.8 us (31%)
  waiting for transfers between devices  7 us (27%)
  between operations  0.8 us (3%)
  other arithmetic  0.52 us (2%)
    ppermute x3, waiting for transfers between devices, local(): lax.ppermute(weight, 'lon', [(i, i ^ bit) for i in range(strips)])  6.99 us
    ppermute x1, starting transfers between devices, local(): from_east = lax.ppermute(send_west, 'lon', westward)  3.12 us
    ppermute x1, starting transfers between devices, local(): from_west = lax.ppermute(send_east, 'lon', eastward)  2.99 us
    ppermute x3, starting transfers between devices, local(): lax.ppermute(weight, 'lon', [(i, i ^ bit) for i in range(strips)])  2.99 us
    pallas_call x1, Pallas kernels, local(): pl.pallas_call(functools.partial(bulk, sizes), out_shape=(shape(rows, lat...  2.99 us
    pallas_call x1, Pallas kernels, local(): pl.pallas_call(functools.partial(prepare, sizes), out_shape=(packet, pack...  2.33 us
    pallas_call x1, Pallas kernels, local(): pl.pallas_call(functools.partial(assemble, sizes), out_shape=shape(partic...  1.58 us
    pallas_call x1, Pallas kernels, local(): pl.pallas_call(functools.partial(correct, sizes), out_shape=(shape(1, 128...  0.75 us
  transfers between devices with their start and end apart: 6, of which 3 were waited for; matrix products, arithmetic and copies ran while one was open for 0% of the time, Pallas kernels for 18%

profile of v4, /device:TPU:0, one launch (start us, length us, event | category | flops | bytes accessed | tf_op | source)
XLA Modules:
  0.0 25.4 jit_solution(13790291817774490347)
XLA Ops:
  0.6 0.0 copy-start
  0.6 0.0 copy-start.1
  0.7 0.0 copy-start.2
  0.7 0.0 copy-start.7
  0.7 2.3 %shard_map.105 = (f32[72,256]{1,0:T(8,128)}, f32[72,256]{1,0:T(8,128)}) custom-call(f32[32,32,256]{2,1,0:T(8,128)} %bitcast.8, bf16[2,1024,256]{2,1,0:T(8,128)(2,1)} %bitcast.10, f32[2,32,256]{2,1,0:T(8,128)} %courant_hbm.1, f32[4]{0:T(128)} %diffusion_hbm.1, f32[4,4]{1,0:T(4,128)} %mixing.3, s32[1,256]{1,0:T(1,128)} %bitcast.14, f32[1,256]{1,0:T(1,128)} %bitcast.16), custom_call_target="tpu_custom_call" | custom-call | flops 1000000 | bytes 2000000 | tf_op jit(solution)/shard_map/pallas_call | solution.py:324
  3.0 0.0 copy-start.5
  3.0 3.0 %collective-permute-start = (f32[72,256]{1,0:T(8,128)}, f32[72,256]{1,0:T(8,128)S(1)}, u32[]{:S(2)}, u32[]{:S(2)}) collective-permute-start(f32[72,256]{1,0:T(8,128)} %get-tuple-element.15.own_east), channel_id=1, source_target_pairs={{0,2},{2,4},{4,6},{6,8},{8,10},{10,12},{12,14},{14,0},{1,3},{3,5},... | collective-permute-start | bytes 221192 | tf_op jit(solution)/shard_map/ppermute | solution.py:346
  6.0 0.0 copy-start.6
  6.0 0.0 copy-start.8
  6.0 3.1 %collective-permute-start.1 = (f32[72,256]{1,0:T(8,128)}, f32[72,256]{1,0:T(8,128)S(1)}, u32[]{:S(2)}, u32[]{:S(2)}) collective-permute-start(f32[72,256]{1,0:T(8,128)} %get-tuple-element.16.own_west), channel_id=1, source_target_pairs={{0,14},{2,0},{4,2},{6,4},{8,6},{10,8},{12,10},{14,12},{1,15},{3,1}... | collective-permute-start | bytes 221192 | tf_op jit(solution)/shard_map/ppermute | solution.py:347
  9.1 0.0 copy-done
  9.1 0.0 copy-done.1
  9.1 0.0 copy-done.2
  9.2 0.0 copy-done.7
  9.2 0.0 copy-done.5
  9.2 0.0 copy-done.6
  9.2 0.0 copy-done.8
  9.2 0.0 copy-start.3
  9.2 0.0 copy-start.4
  9.2 3.0 %shard_map.104 = (f32[1024,256]{1,0:T(8,128)S(1)}, f32[8,128]{1,0:T(8,128)S(1)}, f32[64,256]{1,0:T(8,128)S(1)}, f32[32,256]{1,0:T(8,128)S(1)}, f32[40,256]{1,0:T(8,128)S(1)}, /*index=5*/f32[12,256]{1,0:T(8,128)S(1)}) custom-call(f32[1024,256]{1,0:T(8,128)S(1)} %bitcast.9, bf16[2,1024,256]{2,1,0:T(8,128)(2,1)S(1)} %bitcast.11, f32[2,32,256]{2,1,0:T(8,128)S(1)} %copy-done.2, ...), custom_call_target="tpu_custom_call" | custom-call | flops 30000000 | bytes 4000000 | tf_op jit(solution)/shard_map/pallas_call | solution.py:349
  12.2 0.0 collective-permute-done.from_west
  12.2 0.0 collective-permute-done.1.from_east
  12.2 0.0 copy-done.3
  12.2 0.0 copy-done.4
  12.2 0.7 %shard_map.106 = (f32[1,128]{1,0:T(1,128)S(1)}, f32[4,32,256]{2,1,0:T(8,128)S(1)}) custom-call(f32[72,256]{1,0:T(8,128)S(1)} %copy-done.3, f32[72,256]{1,0:T(8,128)S(1)} %copy-done.4, f32[72,256]{1,0:T(8,128)S(1)} %collective-permute-done.from_west, f32[72,256]{1,0:T(8,128)S(1)} %collective-permute-done.1.from_east, f32[4,4]{1,0:T(4,128)S(1)} %copy-done.5, ...), custom_call_target="tpu_custom_call" | custom-call | flops 1000000 | bytes 1000000 | tf_op jit(solution)/shard_map/pallas_call | solution.py:361
  13.0 0.2 shard_map.107
  13.2 0.1 collective-permute-start.4
  13.2 0.9 %collective-permute-start.2 = (f32[1,128]{1,0:T(1,128)S(1)}, f32[1,128]{1,0:T(1,128)S(1)}, u32[]{:S(2)}, u32[]{:S(2)}) collective-permute-start(f32[1,128]{1,0:T(1,128)S(1)} %get-tuple-element.23), channel_id=1, source_target_pairs={{0,2},{2,0},{4,6},{6,4},{8,10},{10,8},{12,14},{14,12},{1,3},{3,1},... | collective-permute-start | bytes 1544 | tf_op jit(solution)/shard_map/ppermute | solution.py:384
  14.1 2.7 %collective-permute-done.2 = f32[1,128]{1,0:T(1,128)S(1)} collective-permute-done((f32[1,128]{1,0:T(1,128)S(1)}, f32[1,128]{1,0:T(1,128)S(1)}, u32[]{:S(2)}, u32[]{:S(2)}) %collective-permute-start.2) | collective-permute-done | bytes 544 | tf_op jit(solution)/shard_map/ppermute | solution.py:384
  16.8 0.0 copy-start.9
  16.8 0.6 %collective-permute-start.3 = (f32[1,128]{1,0:T(1,128)S(1)}, f32[1,128]{1,0:T(1,128)S(1)}, u32[]{:S(2)}, u32[]{:S(2)}) collective-permute-start(f32[1,128]{1,0:T(1,128)S(1)} %add.9), channel_id=1, source_target_pairs={{0,4},{2,6},{4,0},{6,2},{8,12},{10,14},{12,8},{14,10},{1,5},{3,7},... | collective-permute-start | bytes 1544 | tf_op jit(solution)/shard_map/ppermute | solution.py:384
  17.4 3.0 %collective-permute-done.3 = f32[1,128]{1,0:T(1,128)S(1)} collective-permute-done((f32[1,128]{1,0:T(1,128)S(1)}, f32[1,128]{1,0:T(1,128)S(1)}, u32[]{:S(2)}, u32[]{:S(2)}) %collective-permute-start.3) | collective-permute-done | bytes 544 | tf_op jit(solution)/shard_map/ppermute | solution.py:384
  20.4 0.0 collective-permute-done.4.received
  20.4 1.6 %collective-permute-start.5 = (f32[1,128]{1,0:T(1,128)S(1)}, f32[1,128]{1,0:T(1,128)S(1)}, u32[]{:S(2)}, u32[]{:S(2)}) collective-permute-start(f32[1,128]{1,0:T(1,128)S(1)} %add.10), channel_id=1, source_target_pairs={{0,8},{2,10},{4,12},{6,14},{8,0},{10,2},{12,4},{14,6},{1,9},{3,11}... | collective-permute-start | bytes 1544 | tf_op jit(solution)/shard_map/ppermute | solution.py:384
  22.0 0.0 copy-done.9
  22.0 1.6 %shard_map.108 = f32[8,4,32,256]{3,2,1,0:T(8,128)} custom-call(s32[16]{0:T(128)S(1)} %copy-done.9, f32[8,4,32,256]{3,2,1,0:T(8,128)S(1)} %bitcast.13, f32[8,4,32,256]{3,2,1,0:T(8,128)S(1)} %collective-permute-done.4.received), custom_call_target="tpu_custom_call" | custom-call | bytes 2000000 | tf_op jit(solution)/shard_map/pallas_call | solution.py:387
  23.6 0.0 copy-start.10
  23.6 1.3 %collective-permute-done.5 = f32[1,128]{1,0:T(1,128)S(1)} collective-permute-done((f32[1,128]{1,0:T(1,128)S(1)}, f32[1,128]{1,0:T(1,128)S(1)}, u32[]{:S(2)}, u32[]{:S(2)}) %collective-permute-start.5) | collective-permute-done | bytes 544 | tf_op jit(solution)/shard_map/ppermute | solution.py:384
  24.8 0.0 copy-done.10
  24.8 0.5 %bitcast_subtract_fusion = f32[8]{0:T(128)} fusion(f32[8]{0:T(128)S(1)} %copy-done.10, f32[1,128]{1,0:T(1,128)S(1)} %add.11), kind=kLoop, calls=%fused_computation | loop fusion | flops 16 | bytes 96 | tf_op jit(solution)/shard_map/sub | solution.py:397
  (3 shorter events, 0.0 us)
Async XLA Ops:
  0.6 8.5 %copy-start = (f32[8,4,32,256]{3,2,1,0:T(8,128)S(1)}, f32[8,4,32,256]{3,2,1,0:T(8,128)}, u32[]{:S(2)}) copy-start(f32[8,4,32,256]{3,2,1,0:T(8,128)} %param.9) | copy-start | bytes 3145732
  0.6 8.5 %copy-start.1 = (bf16[2,8,4,32,256]{4,3,2,1,0:T(8,128)(2,1)S(1)}, bf16[2,8,4,32,256]{4,3,2,1,0:T(8,128)(2,1)}, u32[]{:S(2)}) copy-start(bf16[2,8,4,32,256]{4,3,2,1,0:T(8,128)(2,1)} %param.10) | copy-start | bytes 3145732
  0.7 8.5 %copy-start.2 = (f32[2,32,256]{2,1,0:T(8,128)S(1)}, f32[2,32,256]{2,1,0:T(8,128)}, u32[]{:S(2)}) copy-start(f32[2,32,256]{2,1,0:T(8,128)} %courant_hbm.1) | copy-start | bytes 196612
  0.7 8.5 %copy-start.7 = (f32[256]{0:T(256)S(1)}, f32[256]{0:T(256)}, u32[]{:S(2)}) copy-start(f32[256]{0:T(256)} %param.16) | copy-start | bytes 3076
  3.0 6.1 %copy-start.5 = (f32[4,4]{1,0:T(4,128)S(1)}, f32[4,4]{1,0:T(4,128)}, u32[]{:S(2)}) copy-start(f32[4,4]{1,0:T(4,128)} %mixing.3) | copy-start | bytes 196
  3.0 9.2 %collective-permute-start = (f32[72,256]{1,0:T(8,128)}, f32[72,256]{1,0:T(8,128)S(1)}, u32[]{:S(2)}, u32[]{:S(2)}) collective-permute-start(f32[72,256]{1,0:T(8,128)} %get-tuple-element.15.own_east), channel_id=1, source_target_pairs={{0,2},{2,4},{4,6},{6,8},{8,10},{10,12},{12,14},{14,0},{1,3},{3,5},... | collective-permute-start | bytes 221192 | tf_op jit(solution)/shard_map/ppermute | solution.py:346
  6.0 3.2 %copy-start.6 = (s32[256]{0:T(256)S(1)}, s32[256]{0:T(256)}, u32[]{:S(2)}) copy-start(s32[256]{0:T(256)} %param.15) | copy-start | bytes 3076
  6.0 3.2 %copy-start.8 = (f32[4]{0:T(128)S(1)}, f32[4]{0:T(128)}, u32[]{:S(2)}) copy-start(f32[4]{0:T(128)} %diffusion_hbm.1) | copy-start | bytes 52
  6.0 6.2 %collective-permute-start.1 = (f32[72,256]{1,0:T(8,128)}, f32[72,256]{1,0:T(8,128)S(1)}, u32[]{:S(2)}, u32[]{:S(2)}) collective-permute-start(f32[72,256]{1,0:T(8,128)} %get-tuple-element.16.own_west), channel_id=1, source_target_pairs={{0,14},{2,0},{4,2},{6,4},{8,6},{10,8},{12,10},{14,12},{1,15},{3,1}... | collective-permute-start | bytes 221192 | tf_op jit(solution)/shard_map/ppermute | solution.py:347
  9.2 3.0 %copy-start.3 = (f32[72,256]{1,0:T(8,128)S(1)}, f32[72,256]{1,0:T(8,128)}, u32[]{:S(2)}) copy-start(f32[72,256]{1,0:T(8,128)} %get-tuple-element.15.own_east) | copy-start | bytes 221188
  9.2 3.0 %copy-start.4 = (f32[72,256]{1,0:T(8,128)S(1)}, f32[72,256]{1,0:T(8,128)}, u32[]{:S(2)}) copy-start(f32[72,256]{1,0:T(8,128)} %get-tuple-element.16.own_west) | copy-start | bytes 221188
  13.2 7.2 %collective-permute-start.4 = (f32[8,4,32,256]{3,2,1,0:T(8,128)S(1)}, f32[8,4,32,256]{3,2,1,0:T(8,128)S(1)}, u32[]{:S(2)}, u32[]{:S(2)}) collective-permute-start(f32[8,4,32,256]{3,2,1,0:T(8,128)S(1)} %bitcast.12), channel_id=1, source_target_pairs={{0,1},{1,0},{2,3},{3,2},{4,5},{5,4},{6,7},{7,6},{8,9},{9,8},{10,11... | collective-permute-start | bytes 3145736 | tf_op jit(solution)/shard_map/ppermute | solution.py:379
  13.2 3.6 %collective-permute-start.2 = (f32[1,128]{1,0:T(1,128)S(1)}, f32[1,128]{1,0:T(1,128)S(1)}, u32[]{:S(2)}, u32[]{:S(2)}) collective-permute-start(f32[1,128]{1,0:T(1,128)S(1)} %get-tuple-element.23), channel_id=1, source_target_pairs={{0,2},{2,0},{4,6},{6,4},{8,10},{10,8},{12,14},{14,12},{1,3},{3,1},... | collective-permute-start | bytes 1544 | tf_op jit(solution)/shard_map/ppermute | solution.py:384
  16.8 5.1 %copy-start.9 = (s32[16]{0:T(128)S(1)}, s32[16]{0:T(128)}, u32[]{:S(2)}) copy-start(s32[16]{0:T(128)} %source.1) | copy-start | bytes 196
  16.8 3.5 %collective-permute-start.3 = (f32[1,128]{1,0:T(1,128)S(1)}, f32[1,128]{1,0:T(1,128)S(1)}, u32[]{:S(2)}, u32[]{:S(2)}) collective-permute-start(f32[1,128]{1,0:T(1,128)S(1)} %add.9), channel_id=1, source_target_pairs={{0,4},{2,6},{4,0},{6,2},{8,12},{10,14},{12,8},{14,10},{1,5},{3,7},... | collective-permute-start | bytes 1544 | tf_op jit(solution)/shard_map/ppermute | solution.py:384
  20.4 4.4 %collective-permute-start.5 = (f32[1,128]{1,0:T(1,128)S(1)}, f32[1,128]{1,0:T(1,128)S(1)}, u32[]{:S(2)}, u32[]{:S(2)}) collective-permute-start(f32[1,128]{1,0:T(1,128)S(1)} %add.10), channel_id=1, source_target_pairs={{0,8},{2,10},{4,12},{6,14},{8,0},{10,2},{12,4},{14,6},{1,9},{3,11}... | collective-permute-start | bytes 1544 | tf_op jit(solution)/shard_map/ppermute | solution.py:384
  23.6 1.3 %copy-start.10 = (f32[8]{0:T(128)S(1)}, f32[8]{0:T(128)}, u32[]{:S(2)}) copy-start(f32[8]{0:T(128)} %param.14) | copy-start | bytes 100

commit v5 on v4

--- a/solution.py
+++ b/solution.py
@@ -212,7 +212,7 @@
 
 
 def correct(sizes, own_east, own_west, from_west, from_east, mixing, edge_coefs, edge_maps, noise_rows, first_rows,
-            partial, weight, changes):
+            partial, weights, changes):
     particles, fields, strip, lats, strips = sizes
     n = fields * particles
 
@@ -266,7 +266,9 @@
             changes[k_in, f * particles:(f + 1) * particles] = beside
     total = jnp.broadcast_to(jnp.sum(total, axis=1, keepdims=True), total.shape)
     diagonal = lax.broadcasted_iota(jnp.int32, total.shape, 0) == lax.broadcasted_iota(jnp.int32, total.shape, 1)
-    weight[...] = jnp.sum(jnp.where(diagonal, total, 0.0), axis=0, keepdims=True)
+    total = jnp.sum(jnp.where(diagonal, total, 0.0), axis=0, keepdims=True)
+    for k in range(strips):
+        weights[k] = total
 
 
 def apply_changes(sizes, current, changes, out):
@@ -284,8 +286,8 @@
                 sub == 7, rows[3], jnp.where(sub == 6, rows[2], 0.0))
 
 
-def assemble(sizes, source, current, received, out, sems):
-    particles = sizes[0]
+def assemble(sizes, scale, source, current, received, weights, prior, out, log_weight, held, sems):
+    particles, strips = sizes[0], sizes[4]
     dom = lax.axis_index("dom")
 
     def copy(j, ref, at):
@@ -304,8 +306,15 @@
         def _():
             copy(j, received, at).start()
 
+    total = weights[0]
+    for k in range(1, strips):
+        total = total + weights[k]
+    held[...] = prior[...] - scale * total[:, :particles]
+    last = pltpu.make_async_copy(held, log_weight, sems.at[particles])
+    last.start()
     for j in range(particles):
         copy(j, current, 0).wait()
+    last.wait()
 
 
 def local(ensemble_state, proposal_noise, courant, diffusion, mixing, prior_weight, obs_cell, obs_value, source):
@@ -358,9 +367,9 @@
         cost_estimate=pl.CostEstimate(flops=30000000, bytes_accessed=4000000, transcendentals=0),
     )(state, noise, courant, diffusion, mixing, cell, value)
 
-    weight, changes = pl.pallas_call(
+    weights, changes = pl.pallas_call(
         functools.partial(correct, sizes),
-        out_shape=(shape(1, 128), shape(4, particles * fields, lats)),
+        out_shape=(shape(strips, 1, 128), shape(4, particles * fields, lats)),
         in_specs=[VMEM] * 4 + [SMEM] + [VMEM] * 5,
         out_specs=(VMEM,) * 2,
         compiler_params=LIMIT,
@@ -377,25 +386,18 @@
     )(current, changes).reshape(particles, fields, strip, lats)
 
     received = lax.ppermute(current, "dom", [(0, 1), (1, 0)])
-    bit = 1
-    while bit < strips:
-        if 2 * bit >= strips:
-            weight, received = lax.optimization_barrier((weight, received))
-        weight = weight + lax.ppermute(weight, "lon", [(i, i ^ bit) for i in range(strips)])
-        bit *= 2
-
-    new_state = pl.pallas_call(
-        functools.partial(assemble, sizes),
-        out_shape=shape(particles, fields, strip, lats),
-        in_specs=[SMEM, VMEM, VMEM],
-        out_specs=HBM,
-        scratch_shapes=[pltpu.SemaphoreType.DMA((particles,))],
+    weights = lax.all_to_all(weights, "lon", 0, 0)
+
+    new_state, log_weight = pl.pallas_call(
+        functools.partial(assemble, sizes, 1.0 / (256.0 * obs_cell.shape[0])),
+        out_shape=(shape(particles, fields, strip, lats), shape(1, particles)),
+        in_specs=[SMEM, VMEM, VMEM, VMEM, VMEM],
+        out_specs=(HBM, HBM),
+        scratch_shapes=[pltpu.VMEM((1, particles), F32), pltpu.SemaphoreType.DMA((particles + 1,))],
         compiler_params=LIMIT,
         cost_estimate=pl.CostEstimate(flops=0, bytes_accessed=2000000, transcendentals=0),
-    )(source, current, received)
-
-    log_weight = prior_weight - weight[0, :particles] / (256.0 * obs_cell.shape[0])
-    return new_state, log_weight
+    )(source, current, received, weights, prior_weight[None])
+    return new_state, log_weight[0]
 
 
 def solution(mesh):

time: 25.5 us -> 27.3 us (1.071)
  blocking collectives: 0 us -> 11.7 us
  waiting for transfers between devices: 7 us -> 0.01 us
  starting transfers between devices: 9.17 us -> 6.19 us
  local copies, waits for them, and re-layouts: 0.05 us -> 0.71 us
  other arithmetic: 0.52 us -> 0 us
    all_to_all x0 -> x1, blocking collectives: none -> 11.7 us  [local(): weights = lax.all_to_all(weights, 'lon', 0, 0)]
    ppermute x3 -> x0, waiting for transfers between devices: 6.99 us -> none  [local(): lax.ppermute(weight, 'lon', [(i, i ^ bit) for i in range(strips)])]
    ppermute x3 -> x0, starting transfers between devices: 2.99 us -> none  [local(): lax.ppermute(weight, 'lon', [(i, i ^ bit) for i in range(strips)])]
    unnamed x22, local copies, waits for them, and re-layouts: 0.05 us -> 0.71 us
    sub x1 -> x0, other arithmetic: 0.51 us -> none  [local(): prior_weight - weight[0, :particles] / (256.0 * obs_cell.shape[0])]
  transfers between devices with their start and end apart: 6 -> 3, of which waited for: 3 -> 0; matrix products, arithmetic and copies ran while one was open for 0% -> 0% of each run, Pallas kernels for 18% -> 11%
where the time goes in v5:
time: 27.3 us; the launch traced here: 27.2 us
  blocking collectives  11.7 us (43%)
  Pallas kernels  7.77 us (28%)
  starting transfers between devices  6.19 us (23%)
  between operations  0.78 us (3%)
  local copies, waits for them, and re-layouts  0.71 us (3%)
    all_to_all x1, blocking collectives, local(): weights = lax.all_to_all(weights, 'lon', 0, 0)  11.7 us
    ppermute x1, starting transfers between devices, local(): from_east = lax.ppermute(send_west, 'lon', westward)  3.12 us
    ppermute x1, starting transfers between devices, local(): from_west = lax.ppermute(send_east, 'lon', eastward)  2.99 us
    pallas_call x1, Pallas kernels, local(): pl.pallas_call(functools.partial(bulk, sizes), out_shape=(shape(rows, lat...  2.99 us
    pallas_call x1, Pallas kernels, local(): pl.pallas_call(functools.partial(prepare, sizes), out_shape=(packet, pack...  2.33 us
    pallas_call x1, Pallas kernels, local(): pl.pallas_call(functools.partial(assemble, sizes, 1.0 / (256.0 * obs_cell...  1.59 us
    pallas_call x1, Pallas kernels, local(): pl.pallas_call(functools.partial(correct, sizes), out_shape=(shape(strips...  0.75 us
    unnamed x22, local copies, waits for them, and re-layouts  0.71 us
  transfers between devices with their start and end apart: 3, of which 0 were waited for; matrix products, arithmetic and copies ran while one was open for 0% of the time, Pallas kernels for 11%

profile of v5, /device:TPU:0, one launch (start us, length us, event | category | flops | bytes accessed | tf_op | source)
XLA Modules:
  0.0 27.2 jit_solution(3754136070152228804)
XLA Ops:
  0.6 0.0 copy-start
  0.6 0.0 copy-start.1
  0.7 0.0 copy-start.2
  0.7 0.0 copy-start.7
  0.7 2.3 %shard_map.105 = (f32[72,256]{1,0:T(8,128)}, f32[72,256]{1,0:T(8,128)}) custom-call(f32[32,32,256]{2,1,0:T(8,128)} %bitcast.8, bf16[2,1024,256]{2,1,0:T(8,128)(2,1)} %bitcast.10, f32[2,32,256]{2,1,0:T(8,128)} %courant_hbm.1, f32[4]{0:T(128)} %diffusion_hbm.1, f32[4,4]{1,0:T(4,128)} %mixing.3, s32[1,256]{1,0:T(1,128)} %bitcast.14, f32[1,256]{1,0:T(1,128)} %bitcast.16), custom_call_target="tpu_custom_call" | custom-call | flops 1000000 | bytes 2000000 | tf_op jit(solution)/shard_map/pallas_call | solution.py:333
  3.0 0.0 copy-start.5
  3.0 3.0 %collective-permute-start = (f32[72,256]{1,0:T(8,128)}, f32[72,256]{1,0:T(8,128)S(1)}, u32[]{:S(2)}, u32[]{:S(2)}) collective-permute-start(f32[72,256]{1,0:T(8,128)} %get-tuple-element.15.own_east), channel_id=1, source_target_pairs={{0,2},{2,4},{4,6},{6,8},{8,10},{10,12},{12,14},{14,0},{1,3},{3,5},... | collective-permute-start | bytes 221192 | tf_op jit(solution)/shard_map/ppermute | solution.py:355
  6.0 0.0 copy-start.6
  6.0 0.0 copy-start.8
  6.0 3.1 %collective-permute-start.1 = (f32[72,256]{1,0:T(8,128)}, f32[72,256]{1,0:T(8,128)S(1)}, u32[]{:S(2)}, u32[]{:S(2)}) collective-permute-start(f32[72,256]{1,0:T(8,128)} %get-tuple-element.16.own_west), channel_id=1, source_target_pairs={{0,14},{2,0},{4,2},{6,4},{8,6},{10,8},{12,10},{14,12},{1,15},{3,1}... | collective-permute-start | bytes 221192 | tf_op jit(solution)/shard_map/ppermute | solution.py:356
  9.1 0.0 copy-done
  9.1 0.0 copy-done.1
  9.2 0.0 copy-done.2
  9.2 0.0 copy-done.7
  9.2 0.0 copy-done.5
  9.2 0.0 copy-done.6
  9.2 0.0 copy-done.8
  9.2 0.0 copy-start.3
  9.2 0.0 copy-start.4
  9.2 3.0 %shard_map.104 = (f32[1024,256]{1,0:T(8,128)S(1)}, f32[8,128]{1,0:T(8,128)S(1)}, f32[64,256]{1,0:T(8,128)S(1)}, f32[32,256]{1,0:T(8,128)S(1)}, f32[40,256]{1,0:T(8,128)S(1)}, /*index=5*/f32[12,256]{1,0:T(8,128)S(1)}) custom-call(f32[1024,256]{1,0:T(8,128)S(1)} %bitcast.9, bf16[2,1024,256]{2,1,0:T(8,128)(2,1)S(1)} %bitcast.11, f32[2,32,256]{2,1,0:T(8,128)S(1)} %copy-done.2, ...), custom_call_target="tpu_custom_call" | custom-call | flops 30000000 | bytes 4000000 | tf_op jit(solution)/shard_map/pallas_call | solution.py:358
  12.2 0.0 collective-permute-done.from_west
  12.2 0.0 collective-permute-done.1.from_east
  12.2 0.0 copy-done.3
  12.2 0.0 copy-done.4
  12.2 0.8 %shard_map.106 = (f32[8,1,128]{2,1,0:T(1,128)S(1)}, f32[4,32,256]{2,1,0:T(8,128)S(1)}) custom-call(f32[72,256]{1,0:T(8,128)S(1)} %copy-done.3, f32[72,256]{1,0:T(8,128)S(1)} %copy-done.4, f32[72,256]{1,0:T(8,128)S(1)} %collective-permute-done.from_west, f32[72,256]{1,0:T(8,128)S(1)} %collective-permute-done.1.from_east, f32[4,4]{1,0:T(4,128)S(1)} %copy-done.5, ...), custom_call_target="tpu_custom_call" | custom-call | flops 1000000 | bytes 1000000 | tf_op jit(solution)/shard_map/pallas_call | solution.py:370
  13.0 0.1 shard_map.107
  13.1 0.1 collective-permute-start.2
  13.2 11.7 %all_to_all.5.weights = f32[8,1,128]{2,1,0:T(1,128)S(1)} all-to-all(f32[8,1,128]{2,1,0:T(1,128)S(1)} %get-tuple-element.23), channel_id=1, replica_groups=mesh['groups'=2,'lon'=8,'dom'=2] {'lon'}, dimensions={0} | all-to-all | bytes 8192 | tf_op jit(solution)/shard_map/all_to_all | solution.py:389
  24.9 0.0 copy-start.9
  24.9 0.0 copy-start.10
  24.9 0.0 collective-permute-done.2.received
  24.9 0.6 %copy-done.9 = s32[16]{0:T(128)S(1)} copy-done((s32[16]{0:T(128)S(1)}, s32[16]{0:T(128)}, u32[]{:S(2)}) %copy-start.9) | copy-done | bytes 88
  25.6 0.0 copy-done.10
  25.6 1.6 %shard_map.108 = (f32[8,4,32,256]{3,2,1,0:T(8,128)}, f32[1,8]{1,0:T(1,128)}) custom-call(s32[16]{0:T(128)S(1)} %copy-done.9, f32[8,4,32,256]{3,2,1,0:T(8,128)S(1)} %bitcast.13, f32[8,4,32,256]{3,2,1,0:T(8,128)S(1)} %collective-permute-done.2.received, f32[8,1,128]{2,1,0:T(1,128)S(1)} %all_to_all.5.weights, f32[1,8]{1,0:T(1,128)S(1)} %bitcast.18), custom_call_target="tpu_custom_call" | custom-call | bytes 2000000 | tf_op jit(solution)/shard_map/pallas_call | solution.py:391
Async XLA Ops:
  0.6 8.5 %copy-start = (f32[8,4,32,256]{3,2,1,0:T(8,128)S(1)}, f32[8,4,32,256]{3,2,1,0:T(8,128)}, u32[]{:S(2)}) copy-start(f32[8,4,32,256]{3,2,1,0:T(8,128)} %param.9) | copy-start | bytes 3145732
  0.6 8.5 %copy-start.1 = (bf16[2,8,4,32,256]{4,3,2,1,0:T(8,128)(2,1)S(1)}, bf16[2,8,4,32,256]{4,3,2,1,0:T(8,128)(2,1)}, u32[]{:S(2)}) copy-start(bf16[2,8,4,32,256]{4,3,2,1,0:T(8,128)(2,1)} %param.10) | copy-start | bytes 3145732
  0.7 8.5 %copy-start.2 = (f32[2,32,256]{2,1,0:T(8,128)S(1)}, f32[2,32,256]{2,1,0:T(8,128)}, u32[]{:S(2)}) copy-start(f32[2,32,256]{2,1,0:T(8,128)} %courant_hbm.1) | copy-start | bytes 196612
  0.7 8.5 %copy-start.7 = (f32[256]{0:T(256)S(1)}, f32[256]{0:T(256)}, u32[]{:S(2)}) copy-start(f32[256]{0:T(256)} %param.16) | copy-start | bytes 3076
  3.0 6.1 %copy-start.5 = (f32[4,4]{1,0:T(4,128)S(1)}, f32[4,4]{1,0:T(4,128)}, u32[]{:S(2)}) copy-start(f32[4,4]{1,0:T(4,128)} %mixing.3) | copy-start | bytes 196
  3.0 9.2 %collective-permute-start = (f32[72,256]{1,0:T(8,128)}, f32[72,256]{1,0:T(8,128)S(1)}, u32[]{:S(2)}, u32[]{:S(2)}) collective-permute-start(f32[72,256]{1,0:T(8,128)} %get-tuple-element.15.own_east), channel_id=1, source_target_pairs={{0,2},{2,4},{4,6},{6,8},{8,10},{10,12},{12,14},{14,0},{1,3},{3,5},... | collective-permute-start | bytes 221192 | tf_op jit(solution)/shard_map/ppermute | solution.py:355
  6.0 3.2 %copy-start.6 = (s32[256]{0:T(256)S(1)}, s32[256]{0:T(256)}, u32[]{:S(2)}) copy-start(s32[256]{0:T(256)} %param.15) | copy-start | bytes 3076
  6.0 3.2 %copy-start.8 = (f32[4]{0:T(128)S(1)}, f32[4]{0:T(128)}, u32[]{:S(2)}) copy-start(f32[4]{0:T(128)} %diffusion_hbm.1) | copy-start | bytes 52
  6.0 6.2 %collective-permute-start.1 = (f32[72,256]{1,0:T(8,128)}, f32[72,256]{1,0:T(8,128)S(1)}, u32[]{:S(2)}, u32[]{:S(2)}) collective-permute-start(f32[72,256]{1,0:T(8,128)} %get-tuple-element.16.own_west), channel_id=1, source_target_pairs={{0,14},{2,0},{4,2},{6,4},{8,6},{10,8},{12,10},{14,12},{1,15},{3,1}... | collective-permute-start | bytes 221192 | tf_op jit(solution)/shard_map/ppermute | solution.py:356
  9.2 3.0 %copy-start.3 = (f32[72,256]{1,0:T(8,128)S(1)}, f32[72,256]{1,0:T(8,128)}, u32[]{:S(2)}) copy-start(f32[72,256]{1,0:T(8,128)} %get-tuple-element.15.own_east) | copy-start | bytes 221188
  9.2 3.0 %copy-start.4 = (f32[72,256]{1,0:T(8,128)S(1)}, f32[72,256]{1,0:T(8,128)}, u32[]{:S(2)}) copy-start(f32[72,256]{1,0:T(8,128)} %get-tuple-element.16.own_west) | copy-start | bytes 221188
  13.1 11.8 %collective-permute-start.2 = (f32[8,4,32,256]{3,2,1,0:T(8,128)S(1)}, f32[8,4,32,256]{3,2,1,0:T(8,128)S(1)}, u32[]{:S(2)}, u32[]{:S(2)}) collective-permute-start(f32[8,4,32,256]{3,2,1,0:T(8,128)S(1)} %bitcast.12), channel_id=1, source_target_pairs={{0,1},{1,0},{2,3},{3,2},{4,5},{5,4},{6,7},{7,6},{8,9},{9,8},{10,11... | collective-permute-start | bytes 3145736 | tf_op jit(solution)/shard_map/ppermute | solution.py:388
  24.9 0.7 %copy-start.9 = (s32[16]{0:T(128)S(1)}, s32[16]{0:T(128)}, u32[]{:S(2)}) copy-start(s32[16]{0:T(128)} %source.1) | copy-start | bytes 196
  24.9 0.7 %copy-start.10 = (f32[8]{0:T(128)S(1)}, f32[8]{0:T(128)}, u32[]{:S(2)}) copy-start(f32[8]{0:T(128)} %param.14) | copy-start | bytes 100

commit v6 on v4

v6 whole, which is shorter than its diff:
```python
import functools

import jax
import jax.numpy as jnp
from jax import lax
from jax.experimental import pallas as pl
from jax.experimental.pallas import tpu as pltpu
from jax.sharding import PartitionSpec as P

noise_var = 0.04
VMEM = pl.BlockSpec(memory_space=pltpu.VMEM)
SMEM = pl.BlockSpec(memory_space=pltpu.SMEM)
HBM = pl.BlockSpec(memory_space=pltpu.HBM)
LIMIT = pltpu.CompilerParams(vmem_limit_bytes=16 * 1024 * 1024)
BF16 = jnp.bfloat16
F32 = jnp.float32


def north(v):
    return pltpu.roll(v, v.shape[1] - 1, 1)


def south(v):
    return pltpu.roll(v, 1, 1)


def coefficients(zonal, merid, rate, self_mix):
    lat = lax.broadcasted_iota(jnp.int32, zonal.shape, 1)
    zonal_half, zonal_rate = 0.5 * zonal, 0.5 * zonal * zonal + rate
    merid_half, merid_rate = 0.5 * merid, 0.5 * merid * merid + rate
    east, west = zonal_rate - zonal_half, zonal_rate + zonal_half
    to_north, to_south = merid_rate - merid_half, merid_rate + merid_half
    centre = 1.0 + self_mix - 2.0 * zonal_rate - 2.0 * merid_rate
    last, first = lat == zonal.shape[1] - 1, lat == 0
    centre = centre + jnp.where(last, to_north, 0.0) + jnp.where(first, to_south, 0.0)
    to_north = jnp.where(last, 0.0, to_north)
    to_south = jnp.where(first, 0.0, to_south)
    return centre, east, west, to_north, to_south


def mixed(mixing, field, values):
    total = None
    for other, value in enumerate(values):
        if other != field:
            term = mixing[field, other] * value
            total = term if total is None else total + term
    return total


def pick_rows(kinds, particles, fields, strip, columns):
    rows = len(kinds) * particles
    out = lax.broadcasted_iota(jnp.int32, (rows, columns), 0)
    col = lax.broadcasted_iota(jnp.int32, (rows, columns), 1)
    want = jnp.full((rows, columns), -1, jnp.int32)
    for place, (field, x) in enumerate(kinds):
        inside = (out >= place * particles) & (out < (place + 1) * particles)
        target = (out - place * particles) * (fields * strip) + field * strip + x
        want = jnp.where(inside, target, want)
    return (col == want).astype(BF16)


def stack_rows(rows):
    sub = lax.broadcasted_iota(jnp.int32, (len(rows), rows[0].shape[1]), 0)
    out = None
    for p, row in enumerate(rows):
        row = jnp.broadcast_to(row, sub.shape)
        out = row if out is None else jnp.where(sub == p, row, out)
    return out


def in_row(column):
    total = jnp.broadcast_to(jnp.sum(column, axis=1, keepdims=True), column.shape)
    diagonal = lax.broadcasted_iota(jnp.int32, total.shape, 0) == lax.broadcasted_iota(jnp.int32, total.shape, 1)
    return jnp.sum(jnp.where(diagonal, total, 0.0), axis=0, keepdims=True)


def wide(v):
    return v[:, :128] + v[:, 128:]


def observation_maps(sizes, cell, value):
    particles, fields, strip, lats, strips = sizes
    x0 = lax.axis_index("lon") * strip
    shift = lats.bit_length() - 1
    local_cell = cell - x0 * lats
    obs_lon = lax.shift_right_arithmetic(local_cell, shift)
    obs_lat = local_cell & (lats - 1)
    count = cell.shape[1]
    here = lax.broadcasted_iota(jnp.int32, (strip, count), 0) == obs_lon
    high = value.astype(BF16)
    rest = value - high.astype(F32)
    mid = rest.astype(BF16)
    low = (rest - mid.astype(F32)).astype(BF16)
    zero = jnp.zeros((strip, count), F32)
    parts = [jnp.where(here, 1.0, zero)]
    parts += [jnp.where(here, p.astype(F32), zero) for p in (high, mid, low)]
    left = jnp.concatenate(parts, 0).astype(BF16)
    right = (lax.broadcasted_iota(jnp.int32, (lats, count), 0) == obs_lat).astype(F32).astype(BF16)
    dense = lax.dot_general(left, right, (((1,), (1,)), ((), ())), preferred_element_type=F32)
    lon = (lax.broadcasted_iota(jnp.int32, (strip, lats), 0) + x0).astype(F32)
    precision = 1.0 + 2.0 * lon / (strip * strips)
    target = dense[strip:2 * strip] + (dense[2 * strip:3 * strip] + dense[3 * strip:])
    return dense[:strip] * (0.25 * precision), target


def prepare(sizes, state_hbm, noise_hbm, courant_hbm, diffusion_hbm, mixing_hbm, cell_hbm, value_hbm,
            send_east, send_west,
            low, high, noise0, noise1, courant, diffusion, mixing, cell, value, sems):
    particles, fields, strip, lats, strips = sizes
    n = fields * particles
    copies = [pltpu.make_async_copy(source, target, sems.at[k]) for k, (source, target) in enumerate((
        (cell_hbm, cell), (value_hbm, value), (courant_hbm, courant), (diffusion_hbm, diffusion),
        (mixing_hbm, mixing), (noise_hbm.at[0], noise0), (noise_hbm.at[1, :, 0], noise1),
        (state_hbm.at[:, :, :8], low), (state_hbm.at[:, :, strip - 8:], high)))]
    for copy in copies:
        copy.start()
    copies[0].wait()
    copies[1].wait()
    gain, target = observation_maps(sizes, cell[...], value[...])
    kinds = []
    for x, step in ((strip - 1, -1), (0, 1)):
        kinds += [(f, x) for f in range(fields)] + [(f, x + step) for f in range(fields)] + [(0, x + 2 * step)]
    pick0 = pick_rows(kinds, particles, fields, strip, n * strip)
    pick1 = pick_rows([(0, x) for x in (strip - 1, strip - 2, 0, 1)], particles, 1, strip, particles * strip)
    for copy in copies[2:5]:
        copy.wait()

    sides = []
    for first, inward, outward in ((strip - 8, 2, 1), (0, 1, 2)):
        tile = [coefficients(courant[0, first:first + 8], courant[1, first:first + 8], diffusion[f], mixing[f, f])
                for f in range(fields)]
        sides.append([[c[0], c[inward], c[outward], c[3], c[4]] for c in tile])
    copies[5].wait()
    rows0 = jnp.dot(pick0, noise0[...].reshape(n * strip, lats), preferred_element_type=F32)
    copies[6].wait()
    rows1 = jnp.dot(pick1, noise1[...].reshape(particles * strip, lats), preferred_element_type=F32)
    copies[7].wait()
    copies[8].wait()

    def edge(side, out):
        tile, x, first, step = ((high, strip - 1, strip - 8, -1), (low, 0, 0, 1))[side]
        base0, base1 = side * (2 * fields + 1) * particles, side * 2 * particles

        def coefs_at(f, k):
            at = x + k * step - first
            return [c[at:at + 1] for c in sides[side][f]]

        def maps_at(k):
            at = x + k * step
            return gain[at:at + 1], target[at:at + 1]

        def state_at(f, k):
            at = x + k * step - first
            return stack_rows([tile[p, f, at:at + 1] for p in range(particles)])

        def moved(f, k, here, inner, outer):
            centre, inward, outward, to_north, to_south = coefs_at(f, k)
            v = here[f]
            total = centre * v + inward * inner + to_north * north(v) + to_south * south(v) + mixed(mixing, f, here)
            return total if outer is None else total + outward * outer

        def noisy0(k, f):
            at = base0 + (k * fields + f) * particles
            return rows0[at:at + particles]

        def noisy1(k):
            at = base1 + k * particles
            return rows1[at:at + particles]

        def nudged(value, k):
            g, v = maps_at(k)
            push = g * (v - value)
            return value + push, push

        state = [[state_at(f, k) for f in range(fields)] for k in range(3)]
        third = state_at(0, 3)
        result = [[], []]
        pushes = []
        for k in range(2):
            for f in range(fields):
                new = moved(f, k, state[k], state[k + 1][f], state[k - 1][f] if k else None)
                if f == 0:
                    new, push = nudged(new, k)
                    pushes.append(push)
                result[k].append(new + noisy0(k, f))
        new, _ = nudged(moved(0, 2, state[2], third, state[1][0]), 2)
        inside = new + noisy0(2, 0)

        g0, _ = maps_at(0)
        g1, _ = maps_at(1)
        slope = [-(1.0 / noise_var) * g0 * (pushes[0] + noisy0(0, 0))]
        bend = [(0.5 / noise_var) * g0 * g0]
        for k, g in enumerate((g0, g1)):
            new = moved(0, k, result[k], result[1][0] if k == 0 else inside, result[0][0] if k else None)
            new, push = nudged(new, k)
            miss = maps_at(k)[1] - (new + noisy1(k))
            weight = 4.0 * g
            slope.append(-(1.0 / noise_var) * g * (push + noisy1(k)) - weight * (1.0 - g) * miss)
            bend.append((0.5 / noise_var) * g * g + 0.5 * weight * (1.0 - g) * (1.0 - g))
        outward = coefs_at(0, 0)[2]
        onward = coefs_at(0, 1)[2] * (1.0 - g0) * outward

        for f in range(fields):
            out[f * particles:(f + 1) * particles] = state[0][f]
            out[n + f * particles:n + (f + 1) * particles] = result[0][f]
        out[2 * n:2 * n + particles] = outward * slope[0] + onward * slope[2]
        out[2 * n + particles:2 * n + 2 * particles] = slope[1]
        inner = x + step
        last = (outward * outward * bend[0] + onward * onward * bend[2], bend[1],
                courant[0, x:x + 1], courant[1, x:x + 1], g0, courant[0, inner:inner + 1], g1,
                jnp.zeros((1, lats), F32))
        out[2 * n + 2 * particles:] = stack_rows(last)

    edge(0, send_east)
    edge(1, send_west)


def zero_halo(sizes, courant, diffusion, mixing, coefs):
    particles, fields, strip, lats, strips = sizes
    lon = lax.broadcasted_iota(jnp.int32, (strip, lats), 0)
    for f in range(fields):
        centre, east, west, to_north, to_south = coefficients(
            courant[0], courant[1], diffusion[f], mixing[f, f])
        coefs[f, 0] = centre
        coefs[f, 1] = jnp.where(lon == strip - 1, 0.0, east)
        coefs[f, 2] = jnp.where(lon == 0, 0.0, west)
        coefs[f, 3] = to_north
        coefs[f, 4] = to_south

    def moved(values, f):
        v = values[f]
        return (coefs[f, 0] * v + coefs[f, 1] * pltpu.roll(v, strip - 1, 0) + coefs[f, 2] * pltpu.roll(v, 1, 0)
                + coefs[f, 3] * north(v) + coefs[f, 4] * south(v) + mixed(mixing, f, values))

    return moved


def observed_bulk(sizes, state, noise, courant, diffusion, mixing, cell, value, middle, out, weight,
                  coefs, maps, partial):
    particles, fields, strip, lats, strips = sizes
    maps[0], maps[1] = observation_maps(sizes, cell[...], value[...])
    moved = zero_halo(sizes, courant, diffusion, mixing, coefs)

    def body(p, carry):
        values = [state[p, f] for f in range(fields)]
        total = None
        for f in range(fields):
            new = moved(values, f)
            add = noise[0, p, f].astype(F32)
            if f == 0:
                push = maps[0] * (maps[1] - new)
                new = new + push
                total = push * (push + 2.0 * add)
            middle[p, f] = new + add
        values = [middle[p, f] for f in range(fields)]
        new = moved(values, 0)
        add = noise[1, p, 0].astype(F32)
        push = maps[0] * (maps[1] - new)
        new = new + push + add
        miss = maps[1] - new
        total = (0.5 / noise_var) * (total + push * (push + 2.0 * add)) + (2.0 * maps[0]) * (miss * miss)
        out[p] = new
        partial[pl.ds(p, 1), :] = wide(jnp.sum(total, axis=0, keepdims=True))
        return carry

    lax.fori_loop(0, particles, body, 0)
    weight[...] = in_row(partial[...])


def other_bulk(sizes, middle, observed, noise, courant, diffusion, mixing, out, coefs):
    particles, fields, strip, lats, strips = sizes
    moved = zero_halo(sizes, courant, diffusion, mixing, coefs)

    def body(p, carry):
        values = [middle[p, f] for f in range(fields)]
        out[p, 0] = observed[p]
        for f in range(1, fields):
            out[p, f] = moved(values, f) + noise[1, p, f].astype(F32)
        return carry

    lax.fori_loop(0, particles, body, 0)


def correct(sizes, own_east, own_west, from_west, from_east, diffusion, mixing, bulk_weight, bulk_beside,
            weight, changes):
    particles, fields, strip, lats, strips = sizes
    n = fields * particles

    def field_rows(ref, start, f):
        return ref[start + f * particles:start + (f + 1) * particles]

    packets = (own_east, from_east, own_west, from_west)
    last = 2 * n + 2 * particles
    zonal = stack_rows([ref[last + 2:last + 3] for ref in packets] + [ref[last + 5:last + 6] for ref in packets])
    merid = stack_rows([ref[last + 3:last + 4] for ref in packets] * 2)
    tile = [coefficients(zonal, merid, diffusion[f], mixing[f, f]) for f in range(fields)]
    total = jnp.zeros((particles, lats), F32)
    for k, owner in enumerate(packets):
        other_k = k ^ 1
        other = packets[other_k]
        outward_at = (1, 2, 2, 1)[k]
        outward_other = (1, 2, 2, 1)[other_k]
        gain = owner[last + 4:last + 5]
        gain_other = other[last + 4:last + 5]
        first = []
        for f in range(fields):
            step = tile[f][outward_at][k:k + 1] * field_rows(other, 0, f)
            first.append((1.0 - gain) * step if f == 0 else step)
        mine = k in (0, 2)
        for f in range(fields if mine else 1):
            centre, to_north, to_south = [tile[f][c][k:k + 1] for c in (0, 3, 4)]
            outward = tile[f][outward_at][k:k + 1]
            reach = tile[f][outward_other][other_k:other_k + 1]
            if f == 0:
                reach = (1.0 - gain_other) * reach
            outside = field_rows(other, n, f) + reach * field_rows(owner, 0, f)
            step = (centre * first[f] + outward * outside + to_north * north(first[f])
                    + to_south * south(first[f]) + mixed(mixing, f, first))
            if f == 0:
                seen = field_rows(other, 0, 0)
                slope, slope_step = owner[2 * n:2 * n + particles], owner[2 * n + particles:last]
                bend, bend_step = owner[last:last + 1], owner[last + 1:last + 2]
                total = total + seen * (slope + bend * seen) + step * (slope_step + bend_step * step)
            if mine:
                beside = tile[f][outward_at][4 + k:5 + k] * first[f]
                if f == 0:
                    step = (1.0 - gain) * step
                    beside = (1.0 - owner[last + 6:last + 7]) * beside
                edge, inner = (3, 2) if k == 0 else (0, 1)
                changes[edge, f * particles:(f + 1) * particles] = step
                changes[inner, f * particles:(f + 1) * particles] = beside
    weight[...] = in_row(wide(total)) + (bulk_weight[...] + bulk_beside[...])


def apply_changes(sizes, current, changes, out):
    particles, fields, strip, lats, strips = sizes
    sub = lax.broadcasted_iota(jnp.int32, (8, lats), 0)
    for p in range(particles):
        for f in range(fields):
            row = f * particles + p
            rows = [jnp.broadcast_to(changes[k, row:row + 1], sub.shape) for k in range(4)]
            out[p, f, :8] = current[p, f, :8] + jnp.where(sub == 0, rows[0], jnp.where(sub == 1, rows[1], 0.0))
            out[p, f, 8:strip - 8] = current[p, f, 8:strip - 8]
            out[p, f, strip - 8:] = current[p, f, strip - 8:] + jnp.where(
                sub == 7, rows[3], jnp.where(sub == 6, rows[2], 0.0))


def assemble(sizes, source, current, received, out, sems):
    particles = sizes[0]
    dom = lax.axis_index("dom")

    def copy(j, ref, at):
        return pltpu.make_async_copy(ref.at[at], out.at[j], sems.at[j])

    for j in range(particles):
        wanted = source[dom * particles + j]
        mine = wanted // particles == dom
        at = wanted % particles

        @pl.when(mine)
        def _():
            copy(j, current, at).start()

        @pl.when(jnp.logical_not(mine))
        def _():
            copy(j, received, at).start()

    for j in range(particles):
        copy(j, current, 0).wait()


def local(ensemble_state, proposal_noise, courant, diffusion, mixing, prior_weight, obs_cell, obs_value, source):
    particles, fields, strip, lats = ensemble_state.shape
    strips = lax.axis_size("lon")
    sizes = (particles, fields, strip, lats, strips)
    packet = jax.ShapeDtypeStruct((2 * particles * fields + 2 * particles + 8, lats), F32)
    cell, value = obs_cell[None], obs_value[None]

    def shape(*dims):
        return jax.ShapeDtypeStruct(dims, F32)

    send_east, send_west = pl.pallas_call(
        functools.partial(prepare, sizes),
        out_shape=(packet, packet),
        in_specs=[HBM] * 7,
        out_specs=(VMEM,) * 2,
        scratch_shapes=[
            pltpu.VMEM((particles, fields, 8, lats), F32),
            pltpu.VMEM((particles, fields, 8, lats), F32),
            pltpu.VMEM((particles, fields, strip, lats), BF16),
            pltpu.VMEM((particles, strip, lats), BF16),
            pltpu.VMEM(courant.shape, F32),
            pltpu.SMEM(diffusion.shape, F32),
            pltpu.SMEM(mixing.shape, F32),
            pltpu.VMEM(cell.shape, jnp.int32),
            pltpu.VMEM(value.shape, F32),
            pltpu.SemaphoreType.DMA((9,)),
        ],
        compiler_params=pltpu.CompilerParams(vmem_limit_bytes=60 * 1024 * 1024),
        cost_estimate=pl.CostEstimate(flops=1000000, bytes_accessed=2000000, transcendentals=0),
    )(ensemble_state, proposal_noise, courant, diffusion, mixing, cell, value)

    eastward = [(i, (i + 1) % strips) for i in range(strips)]
    westward = [(i, (i - 1) % strips) for i in range(strips)]
    from_west = lax.ppermute(send_east, "lon", eastward)
    from_east = lax.ppermute(send_west, "lon", westward)

    whole = (particles, fields, strip, lats)
    middle, observed, bulk_weight = pl.pallas_call(
        functools.partial(observed_bulk, sizes),
        out_shape=(shape(*whole), shape(particles, strip, lats), shape(1, 128)),
        in_specs=[VMEM, VMEM, VMEM, SMEM, SMEM, VMEM, VMEM],
        out_specs=(VMEM,) * 3,
        scratch_shapes=[pltpu.VMEM((fields, 5, strip, lats), F32), pltpu.VMEM((2, strip, lats), F32),
                        pltpu.VMEM((particles, 128), F32)],
        compiler_params=LIMIT,
        cost_estimate=pl.CostEstimate(flops=20000000, bytes_accessed=4000000, transcendentals=0),
    )(ensemble_state, proposal_noise, courant, diffusion, mixing, cell, value)
    beside = lax.ppermute(bulk_weight, "lon", [(i, i ^ 1) for i in range(strips)])

    current = pl.pallas_call(
        functools.partial(other_bulk, sizes),
        out_shape=shape(*whole),
        in_specs=[VMEM] * 4 + [SMEM] * 2,
        out_specs=VMEM,
        scratch_shapes=[pltpu.VMEM((fields, 5, strip, lats), F32)],
        compiler_params=LIMIT,
        cost_estimate=pl.CostEstimate(flops=10000000, bytes_accessed=4000000, transcendentals=0),
    )(middle, observed, proposal_noise, courant, diffusion, mixing)

    from_west, from_east, beside = lax.optimization_barrier((from_west, from_east, beside))
    weight, changes = pl.pallas_call(
        functools.partial(correct, sizes),
        out_shape=(shape(1, 128), shape(4, particles * fields, lats)),
        in_specs=[VMEM] * 4 + [SMEM] * 2 + [VMEM] * 2,
        out_specs=(VMEM,) * 2,
        compiler_params=LIMIT,
        cost_estimate=pl.CostEstimate(flops=1000000, bytes_accessed=1000000, transcendentals=0),
    )(send_east, send_west, from_west, from_east, diffusion, mixing, bulk_weight, beside)

    current = pl.pallas_call(
        functools.partial(apply_changes, sizes),
        out_shape=shape(*whole),
        in_specs=[VMEM] * 2,
        out_specs=VMEM,
        compiler_params=LIMIT,
        cost_estimate=pl.CostEstimate(flops=1000000, bytes_accessed=2000000, transcendentals=0),
    )(current, changes)

    received = lax.ppermute(current, "dom", [(0, 1), (1, 0)])
    bit = 2
    while bit < strips:
        if 2 * bit >= strips:
            weight, received = lax.optimization_barrier((weight, received))
        weight = weight + lax.ppermute(weight, "lon", [(i, i ^ bit) for i in range(strips)])
        bit *= 2

    new_state = pl.pallas_call(
        functools.partial(assemble, sizes),
        out_shape=shape(*whole),
        in_specs=[SMEM, VMEM, VMEM],
        out_specs=HBM,
        scratch_shapes=[pltpu.SemaphoreType.DMA((particles,))],
        compiler_params=LIMIT,
        cost_estimate=pl.CostEstimate(flops=0, bytes_accessed=2000000, transcendentals=0),
    )(source, current, received)

    log_weight = prior_weight - weight[0, :particles] / (256.0 * obs_cell.shape[0])
    return new_state, log_weight


def solution(mesh):
    placed = (
        P(("groups", "dom"), None, "lon", None),
        P(None, ("groups", "dom"), None, "lon", None),
        P(None, ("groups", "lon"), None),
        P(),
        P(),
        P(("groups", "dom")),
        P(("groups", "lon")),
        P(("groups", "lon")),
        P("groups"),
    )
    return jax.shard_map(
        local,
        mesh=mesh,
        in_specs=placed,
        out_specs=(P(("groups", "dom"), None, "lon", None), P(("groups", "dom"))),
        check_vma=False,
    )
```

time: 25.5 us -> 25.3 us (level)
  starting transfers between devices: 9.17 us -> 7.16 us
  Pallas kernels: 7.8 us -> 9.34 us
  waiting for transfers between devices: 7 us -> 7.31 us
    ppermute x3 -> x2, starting transfers between devices: 2.99 us -> 0.99 us  [local(): lax.ppermute(weight, 'lon', [(i, i ^ bit) for i in range(strips)])]
    ppermute x0 -> x1, waiting for transfers between devices: none -> 1.85 us  [local(): lax.ppermute(bulk_weight, 'lon', [(i, i ^ 1) for i in range(strips)])]
    ppermute x3 -> x2, waiting for transfers between devices: 6.99 us -> 5.45 us  [local(): lax.ppermute(weight, 'lon', [(i, i ^ bit) for i in range(strips)])]
    pallas_call x3 -> x4, Pallas kernels: 4.72 us -> 5.9 us  [the longest x1 2.52 us: local(): pl.pallas_call(functools.partial(observed_bulk, sizes), out_shape=(shape(...]
    pallas_call x1, Pallas kernels: 2.33 us -> 2.68 us  [local(): pl.pallas_call(functools.partial(prepare, sizes), out_shape=(packet, pack...]
  transfers between devices with their start and end apart: 6 -> 6, of which waited for: 3 -> 3; matrix products, arithmetic and copies ran while one was open for 0% -> 0% of each run, Pallas kernels for 18% -> 23%
where the time goes in v6:
time: 25.3 us; the launch traced here: 25.2 us
  Pallas kernels  9.34 us (37%)
  waiting for transfers between devices  7.31 us (29%)
  starting transfers between devices  7.16 us (28%)
  between operations  0.81 us (3%)
  other arithmetic  0.52 us (2%)
    ppermute x2, waiting for transfers between devices, local(): lax.ppermute(weight, 'lon', [(i, i ^ bit) for i in range(strips)])  5.45 us
    ppermute x1, starting transfers between devices, local(): from_east = lax.ppermute(send_west, 'lon', westward)  3.1 us
    ppermute x1, starting transfers between devices, local(): from_west = lax.ppermute(send_east, 'lon', eastward)  2.99 us
    pallas_call x1, Pallas kernels, local(): pl.pallas_call(functools.partial(prepare, sizes), out_shape=(packet, pack...  2.68 us
    pallas_call x1, Pallas kernels, local(): pl.pallas_call(functools.partial(observed_bulk, sizes), out_shape=(shape(...  2.52 us
    ppermute x1, waiting for transfers between devices, local(): lax.ppermute(bulk_weight, 'lon', [(i, i ^ 1) for i in range(strips)])  1.85 us
    pallas_call x1, Pallas kernels, local(): pl.pallas_call(functools.partial(other_bulk, sizes), out_shape=shape(*who...  1.66 us
    pallas_call x1, Pallas kernels, local(): pl.pallas_call(functools.partial(assemble, sizes), out_shape=shape(*whole...  1.58 us
  transfers between devices with their start and end apart: 6, of which 3 were waited for; matrix products, arithmetic and copies ran while one was open for 0% of the time, Pallas kernels for 23%

profile of v6, /device:TPU:0, one launch (start us, length us, event | category | flops | bytes accessed | tf_op | source)
XLA Modules:
  0.0 25.2 jit_solution(17952477997255543197)
XLA Ops:
  0.6 0.0 copy-start
  0.6 0.0 copy-start.1
  0.7 0.0 copy-start.2
  0.7 0.0 copy-start.8
  0.7 2.7 %shard_map.106 = (f32[88,256]{1,0:T(8,128)}, f32[88,256]{1,0:T(8,128)}) custom-call(f32[8,4,32,256]{3,2,1,0:T(8,128)} %state_hbm.1, bf16[2,8,4,32,256]{4,3,2,1,0:T(8,128)(2,1)} %noise_hbm.1, f32[2,32,256]{2,1,0:T(8,128)} %courant_hbm.1, f32[4]{0:T(128)} %diffusion.5, f32[4,4]{1,0:T(4,128)} %mixing.5, s32[1,256]{1,0:T(1,128)} %bitcast.4, f32[1,256]{1,0:T(1,128)} %bitcast.6), custom_call_target="tpu_custom_call" | custom-call | flops 1000000 | bytes 2000000 | tf_op jit(solution)/shard_map/pallas_call | solution.py:382
  3.4 0.0 copy-start.5
  3.4 0.0 copy-start.6
  3.4 0.0 copy-start.7
  3.4 3.0 %collective-permute-start = (f32[88,256]{1,0:T(8,128)}, f32[88,256]{1,0:T(8,128)S(1)}, u32[]{:S(2)}, u32[]{:S(2)}) collective-permute-start(f32[88,256]{1,0:T(8,128)} %get-tuple-element.16.own_east), channel_id=1, source_target_pairs={{0,2},{2,4},{4,6},{6,8},{8,10},{10,12},{12,14},{14,0},{1,3},{3,5},... | collective-permute-start | bytes 270344 | tf_op jit(solution)/shard_map/ppermute | solution.py:405
  6.4 3.1 %collective-permute-start.1 = (f32[88,256]{1,0:T(8,128)}, f32[88,256]{1,0:T(8,128)S(1)}, u32[]{:S(2)}, u32[]{:S(2)}) collective-permute-start(f32[88,256]{1,0:T(8,128)} %get-tuple-element.17.own_west), channel_id=1, source_target_pairs={{0,14},{2,0},{4,2},{6,4},{8,6},{10,8},{12,10},{14,12},{1,15},{3,1}... | collective-permute-start | bytes 270344 | tf_op jit(solution)/shard_map/ppermute | solution.py:406
  9.5 0.0 copy-done
  9.5 0.0 copy-done.1
  9.5 0.0 copy-done.2
  9.5 0.0 copy-done.8
  9.5 0.0 copy-done.5
  9.5 0.0 copy-done.6
  9.5 0.0 copy-done.7
  9.5 2.5 %shard_map.104 = (f32[8,4,32,256]{3,2,1,0:T(8,128)S(1)}, f32[8,32,256]{2,1,0:T(8,128)S(1)}, f32[1,128]{1,0:T(1,128)S(1)}) custom-call(f32[8,4,32,256]{3,2,1,0:T(8,128)S(1)} %copy-done.1, bf16[2,8,4,32,256]{4,3,2,1,0:T(8,128)(2,1)S(1)} %copy-done, f32[2,32,256]{2,1,0:T(8,128)S(1)} %copy-done.2, f32[4]{0:T(128)S(1)} %copy-done.6, f32[4,4]{1,0:T(4,128)S(1)} %copy-done.5, ...), custom_call_target="tpu_custom_call" | custom-call | flops 20000000 | bytes 4000000 | tf_op jit(solution)/shard_map/pallas_call | solution.py:409
  12.1 0.0 collective-permute-start.2
  12.1 0.0 copy-start.3
  12.1 0.0 copy-start.4
  12.1 1.7 %shard_map.105.current = f32[8,4,32,256]{3,2,1,0:T(8,128)S(1)} custom-call(f32[8,4,32,256]{3,2,1,0:T(8,128)S(1)} %get-tuple-element.14.middle, f32[8,32,256]{2,1,0:T(8,128)S(1)} %get-tuple-element.15.observed, bf16[2,8,4,32,256]{4,3,2,1,0:T(8,128)(2,1)S(1)} %copy-done, f32[2,32,256]{2,1,0:T(8,128)S(1)} %copy-done.2, f32[4]{0:T(128)S(1)} %copy-done.6, ...), custom_call_target="tpu_custom_call" | custom-call | flops 10000000 | bytes 4000000 | tf_op jit(solution)/shard_map/pallas_call | solution.py:421
  13.7 1.9 %collective-permute-done.2.bulk_beside = f32[1,128]{1,0:T(1,128)S(1)} collective-permute-done((f32[1,128]{1,0:T(1,128)S(1)}, f32[1,128]{1,0:T(1,128)S(1)}, u32[]{:S(2)}, u32[]{:S(2)}) %collective-permute-start.2) | collective-permute-done | bytes 544 | tf_op jit(solution)/shard_map/ppermute | solution.py:419
  15.6 0.0 collective-permute-done.from_west
  15.6 0.0 collective-permute-done.1.from_east
  15.6 0.0 copy-done.3
  15.6 0.0 copy-done.4
  15.6 0.8 %shard_map.107 = (f32[1,128]{1,0:T(1,128)S(1)}, f32[4,32,256]{2,1,0:T(8,128)S(1)}) custom-call(f32[88,256]{1,0:T(8,128)S(1)} %copy-done.3, f32[88,256]{1,0:T(8,128)S(1)} %copy-done.4, f32[88,256]{1,0:T(8,128)S(1)} %collective-permute-done.from_west, f32[88,256]{1,0:T(8,128)S(1)} %collective-permute-done.1.from_east, f32[4]{0:T(128)S(1)} %copy-done.6, ...), custom_call_target="tpu_custom_call" | custom-call | flops 1000000 | bytes 1000000 | tf_op jit(solution)/shard_map/pallas_call | solution.py:432
  16.4 0.1 shard_map.108.current
  16.5 0.1 collective-permute-start.4
  16.6 0.0 copy-start.9
  16.6 0.1 collective-permute-start.3
  16.7 3.5 %collective-permute-done.3 = f32[1,128]{1,0:T(1,128)S(1)} collective-permute-done((f32[1,128]{1,0:T(1,128)S(1)}, f32[1,128]{1,0:T(1,128)S(1)}, u32[]{:S(2)}, u32[]{:S(2)}) %collective-permute-start.3) | collective-permute-done | bytes 544 | tf_op jit(solution)/shard_map/ppermute | solution.py:455
  20.2 0.0 collective-permute-done.4.received
  20.2 0.9 %collective-permute-start.5 = (f32[1,128]{1,0:T(1,128)S(1)}, f32[1,128]{1,0:T(1,128)S(1)}, u32[]{:S(2)}, u32[]{:S(2)}) collective-permute-start(f32[1,128]{1,0:T(1,128)S(1)} %add.6), channel_id=1, source_target_pairs={{0,8},{2,10},{4,12},{6,14},{8,0},{10,2},{12,4},{14,6},{1,9},{3,11}... | collective-permute-start | bytes 1544 | tf_op jit(solution)/shard_map/ppermute | solution.py:455
  21.1 0.0 copy-done.9
  21.2 1.6 %shard_map.109 = f32[8,4,32,256]{3,2,1,0:T(8,128)} custom-call(s32[16]{0:T(128)S(1)} %copy-done.9, f32[8,4,32,256]{3,2,1,0:T(8,128)S(1)} %shard_map.108.current, f32[8,4,32,256]{3,2,1,0:T(8,128)S(1)} %collective-permute-done.4.received), custom_call_target="tpu_custom_call" | custom-call | bytes 2000000 | tf_op jit(solution)/shard_map/pallas_call | solution.py:458
  22.7 0.0 copy-start.10
  22.8 1.9 %collective-permute-done.5 = f32[1,128]{1,0:T(1,128)S(1)} collective-permute-done((f32[1,128]{1,0:T(1,128)S(1)}, f32[1,128]{1,0:T(1,128)S(1)}, u32[]{:S(2)}, u32[]{:S(2)}) %collective-permute-start.5) | collective-permute-done | bytes 544 | tf_op jit(solution)/shard_map/ppermute | solution.py:455
  24.7 0.0 copy-done.10
  24.7 0.5 %bitcast_subtract_fusion = f32[8]{0:T(128)} fusion(f32[8]{0:T(128)S(1)} %copy-done.10, f32[1,128]{1,0:T(1,128)S(1)} %add.7), kind=kLoop, calls=%fused_computation | loop fusion | flops 16 | bytes 96 | tf_op jit(solution)/shard_map/sub | solution.py:468
  (2 shorter events, 0.0 us)
Async XLA Ops:
  0.6 8.9 %copy-start = (bf16[2,8,4,32,256]{4,3,2,1,0:T(8,128)(2,1)S(1)}, bf16[2,8,4,32,256]{4,3,2,1,0:T(8,128)(2,1)}, u32[]{:S(2)}) copy-start(bf16[2,8,4,32,256]{4,3,2,1,0:T(8,128)(2,1)} %noise_hbm.1) | copy-start | bytes 3145732
  0.6 8.9 %copy-start.1 = (f32[8,4,32,256]{3,2,1,0:T(8,128)S(1)}, f32[8,4,32,256]{3,2,1,0:T(8,128)}, u32[]{:S(2)}) copy-start(f32[8,4,32,256]{3,2,1,0:T(8,128)} %state_hbm.1) | copy-start | bytes 3145732
  0.7 8.8 %copy-start.2 = (f32[2,32,256]{2,1,0:T(8,128)S(1)}, f32[2,32,256]{2,1,0:T(8,128)}, u32[]{:S(2)}) copy-start(f32[2,32,256]{2,1,0:T(8,128)} %courant_hbm.1) | copy-start | bytes 196612
  0.7 8.8 %copy-start.8 = (f32[256]{0:T(256)S(1)}, f32[256]{0:T(256)}, u32[]{:S(2)}) copy-start(f32[256]{0:T(256)} %param.16) | copy-start | bytes 3076
  3.4 6.1 %copy-start.5 = (f32[4,4]{1,0:T(4,128)S(1)}, f32[4,4]{1,0:T(4,128)}, u32[]{:S(2)}) copy-start(f32[4,4]{1,0:T(4,128)} %mixing.5) | copy-start | bytes 196
  3.4 6.1 %copy-start.6 = (f32[4]{0:T(128)S(1)}, f32[4]{0:T(128)}, u32[]{:S(2)}) copy-start(f32[4]{0:T(128)} %diffusion.5) | copy-start | bytes 52
  3.4 6.1 %copy-start.7 = (s32[256]{0:T(256)S(1)}, s32[256]{0:T(256)}, u32[]{:S(2)}) copy-start(s32[256]{0:T(256)} %param.15) | copy-start | bytes 3076
  3.4 12.2 %collective-permute-start = (f32[88,256]{1,0:T(8,128)}, f32[88,256]{1,0:T(8,128)S(1)}, u32[]{:S(2)}, u32[]{:S(2)}) collective-permute-start(f32[88,256]{1,0:T(8,128)} %get-tuple-element.16.own_east), channel_id=1, source_target_pairs={{0,2},{2,4},{4,6},{6,8},{8,10},{10,12},{12,14},{14,0},{1,3},{3,5},... | collective-permute-start | bytes 270344 | tf_op jit(solution)/shard_map/ppermute | solution.py:405
  6.4 9.2 %collective-permute-start.1 = (f32[88,256]{1,0:T(8,128)}, f32[88,256]{1,0:T(8,128)S(1)}, u32[]{:S(2)}, u32[]{:S(2)}) collective-permute-start(f32[88,256]{1,0:T(8,128)} %get-tuple-element.17.own_west), channel_id=1, source_target_pairs={{0,14},{2,0},{4,2},{6,4},{8,6},{10,8},{12,10},{14,12},{1,15},{3,1}... | collective-permute-start | bytes 270344 | tf_op jit(solution)/shard_map/ppermute | solution.py:406
  12.1 3.5 %collective-permute-start.2 = (f32[1,128]{1,0:T(1,128)S(1)}, f32[1,128]{1,0:T(1,128)S(1)}, u32[]{:S(2)}, u32[]{:S(2)}) collective-permute-start(f32[1,128]{1,0:T(1,128)S(1)} %get-tuple-element.18.bulk_weight), channel_id=1, source_target_pairs={{0,2},{2,0},{4,6},{6,4},{8,10},{10,8},{12,14},{14,12},{1,3},{3,1},... | collective-permute-start | bytes 1544 | tf_op jit(solution)/shard_map/ppermute | solution.py:419
  12.1 3.5 %copy-start.3 = (f32[88,256]{1,0:T(8,128)S(1)}, f32[88,256]{1,0:T(8,128)}, u32[]{:S(2)}) copy-start(f32[88,256]{1,0:T(8,128)} %get-tuple-element.16.own_east) | copy-start | bytes 270340
  12.1 3.5 %copy-start.4 = (f32[88,256]{1,0:T(8,128)S(1)}, f32[88,256]{1,0:T(8,128)}, u32[]{:S(2)}) copy-start(f32[88,256]{1,0:T(8,128)} %get-tuple-element.17.own_west) | copy-start | bytes 270340
  16.5 3.7 %collective-permute-start.4 = (f32[8,4,32,256]{3,2,1,0:T(8,128)S(1)}, f32[8,4,32,256]{3,2,1,0:T(8,128)S(1)}, u32[]{:S(2)}, u32[]{:S(2)}) collective-permute-start(f32[8,4,32,256]{3,2,1,0:T(8,128)S(1)} %shard_map.108.current), channel_id=1, source_target_pairs={{0,1},{1,0},{2,3},{3,2},{4,5},{5,4},{6,7},{7,6},{8,9},{9,8},{10,11... | collective-permute-start | bytes 3145736 | tf_op jit(solution)/shard_map/ppermute | solution.py:450
  16.6 4.5 %copy-start.9 = (s32[16]{0:T(128)S(1)}, s32[16]{0:T(128)}, u32[]{:S(2)}) copy-start(s32[16]{0:T(128)} %source.1) | copy-start | bytes 196
  16.6 3.6 %collective-permute-start.3 = (f32[1,128]{1,0:T(1,128)S(1)}, f32[1,128]{1,0:T(1,128)S(1)}, u32[]{:S(2)}, u32[]{:S(2)}) collective-permute-start(f32[1,128]{1,0:T(1,128)S(1)} %get-tuple-element.23), channel_id=1, source_target_pairs={{0,4},{2,6},{4,0},{6,2},{8,12},{10,14},{12,8},{14,10},{1,5},{3,7},... | collective-permute-start | bytes 1544 | tf_op jit(solution)/shard_map/ppermute | solution.py:455
  20.2 4.4 %collective-permute-start.5 = (f32[1,128]{1,0:T(1,128)S(1)}, f32[1,128]{1,0:T(1,128)S(1)}, u32[]{:S(2)}, u32[]{:S(2)}) collective-permute-start(f32[1,128]{1,0:T(1,128)S(1)} %add.6), channel_id=1, source_target_pairs={{0,8},{2,10},{4,12},{6,14},{8,0},{10,2},{12,4},{14,6},{1,9},{3,11}... | collective-permute-start | bytes 1544 | tf_op jit(solution)/shard_map/ppermute | solution.py:455
  22.7 1.9 %copy-start.10 = (f32[8]{0:T(128)S(1)}, f32[8]{0:T(128)}, u32[]{:S(2)}) copy-start(f32[8]{0:T(128)} %param.14) | copy-start | bytes 100

commit v7 on v6

--- a/solution.py
+++ b/solution.py
@@ -12,6 +12,7 @@
 SMEM = pl.BlockSpec(memory_space=pltpu.SMEM)
 HBM = pl.BlockSpec(memory_space=pltpu.HBM)
 LIMIT = pltpu.CompilerParams(vmem_limit_bytes=16 * 1024 * 1024)
+FREE = pl.CostEstimate(flops=0, bytes_accessed=0, transcendentals=0)
 BF16 = jnp.bfloat16
 F32 = jnp.float32
 
@@ -110,8 +111,8 @@
     n = fields * particles
     copies = [pltpu.make_async_copy(source, target, sems.at[k]) for k, (source, target) in enumerate((
         (cell_hbm, cell), (value_hbm, value), (courant_hbm, courant), (diffusion_hbm, diffusion),
-        (mixing_hbm, mixing), (noise_hbm.at[0], noise0), (noise_hbm.at[1, :, 0], noise1),
-        (state_hbm.at[:, :, :8], low), (state_hbm.at[:, :, strip - 8:], high)))]
+        (mixing_hbm, mixing), (state_hbm.at[:, :, :8], low), (state_hbm.at[:, :, strip - 8:], high),
+        (noise_hbm.at[0], noise0), (noise_hbm.at[1, :, 0], noise1)))]
     for copy in copies:
         copy.start()
     copies[0].wait()
@@ -130,34 +131,58 @@
         tile = [coefficients(courant[0, first:first + 8], courant[1, first:first + 8], diffusion[f], mixing[f, f])
                 for f in range(fields)]
         sides.append([[c[0], c[inward], c[outward], c[3], c[4]] for c in tile])
+    def coefs_at(side, f, k):
+        at = places[side][0] + k * places[side][2] - places[side][1]
+        return [c[at:at + 1] for c in sides[side][f]]
+
+    def maps_at(side, k):
+        at = places[side][0] + k * places[side][2]
+        return gain[at:at + 1], target[at:at + 1]
+
+    def moved(side, f, k, here, inner, outer):
+        centre, inward, outward, to_north, to_south = coefs_at(side, f, k)
+        v = here[f]
+        total = centre * v + inward * inner + to_north * north(v) + to_south * south(v) + mixed(mixing, f, here)
+        return total if outer is None else total + outward * outer
+
+    def nudged(side, value, k):
+        g, v = maps_at(side, k)
+        push = g * (v - value)
+        return value + push, push
+
+    def first_step(side, tile, out):
+        def state_at(f, k):
+            at = places[side][0] + k * places[side][2] - places[side][1]
+            return stack_rows([tile[p, f, at:at + 1] for p in range(particles)])
+
+        state = [[state_at(f, k) for f in range(fields)] for k in range(3)]
+        third = state_at(0, 3)
+        for f in range(fields):
+            out[f * particles:(f + 1) * particles] = state[0][f]
+        result, pushes = [[], []], []
+        for k in range(2):
+            for f in range(fields):
+                new = moved(side, f, k, state[k], state[k + 1][f], state[k - 1][f] if k else None)
+                if f == 0:
+                    new, push = nudged(side, new, k)
+                    pushes.append(push)
+                result[k].append(new)
+        inside, _ = nudged(side, moved(side, 0, 2, state[2], third, state[1][0]), 2)
+        return result, pushes, inside
+
+    places = ((strip - 1, strip - 8, -1), (0, 0, 1))
     copies[5].wait()
-    rows0 = jnp.dot(pick0, noise0[...].reshape(n * strip, lats), preferred_element_type=F32)
     copies[6].wait()
-    rows1 = jnp.dot(pick1, noise1[...].reshape(particles * strip, lats), preferred_element_type=F32)
+    started = [first_step(0, high, send_east), first_step(1, low, send_west)]
     copies[7].wait()
     copies[8].wait()
+    rows0 = jnp.dot(pick0, noise0[...].reshape(n * strip, lats), preferred_element_type=F32)
+    rows1 = jnp.dot(pick1, noise1[...].reshape(particles * strip, lats), preferred_element_type=F32)
 
     def edge(side, out):
-        tile, x, first, step = ((high, strip - 1, strip - 8, -1), (low, 0, 0, 1))[side]
+        x, _, step = places[side]
         base0, base1 = side * (2 * fields + 1) * particles, side * 2 * particles
-
-        def coefs_at(f, k):
-            at = x + k * step - first
-            return [c[at:at + 1] for c in sides[side][f]]
-
-        def maps_at(k):
-            at = x + k * step
-            return gain[at:at + 1], target[at:at + 1]
-
-        def state_at(f, k):
-            at = x + k * step - first
-            return stack_rows([tile[p, f, at:at + 1] for p in range(particles)])
-
-        def moved(f, k, here, inner, outer):
-            centre, inward, outward, to_north, to_south = coefs_at(f, k)
-            v = here[f]
-            total = centre * v + inward * inner + to_north * north(v) + to_south * south(v) + mixed(mixing, f, here)
-            return total if outer is None else total + outward * outer
+        result, pushes, inside = started[side]
 
         def noisy0(k, f):
             at = base0 + (k * fields + f) * particles
@@ -167,41 +192,22 @@
             at = base1 + k * particles
             return rows1[at:at + particles]
 
-        def nudged(value, k):
-            g, v = maps_at(k)
-            push = g * (v - value)
-            return value + push, push
-
-        state = [[state_at(f, k) for f in range(fields)] for k in range(3)]
-        third = state_at(0, 3)
-        result = [[], []]
-        pushes = []
-        for k in range(2):
-            for f in range(fields):
-                new = moved(f, k, state[k], state[k + 1][f], state[k - 1][f] if k else None)
-                if f == 0:
-                    new, push = nudged(new, k)
-                    pushes.append(push)
-                result[k].append(new + noisy0(k, f))
-        new, _ = nudged(moved(0, 2, state[2], third, state[1][0]), 2)
-        inside = new + noisy0(2, 0)
-
-        g0, _ = maps_at(0)
-        g1, _ = maps_at(1)
+        result = [[result[k][f] + noisy0(k, f) for f in range(fields)] for k in range(2)]
+        inside = inside + noisy0(2, 0)
+        g0, _ = maps_at(side, 0)
+        g1, _ = maps_at(side, 1)
         slope = [-(1.0 / noise_var) * g0 * (pushes[0] + noisy0(0, 0))]
         bend = [(0.5 / noise_var) * g0 * g0]
         for k, g in enumerate((g0, g1)):
-            new = moved(0, k, result[k], result[1][0] if k == 0 else inside, result[0][0] if k else None)
-            new, push = nudged(new, k)
-            miss = maps_at(k)[1] - (new + noisy1(k))
+            new = moved(side, 0, k, result[k], result[1][0] if k == 0 else inside, result[0][0] if k else None)
+            new, push = nudged(side, new, k)
+            miss = maps_at(side, k)[1] - (new + noisy1(k))
             weight = 4.0 * g
             slope.append(-(1.0 / noise_var) * g * (push + noisy1(k)) - weight * (1.0 - g) * miss)
             bend.append((0.5 / noise_var) * g * g + 0.5 * weight * (1.0 - g) * (1.0 - g))
-        outward = coefs_at(0, 0)[2]
-        onward = coefs_at(0, 1)[2] * (1.0 - g0) * outward
-
+        outward = coefs_at(side, 0, 0)[2]
+        onward = coefs_at(side, 0, 1)[2] * (1.0 - g0) * outward
         for f in range(fields):
-            out[f * particles:(f + 1) * particles] = state[0][f]
             out[n + f * particles:n + (f + 1) * particles] = result[0][f]
         out[2 * n:2 * n + particles] = outward * slope[0] + onward * slope[2]
         out[2 * n + particles:2 * n + 2 * particles] = slope[1]
@@ -215,12 +221,21 @@
     edge(1, send_west)
 
 
-def zero_halo(sizes, courant, diffusion, mixing, coefs):
-    particles, fields, strip, lats, strips = sizes
+class Spread:
+    def __init__(self, ref):
+        self.ref = ref
+
+    def __getitem__(self, at):
+        return self.ref[at[0]:at[0] + 1, at[1]:at[1] + 1]
+
+
+def zero_halo(sizes, courant, diffusion, mixing, mixing_scalars, coefs):
+    particles, fields, strip, lats, strips = sizes
+    diffusion, mixing = Spread(diffusion), Spread(mixing)
     lon = lax.broadcasted_iota(jnp.int32, (strip, lats), 0)
     for f in range(fields):
         centre, east, west, to_north, to_south = coefficients(
-            courant[0], courant[1], diffusion[f], mixing[f, f])
+            courant[0], courant[1], diffusion[0, f], mixing[f, f])
         coefs[f, 0] = centre
         coefs[f, 1] = jnp.where(lon == strip - 1, 0.0, east)
         coefs[f, 2] = jnp.where(lon == 0, 0.0, west)
@@ -230,20 +245,23 @@
     def moved(values, f):
         v = values[f]
         return (coefs[f, 0] * v + coefs[f, 1] * pltpu.roll(v, strip - 1, 0) + coefs[f, 2] * pltpu.roll(v, 1, 0)
-                + coefs[f, 3] * north(v) + coefs[f, 4] * south(v) + mixed(mixing, f, values))
+                + coefs[f, 3] * north(v) + coefs[f, 4] * south(v) + mixed(mixing_scalars, f, values))
 
     return moved
 
 
 def observed_bulk(sizes, state, noise, courant, diffusion, mixing, cell, value, middle, out, weight,
-                  coefs, maps, partial):
-    particles, fields, strip, lats, strips = sizes
+                  coefs, maps, partial, mixing_scalars, sem):
+    particles, fields, strip, lats, strips = sizes
+    copy = pltpu.make_async_copy(mixing, mixing_scalars, sem)
+    copy.start()
     maps[0], maps[1] = observation_maps(sizes, cell[...], value[...])
-    moved = zero_halo(sizes, courant, diffusion, mixing, coefs)
-
-    def body(p, carry):
+    moved = zero_halo(sizes, courant, diffusion, mixing, mixing_scalars, coefs)
+    copy.wait()
+
+    def one(p):
         values = [state[p, f] for f in range(fields)]
-        total = None
+        results = []
         for f in range(fields):
             new = moved(values, f)
             add = noise[0, p, f].astype(F32)
@@ -251,9 +269,9 @@
                 push = maps[0] * (maps[1] - new)
                 new = new + push
                 total = push * (push + 2.0 * add)
+            results.append(new + add)
             middle[p, f] = new + add
-        values = [middle[p, f] for f in range(fields)]
-        new = moved(values, 0)
+        new = moved(results, 0)
         add = noise[1, p, 0].astype(F32)
         push = maps[0] * (maps[1] - new)
         new = new + push + add
@@ -261,15 +279,22 @@
         total = (0.5 / noise_var) * (total + push * (push + 2.0 * add)) + (2.0 * maps[0]) * (miss * miss)
         out[p] = new
         partial[pl.ds(p, 1), :] = wide(jnp.sum(total, axis=0, keepdims=True))
+
+    def body(pair, carry):
+        one(2 * pair)
+        one(2 * pair + 1)
         return carry
 
-    lax.fori_loop(0, particles, body, 0)
+    lax.fori_loop(0, particles // 2, body, 0)
     weight[...] = in_row(partial[...])
 
 
-def other_bulk(sizes, middle, observed, noise, courant, diffusion, mixing, out, coefs):
-    particles, fields, strip, lats, strips = sizes
-    moved = zero_halo(sizes, courant, diffusion, mixing, coefs)
+def other_bulk(sizes, middle, observed, noise, courant, diffusion, mixing, out, coefs, mixing_scalars, sem):
+    particles, fields, strip, lats, strips = sizes
+    copy = pltpu.make_async_copy(mixing, mixing_scalars, sem)
+    copy.start()
+    moved = zero_halo(sizes, courant, diffusion, mixing, mixing_scalars, coefs)
+    copy.wait()
 
     def body(p, carry):
         values = [middle[p, f] for f in range(fields)]
@@ -281,10 +306,10 @@
     lax.fori_loop(0, particles, body, 0)
 
 
-def correct(sizes, own_east, own_west, from_west, from_east, diffusion, mixing, bulk_weight, bulk_beside,
-            weight, changes):
+def correct(sizes, own_east, own_west, from_west, from_east, diffusion, mixing, bulk_weight, weight, changes):
     particles, fields, strip, lats, strips = sizes
     n = fields * particles
+    diffusion, mixing = Spread(diffusion), Spread(mixing)
 
     def field_rows(ref, start, f):
         return ref[start + f * particles:start + (f + 1) * particles]
@@ -293,7 +318,7 @@
     last = 2 * n + 2 * particles
     zonal = stack_rows([ref[last + 2:last + 3] for ref in packets] + [ref[last + 5:last + 6] for ref in packets])
     merid = stack_rows([ref[last + 3:last + 4] for ref in packets] * 2)
-    tile = [coefficients(zonal, merid, diffusion[f], mixing[f, f]) for f in range(fields)]
+    tile = [coefficients(zonal, merid, diffusion[0, f], mixing[f, f]) for f in range(fields)]
     total = jnp.zeros((particles, lats), F32)
     for k, owner in enumerate(packets):
         other_k = k ^ 1
@@ -329,7 +354,7 @@
                 edge, inner = (3, 2) if k == 0 else (0, 1)
                 changes[edge, f * particles:(f + 1) * particles] = step
                 changes[inner, f * particles:(f + 1) * particles] = beside
-    weight[...] = in_row(wide(total)) + (bulk_weight[...] + bulk_beside[...])
+    weight[...] = in_row(wide(total)) + bulk_weight[...]
 
 
 def apply_changes(sizes, current, changes, out):
@@ -406,37 +431,38 @@
     from_east = lax.ppermute(send_west, "lon", westward)
 
     whole = (particles, fields, strip, lats)
+    spread = diffusion[None]
+    scalars = [pltpu.SMEM(mixing.shape, F32), pltpu.SemaphoreType.DMA]
     middle, observed, bulk_weight = pl.pallas_call(
         functools.partial(observed_bulk, sizes),
         out_shape=(shape(*whole), shape(particles, strip, lats), shape(1, 128)),
-        in_specs=[VMEM, VMEM, VMEM, SMEM, SMEM, VMEM, VMEM],
+        in_specs=[VMEM] * 7,
         out_specs=(VMEM,) * 3,
         scratch_shapes=[pltpu.VMEM((fields, 5, strip, lats), F32), pltpu.VMEM((2, strip, lats), F32),
-                        pltpu.VMEM((particles, 128), F32)],
+                        pltpu.VMEM((particles, 128), F32)] + scalars,
         compiler_params=LIMIT,
         cost_estimate=pl.CostEstimate(flops=20000000, bytes_accessed=4000000, transcendentals=0),
-    )(ensemble_state, proposal_noise, courant, diffusion, mixing, cell, value)
+    )(ensemble_state, proposal_noise, courant, spread, mixing, cell, value)
     beside = lax.ppermute(bulk_weight, "lon", [(i, i ^ 1) for i in range(strips)])
+
+    weight, changes = pl.pallas_call(
+        functools.partial(correct, sizes),
+        out_shape=(shape(1, 128), shape(4, particles * fields, lats)),
+        in_specs=[VMEM] * 7,
+        out_specs=(VMEM,) * 2,
+        compiler_params=LIMIT,
+        cost_estimate=FREE,
+    )(send_east, send_west, from_west, from_east, spread, mixing, bulk_weight)
 
     current = pl.pallas_call(
         functools.partial(other_bulk, sizes),
         out_shape=shape(*whole),
-        in_specs=[VMEM] * 4 + [SMEM] * 2,
+        in_specs=[VMEM] * 6,
         out_specs=VMEM,
-        scratch_shapes=[pltpu.VMEM((fields, 5, strip, lats), F32)],
+        scratch_shapes=[pltpu.VMEM((fields, 5, strip, lats), F32)] + scalars,
         compiler_params=LIMIT,
-        cost_estimate=pl.CostEstimate(flops=10000000, bytes_accessed=4000000, transcendentals=0),
-    )(middle, observed, proposal_noise, courant, diffusion, mixing)
-
-    from_west, from_east, beside = lax.optimization_barrier((from_west, from_east, beside))
-    weight, changes = pl.pallas_call(
-        functools.partial(correct, sizes),
-        out_shape=(shape(1, 128), shape(4, particles * fields, lats)),
-        in_specs=[VMEM] * 4 + [SMEM] * 2 + [VMEM] * 2,
-        out_specs=(VMEM,) * 2,
-        compiler_params=LIMIT,
-        cost_estimate=pl.CostEstimate(flops=1000000, bytes_accessed=1000000, transcendentals=0),
-    )(send_east, send_west, from_west, from_east, diffusion, mixing, bulk_weight, beside)
+        cost_estimate=FREE,
+    )(middle, observed, proposal_noise, courant, spread, mixing)
 
     current = pl.pallas_call(
         functools.partial(apply_changes, sizes),
@@ -444,9 +470,11 @@
         in_specs=[VMEM] * 2,
         out_specs=VMEM,
         compiler_params=LIMIT,
-        cost_estimate=pl.CostEstimate(flops=1000000, bytes_accessed=2000000, transcendentals=0),
+        cost_estimate=FREE,
     )(current, changes)
 
+    current, beside = lax.optimization_barrier((current, beside))
+    weight = weight + beside
     received = lax.ppermute(current, "dom", [(0, 1), (1, 0)])
     bit = 2
     while bit < strips:

time: 25.3 us -> 23.8 us (0.941)
  Pallas kernels: 9.34 us -> 8.15 us
  waiting for transfers between devices: 7.31 us -> 6.9 us
    pallas_call x1, Pallas kernels: 2.52 us -> 2.01 us  [local(): pl.pallas_call(functools.partial(observed_bulk, sizes), out_shape=(shape(...]
    pallas_call x1, Pallas kernels: 0.76 us -> 0.26 us  [local(): pl.pallas_call(functools.partial(correct, sizes), out_shape=(shape(1, 128...]
    ppermute x1, waiting for transfers between devices: 1.85 us -> 1.43 us  [local(): lax.ppermute(bulk_weight, 'lon', [(i, i ^ 1) for i in range(strips)])]
  transfers between devices with their start and end apart: 6 -> 6, of which waited for: 3 -> 3; matrix products, arithmetic and copies ran while one was open for 0% -> 0% of each run, Pallas kernels for 23% -> 24%
where the time goes in v7:
time: 23.8 us; the launch traced here: 23.6 us
  Pallas kernels  8.15 us (34%)
  starting transfers between devices  7.16 us (30%)
  waiting for transfers between devices  6.9 us (29%)
  between operations  0.81 us (3%)
  other arithmetic  0.52 us (2%)
    ppermute x2, waiting for transfers between devices, local(): lax.ppermute(weight, 'lon', [(i, i ^ bit) for i in range(strips)])  5.46 us
    ppermute x1, starting transfers between devices, local(): from_east = lax.ppermute(send_west, 'lon', westward)  3.12 us
    ppermute x1, starting transfers between devices, local(): from_west = lax.ppermute(send_east, 'lon', eastward)  2.99 us
    pallas_call x1, Pallas kernels, local(): pl.pallas_call(functools.partial(prepare, sizes), out_shape=(packet, pack...  2.54 us
    pallas_call x1, Pallas kernels, local(): pl.pallas_call(functools.partial(observed_bulk, sizes), out_shape=(shape(...  2.01 us
    pallas_call x1, Pallas kernels, local(): pl.pallas_call(functools.partial(other_bulk, sizes), out_shape=shape(*who...  1.6 us
    pallas_call x1, Pallas kernels, local(): pl.pallas_call(functools.partial(assemble, sizes), out_shape=shape(*whole...  1.58 us
    ppermute x1, waiting for transfers between devices, local(): lax.ppermute(bulk_weight, 'lon', [(i, i ^ 1) for i in range(strips)])  1.43 us
  transfers between devices with their start and end apart: 6, of which 3 were waited for; matrix products, arithmetic and copies ran while one was open for 0% of the time, Pallas kernels for 24%

profile of v7, /device:TPU:0, one launch (start us, length us, event | category | flops | bytes accessed | tf_op | source)
XLA Modules:
  0.0 23.6 jit_solution(3137179222069459711)
XLA Ops:
  0.6 0.0 copy-start
  0.6 0.0 copy-start.1
  0.7 0.0 copy-start.2
  0.7 0.0 copy-start.8
  0.7 2.5 %shard_map.106 = (f32[88,256]{1,0:T(8,128)}, f32[88,256]{1,0:T(8,128)}) custom-call(f32[8,4,32,256]{3,2,1,0:T(8,128)} %state_hbm.1, bf16[2,8,4,32,256]{4,3,2,1,0:T(8,128)(2,1)} %noise_hbm.1, f32[2,32,256]{2,1,0:T(8,128)} %courant_hbm.1, f32[4]{0:T(128)} %diffusion_hbm.1, f32[4,4]{1,0:T(4,128)} %mixing.5, s32[1,256]{1,0:T(1,128)} %bitcast.8, f32[1,256]{1,0:T(1,128)} %bitcast.10), custom_call_target="tpu_custom_call" | custom-call | flops 1000000 | bytes 2000000 | tf_op jit(solution)/shard_map/pallas_call | solution.py:407
  3.2 0.0 copy-start.5
  3.2 3.0 %collective-permute-start = (f32[88,256]{1,0:T(8,128)}, f32[88,256]{1,0:T(8,128)S(1)}, u32[]{:S(2)}, u32[]{:S(2)}) collective-permute-start(f32[88,256]{1,0:T(8,128)} %get-tuple-element.15.own_east), channel_id=1, source_target_pairs={{0,2},{2,4},{4,6},{6,8},{8,10},{10,12},{12,14},{14,0},{1,3},{3,5},... | collective-permute-start | bytes 270344 | tf_op jit(solution)/shard_map/ppermute | solution.py:430
  6.2 0.0 copy-start.6
  6.2 0.0 copy-start.7
  6.2 3.1 %collective-permute-start.1 = (f32[88,256]{1,0:T(8,128)}, f32[88,256]{1,0:T(8,128)S(1)}, u32[]{:S(2)}, u32[]{:S(2)}) collective-permute-start(f32[88,256]{1,0:T(8,128)} %get-tuple-element.16.own_west), channel_id=1, source_target_pairs={{0,14},{2,0},{4,2},{6,4},{8,6},{10,8},{12,10},{14,12},{1,15},{3,1}... | collective-permute-start | bytes 270344 | tf_op jit(solution)/shard_map/ppermute | solution.py:431
  9.4 0.0 copy-done
  9.4 0.0 copy-done.1
  9.4 0.0 copy-done.2
  9.4 0.0 copy-done.8
  9.4 0.0 copy-done.5
  9.4 0.0 copy-done.6
  9.4 0.0 copy-done.7
  9.4 2.0 %shard_map.104 = (f32[8,4,32,256]{3,2,1,0:T(8,128)S(1)}, f32[8,32,256]{2,1,0:T(8,128)S(1)}, f32[1,128]{1,0:T(1,128)S(1)}) custom-call(f32[8,4,32,256]{3,2,1,0:T(8,128)S(1)} %copy-done.1, bf16[2,8,4,32,256]{4,3,2,1,0:T(8,128)(2,1)S(1)} %copy-done, f32[2,32,256]{2,1,0:T(8,128)S(1)} %copy-done.2, f32[1,4]{1,0:T(1,128)S(1)} %bitcast.5, f32[4,4]{1,0:T(4,128)S(1)} %copy-done.5, ...), custom_call_target="tpu_custom_call" | custom-call | flops 20000000 | bytes 4000000 | tf_op jit(solution)/shard_map/pallas_call | solution.py:436
  11.4 0.1 collective-permute-start.2
  11.5 0.0 copy-start.3
  11.5 0.0 copy-start.4
  11.5 1.6 %shard_map.105.current = f32[8,4,32,256]{3,2,1,0:T(8,128)S(1)} custom-call(f32[8,4,32,256]{3,2,1,0:T(8,128)S(1)} %get-tuple-element.13.middle, f32[8,32,256]{2,1,0:T(8,128)S(1)} %get-tuple-element.14.observed, bf16[2,8,4,32,256]{4,3,2,1,0:T(8,128)(2,1)S(1)} %copy-done, f32[2,32,256]{2,1,0:T(8,128)S(1)} %copy-done.2, f32[1,4]{1,0:T(1,128)S(1)} %bitcast.6, ...), custom_call_target="tpu_custom_call" | custom-call | tf_op jit(solution)/shard_map/pallas_call | solution.py:457
  13.1 0.0 collective-permute-done.from_west
  13.1 0.0 collective-permute-done.1.from_east
  13.1 0.0 copy-done.3
  13.2 0.0 copy-done.4
  13.2 0.3 %shard_map.107 = (f32[1,128]{1,0:T(1,128)S(1)}, f32[4,32,256]{2,1,0:T(8,128)S(1)}) custom-call(f32[88,256]{1,0:T(8,128)S(1)} %copy-done.3, f32[88,256]{1,0:T(8,128)S(1)} %copy-done.4, f32[88,256]{1,0:T(8,128)S(1)} %collective-permute-done.from_west, f32[88,256]{1,0:T(8,128)S(1)} %collective-permute-done.1.from_east, f32[1,4]{1,0:T(1,128)S(1)} %bitcast.7, ...), custom_call_target="tpu_custom_call" | custom-call | tf_op jit(solution)/shard_map/pallas_call | solution.py:448
  13.4 0.2 shard_map.108.current
  13.6 1.4 %collective-permute-done.2 = f32[1,128]{1,0:T(1,128)S(1)} collective-permute-done((f32[1,128]{1,0:T(1,128)S(1)}, f32[1,128]{1,0:T(1,128)S(1)}, u32[]{:S(2)}, u32[]{:S(2)}) %collective-permute-start.2) | collective-permute-done | bytes 544 | tf_op jit(solution)/shard_map/ppermute | solution.py:446
  15.0 0.0 collective-permute-start.4
  15.0 0.0 copy-start.9
  15.0 0.1 collective-permute-start.3
  15.1 3.5 %collective-permute-done.3 = f32[1,128]{1,0:T(1,128)S(1)} collective-permute-done((f32[1,128]{1,0:T(1,128)S(1)}, f32[1,128]{1,0:T(1,128)S(1)}, u32[]{:S(2)}, u32[]{:S(2)}) %collective-permute-start.3) | collective-permute-done | bytes 544 | tf_op jit(solution)/shard_map/ppermute | solution.py:483
  18.6 0.0 collective-permute-done.4.received
  18.6 0.9 %collective-permute-start.5 = (f32[1,128]{1,0:T(1,128)S(1)}, f32[1,128]{1,0:T(1,128)S(1)}, u32[]{:S(2)}, u32[]{:S(2)}) collective-permute-start(f32[1,128]{1,0:T(1,128)S(1)} %add.10), channel_id=1, source_target_pairs={{0,8},{2,10},{4,12},{6,14},{8,0},{10,2},{12,4},{14,6},{1,9},{3,11}... | collective-permute-start | bytes 1544 | tf_op jit(solution)/shard_map/ppermute | solution.py:483
  19.5 0.0 copy-done.9
  19.5 1.6 %shard_map.109 = f32[8,4,32,256]{3,2,1,0:T(8,128)} custom-call(s32[16]{0:T(128)S(1)} %copy-done.9, f32[8,4,32,256]{3,2,1,0:T(8,128)S(1)} %shard_map.108.current, f32[8,4,32,256]{3,2,1,0:T(8,128)S(1)} %collective-permute-done.4.received), custom_call_target="tpu_custom_call" | custom-call | bytes 2000000 | tf_op jit(solution)/shard_map/pallas_call | solution.py:486
  21.1 0.0 copy-start.10
  21.1 1.9 %collective-permute-done.5 = f32[1,128]{1,0:T(1,128)S(1)} collective-permute-done((f32[1,128]{1,0:T(1,128)S(1)}, f32[1,128]{1,0:T(1,128)S(1)}, u32[]{:S(2)}, u32[]{:S(2)}) %collective-permute-start.5) | collective-permute-done | bytes 544 | tf_op jit(solution)/shard_map/ppermute | solution.py:483
  23.1 0.0 copy-done.10
  23.1 0.5 %bitcast_subtract_fusion = f32[8]{0:T(128)} fusion(f32[8]{0:T(128)S(1)} %copy-done.10, f32[1,128]{1,0:T(1,128)S(1)} %add.11), kind=kLoop, calls=%fused_computation | loop fusion | flops 16 | bytes 96 | tf_op jit(solution)/shard_map/sub | solution.py:496
  (3 shorter events, 0.0 us)
Async XLA Ops:
  0.6 8.7 %copy-start = (bf16[2,8,4,32,256]{4,3,2,1,0:T(8,128)(2,1)S(1)}, bf16[2,8,4,32,256]{4,3,2,1,0:T(8,128)(2,1)}, u32[]{:S(2)}) copy-start(bf16[2,8,4,32,256]{4,3,2,1,0:T(8,128)(2,1)} %noise_hbm.1) | copy-start | bytes 3145732
  0.6 8.7 %copy-start.1 = (f32[8,4,32,256]{3,2,1,0:T(8,128)S(1)}, f32[8,4,32,256]{3,2,1,0:T(8,128)}, u32[]{:S(2)}) copy-start(f32[8,4,32,256]{3,2,1,0:T(8,128)} %state_hbm.1) | copy-start | bytes 3145732
  0.7 8.7 %copy-start.2 = (f32[2,32,256]{2,1,0:T(8,128)S(1)}, f32[2,32,256]{2,1,0:T(8,128)}, u32[]{:S(2)}) copy-start(f32[2,32,256]{2,1,0:T(8,128)} %courant_hbm.1) | copy-start | bytes 196612
  0.7 8.7 %copy-start.8 = (f32[256]{0:T(256)S(1)}, f32[256]{0:T(256)}, u32[]{:S(2)}) copy-start(f32[256]{0:T(256)} %param.16) | copy-start | bytes 3076
  3.2 6.1 %copy-start.5 = (f32[4,4]{1,0:T(4,128)S(1)}, f32[4,4]{1,0:T(4,128)}, u32[]{:S(2)}) copy-start(f32[4,4]{1,0:T(4,128)} %mixing.5) | copy-start | bytes 196
  3.2 9.9 %collective-permute-start = (f32[88,256]{1,0:T(8,128)}, f32[88,256]{1,0:T(8,128)S(1)}, u32[]{:S(2)}, u32[]{:S(2)}) collective-permute-start(f32[88,256]{1,0:T(8,128)} %get-tuple-element.15.own_east), channel_id=1, source_target_pairs={{0,2},{2,4},{4,6},{6,8},{8,10},{10,12},{12,14},{14,0},{1,3},{3,5},... | collective-permute-start | bytes 270344 | tf_op jit(solution)/shard_map/ppermute | solution.py:430
  6.2 3.2 %copy-start.6 = (f32[4]{0:T(128)S(1)}, f32[4]{0:T(128)}, u32[]{:S(2)}) copy-start(f32[4]{0:T(128)} %diffusion_hbm.1) | copy-start | bytes 52
  6.2 3.2 %copy-start.7 = (s32[256]{0:T(256)S(1)}, s32[256]{0:T(256)}, u32[]{:S(2)}) copy-start(s32[256]{0:T(256)} %param.15) | copy-start | bytes 3076
  6.2 6.9 %collective-permute-start.1 = (f32[88,256]{1,0:T(8,128)}, f32[88,256]{1,0:T(8,128)S(1)}, u32[]{:S(2)}, u32[]{:S(2)}) collective-permute-start(f32[88,256]{1,0:T(8,128)} %get-tuple-element.16.own_west), channel_id=1, source_target_pairs={{0,14},{2,0},{4,2},{6,4},{8,6},{10,8},{12,10},{14,12},{1,15},{3,1}... | collective-permute-start | bytes 270344 | tf_op jit(solution)/shard_map/ppermute | solution.py:431
  11.4 3.6 %collective-permute-start.2 = (f32[1,128]{1,0:T(1,128)S(1)}, f32[1,128]{1,0:T(1,128)S(1)}, u32[]{:S(2)}, u32[]{:S(2)}) collective-permute-start(f32[1,128]{1,0:T(1,128)S(1)} %get-tuple-element.17.bulk_weight), channel_id=1, source_target_pairs={{0,2},{2,0},{4,6},{6,4},{8,10},{10,8},{12,14},{14,12},{1,3},{3,1},... | collective-permute-start | bytes 1544 | tf_op jit(solution)/shard_map/ppermute | solution.py:446
  11.5 1.7 %copy-start.3 = (f32[88,256]{1,0:T(8,128)S(1)}, f32[88,256]{1,0:T(8,128)}, u32[]{:S(2)}) copy-start(f32[88,256]{1,0:T(8,128)} %get-tuple-element.15.own_east) | copy-start | bytes 270340
  11.5 1.7 %copy-start.4 = (f32[88,256]{1,0:T(8,128)S(1)}, f32[88,256]{1,0:T(8,128)}, u32[]{:S(2)}) copy-start(f32[88,256]{1,0:T(8,128)} %get-tuple-element.16.own_west) | copy-start | bytes 270340
  15.0 3.6 %collective-permute-start.4 = (f32[8,4,32,256]{3,2,1,0:T(8,128)S(1)}, f32[8,4,32,256]{3,2,1,0:T(8,128)S(1)}, u32[]{:S(2)}, u32[]{:S(2)}) collective-permute-start(f32[8,4,32,256]{3,2,1,0:T(8,128)S(1)} %shard_map.108.current), channel_id=1, source_target_pairs={{0,1},{1,0},{2,3},{3,2},{4,5},{5,4},{6,7},{7,6},{8,9},{9,8},{10,11... | collective-permute-start | bytes 3145736 | tf_op jit(solution)/shard_map/ppermute | solution.py:478
  15.0 4.5 %copy-start.9 = (s32[16]{0:T(128)S(1)}, s32[16]{0:T(128)}, u32[]{:S(2)}) copy-start(s32[16]{0:T(128)} %source.1) | copy-start | bytes 196
  15.0 3.6 %collective-permute-start.3 = (f32[1,128]{1,0:T(1,128)S(1)}, f32[1,128]{1,0:T(1,128)S(1)}, u32[]{:S(2)}, u32[]{:S(2)}) collective-permute-start(f32[1,128]{1,0:T(1,128)S(1)} %add.9), channel_id=1, source_target_pairs={{0,4},{2,6},{4,0},{6,2},{8,12},{10,14},{12,8},{14,10},{1,5},{3,7},... | collective-permute-start | bytes 1544 | tf_op jit(solution)/shard_map/ppermute | solution.py:483
  18.6 4.4 %collective-permute-start.5 = (f32[1,128]{1,0:T(1,128)S(1)}, f32[1,128]{1,0:T(1,128)S(1)}, u32[]{:S(2)}, u32[]{:S(2)}) collective-permute-start(f32[1,128]{1,0:T(1,128)S(1)} %add.10), channel_id=1, source_target_pairs={{0,8},{2,10},{4,12},{6,14},{8,0},{10,2},{12,4},{14,6},{1,9},{3,11}... | collective-permute-start | bytes 1544 | tf_op jit(solution)/shard_map/ppermute | solution.py:483
  21.1 2.0 %copy-start.10 = (f32[8]{0:T(128)S(1)}, f32[8]{0:T(128)}, u32[]{:S(2)}) copy-start(f32[8]{0:T(128)} %param.14) | copy-start | bytes 100

commit v8 on v7

--- a/solution.py
+++ b/solution.py
@@ -48,16 +48,11 @@
     return total
 
 
-def pick_rows(kinds, particles, fields, strip, columns):
-    rows = len(kinds) * particles
-    out = lax.broadcasted_iota(jnp.int32, (rows, columns), 0)
-    col = lax.broadcasted_iota(jnp.int32, (rows, columns), 1)
-    want = jnp.full((rows, columns), -1, jnp.int32)
-    for place, (field, x) in enumerate(kinds):
-        inside = (out >= place * particles) & (out < (place + 1) * particles)
-        target = (out - place * particles) * (fields * strip) + field * strip + x
-        want = jnp.where(inside, target, want)
-    return (col == want).astype(BF16)
+def pick_rows(kinds, particles, fields, strip):
+    shape = (particles, particles * fields * strip)
+    place = lax.broadcasted_iota(jnp.int32, shape, 1) - lax.broadcasted_iota(jnp.int32, shape, 0) * (fields * strip)
+    blocks = [jnp.where(place == f * strip + x, 1.0, 0.0) for f, x in kinds]
+    return jnp.concatenate(blocks, 0).astype(BF16)
 
 
 def stack_rows(rows):
@@ -121,8 +116,8 @@
     kinds = []
     for x, step in ((strip - 1, -1), (0, 1)):
         kinds += [(f, x) for f in range(fields)] + [(f, x + step) for f in range(fields)] + [(0, x + 2 * step)]
-    pick0 = pick_rows(kinds, particles, fields, strip, n * strip)
-    pick1 = pick_rows([(0, x) for x in (strip - 1, strip - 2, 0, 1)], particles, 1, strip, particles * strip)
+    pick0 = pick_rows(kinds, particles, fields, strip)
+    pick1 = pick_rows([(0, x) for x in (strip - 1, strip - 2, 0, 1)], particles, 1, strip)
     for copy in copies[2:5]:
         copy.wait()
 

time: 23.8 us -> 23.8 us (level)
  no operation moved by 1% of the time
where the time goes in v8:
time: 23.8 us; the launch traced here: 23.6 us
  Pallas kernels  8.15 us (34%)
  starting transfers between devices  7.16 us (30%)
  waiting for transfers between devices  6.9 us (29%)
  between operations  0.81 us (3%)
  other arithmetic  0.52 us (2%)
    ppermute x2, waiting for transfers between devices, local(): lax.ppermute(weight, 'lon', [(i, i ^ bit) for i in range(strips)])  5.46 us
    ppermute x1, starting transfers between devices, local(): from_east = lax.ppermute(send_west, 'lon', westward)  3.12 us
    ppermute x1, starting transfers between devices, local(): from_west = lax.ppermute(send_east, 'lon', eastward)  2.99 us
    pallas_call x1, Pallas kernels, local(): pl.pallas_call(functools.partial(prepare, sizes), out_shape=(packet, pack...  2.54 us
    pallas_call x1, Pallas kernels, local(): pl.pallas_call(functools.partial(observed_bulk, sizes), out_shape=(shape(...  2.01 us
    pallas_call x1, Pallas kernels, local(): pl.pallas_call(functools.partial(other_bulk, sizes), out_shape=shape(*who...  1.6 us
    pallas_call x1, Pallas kernels, local(): pl.pallas_call(functools.partial(assemble, sizes), out_shape=shape(*whole...  1.58 us
    ppermute x1, waiting for transfers between devices, local(): lax.ppermute(bulk_weight, 'lon', [(i, i ^ 1) for i in range(strips)])  1.43 us
  transfers between devices with their start and end apart: 6, of which 3 were waited for; matrix products, arithmetic and copies ran while one was open for 0% of the time, Pallas kernels for 24%

profile of v8, /device:TPU:0, one launch (start us, length us, event | category | flops | bytes accessed | tf_op | source)
XLA Modules:
  0.0 23.6 jit_solution(7965732748087118651)
XLA Ops:
  0.6 0.0 copy-start
  0.6 0.0 copy-start.1
  0.7 0.0 copy-start.2
  0.7 0.0 copy-start.8
  0.7 2.5 %shard_map.106 = (f32[88,256]{1,0:T(8,128)}, f32[88,256]{1,0:T(8,128)}) custom-call(f32[8,4,32,256]{3,2,1,0:T(8,128)} %state_hbm.1, bf16[2,8,4,32,256]{4,3,2,1,0:T(8,128)(2,1)} %noise_hbm.1, f32[2,32,256]{2,1,0:T(8,128)} %courant_hbm.1, f32[4]{0:T(128)} %diffusion_hbm.1, f32[4,4]{1,0:T(4,128)} %mixing.5, s32[1,256]{1,0:T(1,128)} %bitcast.8, f32[1,256]{1,0:T(1,128)} %bitcast.10), custom_call_target="tpu_custom_call" | custom-call | flops 1000000 | bytes 2000000 | tf_op jit(solution)/shard_map/pallas_call | solution.py:402
  3.2 0.0 copy-start.5
  3.2 3.0 %collective-permute-start = (f32[88,256]{1,0:T(8,128)}, f32[88,256]{1,0:T(8,128)S(1)}, u32[]{:S(2)}, u32[]{:S(2)}) collective-permute-start(f32[88,256]{1,0:T(8,128)} %get-tuple-element.15.own_east), channel_id=1, source_target_pairs={{0,2},{2,4},{4,6},{6,8},{8,10},{10,12},{12,14},{14,0},{1,3},{3,5},... | collective-permute-start | bytes 270344 | tf_op jit(solution)/shard_map/ppermute | solution.py:425
  6.2 0.0 copy-start.6
  6.2 0.0 copy-start.7
  6.2 3.1 %collective-permute-start.1 = (f32[88,256]{1,0:T(8,128)}, f32[88,256]{1,0:T(8,128)S(1)}, u32[]{:S(2)}, u32[]{:S(2)}) collective-permute-start(f32[88,256]{1,0:T(8,128)} %get-tuple-element.16.own_west), channel_id=1, source_target_pairs={{0,14},{2,0},{4,2},{6,4},{8,6},{10,8},{12,10},{14,12},{1,15},{3,1}... | collective-permute-start | bytes 270344 | tf_op jit(solution)/shard_map/ppermute | solution.py:426
  9.4 0.0 copy-done
  9.4 0.0 copy-done.1
  9.4 0.0 copy-done.2
  9.4 0.0 copy-done.8
  9.4 0.0 copy-done.5
  9.4 0.0 copy-done.6
  9.4 0.0 copy-done.7
  9.4 2.0 %shard_map.104 = (f32[8,4,32,256]{3,2,1,0:T(8,128)S(1)}, f32[8,32,256]{2,1,0:T(8,128)S(1)}, f32[1,128]{1,0:T(1,128)S(1)}) custom-call(f32[8,4,32,256]{3,2,1,0:T(8,128)S(1)} %copy-done.1, bf16[2,8,4,32,256]{4,3,2,1,0:T(8,128)(2,1)S(1)} %copy-done, f32[2,32,256]{2,1,0:T(8,128)S(1)} %copy-done.2, f32[1,4]{1,0:T(1,128)S(1)} %bitcast.5, f32[4,4]{1,0:T(4,128)S(1)} %copy-done.5, ...), custom_call_target="tpu_custom_call" | custom-call | flops 20000000 | bytes 4000000 | tf_op jit(solution)/shard_map/pallas_call | solution.py:431
  11.4 0.1 collective-permute-start.2
  11.5 0.0 copy-start.3
  11.5 0.0 copy-start.4
  11.5 1.6 %shard_map.105.current = f32[8,4,32,256]{3,2,1,0:T(8,128)S(1)} custom-call(f32[8,4,32,256]{3,2,1,0:T(8,128)S(1)} %get-tuple-element.13.middle, f32[8,32,256]{2,1,0:T(8,128)S(1)} %get-tuple-element.14.observed, bf16[2,8,4,32,256]{4,3,2,1,0:T(8,128)(2,1)S(1)} %copy-done, f32[2,32,256]{2,1,0:T(8,128)S(1)} %copy-done.2, f32[1,4]{1,0:T(1,128)S(1)} %bitcast.6, ...), custom_call_target="tpu_custom_call" | custom-call | tf_op jit(solution)/shard_map/pallas_call | solution.py:452
  13.1 0.0 collective-permute-done.from_west
  13.1 0.0 collective-permute-done.1.from_east
  13.1 0.0 copy-done.3
  13.2 0.0 copy-done.4
  13.2 0.3 %shard_map.107 = (f32[1,128]{1,0:T(1,128)S(1)}, f32[4,32,256]{2,1,0:T(8,128)S(1)}) custom-call(f32[88,256]{1,0:T(8,128)S(1)} %copy-done.3, f32[88,256]{1,0:T(8,128)S(1)} %copy-done.4, f32[88,256]{1,0:T(8,128)S(1)} %collective-permute-done.from_west, f32[88,256]{1,0:T(8,128)S(1)} %collective-permute-done.1.from_east, f32[1,4]{1,0:T(1,128)S(1)} %bitcast.7, ...), custom_call_target="tpu_custom_call" | custom-call | tf_op jit(solution)/shard_map/pallas_call | solution.py:443
  13.4 0.2 shard_map.108.current
  13.6 1.4 %collective-permute-done.2 = f32[1,128]{1,0:T(1,128)S(1)} collective-permute-done((f32[1,128]{1,0:T(1,128)S(1)}, f32[1,128]{1,0:T(1,128)S(1)}, u32[]{:S(2)}, u32[]{:S(2)}) %collective-permute-start.2) | collective-permute-done | bytes 544 | tf_op jit(solution)/shard_map/ppermute | solution.py:441
  15.0 0.0 collective-permute-start.4
  15.0 0.0 copy-start.9
  15.0 0.1 collective-permute-start.3
  15.1 3.5 %collective-permute-done.3 = f32[1,128]{1,0:T(1,128)S(1)} collective-permute-done((f32[1,128]{1,0:T(1,128)S(1)}, f32[1,128]{1,0:T(1,128)S(1)}, u32[]{:S(2)}, u32[]{:S(2)}) %collective-permute-start.3) | collective-permute-done | bytes 544 | tf_op jit(solution)/shard_map/ppermute | solution.py:478
  18.6 0.0 collective-permute-done.4.received
  18.6 0.9 %collective-permute-start.5 = (f32[1,128]{1,0:T(1,128)S(1)}, f32[1,128]{1,0:T(1,128)S(1)}, u32[]{:S(2)}, u32[]{:S(2)}) collective-permute-start(f32[1,128]{1,0:T(1,128)S(1)} %add.10), channel_id=1, source_target_pairs={{0,8},{2,10},{4,12},{6,14},{8,0},{10,2},{12,4},{14,6},{1,9},{3,11}... | collective-permute-start | bytes 1544 | tf_op jit(solution)/shard_map/ppermute | solution.py:478
  19.5 0.0 copy-done.9
  19.5 1.6 %shard_map.109 = f32[8,4,32,256]{3,2,1,0:T(8,128)} custom-call(s32[16]{0:T(128)S(1)} %copy-done.9, f32[8,4,32,256]{3,2,1,0:T(8,128)S(1)} %shard_map.108.current, f32[8,4,32,256]{3,2,1,0:T(8,128)S(1)} %collective-permute-done.4.received), custom_call_target="tpu_custom_call" | custom-call | bytes 2000000 | tf_op jit(solution)/shard_map/pallas_call | solution.py:481
  21.1 0.0 copy-start.10
  21.1 1.9 %collective-permute-done.5 = f32[1,128]{1,0:T(1,128)S(1)} collective-permute-done((f32[1,128]{1,0:T(1,128)S(1)}, f32[1,128]{1,0:T(1,128)S(1)}, u32[]{:S(2)}, u32[]{:S(2)}) %collective-permute-start.5) | collective-permute-done | bytes 544 | tf_op jit(solution)/shard_map/ppermute | solution.py:478
  23.1 0.0 copy-done.10
  23.1 0.5 %bitcast_subtract_fusion = f32[8]{0:T(128)} fusion(f32[8]{0:T(128)S(1)} %copy-done.10, f32[1,128]{1,0:T(1,128)S(1)} %add.11), kind=kLoop, calls=%fused_computation | loop fusion | flops 16 | bytes 96 | tf_op jit(solution)/shard_map/sub | solution.py:491
  (3 shorter events, 0.0 us)
Async XLA Ops:
  0.6 8.7 %copy-start = (bf16[2,8,4,32,256]{4,3,2,1,0:T(8,128)(2,1)S(1)}, bf16[2,8,4,32,256]{4,3,2,1,0:T(8,128)(2,1)}, u32[]{:S(2)}) copy-start(bf16[2,8,4,32,256]{4,3,2,1,0:T(8,128)(2,1)} %noise_hbm.1) | copy-start | bytes 3145732
  0.6 8.7 %copy-start.1 = (f32[8,4,32,256]{3,2,1,0:T(8,128)S(1)}, f32[8,4,32,256]{3,2,1,0:T(8,128)}, u32[]{:S(2)}) copy-start(f32[8,4,32,256]{3,2,1,0:T(8,128)} %state_hbm.1) | copy-start | bytes 3145732
  0.7 8.7 %copy-start.2 = (f32[2,32,256]{2,1,0:T(8,128)S(1)}, f32[2,32,256]{2,1,0:T(8,128)}, u32[]{:S(2)}) copy-start(f32[2,32,256]{2,1,0:T(8,128)} %courant_hbm.1) | copy-start | bytes 196612
  0.7 8.7 %copy-start.8 = (f32[256]{0:T(256)S(1)}, f32[256]{0:T(256)}, u32[]{:S(2)}) copy-start(f32[256]{0:T(256)} %param.16) | copy-start | bytes 3076
  3.2 6.1 %copy-start.5 = (f32[4,4]{1,0:T(4,128)S(1)}, f32[4,4]{1,0:T(4,128)}, u32[]{:S(2)}) copy-start(f32[4,4]{1,0:T(4,128)} %mixing.5) | copy-start | bytes 196
  3.2 9.9 %collective-permute-start = (f32[88,256]{1,0:T(8,128)}, f32[88,256]{1,0:T(8,128)S(1)}, u32[]{:S(2)}, u32[]{:S(2)}) collective-permute-start(f32[88,256]{1,0:T(8,128)} %get-tuple-element.15.own_east), channel_id=1, source_target_pairs={{0,2},{2,4},{4,6},{6,8},{8,10},{10,12},{12,14},{14,0},{1,3},{3,5},... | collective-permute-start | bytes 270344 | tf_op jit(solution)/shard_map/ppermute | solution.py:425
  6.2 3.2 %copy-start.6 = (f32[4]{0:T(128)S(1)}, f32[4]{0:T(128)}, u32[]{:S(2)}) copy-start(f32[4]{0:T(128)} %diffusion_hbm.1) | copy-start | bytes 52
  6.2 3.2 %copy-start.7 = (s32[256]{0:T(256)S(1)}, s32[256]{0:T(256)}, u32[]{:S(2)}) copy-start(s32[256]{0:T(256)} %param.15) | copy-start | bytes 3076
  6.2 6.9 %collective-permute-start.1 = (f32[88,256]{1,0:T(8,128)}, f32[88,256]{1,0:T(8,128)S(1)}, u32[]{:S(2)}, u32[]{:S(2)}) collective-permute-start(f32[88,256]{1,0:T(8,128)} %get-tuple-element.16.own_west), channel_id=1, source_target_pairs={{0,14},{2,0},{4,2},{6,4},{8,6},{10,8},{12,10},{14,12},{1,15},{3,1}... | collective-permute-start | bytes 270344 | tf_op jit(solution)/shard_map/ppermute | solution.py:426
  11.4 3.6 %collective-permute-start.2 = (f32[1,128]{1,0:T(1,128)S(1)}, f32[1,128]{1,0:T(1,128)S(1)}, u32[]{:S(2)}, u32[]{:S(2)}) collective-permute-start(f32[1,128]{1,0:T(1,128)S(1)} %get-tuple-element.17.bulk_weight), channel_id=1, source_target_pairs={{0,2},{2,0},{4,6},{6,4},{8,10},{10,8},{12,14},{14,12},{1,3},{3,1},... | collective-permute-start | bytes 1544 | tf_op jit(solution)/shard_map/ppermute | solution.py:441
  11.5 1.7 %copy-start.3 = (f32[88,256]{1,0:T(8,128)S(1)}, f32[88,256]{1,0:T(8,128)}, u32[]{:S(2)}) copy-start(f32[88,256]{1,0:T(8,128)} %get-tuple-element.15.own_east) | copy-start | bytes 270340
  11.5 1.7 %copy-start.4 = (f32[88,256]{1,0:T(8,128)S(1)}, f32[88,256]{1,0:T(8,128)}, u32[]{:S(2)}) copy-start(f32[88,256]{1,0:T(8,128)} %get-tuple-element.16.own_west) | copy-start | bytes 270340
  15.0 3.6 %collective-permute-start.4 = (f32[8,4,32,256]{3,2,1,0:T(8,128)S(1)}, f32[8,4,32,256]{3,2,1,0:T(8,128)S(1)}, u32[]{:S(2)}, u32[]{:S(2)}) collective-permute-start(f32[8,4,32,256]{3,2,1,0:T(8,128)S(1)} %shard_map.108.current), channel_id=1, source_target_pairs={{0,1},{1,0},{2,3},{3,2},{4,5},{5,4},{6,7},{7,6},{8,9},{9,8},{10,11... | collective-permute-start | bytes 3145736 | tf_op jit(solution)/shard_map/ppermute | solution.py:473
  15.0 4.5 %copy-start.9 = (s32[16]{0:T(128)S(1)}, s32[16]{0:T(128)}, u32[]{:S(2)}) copy-start(s32[16]{0:T(128)} %source.1) | copy-start | bytes 196
  15.0 3.6 %collective-permute-start.3 = (f32[1,128]{1,0:T(1,128)S(1)}, f32[1,128]{1,0:T(1,128)S(1)}, u32[]{:S(2)}, u32[]{:S(2)}) collective-permute-start(f32[1,128]{1,0:T(1,128)S(1)} %add.9), channel_id=1, source_target_pairs={{0,4},{2,6},{4,0},{6,2},{8,12},{10,14},{12,8},{14,10},{1,5},{3,7},... | collective-permute-start | bytes 1544 | tf_op jit(solution)/shard_map/ppermute | solution.py:478
  18.6 4.4 %collective-permute-start.5 = (f32[1,128]{1,0:T(1,128)S(1)}, f32[1,128]{1,0:T(1,128)S(1)}, u32[]{:S(2)}, u32[]{:S(2)}) collective-permute-start(f32[1,128]{1,0:T(1,128)S(1)} %add.10), channel_id=1, source_target_pairs={{0,8},{2,10},{4,12},{6,14},{8,0},{10,2},{12,4},{14,6},{1,9},{3,11}... | collective-permute-start | bytes 1544 | tf_op jit(solution)/shard_map/ppermute | solution.py:478
  21.1 2.0 %copy-start.10 = (f32[8]{0:T(128)S(1)}, f32[8]{0:T(128)}, u32[]{:S(2)}) copy-start(f32[8]{0:T(128)} %param.14) | copy-start | bytes 100

commit v9 on v8

--- a/solution.py
+++ b/solution.py
@@ -99,20 +99,32 @@
     return dense[:strip] * (0.25 * precision), target
 
 
+class Spread:
+    def __init__(self, ref):
+        self.ref = ref
+
+    def __getitem__(self, at):
+        return self.ref[at[0]:at[0] + 1, at[1]:at[1] + 1]
+
+
 def prepare(sizes, state_hbm, noise_hbm, courant_hbm, diffusion_hbm, mixing_hbm, cell_hbm, value_hbm,
-            send_east, send_west,
-            low, high, noise0, noise1, courant, diffusion, mixing, cell, value, sems):
+            send_east, send_west, state, noise, maps,
+            courant, diffusion, mixing, cell, value, sems):
     particles, fields, strip, lats, strips = sizes
     n = fields * particles
     copies = [pltpu.make_async_copy(source, target, sems.at[k]) for k, (source, target) in enumerate((
         (cell_hbm, cell), (value_hbm, value), (courant_hbm, courant), (diffusion_hbm, diffusion),
-        (mixing_hbm, mixing), (state_hbm.at[:, :, :8], low), (state_hbm.at[:, :, strip - 8:], high),
-        (noise_hbm.at[0], noise0), (noise_hbm.at[1, :, 0], noise1)))]
+        (mixing_hbm, mixing), (state_hbm.at[:, :, :8], state.at[:, :, :8]),
+        (state_hbm.at[:, :, strip - 8:], state.at[:, :, strip - 8:]), (noise_hbm.at[0], noise.at[0]),
+        (noise_hbm.at[1, :, 0], noise.at[1, :, 0]), (state_hbm.at[:, :, 8:strip - 8], state.at[:, :, 8:strip - 8]),
+        (noise_hbm.at[1, :, 1:], noise.at[1, :, 1:])))]
     for copy in copies:
         copy.start()
     copies[0].wait()
     copies[1].wait()
     gain, target = observation_maps(sizes, cell[...], value[...])
+    maps[0], maps[1] = gain, target
+    diffusion, mixing = Spread(diffusion), Spread(mixing)
     kinds = []
     for x, step in ((strip - 1, -1), (0, 1)):
         kinds += [(f, x) for f in range(fields)] + [(f, x + step) for f in range(fields)] + [(0, x + 2 * step)]
@@ -123,7 +135,7 @@
 
     sides = []
     for first, inward, outward in ((strip - 8, 2, 1), (0, 1, 2)):
-        tile = [coefficients(courant[0, first:first + 8], courant[1, first:first + 8], diffusion[f], mixing[f, f])
+        tile = [coefficients(courant[0, first:first + 8], courant[1, first:first + 8], diffusion[0, f], mixing[f, f])
                 for f in range(fields)]
         sides.append([[c[0], c[inward], c[outward], c[3], c[4]] for c in tile])
     def coefs_at(side, f, k):
@@ -145,34 +157,34 @@
         push = g * (v - value)
         return value + push, push
 
-    def first_step(side, tile, out):
+    def first_step(side, out):
         def state_at(f, k):
-            at = places[side][0] + k * places[side][2] - places[side][1]
-            return stack_rows([tile[p, f, at:at + 1] for p in range(particles)])
-
-        state = [[state_at(f, k) for f in range(fields)] for k in range(3)]
+            at = places[side][0] + k * places[side][2]
+            return stack_rows([state[p, f, at:at + 1] for p in range(particles)])
+
+        near = [[state_at(f, k) for f in range(fields)] for k in range(3)]
         third = state_at(0, 3)
         for f in range(fields):
-            out[f * particles:(f + 1) * particles] = state[0][f]
+            out[f * particles:(f + 1) * particles] = near[0][f]
         result, pushes = [[], []], []
         for k in range(2):
             for f in range(fields):
-                new = moved(side, f, k, state[k], state[k + 1][f], state[k - 1][f] if k else None)
+                new = moved(side, f, k, near[k], near[k + 1][f], near[k - 1][f] if k else None)
                 if f == 0:
                     new, push = nudged(side, new, k)
                     pushes.append(push)
                 result[k].append(new)
-        inside, _ = nudged(side, moved(side, 0, 2, state[2], third, state[1][0]), 2)
+        inside, _ = nudged(side, moved(side, 0, 2, near[2], third, near[1][0]), 2)
         return result, pushes, inside
 
     places = ((strip - 1, strip - 8, -1), (0, 0, 1))
     copies[5].wait()
     copies[6].wait()
-    started = [first_step(0, high, send_east), first_step(1, low, send_west)]
+    started = [first_step(0, send_east), first_step(1, send_west)]
     copies[7].wait()
     copies[8].wait()
-    rows0 = jnp.dot(pick0, noise0[...].reshape(n * strip, lats), preferred_element_type=F32)
-    rows1 = jnp.dot(pick1, noise1[...].reshape(particles * strip, lats), preferred_element_type=F32)
+    rows0 = jnp.dot(pick0, noise[0].reshape(n * strip, lats), preferred_element_type=F32)
+    rows1 = jnp.dot(pick1, noise[1, :, 0].reshape(particles * strip, lats), preferred_element_type=F32)
 
     def edge(side, out):
         x, _, step = places[side]
@@ -214,14 +226,8 @@
 
     edge(0, send_east)
     edge(1, send_west)
-
-
-class Spread:
-    def __init__(self, ref):
-        self.ref = ref
-
-    def __getitem__(self, at):
-        return self.ref[at[0]:at[0] + 1, at[1]:at[1] + 1]
+    copies[9].wait()
+    copies[10].wait()
 
 
 def zero_halo(sizes, courant, diffusion, mixing, mixing_scalars, coefs):
@@ -245,12 +251,11 @@
     return moved
 
 
-def observed_bulk(sizes, state, noise, courant, diffusion, mixing, cell, value, middle, out, weight,
-                  coefs, maps, partial, mixing_scalars, sem):
+def observed_bulk(sizes, state, noise, maps, courant, diffusion, mixing, middle, out, weight,
+                  coefs, partial, mixing_scalars, sem):
     particles, fields, strip, lats, strips = sizes
     copy = pltpu.make_async_copy(mixing, mixing_scalars, sem)
     copy.start()
-    maps[0], maps[1] = observation_maps(sizes, cell[...], value[...])
     moved = zero_halo(sizes, courant, diffusion, mixing, mixing_scalars, coefs)
     copy.wait()
 
@@ -399,45 +404,39 @@
     def shape(*dims):
         return jax.ShapeDtypeStruct(dims, F32)
 
-    send_east, send_west = pl.pallas_call(
+    whole = (particles, fields, strip, lats)
+    spread = diffusion[None]
+
+    def in_hbm(array):
+        return pltpu.with_memory_space_constraint(array, pltpu.HBM)
+
+    arrays = (ensemble_state, proposal_noise, courant, spread, mixing, cell, value)
+    send_east, send_west, state, noise, maps = pl.pallas_call(
         functools.partial(prepare, sizes),
-        out_shape=(packet, packet),
+        out_shape=(packet, packet, shape(*whole), jax.ShapeDtypeStruct((2,) + whole, BF16), shape(2, strip, lats)),
         in_specs=[HBM] * 7,
-        out_specs=(VMEM,) * 2,
-        scratch_shapes=[
-            pltpu.VMEM((particles, fields, 8, lats), F32),
-            pltpu.VMEM((particles, fields, 8, lats), F32),
-            pltpu.VMEM((particles, fields, strip, lats), BF16),
-            pltpu.VMEM((particles, strip, lats), BF16),
-            pltpu.VMEM(courant.shape, F32),
-            pltpu.SMEM(diffusion.shape, F32),
-            pltpu.SMEM(mixing.shape, F32),
-            pltpu.VMEM(cell.shape, jnp.int32),
-            pltpu.VMEM(value.shape, F32),
-            pltpu.SemaphoreType.DMA((9,)),
-        ],
-        compiler_params=pltpu.CompilerParams(vmem_limit_bytes=60 * 1024 * 1024),
+        out_specs=(VMEM,) * 5,
+        scratch_shapes=[pltpu.VMEM(array.shape, array.dtype) for array in arrays[2:]]
+        + [pltpu.SemaphoreType.DMA((11,))],
+        compiler_params=LIMIT,
         cost_estimate=pl.CostEstimate(flops=1000000, bytes_accessed=2000000, transcendentals=0),
-    )(ensemble_state, proposal_noise, courant, diffusion, mixing, cell, value)
+    )(*[in_hbm(array) for array in arrays])
 
     eastward = [(i, (i + 1) % strips) for i in range(strips)]
     westward = [(i, (i - 1) % strips) for i in range(strips)]
     from_west = lax.ppermute(send_east, "lon", eastward)
     from_east = lax.ppermute(send_west, "lon", westward)
 
-    whole = (particles, fields, strip, lats)
-    spread = diffusion[None]
     scalars = [pltpu.SMEM(mixing.shape, F32), pltpu.SemaphoreType.DMA]
     middle, observed, bulk_weight = pl.pallas_call(
         functools.partial(observed_bulk, sizes),
         out_shape=(shape(*whole), shape(particles, strip, lats), shape(1, 128)),
-        in_specs=[VMEM] * 7,
+        in_specs=[VMEM] * 6,
         out_specs=(VMEM,) * 3,
-        scratch_shapes=[pltpu.VMEM((fields, 5, strip, lats), F32), pltpu.VMEM((2, strip, lats), F32),
-                        pltpu.VMEM((particles, 128), F32)] + scalars,
+        scratch_shapes=[pltpu.VMEM((fields, 5, strip, lats), F32), pltpu.VMEM((particles, 128), F32)] + scalars,
         compiler_params=LIMIT,
         cost_estimate=pl.CostEstimate(flops=20000000, bytes_accessed=4000000, transcendentals=0),
-    )(ensemble_state, proposal_noise, courant, spread, mixing, cell, value)
+    )(state, noise, maps, courant, spread, mixing)
     beside = lax.ppermute(bulk_weight, "lon", [(i, i ^ 1) for i in range(strips)])
 
     weight, changes = pl.pallas_call(
@@ -457,7 +456,7 @@
         scratch_shapes=[pltpu.VMEM((fields, 5, strip, lats), F32)] + scalars,
         compiler_params=LIMIT,
         cost_estimate=FREE,
-    )(middle, observed, proposal_noise, courant, spread, mixing)
+    )(middle, observed, noise, courant, spread, mixing)
 
     current = pl.pallas_call(
         functools.partial(apply_changes, sizes),

time: 23.8 us -> 23.7 us (level)
  local copies, waits for them, and re-layouts: 0.05 us -> 0.69 us
  Pallas kernels: 8.15 us -> 7.55 us
    pallas_call x1, Pallas kernels: 2.54 us -> 1.85 us  [local(): pl.pallas_call(functools.partial(prepare, sizes), out_shape=(packet, pack...]
    unnamed x22 -> x10, local copies, waits for them, and re-layouts: 0.05 us -> 0.69 us
where the time goes in v9:
time: 23.7 us; the launch traced here: 23.5 us
  Pallas kernels  7.55 us (32%)
  starting transfers between devices  7.16 us (30%)
  waiting for transfers between devices  6.9 us (29%)
  between operations  0.72 us (3%)
  local copies, waits for them, and re-layouts  0.69 us (3%)
  other arithmetic  0.52 us (2%)
    ppermute x2, waiting for transfers between devices, local(): lax.ppermute(weight, 'lon', [(i, i ^ bit) for i in range(strips)])  5.44 us
    ppermute x1, starting transfers between devices, local(): from_east = lax.ppermute(send_west, 'lon', westward)  3.1 us
    ppermute x1, starting transfers between devices, local(): from_west = lax.ppermute(send_east, 'lon', eastward)  2.99 us
    pallas_call x1, Pallas kernels, local(): pl.pallas_call(functools.partial(observed_bulk, sizes), out_shape=(shape(...  2.07 us
    pallas_call x1, Pallas kernels, local(): pl.pallas_call(functools.partial(prepare, sizes), out_shape=(packet, pack...  1.85 us
    pallas_call x1, Pallas kernels, local(): pl.pallas_call(functools.partial(other_bulk, sizes), out_shape=shape(*who...  1.63 us
    pallas_call x1, Pallas kernels, local(): pl.pallas_call(functools.partial(assemble, sizes), out_shape=shape(*whole...  1.58 us
    ppermute x1, waiting for transfers between devices, local(): lax.ppermute(bulk_weight, 'lon', [(i, i ^ 1) for i in range(strips)])  1.45 us
  transfers between devices with their start and end apart: 6, of which 3 were waited for; matrix products, arithmetic and copies ran while one was open for 0% of the time, Pallas kernels for 24%

profile of v9, /device:TPU:0, one launch (start us, length us, event | category | flops | bytes accessed | tf_op | source)
XLA Modules:
  0.0 23.5 jit_solution(8029875708031594522)
XLA Ops:
  0.6 0.0 copy-start
  0.6 1.9 %shard_map.104 = (f32[88,256]{1,0:T(8,128)S(1)}, f32[88,256]{1,0:T(8,128)S(1)}, f32[8,4,32,256]{3,2,1,0:T(8,128)S(1)}, bf16[2,8,4,32,256]{4,3,2,1,0:T(8,128)(2,1)S(1)}, f32[2,32,256]{2,1,0:T(8,128)S(1)}) custom-call(f32[8,4,32,256]{3,2,1,0:T(8,128)} %state_hbm.1, bf16[2,8,4,32,256]{4,3,2,1,0:T(8,128)(2,1)} %noise_hbm.1, f32[2,32,256]{2,1,0:T(8,128)} %courant.3, ...), custom_call_target="tpu_custom_call" | custom-call | flops 1000000 | bytes 2000000 | tf_op jit(solution)/shard_map/pallas_call | solution.py:414
  2.5 3.0 %collective-permute-start = (f32[88,256]{1,0:T(8,128)S(1)}, f32[88,256]{1,0:T(8,128)S(1)}, u32[]{:S(2)}, u32[]{:S(2)}) collective-permute-start(f32[88,256]{1,0:T(8,128)S(1)} %get-tuple-element.21.own_east), channel_id=1, source_target_pairs={{0,2},{2,4},{4,6},{6,8},{8,10},{10,12},{12,14},{14,0},{1,3},{3,5},... | collective-permute-start | bytes 270344 | tf_op jit(solution)/shard_map/ppermute | solution.py:427
  5.5 3.1 %collective-permute-start.1 = (f32[88,256]{1,0:T(8,128)S(1)}, f32[88,256]{1,0:T(8,128)S(1)}, u32[]{:S(2)}, u32[]{:S(2)}) collective-permute-start(f32[88,256]{1,0:T(8,128)S(1)} %get-tuple-element.22.own_west), channel_id=1, source_target_pairs={{0,14},{2,0},{4,2},{6,4},{8,6},{10,8},{12,10},{14,12},{1,15},{3,1}... | collective-permute-start | bytes 270344 | tf_op jit(solution)/shard_map/ppermute | solution.py:428
  8.6 0.0 copy-start.1
  8.6 0.0 copy-start.2
  8.6 0.0 copy-done
  8.6 0.7 %copy-done.1 = f32[4,4]{1,0:T(4,128)S(1)} copy-done((f32[4,4]{1,0:T(4,128)S(1)}, f32[4,4]{1,0:T(4,128)}, u32[]{:S(2)}) %copy-start.1) | copy-done | bytes 88
  9.3 0.0 copy-done.2
  9.3 2.1 %shard_map.105 = (f32[8,4,32,256]{3,2,1,0:T(8,128)S(1)}, f32[8,32,256]{2,1,0:T(8,128)S(1)}, f32[1,128]{1,0:T(1,128)S(1)}) custom-call(f32[8,4,32,256]{3,2,1,0:T(8,128)S(1)} %get-tuple-element.16.state, bf16[2,8,4,32,256]{4,3,2,1,0:T(8,128)(2,1)S(1)} %get-tuple-element.17.noise, f32[2,32,256]{2,1,0:T(8,128)S(1)} %get-tuple-element.18.maps, ...), custom_call_target="tpu_custom_call" | custom-call | flops 20000000 | bytes 4000000 | tf_op jit(solution)/shard_map/pallas_call | solution.py:431
  11.4 0.1 collective-permute-start.2
  11.4 1.6 %shard_map.106.current = f32[8,4,32,256]{3,2,1,0:T(8,128)S(1)} custom-call(f32[8,4,32,256]{3,2,1,0:T(8,128)S(1)} %get-tuple-element.19.middle, f32[8,32,256]{2,1,0:T(8,128)S(1)} %get-tuple-element.20.observed, bf16[2,8,4,32,256]{4,3,2,1,0:T(8,128)(2,1)S(1)} %get-tuple-element.17.noise, f32[2,32,256]{2,1,0:T(8,128)S(1)} %copy-done, f32[1,4]{1,0:T(1,128)S(1)} %bitcast.7, ...), custom_call_target="tpu_custom_call" | custom-call | tf_op jit(solution)/shard_map/pallas_call | solution.py:451
  13.1 0.0 collective-permute-done.from_west
  13.1 0.0 collective-permute-done.1.from_east
  13.1 0.3 %shard_map.107 = (f32[1,128]{1,0:T(1,128)S(1)}, f32[4,32,256]{2,1,0:T(8,128)S(1)}) custom-call(f32[88,256]{1,0:T(8,128)S(1)} %get-tuple-element.21.own_east, f32[88,256]{1,0:T(8,128)S(1)} %get-tuple-element.22.own_west, f32[88,256]{1,0:T(8,128)S(1)} %collective-permute-done.from_west, f32[88,256]{1,0:T(8,128)S(1)} %collective-permute-done.1.from_east, ...), custom_call_target="tpu_custom_call" | custom-call | tf_op jit(solution)/shard_map/pallas_call | solution.py:442
  13.4 0.2 shard_map.108.current
  13.5 1.4 %collective-permute-done.2 = f32[1,128]{1,0:T(1,128)S(1)} collective-permute-done((f32[1,128]{1,0:T(1,128)S(1)}, f32[1,128]{1,0:T(1,128)S(1)}, u32[]{:S(2)}, u32[]{:S(2)}) %collective-permute-start.2) | collective-permute-done | bytes 544 | tf_op jit(solution)/shard_map/ppermute | solution.py:440
  15.0 0.0 collective-permute-start.4
  15.0 0.0 copy-start.3
  15.0 0.1 collective-permute-start.3
  15.1 3.5 %collective-permute-done.3 = f32[1,128]{1,0:T(1,128)S(1)} collective-permute-done((f32[1,128]{1,0:T(1,128)S(1)}, f32[1,128]{1,0:T(1,128)S(1)}, u32[]{:S(2)}, u32[]{:S(2)}) %collective-permute-start.3) | collective-permute-done | bytes 544 | tf_op jit(solution)/shard_map/ppermute | solution.py:477
  18.6 0.0 collective-permute-done.4.received
  18.6 0.9 %collective-permute-start.5 = (f32[1,128]{1,0:T(1,128)S(1)}, f32[1,128]{1,0:T(1,128)S(1)}, u32[]{:S(2)}, u32[]{:S(2)}) collective-permute-start(f32[1,128]{1,0:T(1,128)S(1)} %add.10), channel_id=1, source_target_pairs={{0,8},{2,10},{4,12},{6,14},{8,0},{10,2},{12,4},{14,6},{1,9},{3,11}... | collective-permute-start | bytes 1544 | tf_op jit(solution)/shard_map/ppermute | solution.py:477
  19.5 0.0 copy-done.3
  19.5 1.6 %shard_map.109 = f32[8,4,32,256]{3,2,1,0:T(8,128)} custom-call(s32[16]{0:T(128)S(1)} %copy-done.3, f32[8,4,32,256]{3,2,1,0:T(8,128)S(1)} %shard_map.108.current, f32[8,4,32,256]{3,2,1,0:T(8,128)S(1)} %collective-permute-done.4.received), custom_call_target="tpu_custom_call" | custom-call | bytes 2000000 | tf_op jit(solution)/shard_map/pallas_call | solution.py:480
  21.1 0.0 copy-start.4
  21.1 1.9 %collective-permute-done.5 = f32[1,128]{1,0:T(1,128)S(1)} collective-permute-done((f32[1,128]{1,0:T(1,128)S(1)}, f32[1,128]{1,0:T(1,128)S(1)}, u32[]{:S(2)}, u32[]{:S(2)}) %collective-permute-start.5) | collective-permute-done | bytes 544 | tf_op jit(solution)/shard_map/ppermute | solution.py:477
  23.0 0.0 copy-done.4
  23.0 0.5 %bitcast_subtract_fusion = f32[8]{0:T(128)} fusion(f32[8]{0:T(128)S(1)} %copy-done.4, f32[1,128]{1,0:T(1,128)S(1)} %add.11), kind=kLoop, calls=%fused_computation | loop fusion | flops 16 | bytes 96 | tf_op jit(solution)/shard_map/sub | solution.py:490
  (3 shorter events, 0.0 us)
Async XLA Ops:
  0.6 8.0 %copy-start = (f32[2,32,256]{2,1,0:T(8,128)S(1)}, f32[2,32,256]{2,1,0:T(8,128)}, u32[]{:S(2)}) copy-start(f32[2,32,256]{2,1,0:T(8,128)} %courant.3) | copy-start | bytes 196612
  2.5 10.6 %collective-permute-start = (f32[88,256]{1,0:T(8,128)S(1)}, f32[88,256]{1,0:T(8,128)S(1)}, u32[]{:S(2)}, u32[]{:S(2)}) collective-permute-start(f32[88,256]{1,0:T(8,128)S(1)} %get-tuple-element.21.own_east), channel_id=1, source_target_pairs={{0,2},{2,4},{4,6},{6,8},{8,10},{10,12},{12,14},{14,0},{1,3},{3,5},... | collective-permute-start | bytes 270344 | tf_op jit(solution)/shard_map/ppermute | solution.py:427
  5.5 7.6 %collective-permute-start.1 = (f32[88,256]{1,0:T(8,128)S(1)}, f32[88,256]{1,0:T(8,128)S(1)}, u32[]{:S(2)}, u32[]{:S(2)}) collective-permute-start(f32[88,256]{1,0:T(8,128)S(1)} %get-tuple-element.22.own_west), channel_id=1, source_target_pairs={{0,14},{2,0},{4,2},{6,4},{8,6},{10,8},{12,10},{14,12},{1,15},{3,1}... | collective-permute-start | bytes 270344 | tf_op jit(solution)/shard_map/ppermute | solution.py:428
  8.6 0.7 %copy-start.1 = (f32[4,4]{1,0:T(4,128)S(1)}, f32[4,4]{1,0:T(4,128)}, u32[]{:S(2)}) copy-start(f32[4,4]{1,0:T(4,128)} %mixing.5) | copy-start | bytes 196
  8.6 0.7 %copy-start.2 = (f32[4]{0:T(128)S(1)}, f32[4]{0:T(128)}, u32[]{:S(2)}) copy-start(f32[4]{0:T(128)} %param.12) | copy-start | bytes 52
  11.4 3.6 %collective-permute-start.2 = (f32[1,128]{1,0:T(1,128)S(1)}, f32[1,128]{1,0:T(1,128)S(1)}, u32[]{:S(2)}, u32[]{:S(2)}) collective-permute-start(f32[1,128]{1,0:T(1,128)S(1)} %get-tuple-element.23.bulk_weight), channel_id=1, source_target_pairs={{0,2},{2,0},{4,6},{6,4},{8,10},{10,8},{12,14},{14,12},{1,3},{3,1},... | collective-permute-start | bytes 1544 | tf_op jit(solution)/shard_map/ppermute | solution.py:440
  15.0 3.6 %collective-permute-start.4 = (f32[8,4,32,256]{3,2,1,0:T(8,128)S(1)}, f32[8,4,32,256]{3,2,1,0:T(8,128)S(1)}, u32[]{:S(2)}, u32[]{:S(2)}) collective-permute-start(f32[8,4,32,256]{3,2,1,0:T(8,128)S(1)} %shard_map.108.current), channel_id=1, source_target_pairs={{0,1},{1,0},{2,3},{3,2},{4,5},{5,4},{6,7},{7,6},{8,9},{9,8},{10,11... | collective-permute-start | bytes 3145736 | tf_op jit(solution)/shard_map/ppermute | solution.py:472
  15.0 4.5 %copy-start.3 = (s32[16]{0:T(128)S(1)}, s32[16]{0:T(128)}, u32[]{:S(2)}) copy-start(s32[16]{0:T(128)} %source.1) | copy-start | bytes 196
  15.0 3.6 %collective-permute-start.3 = (f32[1,128]{1,0:T(1,128)S(1)}, f32[1,128]{1,0:T(1,128)S(1)}, u32[]{:S(2)}, u32[]{:S(2)}) collective-permute-start(f32[1,128]{1,0:T(1,128)S(1)} %add.9), channel_id=1, source_target_pairs={{0,4},{2,6},{4,0},{6,2},{8,12},{10,14},{12,8},{14,10},{1,5},{3,7},... | collective-permute-start | bytes 1544 | tf_op jit(solution)/shard_map/ppermute | solution.py:477
  18.6 4.4 %collective-permute-start.5 = (f32[1,128]{1,0:T(1,128)S(1)}, f32[1,128]{1,0:T(1,128)S(1)}, u32[]{:S(2)}, u32[]{:S(2)}) collective-permute-start(f32[1,128]{1,0:T(1,128)S(1)} %add.10), channel_id=1, source_target_pairs={{0,8},{2,10},{4,12},{6,14},{8,0},{10,2},{12,4},{14,6},{1,9},{3,11}... | collective-permute-start | bytes 1544 | tf_op jit(solution)/shard_map/ppermute | solution.py:477
  21.1 1.9 %copy-start.4 = (f32[8]{0:T(128)S(1)}, f32[8]{0:T(128)}, u32[]{:S(2)}) copy-start(f32[8]{0:T(128)} %param.14) | copy-start | bytes 100

commit v10 on v9

--- a/solution.py
+++ b/solution.py
@@ -99,17 +99,22 @@
     return dense[:strip] * (0.25 * precision), target
 
 
-class Spread:
-    def __init__(self, ref):
-        self.ref = ref
+class Rows:
+    def __init__(self, ref, first, columns):
+        self.ref, self.first, self.columns = ref, first, columns
 
     def __getitem__(self, at):
-        return self.ref[at[0]:at[0] + 1, at[1]:at[1] + 1]
+        row = self.first + at[0] * self.columns + at[1]
+        return self.ref[row:row + 1]
+
+
+def scalars_in(ref, fields):
+    return Rows(ref, fields * fields, fields), Rows(ref, 0, fields)
 
 
 def prepare(sizes, state_hbm, noise_hbm, courant_hbm, diffusion_hbm, mixing_hbm, cell_hbm, value_hbm,
-            send_east, send_west, state, noise, maps,
-            courant, diffusion, mixing, cell, value, sems):
+            send_east, send_west, state, noise, maps, courant, scalars,
+            diffusion, mixing, cell, value, sems):
     particles, fields, strip, lats, strips = sizes
     n = fields * particles
     copies = [pltpu.make_async_copy(source, target, sems.at[k]) for k, (source, target) in enumerate((
@@ -124,7 +129,6 @@
     copies[1].wait()
     gain, target = observation_maps(sizes, cell[...], value[...])
     maps[0], maps[1] = gain, target
-    diffusion, mixing = Spread(diffusion), Spread(mixing)
     kinds = []
     for x, step in ((strip - 1, -1), (0, 1)):
         kinds += [(f, x) for f in range(fields)] + [(f, x + step) for f in range(fields)] + [(0, x + 2 * step)]
@@ -132,6 +136,12 @@
     pick1 = pick_rows([(0, x) for x in (strip - 1, strip - 2, 0, 1)], particles, 1, strip)
     for copy in copies[2:5]:
         copy.wait()
+    for f in range(fields):
+        for g in range(fields):
+            scalars[f * fields + g:f * fields + g + 1] = jnp.broadcast_to(mixing[f:f + 1, g:g + 1], (1, lats))
+        at = fields * fields + f
+        scalars[at:at + 1] = jnp.broadcast_to(diffusion[:, f:f + 1], (1, lats))
+    diffusion, mixing = scalars_in(scalars, fields)
 
     sides = []
     for first, inward, outward in ((strip - 8, 2, 1), (0, 1, 2)):
@@ -230,9 +240,9 @@
     copies[10].wait()
 
 
-def zero_halo(sizes, courant, diffusion, mixing, mixing_scalars, coefs):
-    particles, fields, strip, lats, strips = sizes
-    diffusion, mixing = Spread(diffusion), Spread(mixing)
+def zero_halo_coefs(sizes, courant, scalars, coefs):
+    particles, fields, strip, lats, strips = sizes
+    diffusion, mixing = scalars_in(scalars, fields)
     lon = lax.broadcasted_iota(jnp.int32, (strip, lats), 0)
     for f in range(fields):
         centre, east, west, to_north, to_south = coefficients(
@@ -243,21 +253,23 @@
         coefs[f, 3] = to_north
         coefs[f, 4] = to_south
 
+
+def zero_halo_step(sizes, scalars, coefs):
+    particles, fields, strip, lats, strips = sizes
+    _, mixing = scalars_in(scalars, fields)
+
     def moved(values, f):
         v = values[f]
         return (coefs[f, 0] * v + coefs[f, 1] * pltpu.roll(v, strip - 1, 0) + coefs[f, 2] * pltpu.roll(v, 1, 0)
-                + coefs[f, 3] * north(v) + coefs[f, 4] * south(v) + mixed(mixing_scalars, f, values))
+                + coefs[f, 3] * north(v) + coefs[f, 4] * south(v) + mixed(mixing, f, values))
 
     return moved
 
 
-def observed_bulk(sizes, state, noise, maps, courant, diffusion, mixing, middle, out, weight,
-                  coefs, partial, mixing_scalars, sem):
-    particles, fields, strip, lats, strips = sizes
-    copy = pltpu.make_async_copy(mixing, mixing_scalars, sem)
-    copy.start()
-    moved = zero_halo(sizes, courant, diffusion, mixing, mixing_scalars, coefs)
-    copy.wait()
+def observed_bulk(sizes, state, noise, maps, courant, scalars, middle, out, weight, coefs, partial):
+    particles, fields, strip, lats, strips = sizes
+    zero_halo_coefs(sizes, courant, scalars, coefs)
+    moved = zero_halo_step(sizes, scalars, coefs)
 
     def one(p):
         values = [state[p, f] for f in range(fields)]
@@ -289,12 +301,9 @@
     weight[...] = in_row(partial[...])
 
 
-def other_bulk(sizes, middle, observed, noise, courant, diffusion, mixing, out, coefs, mixing_scalars, sem):
-    particles, fields, strip, lats, strips = sizes
-    copy = pltpu.make_async_copy(mixing, mixing_scalars, sem)
-    copy.start()
-    moved = zero_halo(sizes, courant, diffusion, mixing, mixing_scalars, coefs)
-    copy.wait()
+def other_bulk(sizes, middle, observed, noise, scalars, coefs, out):
+    particles, fields, strip, lats, strips = sizes
+    moved = zero_halo_step(sizes, scalars, coefs)
 
     def body(p, carry):
         values = [middle[p, f] for f in range(fields)]
@@ -306,10 +315,10 @@
     lax.fori_loop(0, particles, body, 0)
 
 
-def correct(sizes, own_east, own_west, from_west, from_east, diffusion, mixing, bulk_weight, weight, changes):
+def correct(sizes, own_east, own_west, from_west, from_east, scalars, bulk_weight, weight, changes):
     particles, fields, strip, lats, strips = sizes
     n = fields * particles
-    diffusion, mixing = Spread(diffusion), Spread(mixing)
+    diffusion, mixing = scalars_in(scalars, fields)
 
     def field_rows(ref, start, f):
         return ref[start + f * particles:start + (f + 1) * particles]
@@ -405,18 +414,18 @@
         return jax.ShapeDtypeStruct(dims, F32)
 
     whole = (particles, fields, strip, lats)
-    spread = diffusion[None]
 
     def in_hbm(array):
         return pltpu.with_memory_space_constraint(array, pltpu.HBM)
 
-    arrays = (ensemble_state, proposal_noise, courant, spread, mixing, cell, value)
-    send_east, send_west, state, noise, maps = pl.pallas_call(
+    arrays = (ensemble_state, proposal_noise, courant, diffusion[None], mixing, cell, value)
+    send_east, send_west, state, noise, maps, courant, scalars = pl.pallas_call(
         functools.partial(prepare, sizes),
-        out_shape=(packet, packet, shape(*whole), jax.ShapeDtypeStruct((2,) + whole, BF16), shape(2, strip, lats)),
+        out_shape=(packet, packet, shape(*whole), jax.ShapeDtypeStruct((2,) + whole, BF16), shape(2, strip, lats),
+                   shape(*courant.shape), shape(fields * (fields + 2), lats)),
         in_specs=[HBM] * 7,
-        out_specs=(VMEM,) * 5,
-        scratch_shapes=[pltpu.VMEM(array.shape, array.dtype) for array in arrays[2:]]
+        out_specs=(VMEM,) * 7,
+        scratch_shapes=[pltpu.VMEM(array.shape, array.dtype) for array in arrays[3:]]
         + [pltpu.SemaphoreType.DMA((11,))],
         compiler_params=LIMIT,
         cost_estimate=pl.CostEstimate(flops=1000000, bytes_accessed=2000000, transcendentals=0),
@@ -427,36 +436,34 @@
     from_west = lax.ppermute(send_east, "lon", eastward)
     from_east = lax.ppermute(send_west, "lon", westward)
 
-    scalars = [pltpu.SMEM(mixing.shape, F32), pltpu.SemaphoreType.DMA]
-    middle, observed, bulk_weight = pl.pallas_call(
+    middle, observed, bulk_weight, coefs = pl.pallas_call(
         functools.partial(observed_bulk, sizes),
-        out_shape=(shape(*whole), shape(particles, strip, lats), shape(1, 128)),
-        in_specs=[VMEM] * 6,
-        out_specs=(VMEM,) * 3,
-        scratch_shapes=[pltpu.VMEM((fields, 5, strip, lats), F32), pltpu.VMEM((particles, 128), F32)] + scalars,
+        out_shape=(shape(*whole), shape(particles, strip, lats), shape(1, 128), shape(fields, 5, strip, lats)),
+        in_specs=[VMEM] * 5,
+        out_specs=(VMEM,) * 4,
+        scratch_shapes=[pltpu.VMEM((particles, 128), F32)],
         compiler_params=LIMIT,
         cost_estimate=pl.CostEstimate(flops=20000000, bytes_accessed=4000000, transcendentals=0),
-    )(state, noise, maps, courant, spread, mixing)
+    )(state, noise, maps, courant, scalars)
     beside = lax.ppermute(bulk_weight, "lon", [(i, i ^ 1) for i in range(strips)])
 
     weight, changes = pl.pallas_call(
         functools.partial(correct, sizes),
         out_shape=(shape(1, 128), shape(4, particles * fields, lats)),
-        in_specs=[VMEM] * 7,
+        in_specs=[VMEM] * 6,
         out_specs=(VMEM,) * 2,
         compiler_params=LIMIT,
         cost_estimate=FREE,
-    )(send_east, send_west, from_west, from_east, spread, mixing, bulk_weight)
+    )(send_east, send_west, from_west, from_east, scalars, bulk_weight)
 
     current = pl.pallas_call(
         functools.partial(other_bulk, sizes),
         out_shape=shape(*whole),
-        in_specs=[VMEM] * 6,
+        in_specs=[VMEM] * 5,
         out_specs=VMEM,
-        scratch_shapes=[pltpu.VMEM((fields, 5, strip, lats), F32)] + scalars,
         compiler_params=LIMIT,
         cost_estimate=FREE,
-    )(middle, observed, noise, courant, spread, mixing)
+    )(middle, observed, noise, scalars, coefs)
 
     current = pl.pallas_call(
         functools.partial(apply_changes, sizes),

time: 23.7 us -> 22.5 us (0.949)
  Pallas kernels: 7.55 us -> 6.48 us
  local copies, waits for them, and re-layouts: 0.69 us -> 0.01 us
  waiting for transfers between devices: 6.9 us -> 7.53 us
    unnamed x10 -> x4, local copies, waits for them, and re-layouts: 0.69 us -> 0.01 us
    ppermute x1, waiting for transfers between devices: 0.01 us -> 0.59 us  [local(): from_east = lax.ppermute(send_west, 'lon', westward)]
    pallas_call x1, Pallas kernels: 1.63 us -> 1.1 us  [local(): pl.pallas_call(functools.partial(other_bulk, sizes), out_shape=shape(*who...]
    pallas_call x1, Pallas kernels: 2.07 us -> 1.65 us  [local(): pl.pallas_call(functools.partial(observed_bulk, sizes), out_shape=(shape(...]
  transfers between devices with their start and end apart: 6 -> 6, of which waited for: 3 -> 4; matrix products, arithmetic and copies ran while one was open for 0% -> 0% of each run, Pallas kernels for 24% -> 21%
where the time goes in v10:
time: 22.5 us; the launch traced here: 22.3 us
  waiting for transfers between devices  7.53 us (33%)
  starting transfers between devices  7.09 us (32%)
  Pallas kernels  6.48 us (29%)
  between operations  0.69 us (3%)
  other arithmetic  0.52 us (2%)
    ppermute x2, waiting for transfers between devices, local(): lax.ppermute(weight, 'lon', [(i, i ^ bit) for i in range(strips)])  5.44 us
    ppermute x1, starting transfers between devices, local(): from_east = lax.ppermute(send_west, 'lon', westward)  3.1 us
    ppermute x1, starting transfers between devices, local(): from_west = lax.ppermute(send_east, 'lon', eastward)  2.99 us
    pallas_call x1, Pallas kernels, local(): pl.pallas_call(functools.partial(prepare, sizes), out_shape=(packet, pack...  1.81 us
    pallas_call x1, Pallas kernels, local(): pl.pallas_call(functools.partial(observed_bulk, sizes), out_shape=(shape(...  1.65 us
    pallas_call x1, Pallas kernels, local(): pl.pallas_call(functools.partial(assemble, sizes), out_shape=shape(*whole...  1.58 us
    ppermute x1, waiting for transfers between devices, local(): lax.ppermute(bulk_weight, 'lon', [(i, i ^ 1) for i in range(strips)])  1.5 us
    pallas_call x1, Pallas kernels, local(): pl.pallas_call(functools.partial(other_bulk, sizes), out_shape=shape(*who...  1.1 us
  transfers between devices with their start and end apart: 6, of which 4 were waited for; matrix products, arithmetic and copies ran while one was open for 0% of the time, Pallas kernels for 21%

profile of v10, /device:TPU:0, one launch (start us, length us, event | category | flops | bytes accessed | tf_op | source)
XLA Modules:
  0.0 22.3 jit_solution(6700471624420386558)
XLA Ops:
  0.6 1.8 %shard_map.104 = (f32[88,256]{1,0:T(8,128)S(1)}, f32[88,256]{1,0:T(8,128)S(1)}, f32[8,4,32,256]{3,2,1,0:T(8,128)S(1)}, bf16[2,8,4,32,256]{4,3,2,1,0:T(8,128)(2,1...) custom-call(f32[8,4,32,256]{3,2,1,0:T(8,128)} %state_hbm.1, ...), custom_call_target="tpu_custom_call" | custom-call | flops 1000000 | bytes 2000000 | tf_op jit(solution)/shard_map/pallas_call | solution.py:422
  2.5 3.0 %collective-permute-start = (f32[88,256]{1,0:T(8,128)S(1)}, f32[88,256]{1,0:T(8,128)S(1)}, u32[]{:S(2)}, u32[]{:S(2)}) collective-permute-start(f32[88,256]{1,0:T(8,128)S(1)} %get-tuple-element.27.own_east), channel_id=1, source_target_pairs={{0,2},{2,4},{4,6},{6,8},{8,10},{10,12},{12,14},{14,0},{1,3},{3,5},... | collective-permute-start | bytes 270344 | tf_op jit(solution)/shard_map/ppermute | solution.py:436
  5.4 3.1 %collective-permute-start.1 = (f32[88,256]{1,0:T(8,128)S(1)}, f32[88,256]{1,0:T(8,128)S(1)}, u32[]{:S(2)}, u32[]{:S(2)}) collective-permute-start(f32[88,256]{1,0:T(8,128)S(1)} %get-tuple-element.28.own_west), channel_id=1, source_target_pairs={{0,14},{2,0},{4,2},{6,4},{8,6},{10,8},{12,10},{14,12},{1,15},{3,1}... | collective-permute-start | bytes 270344 | tf_op jit(solution)/shard_map/ppermute | solution.py:437
  8.5 1.7 %shard_map.105 = (f32[8,4,32,256]{3,2,1,0:T(8,128)S(1)}, f32[8,32,256]{2,1,0:T(8,128)S(1)}, f32[1,128]{1,0:T(1,128)S(1)}, f32[4,5,32,256]{3,2,1,0:T(8,128)S(1)}) custom-call(f32[8,4,32,256]{3,2,1,0:T(8,128)S(1)} %get-tuple-element.19.state, bf16[2,8,4,32,256]{4,3,2,1,0:T(8,128)(2,1)S(1)} %get-tuple-element.20.noise, ...), custom_call_target="tpu_custom_call" | custom-call | flops 20000000 | bytes 4000000 | tf_op jit(solution)/shard_map/pallas_call | solution.py:439
  10.2 0.0 collective-permute-start.2
  10.2 1.1 %shard_map.106.current = f32[8,4,32,256]{3,2,1,0:T(8,128)S(1)} custom-call(f32[8,4,32,256]{3,2,1,0:T(8,128)S(1)} %get-tuple-element.24.middle, f32[8,32,256]{2,1,0:T(8,128)S(1)} %get-tuple-element.25.observed, bf16[2,8,4,32,256]{4,3,2,1,0:T(8,128)(2,1)S(1)} %get-tuple-element.20.noise, f32[24,256]{1,0:T(8,128)S(1)} %get-tuple-element.23.scalars, ...), custom_call_target="tpu_custom_call" | custom-call | tf_op jit(solution)/shard_map/pallas_call | solution.py:459
  11.3 0.0 collective-permute-done.from_west
  11.3 0.6 %collective-permute-done.1.from_east = f32[88,256]{1,0:T(8,128)S(1)} collective-permute-done((f32[88,256]{1,0:T(8,128)S(1)}, f32[88,256]{1,0:T(8,128)S(1)}, u32[]{:S(2)}, u32[]{:S(2)}) %collective-permute-start.1) | collective-permute-done | bytes 90144 | tf_op jit(solution)/shard_map/ppermute | solution.py:437
  11.9 0.2 shard_map.107
  12.1 0.1 shard_map.108.current
  12.2 1.5 %collective-permute-done.2 = f32[1,128]{1,0:T(1,128)S(1)} collective-permute-done((f32[1,128]{1,0:T(1,128)S(1)}, f32[1,128]{1,0:T(1,128)S(1)}, u32[]{:S(2)}, u32[]{:S(2)}) %collective-permute-start.2) | collective-permute-done | bytes 544 | tf_op jit(solution)/shard_map/ppermute | solution.py:448
  13.7 0.0 collective-permute-start.4
  13.8 0.0 copy-start
  13.8 0.1 collective-permute-start.3
  13.8 3.5 %collective-permute-done.3 = f32[1,128]{1,0:T(1,128)S(1)} collective-permute-done((f32[1,128]{1,0:T(1,128)S(1)}, f32[1,128]{1,0:T(1,128)S(1)}, u32[]{:S(2)}, u32[]{:S(2)}) %collective-permute-start.3) | collective-permute-done | bytes 544 | tf_op jit(solution)/shard_map/ppermute | solution.py:484
  17.4 0.0 collective-permute-done.4.received
  17.4 0.9 %collective-permute-start.5 = (f32[1,128]{1,0:T(1,128)S(1)}, f32[1,128]{1,0:T(1,128)S(1)}, u32[]{:S(2)}, u32[]{:S(2)}) collective-permute-start(f32[1,128]{1,0:T(1,128)S(1)} %add.10), channel_id=1, source_target_pairs={{0,8},{2,10},{4,12},{6,14},{8,0},{10,2},{12,4},{14,6},{1,9},{3,11}... | collective-permute-start | bytes 1544 | tf_op jit(solution)/shard_map/ppermute | solution.py:484
  18.3 0.0 copy-done
  18.3 1.6 %shard_map.109 = f32[8,4,32,256]{3,2,1,0:T(8,128)} custom-call(s32[16]{0:T(128)S(1)} %copy-done, f32[8,4,32,256]{3,2,1,0:T(8,128)S(1)} %shard_map.108.current, f32[8,4,32,256]{3,2,1,0:T(8,128)S(1)} %collective-permute-done.4.received), custom_call_target="tpu_custom_call" | custom-call | bytes 2000000 | tf_op jit(solution)/shard_map/pallas_call | solution.py:487
  19.9 0.0 copy-start.1
  19.9 1.9 %collective-permute-done.5 = f32[1,128]{1,0:T(1,128)S(1)} collective-permute-done((f32[1,128]{1,0:T(1,128)S(1)}, f32[1,128]{1,0:T(1,128)S(1)}, u32[]{:S(2)}, u32[]{:S(2)}) %collective-permute-start.5) | collective-permute-done | bytes 544 | tf_op jit(solution)/shard_map/ppermute | solution.py:484
  21.8 0.0 copy-done.1
  21.8 0.5 %bitcast_subtract_fusion = f32[8]{0:T(128)} fusion(f32[8]{0:T(128)S(1)} %copy-done.1, f32[1,128]{1,0:T(1,128)S(1)} %add.11), kind=kLoop, calls=%fused_computation | loop fusion | flops 16 | bytes 96 | tf_op jit(solution)/shard_map/sub | solution.py:497
  (3 shorter events, 0.0 us)
Async XLA Ops:
  2.5 8.9 %collective-permute-start = (f32[88,256]{1,0:T(8,128)S(1)}, f32[88,256]{1,0:T(8,128)S(1)}, u32[]{:S(2)}, u32[]{:S(2)}) collective-permute-start(f32[88,256]{1,0:T(8,128)S(1)} %get-tuple-element.27.own_east), channel_id=1, source_target_pairs={{0,2},{2,4},{4,6},{6,8},{8,10},{10,12},{12,14},{14,0},{1,3},{3,5},... | collective-permute-start | bytes 270344 | tf_op jit(solution)/shard_map/ppermute | solution.py:436
  5.4 6.5 %collective-permute-start.1 = (f32[88,256]{1,0:T(8,128)S(1)}, f32[88,256]{1,0:T(8,128)S(1)}, u32[]{:S(2)}, u32[]{:S(2)}) collective-permute-start(f32[88,256]{1,0:T(8,128)S(1)} %get-tuple-element.28.own_west), channel_id=1, source_target_pairs={{0,14},{2,0},{4,2},{6,4},{8,6},{10,8},{12,10},{14,12},{1,15},{3,1}... | collective-permute-start | bytes 270344 | tf_op jit(solution)/shard_map/ppermute | solution.py:437
  10.2 3.5 %collective-permute-start.2 = (f32[1,128]{1,0:T(1,128)S(1)}, f32[1,128]{1,0:T(1,128)S(1)}, u32[]{:S(2)}, u32[]{:S(2)}) collective-permute-start(f32[1,128]{1,0:T(1,128)S(1)} %get-tuple-element.29.bulk_weight), channel_id=1, source_target_pairs={{0,2},{2,0},{4,6},{6,4},{8,10},{10,8},{12,14},{14,12},{1,3},{3,1},... | collective-permute-start | bytes 1544 | tf_op jit(solution)/shard_map/ppermute | solution.py:448
  13.7 3.6 %collective-permute-start.4 = (f32[8,4,32,256]{3,2,1,0:T(8,128)S(1)}, f32[8,4,32,256]{3,2,1,0:T(8,128)S(1)}, u32[]{:S(2)}, u32[]{:S(2)}) collective-permute-start(f32[8,4,32,256]{3,2,1,0:T(8,128)S(1)} %shard_map.108.current), channel_id=1, source_target_pairs={{0,1},{1,0},{2,3},{3,2},{4,5},{5,4},{6,7},{7,6},{8,9},{9,8},{10,11... | collective-permute-start | bytes 3145736 | tf_op jit(solution)/shard_map/ppermute | solution.py:479
  13.8 4.5 %copy-start = (s32[16]{0:T(128)S(1)}, s32[16]{0:T(128)}, u32[]{:S(2)}) copy-start(s32[16]{0:T(128)} %source.1) | copy-start | bytes 196
  13.8 3.6 %collective-permute-start.3 = (f32[1,128]{1,0:T(1,128)S(1)}, f32[1,128]{1,0:T(1,128)S(1)}, u32[]{:S(2)}, u32[]{:S(2)}) collective-permute-start(f32[1,128]{1,0:T(1,128)S(1)} %add.9), channel_id=1, source_target_pairs={{0,4},{2,6},{4,0},{6,2},{8,12},{10,14},{12,8},{14,10},{1,5},{3,7},... | collective-permute-start | bytes 1544 | tf_op jit(solution)/shard_map/ppermute | solution.py:484
  17.4 4.4 %collective-permute-start.5 = (f32[1,128]{1,0:T(1,128)S(1)}, f32[1,128]{1,0:T(1,128)S(1)}, u32[]{:S(2)}, u32[]{:S(2)}) collective-permute-start(f32[1,128]{1,0:T(1,128)S(1)} %add.10), channel_id=1, source_target_pairs={{0,8},{2,10},{4,12},{6,14},{8,0},{10,2},{12,4},{14,6},{1,9},{3,11}... | collective-permute-start | bytes 1544 | tf_op jit(solution)/shard_map/ppermute | solution.py:484
  19.9 1.9 %copy-start.1 = (f32[8]{0:T(128)S(1)}, f32[8]{0:T(128)}, u32[]{:S(2)}) copy-start(f32[8]{0:T(128)} %param.14) | copy-start | bytes 100

commit v11 on v10

--- a/solution.py
+++ b/solution.py
@@ -266,12 +266,11 @@
     return moved
 
 
-def observed_bulk(sizes, state, noise, maps, courant, scalars, middle, out, weight, coefs, partial):
-    particles, fields, strip, lats, strips = sizes
-    zero_halo_coefs(sizes, courant, scalars, coefs)
-    moved = zero_halo_step(sizes, scalars, coefs)
+def observed_bulk(sizes, parity, state, noise, maps, courant, scalars, middle, out, weight, coefs, partial):
+    particles, fields, strip, lats, strips = sizes
 
     def one(p):
+        moved = zero_halo_step(sizes, scalars, coefs)
         values = [state[p, f] for f in range(fields)]
         results = []
         for f in range(fields):
@@ -297,25 +296,48 @@
         one(2 * pair + 1)
         return carry
 
-    lax.fori_loop(0, particles // 2, body, 0)
-    weight[...] = in_row(partial[...])
-
-
-def other_bulk(sizes, middle, observed, noise, scalars, coefs, out):
-    particles, fields, strip, lats, strips = sizes
-    moved = zero_halo_step(sizes, scalars, coefs)
-
-    def body(p, carry):
-        values = [middle[p, f] for f in range(fields)]
-        out[p, 0] = observed[p]
-        for f in range(1, fields):
-            out[p, f] = moved(values, f) + noise[1, p, f].astype(F32)
-        return carry
-
-    lax.fori_loop(0, particles, body, 0)
-
-
-def correct(sizes, own_east, own_west, from_west, from_east, scalars, bulk_weight, weight, changes):
+    here = lax.axis_index("lon") % 2 == parity
+
+    @pl.when(here)
+    def _():
+        zero_halo_coefs(sizes, courant, scalars, coefs)
+        lax.fori_loop(0, particles // 2, body, 0)
+        weight[...] = in_row(partial[...])
+
+    @pl.when(jnp.logical_not(here))
+    def _():
+        weight[...] = jnp.zeros_like(weight)
+
+
+def other_bulk(sizes, even_middle, even_observed, even_coefs, odd_middle, odd_observed, odd_coefs,
+               noise, scalars, out):
+    particles, fields, strip, lats, strips = sizes
+
+    def run(middle, observed, coefs):
+        moved = zero_halo_step(sizes, scalars, coefs)
+
+        def body(p, carry):
+            values = [middle[p, f] for f in range(fields)]
+            out[p, 0] = observed[p]
+            for f in range(1, fields):
+                out[p, f] = moved(values, f) + noise[1, p, f].astype(F32)
+            return carry
+
+        lax.fori_loop(0, particles, body, 0)
+
+    even = lax.axis_index("lon") % 2 == 0
+
+    @pl.when(even)
+    def _():
+        run(even_middle, even_observed, even_coefs)
+
+    @pl.when(jnp.logical_not(even))
+    def _():
+        run(odd_middle, odd_observed, odd_coefs)
+
+
+def correct(sizes, own_east, own_west, from_west, from_east, scalars, even_weight, odd_weight,
+            weight, changes):
     particles, fields, strip, lats, strips = sizes
     n = fields * particles
     diffusion, mixing = scalars_in(scalars, fields)
@@ -363,7 +385,7 @@
                 edge, inner = (3, 2) if k == 0 else (0, 1)
                 changes[edge, f * particles:(f + 1) * particles] = step
                 changes[inner, f * particles:(f + 1) * particles] = beside
-    weight[...] = in_row(wide(total)) + bulk_weight[...]
+    weight[...] = in_row(wide(total)) + (even_weight[...] + odd_weight[...])
 
 
 def apply_changes(sizes, current, changes, out):
@@ -436,34 +458,42 @@
     from_west = lax.ppermute(send_east, "lon", eastward)
     from_east = lax.ppermute(send_west, "lon", westward)
 
-    middle, observed, bulk_weight, coefs = pl.pallas_call(
-        functools.partial(observed_bulk, sizes),
-        out_shape=(shape(*whole), shape(particles, strip, lats), shape(1, 128), shape(fields, 5, strip, lats)),
-        in_specs=[VMEM] * 5,
-        out_specs=(VMEM,) * 4,
-        scratch_shapes=[pltpu.VMEM((particles, 128), F32)],
+    def bulk_of(parity, cost):
+        return pl.pallas_call(
+            functools.partial(observed_bulk, sizes, parity),
+            out_shape=(shape(*whole), shape(particles, strip, lats), shape(1, 128), shape(fields, 5, strip, lats)),
+            in_specs=[VMEM] * 5,
+            out_specs=(VMEM,) * 4,
+            scratch_shapes=[pltpu.VMEM((particles, 128), F32)],
+            compiler_params=LIMIT,
+            cost_estimate=cost,
+        )(state, noise, maps, courant, scalars)
+
+    odd_middle, odd_observed, odd_weight, odd_coefs = bulk_of(
+        1, pl.CostEstimate(flops=20000000, bytes_accessed=4000000, transcendentals=0))
+    to_even = lax.ppermute(odd_weight, "lon", [(i + 1, i) for i in range(0, strips, 2)])
+    even_middle, even_observed, even_weight, even_coefs = bulk_of(0, FREE)
+
+    current = pl.pallas_call(
+        functools.partial(other_bulk, sizes),
+        out_shape=shape(*whole),
+        in_specs=[VMEM] * 8,
+        out_specs=VMEM,
         compiler_params=LIMIT,
-        cost_estimate=pl.CostEstimate(flops=20000000, bytes_accessed=4000000, transcendentals=0),
-    )(state, noise, maps, courant, scalars)
-    beside = lax.ppermute(bulk_weight, "lon", [(i, i ^ 1) for i in range(strips)])
-
+        cost_estimate=FREE,
+    )(even_middle, even_observed, even_coefs, odd_middle, odd_observed, odd_coefs, noise, scalars)
+
+    current, from_west, from_east = lax.optimization_barrier((current, from_west, from_east))
     weight, changes = pl.pallas_call(
         functools.partial(correct, sizes),
         out_shape=(shape(1, 128), shape(4, particles * fields, lats)),
-        in_specs=[VMEM] * 6,
+        in_specs=[VMEM] * 7,
         out_specs=(VMEM,) * 2,
         compiler_params=LIMIT,
         cost_estimate=FREE,
-    )(send_east, send_west, from_west, from_east, scalars, bulk_weight)
-
-    current = pl.pallas_call(
-        functools.partial(other_bulk, sizes),
-        out_shape=shape(*whole),
-        in_specs=[VMEM] * 5,
-        out_specs=VMEM,
-        compiler_params=LIMIT,
-        cost_estimate=FREE,
-    )(middle, observed, noise, scalars, coefs)
+    )(send_east, send_west, from_west, from_east, scalars, even_weight, odd_weight)
+    even_weight, changes = lax.optimization_barrier((even_weight, changes))
+    to_odd = lax.ppermute(even_weight, "lon", [(i, i + 1) for i in range(0, strips, 2)])
 
     current = pl.pallas_call(
         functools.partial(apply_changes, sizes),
@@ -474,8 +504,8 @@
         cost_estimate=FREE,
     )(current, changes)
 
-    current, beside = lax.optimization_barrier((current, beside))
-    weight = weight + beside
+    current, to_even, to_odd = lax.optimization_barrier((current, to_even, to_odd))
+    weight = weight + (to_even + to_odd)
     received = lax.ppermute(current, "dom", [(0, 1), (1, 0)])
     bit = 2
     while bit < strips:

time: 22.5 us -> 25.8 us (1.15)
  starting transfers between devices: 7.09 us -> 12.1 us
  waiting for transfers between devices: 7.53 us -> 5.83 us
    ppermute x1 -> x2, starting transfers between devices: 0.01 us -> 4.23 us  [the longest x1 2.95 us: local(): lax.ppermute(even_weight, 'lon', [(i, i + 1) for i in range(0, strips, 2)])]
    ppermute x2, starting transfers between devices: 0.99 us -> 1.74 us  [local(): lax.ppermute(weight, 'lon', [(i, i ^ bit) for i in range(strips)])]
    ppermute x2, waiting for transfers between devices: 5.44 us -> 4.7 us  [local(): lax.ppermute(weight, 'lon', [(i, i ^ bit) for i in range(strips)])]
    ppermute x1, waiting for transfers between devices: 0.59 us -> 0.01 us  [local(): from_east = lax.ppermute(send_west, 'lon', westward)]
    ppermute x1 -> x2, waiting for transfers between devices: 1.5 us -> 1.12 us  [the longest x1 1.12 us: local(): lax.ppermute(even_weight, 'lon', [(i, i + 1) for i in range(0, strips, 2)])]
    pallas_call x1 -> x2, Pallas kernels: 1.65 us -> 1.66 us  [bulk_of(): pl.pallas_call(functools.partial(observed_bulk, sizes, parity), out_shape...]
  transfers between devices with their start and end apart: 6 -> 7, of which waited for: 4 -> 3; matrix products, arithmetic and copies ran while one was open for 0% -> 0% of each run, Pallas kernels for 21% -> 18%
where the time goes in v11:
time: 25.8 us; the launch traced here: 25.6 us
  starting transfers between devices  12.1 us (47%)
  Pallas kernels  6.47 us (25%)
  waiting for transfers between devices  5.83 us (23%)
  between operations  0.72 us (3%)
  other arithmetic  0.52 us (2%)
    ppermute x2, waiting for transfers between devices, local(): lax.ppermute(weight, 'lon', [(i, i ^ bit) for i in range(strips)])  4.7 us
    ppermute x1, starting transfers between devices, local(): from_east = lax.ppermute(send_west, 'lon', westward)  3.1 us
    ppermute x1, starting transfers between devices, local(): from_west = lax.ppermute(send_east, 'lon', eastward)  2.99 us
    ppermute x1, starting transfers between devices, local(): lax.ppermute(even_weight, 'lon', [(i, i + 1) for i in range(0, strips, 2)])  2.95 us
    pallas_call x1, Pallas kernels, local(): pl.pallas_call(functools.partial(prepare, sizes), out_shape=(packet, pack...  1.81 us
    ppermute x2, starting transfers between devices, local(): lax.ppermute(weight, 'lon', [(i, i ^ bit) for i in range(strips)])  1.74 us
    pallas_call x2, Pallas kernels, bulk_of(): pl.pallas_call(functools.partial(observed_bulk, sizes, parity), out_shape...  1.66 us
    pallas_call x1, Pallas kernels, local(): pl.pallas_call(functools.partial(assemble, sizes), out_shape=shape(*whole...  1.58 us
  transfers between devices with their start and end apart: 7, of which 3 were waited for; matrix products, arithmetic and copies ran while one was open for 0% of the time, Pallas kernels for 18%

profile of v11, /device:TPU:0, one launch (start us, length us, event | category | flops | bytes accessed | tf_op | source)
XLA Modules:
  0.0 25.6 jit_solution(10579461612676653978)
XLA Ops:
  0.6 1.8 %shard_map.104 = (f32[88,256]{1,0:T(8,128)S(1)}, f32[88,256]{1,0:T(8,128)S(1)}, f32[8,4,32,256]{3,2,1,0:T(8,128)S(1)}, bf16[2,8,4,32,256]{4,3,2,1,0:T(8,128)(2,1...) custom-call(f32[8,4,32,256]{3,2,1,0:T(8,128)} %state_hbm.1, ...), custom_call_target="tpu_custom_call" | custom-call | flops 1000000 | bytes 2000000 | tf_op jit(solution)/shard_map/pallas_call | solution.py:444
  2.4 3.0 %collective-permute-start = (f32[88,256]{1,0:T(8,128)S(1)}, f32[88,256]{1,0:T(8,128)S(1)}, u32[]{:S(2)}, u32[]{:S(2)}) collective-permute-start(f32[88,256]{1,0:T(8,128)S(1)} %get-tuple-element.40.own_east), channel_id=1, source_target_pairs={{0,2},{2,4},{4,6},{6,8},{8,10},{10,12},{12,14},{14,0},{1,3},{3,5},... | collective-permute-start | bytes 270344 | tf_op jit(solution)/shard_map/ppermute | solution.py:458
  5.4 3.1 %collective-permute-start.1 = (f32[88,256]{1,0:T(8,128)S(1)}, f32[88,256]{1,0:T(8,128)S(1)}, u32[]{:S(2)}, u32[]{:S(2)}) collective-permute-start(f32[88,256]{1,0:T(8,128)S(1)} %get-tuple-element.41.own_west), channel_id=1, source_target_pairs={{0,14},{2,0},{4,2},{6,4},{8,6},{10,8},{12,10},{14,12},{1,15},{3,1}... | collective-permute-start | bytes 270344 | tf_op jit(solution)/shard_map/ppermute | solution.py:459
  8.5 1.3 %collective-permute-start.2 = (f32[1,128]{1,0:T(1,128)S(1)}, f32[1,128]{1,0:T(1,128)S(1)}, u32[]{:S(2)}, u32[]{:S(2)}) collective-permute-start(f32[1,128]{1,0:T(1,128)S(1)} %get-tuple-element.46.odd_weight), channel_id=1, source_target_pairs={{2,0},{6,4},{10,8},{14,12},{3,1},{7,5},{11,9},{15,13},{18,16},{22,... | collective-permute-start | bytes 1544 | tf_op jit(solution)/shard_map/ppermute | solution.py:474
  9.8 1.7 %shard_map.105 = (f32[8,4,32,256]{3,2,1,0:T(8,128)S(1)}, f32[8,32,256]{2,1,0:T(8,128)S(1)}, f32[1,128]{1,0:T(1,128)S(1)}, f32[4,5,32,256]{3,2,1,0:T(8,128)S(1)}) custom-call(f32[8,4,32,256]{3,2,1,0:T(8,128)S(1)} %get-tuple-element.29.state, bf16[2,8,4,32,256]{4,3,2,1,0:T(8,128)(2,1)S(1)} %get-tuple-element.30.noise, ...), custom_call_target="tpu_custom_call" | custom-call | tf_op jit(solution)/shard_map/pallas_call | solution.py:462
  11.5 1.1 %shard_map.107.current = f32[8,4,32,256]{3,2,1,0:T(8,128)S(1)} custom-call(f32[8,4,32,256]{3,2,1,0:T(8,128)S(1)} %get-tuple-element.34.even_middle, f32[8,32,256]{2,1,0:T(8,128)S(1)} %get-tuple-element.35.even_observed, f32[4,5,32,256]{3,2,1,0:T(8,128)S(1)} %get-tuple-element.36.even_coefs, f32[8,4,32,256]{3,2,1,0:T(8,128)S(1)} %get-tuple-element.37.odd_middle, ...), custom_call_target="tpu_custom_call" | custom-call | tf_op jit(solution)/shard_map/pallas_call | solution.py:477
  12.6 0.0 collective-permute-done.from_west
  12.6 0.0 collective-permute-done.1.from_east
  12.6 0.2 shard_map.108
  12.8 3.0 %collective-permute-start.3 = (f32[1,128]{1,0:T(1,128)S(1)}, f32[1,128]{1,0:T(1,128)S(1)}, u32[]{:S(2)}, u32[]{:S(2)}) collective-permute-start(f32[1,128]{1,0:T(1,128)S(1)} %get-tuple-element.49.even_weight), channel_id=1, source_target_pairs={{0,2},{4,6},{8,10},{12,14},{1,3},{5,7},{9,11},{13,15},{16,18},{20,... | collective-permute-start | bytes 1544 | tf_op jit(solution)/shard_map/ppermute | solution.py:496
  15.8 0.1 shard_map.109.current
  15.9 0.0 collective-permute-done.2
  15.9 1.1 %collective-permute-done.3 = f32[1,128]{1,0:T(1,128)S(1)} collective-permute-done((f32[1,128]{1,0:T(1,128)S(1)}, f32[1,128]{1,0:T(1,128)S(1)}, u32[]{:S(2)}, u32[]{:S(2)}) %collective-permute-start.3) | collective-permute-done | bytes 544 | tf_op jit(solution)/shard_map/ppermute | solution.py:496
  17.0 0.0 collective-permute-start.5
  17.0 0.0 copy-start
  17.0 0.4 %collective-permute-start.4 = (f32[1,128]{1,0:T(1,128)S(1)}, f32[1,128]{1,0:T(1,128)S(1)}, u32[]{:S(2)}, u32[]{:S(2)}) collective-permute-start(f32[1,128]{1,0:T(1,128)S(1)} %add_add_fusion), channel_id=1, source_target_pairs={{0,4},{2,6},{4,0},{6,2},{8,12},{10,14},{12,8},{14,10},{1,5},{3,7},... | collective-permute-start | bytes 1544 | tf_op jit(solution)/shard_map/ppermute | solution.py:514
  17.4 3.2 %collective-permute-done.4 = f32[1,128]{1,0:T(1,128)S(1)} collective-permute-done((f32[1,128]{1,0:T(1,128)S(1)}, f32[1,128]{1,0:T(1,128)S(1)}, u32[]{:S(2)}, u32[]{:S(2)}) %collective-permute-start.4) | collective-permute-done | bytes 544 | tf_op jit(solution)/shard_map/ppermute | solution.py:514
  20.7 0.0 collective-permute-done.5.received
  20.7 1.3 %collective-permute-start.6 = (f32[1,128]{1,0:T(1,128)S(1)}, f32[1,128]{1,0:T(1,128)S(1)}, u32[]{:S(2)}, u32[]{:S(2)}) collective-permute-start(f32[1,128]{1,0:T(1,128)S(1)} %add.14), channel_id=1, source_target_pairs={{0,8},{2,10},{4,12},{6,14},{8,0},{10,2},{12,4},{14,6},{1,9},{3,11}... | collective-permute-start | bytes 1544 | tf_op jit(solution)/shard_map/ppermute | solution.py:514
  22.0 0.0 copy-done
  22.0 1.6 %shard_map.110 = f32[8,4,32,256]{3,2,1,0:T(8,128)} custom-call(s32[16]{0:T(128)S(1)} %copy-done, f32[8,4,32,256]{3,2,1,0:T(8,128)S(1)} %shard_map.109.current, f32[8,4,32,256]{3,2,1,0:T(8,128)S(1)} %collective-permute-done.5.received), custom_call_target="tpu_custom_call" | custom-call | bytes 2000000 | tf_op jit(solution)/shard_map/pallas_call | solution.py:517
  23.6 0.0 copy-start.1
  23.6 1.5 %collective-permute-done.6 = f32[1,128]{1,0:T(1,128)S(1)} collective-permute-done((f32[1,128]{1,0:T(1,128)S(1)}, f32[1,128]{1,0:T(1,128)S(1)}, u32[]{:S(2)}, u32[]{:S(2)}) %collective-permute-start.6) | collective-permute-done | bytes 544 | tf_op jit(solution)/shard_map/ppermute | solution.py:514
  25.1 0.0 copy-done.1
  25.1 0.5 %bitcast_subtract_fusion = f32[8]{0:T(128)} fusion(f32[8]{0:T(128)S(1)} %copy-done.1, f32[1,128]{1,0:T(1,128)S(1)} %add.15), kind=kLoop, calls=%fused_computation | loop fusion | flops 16 | bytes 96 | tf_op jit(solution)/shard_map/sub | solution.py:527
  (4 shorter events, 0.0 us)
Async XLA Ops:
  2.4 10.1 %collective-permute-start = (f32[88,256]{1,0:T(8,128)S(1)}, f32[88,256]{1,0:T(8,128)S(1)}, u32[]{:S(2)}, u32[]{:S(2)}) collective-permute-start(f32[88,256]{1,0:T(8,128)S(1)} %get-tuple-element.40.own_east), channel_id=1, source_target_pairs={{0,2},{2,4},{4,6},{6,8},{8,10},{10,12},{12,14},{14,0},{1,3},{3,5},... | collective-permute-start | bytes 270344 | tf_op jit(solution)/shard_map/ppermute | solution.py:458
  5.4 7.2 %collective-permute-start.1 = (f32[88,256]{1,0:T(8,128)S(1)}, f32[88,256]{1,0:T(8,128)S(1)}, u32[]{:S(2)}, u32[]{:S(2)}) collective-permute-start(f32[88,256]{1,0:T(8,128)S(1)} %get-tuple-element.41.own_west), channel_id=1, source_target_pairs={{0,14},{2,0},{4,2},{6,4},{8,6},{10,8},{12,10},{14,12},{1,15},{3,1}... | collective-permute-start | bytes 270344 | tf_op jit(solution)/shard_map/ppermute | solution.py:459
  8.5 7.4 %collective-permute-start.2 = (f32[1,128]{1,0:T(1,128)S(1)}, f32[1,128]{1,0:T(1,128)S(1)}, u32[]{:S(2)}, u32[]{:S(2)}) collective-permute-start(f32[1,128]{1,0:T(1,128)S(1)} %get-tuple-element.46.odd_weight), channel_id=1, source_target_pairs={{2,0},{6,4},{10,8},{14,12},{3,1},{7,5},{11,9},{15,13},{18,16},{22,... | collective-permute-start | bytes 1544 | tf_op jit(solution)/shard_map/ppermute | solution.py:474
  12.8 4.2 %collective-permute-start.3 = (f32[1,128]{1,0:T(1,128)S(1)}, f32[1,128]{1,0:T(1,128)S(1)}, u32[]{:S(2)}, u32[]{:S(2)}) collective-permute-start(f32[1,128]{1,0:T(1,128)S(1)} %get-tuple-element.49.even_weight), channel_id=1, source_target_pairs={{0,2},{4,6},{8,10},{12,14},{1,3},{5,7},{9,11},{13,15},{16,18},{20,... | collective-permute-start | bytes 1544 | tf_op jit(solution)/shard_map/ppermute | solution.py:496
  17.0 3.6 %collective-permute-start.5 = (f32[8,4,32,256]{3,2,1,0:T(8,128)S(1)}, f32[8,4,32,256]{3,2,1,0:T(8,128)S(1)}, u32[]{:S(2)}, u32[]{:S(2)}) collective-permute-start(f32[8,4,32,256]{3,2,1,0:T(8,128)S(1)} %shard_map.109.current), channel_id=1, source_target_pairs={{0,1},{1,0},{2,3},{3,2},{4,5},{5,4},{6,7},{7,6},{8,9},{9,8},{10,11... | collective-permute-start | bytes 3145736 | tf_op jit(solution)/shard_map/ppermute | solution.py:509
  17.0 5.0 %copy-start = (s32[16]{0:T(128)S(1)}, s32[16]{0:T(128)}, u32[]{:S(2)}) copy-start(s32[16]{0:T(128)} %source.1) | copy-start | bytes 196
  17.0 3.6 %collective-permute-start.4 = (f32[1,128]{1,0:T(1,128)S(1)}, f32[1,128]{1,0:T(1,128)S(1)}, u32[]{:S(2)}, u32[]{:S(2)}) collective-permute-start(f32[1,128]{1,0:T(1,128)S(1)} %add_add_fusion), channel_id=1, source_target_pairs={{0,4},{2,6},{4,0},{6,2},{8,12},{10,14},{12,8},{14,10},{1,5},{3,7},... | collective-permute-start | bytes 1544 | tf_op jit(solution)/shard_map/ppermute | solution.py:514
  20.7 4.4 %collective-permute-start.6 = (f32[1,128]{1,0:T(1,128)S(1)}, f32[1,128]{1,0:T(1,128)S(1)}, u32[]{:S(2)}, u32[]{:S(2)}) collective-permute-start(f32[1,128]{1,0:T(1,128)S(1)} %add.14), channel_id=1, source_target_pairs={{0,8},{2,10},{4,12},{6,14},{8,0},{10,2},{12,4},{14,6},{1,9},{3,11}... | collective-permute-start | bytes 1544 | tf_op jit(solution)/shard_map/ppermute | solution.py:514
  23.6 1.5 %copy-start.1 = (f32[8]{0:T(128)S(1)}, f32[8]{0:T(128)}, u32[]{:S(2)}) copy-start(f32[8]{0:T(128)} %param.14) | copy-start | bytes 100

commit v12 on v10

--- a/solution.py
+++ b/solution.py
@@ -434,7 +434,6 @@
     eastward = [(i, (i + 1) % strips) for i in range(strips)]
     westward = [(i, (i - 1) % strips) for i in range(strips)]
     from_west = lax.ppermute(send_east, "lon", eastward)
-    from_east = lax.ppermute(send_west, "lon", westward)
 
     middle, observed, bulk_weight, coefs = pl.pallas_call(
         functools.partial(observed_bulk, sizes),
@@ -445,6 +444,8 @@
         compiler_params=LIMIT,
         cost_estimate=pl.CostEstimate(flops=20000000, bytes_accessed=4000000, transcendentals=0),
     )(state, noise, maps, courant, scalars)
+    send_west, bulk_weight = lax.optimization_barrier((send_west, bulk_weight))
+    from_east = lax.ppermute(send_west, "lon", westward)
     beside = lax.ppermute(bulk_weight, "lon", [(i, i ^ 1) for i in range(strips)])
 
     weight, changes = pl.pallas_call(
@@ -456,13 +457,14 @@
         cost_estimate=FREE,
     )(send_east, send_west, from_west, from_east, scalars, bulk_weight)
 
+    middle, from_west = lax.optimization_barrier((middle, from_west))
     current = pl.pallas_call(
         functools.partial(other_bulk, sizes),
         out_shape=shape(*whole),
         in_specs=[VMEM] * 5,
         out_specs=VMEM,
         compiler_params=LIMIT,
-        cost_estimate=FREE,
+        cost_estimate=pl.CostEstimate(flops=10000000, bytes_accessed=4000000, transcendentals=0),
     )(middle, observed, noise, scalars, coefs)
 
     current = pl.pallas_call(

time: 22.5 us -> 22.4 us (level)
    ppermute x1, waiting for transfers between devices: 1.5 us -> 0.31 us  [local(): lax.ppermute(bulk_weight, 'lon', [(i, i ^ 1) for i in range(strips)])]
    ppermute x1, waiting for transfers between devices: 0.01 us -> 1.05 us  [local(): from_west = lax.ppermute(send_east, 'lon', eastward)]
  transfers between devices with their start and end apart: 6 -> 6, of which waited for: 4 -> 5; matrix products, arithmetic and copies ran while one was open for 0% -> 0% of each run, Pallas kernels for 21% -> 21%
where the time goes in v12:
time: 22.4 us; the launch traced here: 22.3 us
  waiting for transfers between devices  7.48 us (33%)
  starting transfers between devices  7.1 us (32%)
  Pallas kernels  6.48 us (29%)
  between operations  0.69 us (3%)
  other arithmetic  0.52 us (2%)
    ppermute x2, waiting for transfers between devices, local(): lax.ppermute(weight, 'lon', [(i, i ^ bit) for i in range(strips)])  5.39 us
    ppermute x1, starting transfers between devices, local(): from_east = lax.ppermute(send_west, 'lon', westward)  3.06 us
    ppermute x1, starting transfers between devices, local(): from_west = lax.ppermute(send_east, 'lon', eastward)  2.99 us
    pallas_call x1, Pallas kernels, local(): pl.pallas_call(functools.partial(prepare, sizes), out_shape=(packet, pack...  1.81 us
    pallas_call x1, Pallas kernels, local(): pl.pallas_call(functools.partial(observed_bulk, sizes), out_shape=(shape(...  1.65 us
    pallas_call x1, Pallas kernels, local(): pl.pallas_call(functools.partial(assemble, sizes), out_shape=shape(*whole...  1.58 us
    pallas_call x1, Pallas kernels, local(): pl.pallas_call(functools.partial(other_bulk, sizes), out_shape=shape(*who...  1.09 us
    ppermute x1, waiting for transfers between devices, local(): from_west = lax.ppermute(send_east, 'lon', eastward)  1.05 us
  transfers between devices with their start and end apart: 6, of which 5 were waited for; matrix products, arithmetic and copies ran while one was open for 0% of the time, Pallas kernels for 21%

profile of v12, /device:TPU:0, one launch (start us, length us, event | category | flops | bytes accessed | tf_op | source)
XLA Modules:
  0.0 22.3 jit_solution(6533967866433234442)
XLA Ops:
  0.6 1.8 %shard_map.104 = (f32[88,256]{1,0:T(8,128)S(1)}, f32[88,256]{1,0:T(8,128)S(1)}, f32[8,4,32,256]{3,2,1,0:T(8,128)S(1)}, bf16[2,8,4,32,256]{4,3,2,1,0:T(8,128)(2,1...) custom-call(f32[8,4,32,256]{3,2,1,0:T(8,128)} %state_hbm.1, ...), custom_call_target="tpu_custom_call" | custom-call | flops 1000000 | bytes 2000000 | tf_op jit(solution)/shard_map/pallas_call | solution.py:422
  2.4 3.0 %collective-permute-start = (f32[88,256]{1,0:T(8,128)S(1)}, f32[88,256]{1,0:T(8,128)S(1)}, u32[]{:S(2)}, u32[]{:S(2)}) collective-permute-start(f32[88,256]{1,0:T(8,128)S(1)} %get-tuple-element.28.own_east), channel_id=1, source_target_pairs={{0,2},{2,4},{4,6},{6,8},{8,10},{10,12},{12,14},{14,0},{1,3},{3,5},... | collective-permute-start | bytes 270344 | tf_op jit(solution)/shard_map/ppermute | solution.py:436
  5.4 1.7 %shard_map.105 = (f32[8,4,32,256]{3,2,1,0:T(8,128)S(1)}, f32[8,32,256]{2,1,0:T(8,128)S(1)}, f32[1,128]{1,0:T(1,128)S(1)}, f32[4,5,32,256]{3,2,1,0:T(8,128)S(1)}) custom-call(f32[8,4,32,256]{3,2,1,0:T(8,128)S(1)} %get-tuple-element.22.state, bf16[2,8,4,32,256]{4,3,2,1,0:T(8,128)(2,1)S(1)} %get-tuple-element.23.noise, ...), custom_call_target="tpu_custom_call" | custom-call | flops 20000000 | bytes 4000000 | tf_op jit(solution)/shard_map/pallas_call | solution.py:438
  7.1 3.1 %collective-permute-start.1 = (f32[88,256]{1,0:T(8,128)S(1)}, f32[88,256]{1,0:T(8,128)S(1)}, u32[]{:S(2)}, u32[]{:S(2)}) collective-permute-start(f32[88,256]{1,0:T(8,128)S(1)} %get-tuple-element.34.own_west), channel_id=1, source_target_pairs={{0,14},{2,0},{4,2},{6,4},{8,6},{10,8},{12,10},{14,12},{1,15},{3,1}... | collective-permute-start | bytes 270344 | tf_op jit(solution)/shard_map/ppermute | solution.py:448
  10.2 0.0 collective-permute-start.2
  10.2 1.0 %collective-permute-done.from_west = f32[88,256]{1,0:T(8,128)S(1)} collective-permute-done((f32[88,256]{1,0:T(8,128)S(1)}, f32[88,256]{1,0:T(8,128)S(1)}, u32[]{:S(2)}, u32[]{:S(2)}) %collective-permute-start) | collective-permute-done | bytes 90144 | tf_op jit(solution)/shard_map/ppermute | solution.py:436
  11.2 1.1 %shard_map.106.current = f32[8,4,32,256]{3,2,1,0:T(8,128)S(1)} custom-call(f32[8,4,32,256]{3,2,1,0:T(8,128)S(1)} %get-tuple-element.29.middle, f32[8,32,256]{2,1,0:T(8,128)S(1)} %get-tuple-element.30.observed, bf16[2,8,4,32,256]{4,3,2,1,0:T(8,128)(2,1)S(1)} %get-tuple-element.23.noise, f32[24,256]{1,0:T(8,128)S(1)} %get-tuple-element.26.scalars, ...), custom_call_target="tpu_custom_call" | custom-call | flops 10000000 | bytes 4000000 | tf_op jit(solution)/shard_map/pallas_call | solution.py:461
  12.3 0.7 %collective-permute-done.1.from_east = f32[88,256]{1,0:T(8,128)S(1)} collective-permute-done((f32[88,256]{1,0:T(8,128)S(1)}, f32[88,256]{1,0:T(8,128)S(1)}, u32[]{:S(2)}, u32[]{:S(2)}) %collective-permute-start.1) | collective-permute-done | bytes 90144 | tf_op jit(solution)/shard_map/ppermute | solution.py:448
  13.0 0.2 shard_map.107
  13.2 0.1 shard_map.108.current
  13.4 0.3 %collective-permute-done.2 = f32[1,128]{1,0:T(1,128)S(1)} collective-permute-done((f32[1,128]{1,0:T(1,128)S(1)}, f32[1,128]{1,0:T(1,128)S(1)}, u32[]{:S(2)}, u32[]{:S(2)}) %collective-permute-start.2) | collective-permute-done | bytes 544 | tf_op jit(solution)/shard_map/ppermute | solution.py:449
  13.7 0.0 collective-permute-start.4
  13.7 0.0 copy-start
  13.7 0.1 collective-permute-start.3
  13.8 3.5 %collective-permute-done.3 = f32[1,128]{1,0:T(1,128)S(1)} collective-permute-done((f32[1,128]{1,0:T(1,128)S(1)}, f32[1,128]{1,0:T(1,128)S(1)}, u32[]{:S(2)}, u32[]{:S(2)}) %collective-permute-start.3) | collective-permute-done | bytes 544 | tf_op jit(solution)/shard_map/ppermute | solution.py:486
  17.3 0.0 collective-permute-done.4.received
  17.3 1.0 %collective-permute-start.5 = (f32[1,128]{1,0:T(1,128)S(1)}, f32[1,128]{1,0:T(1,128)S(1)}, u32[]{:S(2)}, u32[]{:S(2)}) collective-permute-start(f32[1,128]{1,0:T(1,128)S(1)} %add.10), channel_id=1, source_target_pairs={{0,8},{2,10},{4,12},{6,14},{8,0},{10,2},{12,4},{14,6},{1,9},{3,11}... | collective-permute-start | bytes 1544 | tf_op jit(solution)/shard_map/ppermute | solution.py:486
  18.3 0.0 copy-done
  18.3 1.6 %shard_map.109 = f32[8,4,32,256]{3,2,1,0:T(8,128)} custom-call(s32[16]{0:T(128)S(1)} %copy-done, f32[8,4,32,256]{3,2,1,0:T(8,128)S(1)} %shard_map.108.current, f32[8,4,32,256]{3,2,1,0:T(8,128)S(1)} %collective-permute-done.4.received), custom_call_target="tpu_custom_call" | custom-call | bytes 2000000 | tf_op jit(solution)/shard_map/pallas_call | solution.py:489
  19.9 0.0 copy-start.1
  19.9 1.9 %collective-permute-done.5 = f32[1,128]{1,0:T(1,128)S(1)} collective-permute-done((f32[1,128]{1,0:T(1,128)S(1)}, f32[1,128]{1,0:T(1,128)S(1)}, u32[]{:S(2)}, u32[]{:S(2)}) %collective-permute-start.5) | collective-permute-done | bytes 544 | tf_op jit(solution)/shard_map/ppermute | solution.py:486
  21.8 0.0 copy-done.1
  21.8 0.5 %bitcast_subtract_fusion = f32[8]{0:T(128)} fusion(f32[8]{0:T(128)S(1)} %copy-done.1, f32[1,128]{1,0:T(1,128)S(1)} %add.11), kind=kLoop, calls=%fused_computation | loop fusion | flops 16 | bytes 96 | tf_op jit(solution)/shard_map/sub | solution.py:499
  (3 shorter events, 0.0 us)
Async XLA Ops:
  2.4 8.8 %collective-permute-start = (f32[88,256]{1,0:T(8,128)S(1)}, f32[88,256]{1,0:T(8,128)S(1)}, u32[]{:S(2)}, u32[]{:S(2)}) collective-permute-start(f32[88,256]{1,0:T(8,128)S(1)} %get-tuple-element.28.own_east), channel_id=1, source_target_pairs={{0,2},{2,4},{4,6},{6,8},{8,10},{10,12},{12,14},{14,0},{1,3},{3,5},... | collective-permute-start | bytes 270344 | tf_op jit(solution)/shard_map/ppermute | solution.py:436
  7.1 5.9 %collective-permute-start.1 = (f32[88,256]{1,0:T(8,128)S(1)}, f32[88,256]{1,0:T(8,128)S(1)}, u32[]{:S(2)}, u32[]{:S(2)}) collective-permute-start(f32[88,256]{1,0:T(8,128)S(1)} %get-tuple-element.34.own_west), channel_id=1, source_target_pairs={{0,14},{2,0},{4,2},{6,4},{8,6},{10,8},{12,10},{14,12},{1,15},{3,1}... | collective-permute-start | bytes 270344 | tf_op jit(solution)/shard_map/ppermute | solution.py:448
  10.2 3.5 %collective-permute-start.2 = (f32[1,128]{1,0:T(1,128)S(1)}, f32[1,128]{1,0:T(1,128)S(1)}, u32[]{:S(2)}, u32[]{:S(2)}) collective-permute-start(f32[1,128]{1,0:T(1,128)S(1)} %get-tuple-element.35.bulk_weight), channel_id=1, source_target_pairs={{0,2},{2,0},{4,6},{6,4},{8,10},{10,8},{12,14},{14,12},{1,3},{3,1},... | collective-permute-start | bytes 1544 | tf_op jit(solution)/shard_map/ppermute | solution.py:449
  13.7 3.6 %collective-permute-start.4 = (f32[8,4,32,256]{3,2,1,0:T(8,128)S(1)}, f32[8,4,32,256]{3,2,1,0:T(8,128)S(1)}, u32[]{:S(2)}, u32[]{:S(2)}) collective-permute-start(f32[8,4,32,256]{3,2,1,0:T(8,128)S(1)} %shard_map.108.current), channel_id=1, source_target_pairs={{0,1},{1,0},{2,3},{3,2},{4,5},{5,4},{6,7},{7,6},{8,9},{9,8},{10,11... | collective-permute-start | bytes 3145736 | tf_op jit(solution)/shard_map/ppermute | solution.py:481
  13.7 4.6 %copy-start = (s32[16]{0:T(128)S(1)}, s32[16]{0:T(128)}, u32[]{:S(2)}) copy-start(s32[16]{0:T(128)} %source.1) | copy-start | bytes 196
  13.7 3.6 %collective-permute-start.3 = (f32[1,128]{1,0:T(1,128)S(1)}, f32[1,128]{1,0:T(1,128)S(1)}, u32[]{:S(2)}, u32[]{:S(2)}) collective-permute-start(f32[1,128]{1,0:T(1,128)S(1)} %add.9), channel_id=1, source_target_pairs={{0,4},{2,6},{4,0},{6,2},{8,12},{10,14},{12,8},{14,10},{1,5},{3,7},... | collective-permute-start | bytes 1544 | tf_op jit(solution)/shard_map/ppermute | solution.py:486
  17.3 4.4 %collective-permute-start.5 = (f32[1,128]{1,0:T(1,128)S(1)}, f32[1,128]{1,0:T(1,128)S(1)}, u32[]{:S(2)}, u32[]{:S(2)}) collective-permute-start(f32[1,128]{1,0:T(1,128)S(1)} %add.10), channel_id=1, source_target_pairs={{0,8},{2,10},{4,12},{6,14},{8,0},{10,2},{12,4},{14,6},{1,9},{3,11}... | collective-permute-start | bytes 1544 | tf_op jit(solution)/shard_map/ppermute | solution.py:486
  19.9 1.9 %copy-start.1 = (f32[8]{0:T(128)S(1)}, f32[8]{0:T(128)}, u32[]{:S(2)}) copy-start(f32[8]{0:T(128)} %param.14) | copy-start | bytes 100

commit v13 on v11

--- a/solution.py
+++ b/solution.py
@@ -266,7 +266,7 @@
     return moved
 
 
-def observed_bulk(sizes, parity, state, noise, maps, courant, scalars, middle, out, weight, coefs, partial):
+def observed_bulk(sizes, parity, state, noise, maps, courant, scalars, earlier, middle, out, weight, coefs, partial):
     particles, fields, strip, lats, strips = sizes
 
     def one(p):
@@ -306,7 +306,7 @@
 
     @pl.when(jnp.logical_not(here))
     def _():
-        weight[...] = jnp.zeros_like(weight)
+        weight[...] = earlier[:1, :128]
 
 
 def other_bulk(sizes, even_middle, even_observed, even_coefs, odd_middle, odd_observed, odd_coefs,
@@ -336,8 +336,7 @@
         run(odd_middle, odd_observed, odd_coefs)
 
 
-def correct(sizes, own_east, own_west, from_west, from_east, scalars, even_weight, odd_weight,
-            weight, changes):
+def correct(sizes, own_east, own_west, from_west, from_east, scalars, bulk_weight, weight, changes):
     particles, fields, strip, lats, strips = sizes
     n = fields * particles
     diffusion, mixing = scalars_in(scalars, fields)
@@ -385,7 +384,7 @@
                 edge, inner = (3, 2) if k == 0 else (0, 1)
                 changes[edge, f * particles:(f + 1) * particles] = step
                 changes[inner, f * particles:(f + 1) * particles] = beside
-    weight[...] = in_row(wide(total)) + (even_weight[...] + odd_weight[...])
+    weight[...] = in_row(wide(total)) + bulk_weight[...]
 
 
 def apply_changes(sizes, current, changes, out):
@@ -453,26 +452,25 @@
         cost_estimate=pl.CostEstimate(flops=1000000, bytes_accessed=2000000, transcendentals=0),
     )(*[in_hbm(array) for array in arrays])
 
+    def bulk_of(parity, earlier):
+        return pl.pallas_call(
+            functools.partial(observed_bulk, sizes, parity),
+            out_shape=(shape(*whole), shape(particles, strip, lats), shape(1, 128), shape(fields, 5, strip, lats)),
+            in_specs=[VMEM] * 6,
+            out_specs=(VMEM,) * 4,
+            scratch_shapes=[pltpu.VMEM((particles, 128), F32)],
+            compiler_params=LIMIT,
+            cost_estimate=pl.CostEstimate(flops=20000000, bytes_accessed=4000000, transcendentals=0),
+        )(state, noise, maps, courant, scalars, earlier)
+
+    even_middle, even_observed, bulk_weight, even_coefs = bulk_of(0, scalars)
+    send_east, send_west, bulk_weight = lax.optimization_barrier((send_east, send_west, bulk_weight))
     eastward = [(i, (i + 1) % strips) for i in range(strips)]
     westward = [(i, (i - 1) % strips) for i in range(strips)]
     from_west = lax.ppermute(send_east, "lon", eastward)
     from_east = lax.ppermute(send_west, "lon", westward)
-
-    def bulk_of(parity, cost):
-        return pl.pallas_call(
-            functools.partial(observed_bulk, sizes, parity),
-            out_shape=(shape(*whole), shape(particles, strip, lats), shape(1, 128), shape(fields, 5, strip, lats)),
-            in_specs=[VMEM] * 5,
-            out_specs=(VMEM,) * 4,
-            scratch_shapes=[pltpu.VMEM((particles, 128), F32)],
-            compiler_params=LIMIT,
-            cost_estimate=cost,
-        )(state, noise, maps, courant, scalars)
-
-    odd_middle, odd_observed, odd_weight, odd_coefs = bulk_of(
-        1, pl.CostEstimate(flops=20000000, bytes_accessed=4000000, transcendentals=0))
-    to_even = lax.ppermute(odd_weight, "lon", [(i + 1, i) for i in range(0, strips, 2)])
-    even_middle, even_observed, even_weight, even_coefs = bulk_of(0, FREE)
+    odd_middle, odd_observed, bulk_weight, odd_coefs = bulk_of(1, bulk_weight)
+    beside = lax.ppermute(bulk_weight, "lon", [(i, i ^ 1) for i in range(strips)])
 
     current = pl.pallas_call(
         functools.partial(other_bulk, sizes),
@@ -483,17 +481,14 @@
         cost_estimate=FREE,
     )(even_middle, even_observed, even_coefs, odd_middle, odd_observed, odd_coefs, noise, scalars)
 
-    current, from_west, from_east = lax.optimization_barrier((current, from_west, from_east))
     weight, changes = pl.pallas_call(
         functools.partial(correct, sizes),
         out_shape=(shape(1, 128), shape(4, particles * fields, lats)),
-        in_specs=[VMEM] * 7,
+        in_specs=[VMEM] * 6,
         out_specs=(VMEM,) * 2,
         compiler_params=LIMIT,
         cost_estimate=FREE,
-    )(send_east, send_west, from_west, from_east, scalars, even_weight, odd_weight)
-    even_weight, changes = lax.optimization_barrier((even_weight, changes))
-    to_odd = lax.ppermute(even_weight, "lon", [(i, i + 1) for i in range(0, strips, 2)])
+    )(send_east, send_west, from_west, from_east, scalars, bulk_weight)
 
     current = pl.pallas_call(
         functools.partial(apply_changes, sizes),
@@ -504,8 +499,8 @@
         cost_estimate=FREE,
     )(current, changes)
 
-    current, to_even, to_odd = lax.optimization_barrier((current, to_even, to_odd))
-    weight = weight + (to_even + to_odd)
+    current, beside = lax.optimization_barrier((current, beside))
+    weight = weight + beside
     received = lax.ppermute(current, "dom", [(0, 1), (1, 0)])
     bit = 2
     while bit < strips:

time: 25.8 us -> 22.4 us (0.87)
  starting transfers between devices: 12.1 us -> 10.2 us
  waiting for transfers between devices: 5.83 us -> 3.96 us
  local copies, waits for them, and re-layouts: 0.01 us -> 0.29 us
    ppermute x2 -> x1, starting transfers between devices: 4.23 us -> 1.41 us  [local(): lax.ppermute(bulk_weight, 'lon', [(i, i ^ 1) for i in range(strips)])]
    ppermute x2, starting transfers between devices: 1.74 us -> 4 us  [local(): lax.ppermute(weight, 'lon', [(i, i ^ bit) for i in range(strips)])]
    ppermute x2, waiting for transfers between devices: 4.7 us -> 2.44 us  [local(): lax.ppermute(weight, 'lon', [(i, i ^ bit) for i in range(strips)])]
    ppermute x1, starting transfers between devices: 2.99 us -> 1.36 us  [local(): from_west = lax.ppermute(send_east, 'lon', eastward)]
    ppermute x2 -> x1, waiting for transfers between devices: 1.12 us -> 0.01 us  [local(): lax.ppermute(bulk_weight, 'lon', [(i, i ^ 1) for i in range(strips)])]
    ppermute x1, waiting for transfers between devices: 0.01 us -> 0.98 us  [local(): from_east = lax.ppermute(send_west, 'lon', westward)]
    ppermute x1, waiting for transfers between devices: 0.01 us -> 0.54 us  [local(): from_west = lax.ppermute(send_east, 'lon', eastward)]
    unnamed x4, local copies, waits for them, and re-layouts: 0.01 us -> 0.29 us
  transfers between devices with their start and end apart: 7 -> 6, of which waited for: 3 -> 4; matrix products, arithmetic and copies ran while one was open for 0% -> 0% of each run, Pallas kernels for 18% -> 14%
where the time goes in v13:
time: 22.4 us; the launch traced here: 22.2 us
  starting transfers between devices  10.2 us (46%)
  Pallas kernels  6.49 us (29%)
  waiting for transfers between devices  3.96 us (18%)
  between operations  0.71 us (3%)
  other arithmetic  0.52 us (2%)
  local copies, waits for them, and re-layouts  0.29 us (1%)
    ppermute x2, starting transfers between devices, local(): lax.ppermute(weight, 'lon', [(i, i ^ bit) for i in range(strips)])  4 us
    ppermute x1, starting transfers between devices, local(): from_east = lax.ppermute(send_west, 'lon', westward)  3.36 us
    ppermute x2, waiting for transfers between devices, local(): lax.ppermute(weight, 'lon', [(i, i ^ bit) for i in range(strips)])  2.44 us
    pallas_call x1, Pallas kernels, local(): pl.pallas_call(functools.partial(prepare, sizes), out_shape=(packet, pack...  1.81 us
    pallas_call x2, Pallas kernels, bulk_of(): pl.pallas_call(functools.partial(observed_bulk, sizes, parity), out_shape...  1.66 us
    pallas_call x1, Pallas kernels, local(): pl.pallas_call(functools.partial(assemble, sizes), out_shape=shape(*whole...  1.58 us
    ppermute x1, starting transfers between devices, local(): lax.ppermute(bulk_weight, 'lon', [(i, i ^ 1) for i in range(strips)])  1.41 us
    ppermute x1, starting transfers between devices, local(): from_west = lax.ppermute(send_east, 'lon', eastward)  1.36 us
  transfers between devices with their start and end apart: 6, of which 4 were waited for; matrix products, arithmetic and copies ran while one was open for 0% of the time, Pallas kernels for 14%

profile of v13, /device:TPU:0, one launch (start us, length us, event | category | flops | bytes accessed | tf_op | source)
XLA Modules:
  0.0 22.2 jit_solution(6256799074213779661)
XLA Ops:
  0.6 1.8 %shard_map.104 = (f32[88,256]{1,0:T(8,128)S(1)}, f32[88,256]{1,0:T(8,128)S(1)}, f32[8,4,32,256]{3,2,1,0:T(8,128)S(1)}, bf16[2,8,4,32,256]{4,3,2,1,0:T(8,128)(2,1...) custom-call(f32[8,4,32,256]{3,2,1,0:T(8,128)} %state_hbm.1, ...), custom_call_target="tpu_custom_call" | custom-call | flops 1000000 | bytes 2000000 | tf_op jit(solution)/shard_map/pallas_call | solution.py:443
  2.4 1.7 %shard_map.105 = (f32[8,4,32,256]{3,2,1,0:T(8,128)S(1)}, f32[8,32,256]{2,1,0:T(8,128)S(1)}, f32[1,128]{1,0:T(1,128)S(1)}, f32[4,5,32,256]{3,2,1,0:T(8,128)S(1)}) custom-call(f32[8,4,32,256]{3,2,1,0:T(8,128)S(1)} %get-tuple-element.26.state, bf16[2,8,4,32,256]{4,3,2,1,0:T(8,128)(2,1)S(1)} %get-tuple-element.27.noise, ...), custom_call_target="tpu_custom_call" | custom-call | flops 20000000 | bytes 4000000 | tf_op jit(solution)/shard_map/pallas_call | solution.py:456
  4.1 1.4 %collective-permute-start = (f32[88,256]{1,0:T(8,128)S(1)}, f32[88,256]{1,0:T(8,128)S(1)}, u32[]{:S(2)}, u32[]{:S(2)}) collective-permute-start(f32[88,256]{1,0:T(8,128)S(1)} %get-tuple-element.41.own_east), channel_id=1, source_target_pairs={{0,2},{2,4},{4,6},{6,8},{8,10},{10,12},{12,14},{14,0},{1,3},{3,5},... | collective-permute-start | bytes 270344 | tf_op jit(solution)/shard_map/ppermute | solution.py:470
  5.5 3.4 %collective-permute-start.1 = (f32[88,256]{1,0:T(8,128)S(1)}, f32[88,256]{1,0:T(8,128)S(1)}, u32[]{:S(2)}, u32[]{:S(2)}) collective-permute-start(f32[88,256]{1,0:T(8,128)S(1)} %get-tuple-element.42.own_west), channel_id=1, source_target_pairs={{0,14},{2,0},{4,2},{6,4},{8,6},{10,8},{12,10},{14,12},{1,15},{3,1}... | collective-permute-start | bytes 270344 | tf_op jit(solution)/shard_map/ppermute | solution.py:471
  8.8 1.4 %collective-permute-start.2 = (f32[1,128]{1,0:T(1,128)S(1)}, f32[1,128]{1,0:T(1,128)S(1)}, u32[]{:S(2)}, u32[]{:S(2)}) collective-permute-start(f32[1,128]{1,0:T(1,128)S(1)} %get-tuple-element.43.bulk_weight), channel_id=1, source_target_pairs={{0,2},{2,0},{4,6},{6,4},{8,10},{10,8},{12,14},{14,12},{1,3},{3,1},... | collective-permute-start | bytes 1544 | tf_op jit(solution)/shard_map/ppermute | solution.py:473
  10.3 1.1 %shard_map.107.current = f32[8,4,32,256]{3,2,1,0:T(8,128)S(1)} custom-call(f32[8,4,32,256]{3,2,1,0:T(8,128)S(1)} %get-tuple-element.31.even_middle, f32[8,32,256]{2,1,0:T(8,128)S(1)} %get-tuple-element.32.even_observed, f32[4,5,32,256]{3,2,1,0:T(8,128)S(1)} %get-tuple-element.33.even_coefs, f32[8,4,32,256]{3,2,1,0:T(8,128)S(1)} %get-tuple-element.38.odd_middle, ...), custom_call_target="tpu_custom_call" | custom-call | tf_op jit(solution)/shard_map/pallas_call | solution.py:475
  11.4 0.5 %collective-permute-done.from_west = f32[88,256]{1,0:T(8,128)S(1)} collective-permute-done((f32[88,256]{1,0:T(8,128)S(1)}, f32[88,256]{1,0:T(8,128)S(1)}, u32[]{:S(2)}, u32[]{:S(2)}) %collective-permute-start) | collective-permute-done | bytes 90144 | tf_op jit(solution)/shard_map/ppermute | solution.py:470
  11.9 1.0 %collective-permute-done.1.from_east = f32[88,256]{1,0:T(8,128)S(1)} collective-permute-done((f32[88,256]{1,0:T(8,128)S(1)}, f32[88,256]{1,0:T(8,128)S(1)}, u32[]{:S(2)}, u32[]{:S(2)}) %collective-permute-start.1) | collective-permute-done | bytes 90144 | tf_op jit(solution)/shard_map/ppermute | solution.py:471
  12.9 0.2 shard_map.108
  13.1 0.2 shard_map.109.current
  13.2 0.0 collective-permute-done.2
  13.2 0.1 collective-permute-start.4
  13.3 0.0 copy-start
  13.3 1.5 %collective-permute-start.3 = (f32[1,128]{1,0:T(1,128)S(1)}, f32[1,128]{1,0:T(1,128)S(1)}, u32[]{:S(2)}, u32[]{:S(2)}) collective-permute-start(f32[1,128]{1,0:T(1,128)S(1)} %add.9), channel_id=1, source_target_pairs={{0,4},{2,6},{4,0},{6,2},{8,12},{10,14},{12,8},{14,10},{1,5},{3,7},... | collective-permute-start | bytes 1544 | tf_op jit(solution)/shard_map/ppermute | solution.py:509
  14.9 2.1 %collective-permute-done.3 = f32[1,128]{1,0:T(1,128)S(1)} collective-permute-done((f32[1,128]{1,0:T(1,128)S(1)}, f32[1,128]{1,0:T(1,128)S(1)}, u32[]{:S(2)}, u32[]{:S(2)}) %collective-permute-start.3) | collective-permute-done | bytes 544 | tf_op jit(solution)/shard_map/ppermute | solution.py:509
  16.9 0.0 collective-permute-done.4.received
  17.0 2.5 %collective-permute-start.5 = (f32[1,128]{1,0:T(1,128)S(1)}, f32[1,128]{1,0:T(1,128)S(1)}, u32[]{:S(2)}, u32[]{:S(2)}) collective-permute-start(f32[1,128]{1,0:T(1,128)S(1)} %add.10), channel_id=1, source_target_pairs={{0,8},{2,10},{4,12},{6,14},{8,0},{10,2},{12,4},{14,6},{1,9},{3,11}... | collective-permute-start | bytes 1544 | tf_op jit(solution)/shard_map/ppermute | solution.py:509
  19.4 0.0 copy-done
  19.4 1.6 %shard_map.110 = f32[8,4,32,256]{3,2,1,0:T(8,128)} custom-call(s32[16]{0:T(128)S(1)} %copy-done, f32[8,4,32,256]{3,2,1,0:T(8,128)S(1)} %shard_map.109.current, f32[8,4,32,256]{3,2,1,0:T(8,128)S(1)} %collective-permute-done.4.received), custom_call_target="tpu_custom_call" | custom-call | bytes 2000000 | tf_op jit(solution)/shard_map/pallas_call | solution.py:512
  21.0 0.0 copy-start.1
  21.0 0.4 %collective-permute-done.5 = f32[1,128]{1,0:T(1,128)S(1)} collective-permute-done((f32[1,128]{1,0:T(1,128)S(1)}, f32[1,128]{1,0:T(1,128)S(1)}, u32[]{:S(2)}, u32[]{:S(2)}) %collective-permute-start.5) | collective-permute-done | bytes 544 | tf_op jit(solution)/shard_map/ppermute | solution.py:509
  21.4 0.3 %copy-done.1 = f32[8]{0:T(128)S(1)} copy-done((f32[8]{0:T(128)S(1)}, f32[8]{0:T(128)}, u32[]{:S(2)}) %copy-start.1) | copy-done | bytes 56
  21.7 0.5 %bitcast_subtract_fusion = f32[8]{0:T(128)} fusion(f32[8]{0:T(128)S(1)} %copy-done.1, f32[1,128]{1,0:T(1,128)S(1)} %add.11), kind=kLoop, calls=%fused_computation | loop fusion | flops 16 | bytes 96 | tf_op jit(solution)/shard_map/sub | solution.py:522
  (4 shorter events, 0.0 us)
Async XLA Ops:
  4.1 7.8 %collective-permute-start = (f32[88,256]{1,0:T(8,128)S(1)}, f32[88,256]{1,0:T(8,128)S(1)}, u32[]{:S(2)}, u32[]{:S(2)}) collective-permute-start(f32[88,256]{1,0:T(8,128)S(1)} %get-tuple-element.41.own_east), channel_id=1, source_target_pairs={{0,2},{2,4},{4,6},{6,8},{8,10},{10,12},{12,14},{14,0},{1,3},{3,5},... | collective-permute-start | bytes 270344 | tf_op jit(solution)/shard_map/ppermute | solution.py:470
  5.5 7.4 %collective-permute-start.1 = (f32[88,256]{1,0:T(8,128)S(1)}, f32[88,256]{1,0:T(8,128)S(1)}, u32[]{:S(2)}, u32[]{:S(2)}) collective-permute-start(f32[88,256]{1,0:T(8,128)S(1)} %get-tuple-element.42.own_west), channel_id=1, source_target_pairs={{0,14},{2,0},{4,2},{6,4},{8,6},{10,8},{12,10},{14,12},{1,15},{3,1}... | collective-permute-start | bytes 270344 | tf_op jit(solution)/shard_map/ppermute | solution.py:471
  8.8 4.4 %collective-permute-start.2 = (f32[1,128]{1,0:T(1,128)S(1)}, f32[1,128]{1,0:T(1,128)S(1)}, u32[]{:S(2)}, u32[]{:S(2)}) collective-permute-start(f32[1,128]{1,0:T(1,128)S(1)} %get-tuple-element.43.bulk_weight), channel_id=1, source_target_pairs={{0,2},{2,0},{4,6},{6,4},{8,10},{10,8},{12,14},{14,12},{1,3},{3,1},... | collective-permute-start | bytes 1544 | tf_op jit(solution)/shard_map/ppermute | solution.py:473
  13.2 3.7 %collective-permute-start.4 = (f32[8,4,32,256]{3,2,1,0:T(8,128)S(1)}, f32[8,4,32,256]{3,2,1,0:T(8,128)S(1)}, u32[]{:S(2)}, u32[]{:S(2)}) collective-permute-start(f32[8,4,32,256]{3,2,1,0:T(8,128)S(1)} %shard_map.109.current), channel_id=1, source_target_pairs={{0,1},{1,0},{2,3},{3,2},{4,5},{5,4},{6,7},{7,6},{8,9},{9,8},{10,11... | collective-permute-start | bytes 3145736 | tf_op jit(solution)/shard_map/ppermute | solution.py:504
  13.3 6.1 %copy-start = (s32[16]{0:T(128)S(1)}, s32[16]{0:T(128)}, u32[]{:S(2)}) copy-start(s32[16]{0:T(128)} %source.1) | copy-start | bytes 196
  13.3 3.6 %collective-permute-start.3 = (f32[1,128]{1,0:T(1,128)S(1)}, f32[1,128]{1,0:T(1,128)S(1)}, u32[]{:S(2)}, u32[]{:S(2)}) collective-permute-start(f32[1,128]{1,0:T(1,128)S(1)} %add.9), channel_id=1, source_target_pairs={{0,4},{2,6},{4,0},{6,2},{8,12},{10,14},{12,8},{14,10},{1,5},{3,7},... | collective-permute-start | bytes 1544 | tf_op jit(solution)/shard_map/ppermute | solution.py:509
  17.0 4.4 %collective-permute-start.5 = (f32[1,128]{1,0:T(1,128)S(1)}, f32[1,128]{1,0:T(1,128)S(1)}, u32[]{:S(2)}, u32[]{:S(2)}) collective-permute-start(f32[1,128]{1,0:T(1,128)S(1)} %add.10), channel_id=1, source_target_pairs={{0,8},{2,10},{4,12},{6,14},{8,0},{10,2},{12,4},{14,6},{1,9},{3,11}... | collective-permute-start | bytes 1544 | tf_op jit(solution)/shard_map/ppermute | solution.py:509
  21.0 0.7 %copy-start.1 = (f32[8]{0:T(128)S(1)}, f32[8]{0:T(128)}, u32[]{:S(2)}) copy-start(f32[8]{0:T(128)} %param.14) | copy-start | bytes 100

commit v14 on v13

--- a/solution.py
+++ b/solution.py
@@ -266,7 +266,11 @@
     return moved
 
 
-def observed_bulk(sizes, parity, state, noise, maps, courant, scalars, earlier, middle, out, weight, coefs, partial):
+def goes_first():
+    return jnp.logical_or(lax.axis_index("lon") % 2 == 0, lax.axis_index("dom") == 1)
+
+
+def observed_bulk(sizes, first, state, noise, maps, courant, scalars, earlier, middle, out, weight, coefs, partial):
     particles, fields, strip, lats, strips = sizes
 
     def one(p):
@@ -296,7 +300,7 @@
         one(2 * pair + 1)
         return carry
 
-    here = lax.axis_index("lon") % 2 == parity
+    here = goes_first() == first
 
     @pl.when(here)
     def _():
@@ -309,7 +313,7 @@
         weight[...] = earlier[:1, :128]
 
 
-def other_bulk(sizes, even_middle, even_observed, even_coefs, odd_middle, odd_observed, odd_coefs,
+def other_bulk(sizes, early_middle, early_observed, early_coefs, late_middle, late_observed, late_coefs,
                noise, scalars, out):
     particles, fields, strip, lats, strips = sizes
 
@@ -325,15 +329,13 @@
 
         lax.fori_loop(0, particles, body, 0)
 
-    even = lax.axis_index("lon") % 2 == 0
-
-    @pl.when(even)
+    @pl.when(goes_first())
     def _():
-        run(even_middle, even_observed, even_coefs)
-
-    @pl.when(jnp.logical_not(even))
+        run(early_middle, early_observed, early_coefs)
+
+    @pl.when(jnp.logical_not(goes_first()))
     def _():
-        run(odd_middle, odd_observed, odd_coefs)
+        run(late_middle, late_observed, late_coefs)
 
 
 def correct(sizes, own_east, own_west, from_west, from_east, scalars, bulk_weight, weight, changes):
@@ -452,9 +454,9 @@
         cost_estimate=pl.CostEstimate(flops=1000000, bytes_accessed=2000000, transcendentals=0),
     )(*[in_hbm(array) for array in arrays])
 
-    def bulk_of(parity, earlier):
+    def bulk_of(first, earlier):
         return pl.pallas_call(
-            functools.partial(observed_bulk, sizes, parity),
+            functools.partial(observed_bulk, sizes, first),
             out_shape=(shape(*whole), shape(particles, strip, lats), shape(1, 128), shape(fields, 5, strip, lats)),
             in_specs=[VMEM] * 6,
             out_specs=(VMEM,) * 4,
@@ -463,13 +465,13 @@
             cost_estimate=pl.CostEstimate(flops=20000000, bytes_accessed=4000000, transcendentals=0),
         )(state, noise, maps, courant, scalars, earlier)
 
-    even_middle, even_observed, bulk_weight, even_coefs = bulk_of(0, scalars)
+    early_middle, early_observed, bulk_weight, early_coefs = bulk_of(True, scalars)
     send_east, send_west, bulk_weight = lax.optimization_barrier((send_east, send_west, bulk_weight))
     eastward = [(i, (i + 1) % strips) for i in range(strips)]
     westward = [(i, (i - 1) % strips) for i in range(strips)]
     from_west = lax.ppermute(send_east, "lon", eastward)
     from_east = lax.ppermute(send_west, "lon", westward)
-    odd_middle, odd_observed, bulk_weight, odd_coefs = bulk_of(1, bulk_weight)
+    late_middle, late_observed, bulk_weight, late_coefs = bulk_of(False, bulk_weight)
     beside = lax.ppermute(bulk_weight, "lon", [(i, i ^ 1) for i in range(strips)])
 
     current = pl.pallas_call(
@@ -479,7 +481,7 @@
         out_specs=VMEM,
         compiler_params=LIMIT,
         cost_estimate=FREE,
-    )(even_middle, even_observed, even_coefs, odd_middle, odd_observed, odd_coefs, noise, scalars)
+    )(early_middle, early_observed, early_coefs, late_middle, late_observed, late_coefs, noise, scalars)
 
     weight, changes = pl.pallas_call(
         functools.partial(correct, sizes),

time: 22.4 us -> 22.4 us (level)
  waiting for transfers between devices: 3.96 us -> 4.55 us
  starting transfers between devices: 10.2 us -> 9.82 us
    ppermute x2, starting transfers between devices: 4 us -> 3.61 us  [local(): lax.ppermute(weight, 'lon', [(i, i ^ bit) for i in range(strips)])]
    ppermute x2, waiting for transfers between devices: 2.44 us -> 2.83 us  [local(): lax.ppermute(weight, 'lon', [(i, i ^ bit) for i in range(strips)])]
where the time goes in v14:
time: 22.4 us; the launch traced here: 22.2 us
  starting transfers between devices  9.82 us (44%)
  Pallas kernels  6.49 us (29%)
  waiting for transfers between devices  4.55 us (20%)
  between operations  0.71 us (3%)
  other arithmetic  0.52 us (2%)
    ppermute x2, starting transfers between devices, local(): lax.ppermute(weight, 'lon', [(i, i ^ bit) for i in range(strips)])  3.61 us
    ppermute x1, starting transfers between devices, local(): from_east = lax.ppermute(send_west, 'lon', westward)  3.37 us
    ppermute x2, waiting for transfers between devices, local(): lax.ppermute(weight, 'lon', [(i, i ^ bit) for i in range(strips)])  2.83 us
    pallas_call x1, Pallas kernels, local(): pl.pallas_call(functools.partial(prepare, sizes), out_shape=(packet, pack...  1.81 us
    pallas_call x2, Pallas kernels, bulk_of(): pl.pallas_call(functools.partial(observed_bulk, sizes, first), out_shape=...  1.66 us
    pallas_call x1, Pallas kernels, local(): pl.pallas_call(functools.partial(assemble, sizes), out_shape=shape(*whole...  1.58 us
    ppermute x1, starting transfers between devices, local(): lax.ppermute(bulk_weight, 'lon', [(i, i ^ 1) for i in range(strips)])  1.41 us
    ppermute x1, starting transfers between devices, local(): from_west = lax.ppermute(send_east, 'lon', eastward)  1.36 us
  transfers between devices with their start and end apart: 6, of which 4 were waited for; matrix products, arithmetic and copies ran while one was open for 0% of the time, Pallas kernels for 14%

profile of v14, /device:TPU:0, one launch (start us, length us, event | category | flops | bytes accessed | tf_op | source)
XLA Modules:
  0.0 22.2 jit_solution(3628092782621662283)
XLA Ops:
  0.6 1.8 %shard_map.104 = (f32[88,256]{1,0:T(8,128)S(1)}, f32[88,256]{1,0:T(8,128)S(1)}, f32[8,4,32,256]{3,2,1,0:T(8,128)S(1)}, bf16[2,8,4,32,256]{4,3,2,1,0:T(8,128)(2,1...) custom-call(f32[8,4,32,256]{3,2,1,0:T(8,128)} %state_hbm.1, ...), custom_call_target="tpu_custom_call" | custom-call | flops 1000000 | bytes 2000000 | tf_op jit(solution)/shard_map/pallas_call | solution.py:445
  2.4 1.7 %shard_map.105 = (f32[8,4,32,256]{3,2,1,0:T(8,128)S(1)}, f32[8,32,256]{2,1,0:T(8,128)S(1)}, f32[1,128]{1,0:T(1,128)S(1)}, f32[4,5,32,256]{3,2,1,0:T(8,128)S(1)}) custom-call(f32[8,4,32,256]{3,2,1,0:T(8,128)S(1)} %get-tuple-element.26.state, bf16[2,8,4,32,256]{4,3,2,1,0:T(8,128)(2,1)S(1)} %get-tuple-element.27.noise, ...), custom_call_target="tpu_custom_call" | custom-call | flops 20000000 | bytes 4000000 | tf_op jit(solution)/shard_map/pallas_call | solution.py:458
  4.1 1.4 %collective-permute-start = (f32[88,256]{1,0:T(8,128)S(1)}, f32[88,256]{1,0:T(8,128)S(1)}, u32[]{:S(2)}, u32[]{:S(2)}) collective-permute-start(f32[88,256]{1,0:T(8,128)S(1)} %get-tuple-element.41.own_east), channel_id=1, source_target_pairs={{0,2},{2,4},{4,6},{6,8},{8,10},{10,12},{12,14},{14,0},{1,3},{3,5},... | collective-permute-start | bytes 270344 | tf_op jit(solution)/shard_map/ppermute | solution.py:472
  5.5 3.4 %collective-permute-start.1 = (f32[88,256]{1,0:T(8,128)S(1)}, f32[88,256]{1,0:T(8,128)S(1)}, u32[]{:S(2)}, u32[]{:S(2)}) collective-permute-start(f32[88,256]{1,0:T(8,128)S(1)} %get-tuple-element.42.own_west), channel_id=1, source_target_pairs={{0,14},{2,0},{4,2},{6,4},{8,6},{10,8},{12,10},{14,12},{1,15},{3,1}... | collective-permute-start | bytes 270344 | tf_op jit(solution)/shard_map/ppermute | solution.py:473
  8.8 1.4 %collective-permute-start.2 = (f32[1,128]{1,0:T(1,128)S(1)}, f32[1,128]{1,0:T(1,128)S(1)}, u32[]{:S(2)}, u32[]{:S(2)}) collective-permute-start(f32[1,128]{1,0:T(1,128)S(1)} %get-tuple-element.43.bulk_weight), channel_id=1, source_target_pairs={{0,2},{2,0},{4,6},{6,4},{8,10},{10,8},{12,14},{14,12},{1,3},{3,1},... | collective-permute-start | bytes 1544 | tf_op jit(solution)/shard_map/ppermute | solution.py:475
  10.3 1.1 %shard_map.107.current = f32[8,4,32,256]{3,2,1,0:T(8,128)S(1)} custom-call(f32[8,4,32,256]{3,2,1,0:T(8,128)S(1)} %get-tuple-element.31.early_middle, f32[8,32,256]{2,1,0:T(8,128)S(1)} %get-tuple-element.32.early_observed, f32[4,5,32,256]{3,2,1,0:T(8,128)S(1)} %get-tuple-element.33.early_coefs, f32[8,4,32,256]{3,2,1,0:T(8,128)S(1)} %get-tuple-element.38.late_middle, ...), custom_call_target="tpu_custom_call" | custom-call | tf_op jit(solution)/shard_map/pallas_call | solution.py:477
  11.4 0.7 %collective-permute-done.from_west = f32[88,256]{1,0:T(8,128)S(1)} collective-permute-done((f32[88,256]{1,0:T(8,128)S(1)}, f32[88,256]{1,0:T(8,128)S(1)}, u32[]{:S(2)}, u32[]{:S(2)}) %collective-permute-start) | collective-permute-done | bytes 90144 | tf_op jit(solution)/shard_map/ppermute | solution.py:472
  12.1 1.0 %collective-permute-done.1.from_east = f32[88,256]{1,0:T(8,128)S(1)} collective-permute-done((f32[88,256]{1,0:T(8,128)S(1)}, f32[88,256]{1,0:T(8,128)S(1)}, u32[]{:S(2)}, u32[]{:S(2)}) %collective-permute-start.1) | collective-permute-done | bytes 90144 | tf_op jit(solution)/shard_map/ppermute | solution.py:473
  13.1 0.2 shard_map.108
  13.3 0.2 shard_map.109.current
  13.4 0.0 collective-permute-done.2
  13.4 0.1 collective-permute-start.4
  13.5 0.0 copy-start
  13.5 1.3 %collective-permute-start.3 = (f32[1,128]{1,0:T(1,128)S(1)}, f32[1,128]{1,0:T(1,128)S(1)}, u32[]{:S(2)}, u32[]{:S(2)}) collective-permute-start(f32[1,128]{1,0:T(1,128)S(1)} %add.9), channel_id=1, source_target_pairs={{0,4},{2,6},{4,0},{6,2},{8,12},{10,14},{12,8},{14,10},{1,5},{3,7},... | collective-permute-start | bytes 1544 | tf_op jit(solution)/shard_map/ppermute | solution.py:511
  14.9 2.3 %collective-permute-done.3 = f32[1,128]{1,0:T(1,128)S(1)} collective-permute-done((f32[1,128]{1,0:T(1,128)S(1)}, f32[1,128]{1,0:T(1,128)S(1)}, u32[]{:S(2)}, u32[]{:S(2)}) %collective-permute-start.3) | collective-permute-done | bytes 544 | tf_op jit(solution)/shard_map/ppermute | solution.py:511
  17.1 0.0 collective-permute-done.4.received
  17.1 2.3 %collective-permute-start.5 = (f32[1,128]{1,0:T(1,128)S(1)}, f32[1,128]{1,0:T(1,128)S(1)}, u32[]{:S(2)}, u32[]{:S(2)}) collective-permute-start(f32[1,128]{1,0:T(1,128)S(1)} %add.10), channel_id=1, source_target_pairs={{0,8},{2,10},{4,12},{6,14},{8,0},{10,2},{12,4},{14,6},{1,9},{3,11}... | collective-permute-start | bytes 1544 | tf_op jit(solution)/shard_map/ppermute | solution.py:511
  19.4 0.0 copy-done
  19.4 1.6 %shard_map.110 = f32[8,4,32,256]{3,2,1,0:T(8,128)} custom-call(s32[16]{0:T(128)S(1)} %copy-done, f32[8,4,32,256]{3,2,1,0:T(8,128)S(1)} %shard_map.109.current, f32[8,4,32,256]{3,2,1,0:T(8,128)S(1)} %collective-permute-done.4.received), custom_call_target="tpu_custom_call" | custom-call | bytes 2000000 | tf_op jit(solution)/shard_map/pallas_call | solution.py:514
  21.0 0.0 copy-start.1
  21.0 0.6 %collective-permute-done.5 = f32[1,128]{1,0:T(1,128)S(1)} collective-permute-done((f32[1,128]{1,0:T(1,128)S(1)}, f32[1,128]{1,0:T(1,128)S(1)}, u32[]{:S(2)}, u32[]{:S(2)}) %collective-permute-start.5) | collective-permute-done | bytes 544 | tf_op jit(solution)/shard_map/ppermute | solution.py:511
  21.6 0.1 copy-done.1
  21.7 0.5 %bitcast_subtract_fusion = f32[8]{0:T(128)} fusion(f32[8]{0:T(128)S(1)} %copy-done.1, f32[1,128]{1,0:T(1,128)S(1)} %add.11), kind=kLoop, calls=%fused_computation | loop fusion | flops 16 | bytes 96 | tf_op jit(solution)/shard_map/sub | solution.py:524
  (4 shorter events, 0.0 us)
Async XLA Ops:
  4.1 8.0 %collective-permute-start = (f32[88,256]{1,0:T(8,128)S(1)}, f32[88,256]{1,0:T(8,128)S(1)}, u32[]{:S(2)}, u32[]{:S(2)}) collective-permute-start(f32[88,256]{1,0:T(8,128)S(1)} %get-tuple-element.41.own_east), channel_id=1, source_target_pairs={{0,2},{2,4},{4,6},{6,8},{8,10},{10,12},{12,14},{14,0},{1,3},{3,5},... | collective-permute-start | bytes 270344 | tf_op jit(solution)/shard_map/ppermute | solution.py:472
  5.5 7.6 %collective-permute-start.1 = (f32[88,256]{1,0:T(8,128)S(1)}, f32[88,256]{1,0:T(8,128)S(1)}, u32[]{:S(2)}, u32[]{:S(2)}) collective-permute-start(f32[88,256]{1,0:T(8,128)S(1)} %get-tuple-element.42.own_west), channel_id=1, source_target_pairs={{0,14},{2,0},{4,2},{6,4},{8,6},{10,8},{12,10},{14,12},{1,15},{3,1}... | collective-permute-start | bytes 270344 | tf_op jit(solution)/shard_map/ppermute | solution.py:473
  8.8 4.6 %collective-permute-start.2 = (f32[1,128]{1,0:T(1,128)S(1)}, f32[1,128]{1,0:T(1,128)S(1)}, u32[]{:S(2)}, u32[]{:S(2)}) collective-permute-start(f32[1,128]{1,0:T(1,128)S(1)} %get-tuple-element.43.bulk_weight), channel_id=1, source_target_pairs={{0,2},{2,0},{4,6},{6,4},{8,10},{10,8},{12,14},{14,12},{1,3},{3,1},... | collective-permute-start | bytes 1544 | tf_op jit(solution)/shard_map/ppermute | solution.py:475
  13.4 3.7 %collective-permute-start.4 = (f32[8,4,32,256]{3,2,1,0:T(8,128)S(1)}, f32[8,4,32,256]{3,2,1,0:T(8,128)S(1)}, u32[]{:S(2)}, u32[]{:S(2)}) collective-permute-start(f32[8,4,32,256]{3,2,1,0:T(8,128)S(1)} %shard_map.109.current), channel_id=1, source_target_pairs={{0,1},{1,0},{2,3},{3,2},{4,5},{5,4},{6,7},{7,6},{8,9},{9,8},{10,11... | collective-permute-start | bytes 3145736 | tf_op jit(solution)/shard_map/ppermute | solution.py:506
  13.5 5.9 %copy-start = (s32[16]{0:T(128)S(1)}, s32[16]{0:T(128)}, u32[]{:S(2)}) copy-start(s32[16]{0:T(128)} %source.1) | copy-start | bytes 196
  13.5 3.6 %collective-permute-start.3 = (f32[1,128]{1,0:T(1,128)S(1)}, f32[1,128]{1,0:T(1,128)S(1)}, u32[]{:S(2)}, u32[]{:S(2)}) collective-permute-start(f32[1,128]{1,0:T(1,128)S(1)} %add.9), channel_id=1, source_target_pairs={{0,4},{2,6},{4,0},{6,2},{8,12},{10,14},{12,8},{14,10},{1,5},{3,7},... | collective-permute-start | bytes 1544 | tf_op jit(solution)/shard_map/ppermute | solution.py:511
  17.1 4.4 %collective-permute-start.5 = (f32[1,128]{1,0:T(1,128)S(1)}, f32[1,128]{1,0:T(1,128)S(1)}, u32[]{:S(2)}, u32[]{:S(2)}) collective-permute-start(f32[1,128]{1,0:T(1,128)S(1)} %add.10), channel_id=1, source_target_pairs={{0,8},{2,10},{4,12},{6,14},{8,0},{10,2},{12,4},{14,6},{1,9},{3,11}... | collective-permute-start | bytes 1544 | tf_op jit(solution)/shard_map/ppermute | solution.py:511
  21.0 0.7 %copy-start.1 = (f32[8]{0:T(128)S(1)}, f32[8]{0:T(128)}, u32[]{:S(2)}) copy-start(f32[8]{0:T(128)} %param.14) | copy-start | bytes 100

commit v15 on v13

--- a/solution.py
+++ b/solution.py
@@ -504,10 +504,14 @@
     received = lax.ppermute(current, "dom", [(0, 1), (1, 0)])
     bit = 2
     while bit < strips:
-        if 2 * bit >= strips:
-            weight, received = lax.optimization_barrier((weight, received))
-        weight = weight + lax.ppermute(weight, "lon", [(i, i ^ bit) for i in range(strips)])
-        bit *= 2
+        steps = (3, 2, 1) if 2 * bit < strips else (1,)
+        arrived = []
+        for step in steps:
+            if step == 1 and bit * (len(steps) + 1) >= strips:
+                weight, received = lax.optimization_barrier((weight, received))
+            arrived.append(lax.ppermute(weight, "lon", [(i, i ^ (bit * step)) for i in range(strips)]))
+        weight = sum(arrived, weight)
+        bit *= len(steps) + 1
 
     new_state = pl.pallas_call(
         functools.partial(assemble, sizes),

time: 22.4 us -> 21.9 us (0.978)
  local copies, waits for them, and re-layouts: 0.29 us -> 0.01 us
  waiting for transfers between devices: 3.96 us -> 3.71 us
    unnamed x4, local copies, waits for them, and re-layouts: 0.29 us -> 0.01 us
    ppermute x2 -> x3, waiting for transfers between devices: 2.44 us -> 2.19 us  [local(): lax.ppermute(weight, 'lon', [(i, i ^ bit * step) for i in range(strips)])]
    ppermute x2 -> x3, starting transfers between devices: 4 us -> 4.08 us  [local(): lax.ppermute(weight, 'lon', [(i, i ^ bit * step) for i in range(strips)])]
  transfers between devices with their start and end apart: 6 -> 7, of which waited for: 4 -> 3; matrix products, arithmetic and copies ran while one was open for 0% -> 0% of each run, Pallas kernels for 14% -> 14%
where the time goes in v15:
time: 21.9 us; the launch traced here: 21.8 us
  starting transfers between devices  10.3 us (47%)
  Pallas kernels  6.49 us (30%)
  waiting for transfers between devices  3.71 us (17%)
  between operations  0.72 us (3%)
  other arithmetic  0.52 us (2%)
    ppermute x3, starting transfers between devices, local(): lax.ppermute(weight, 'lon', [(i, i ^ bit * step) for i in range(strips)])  4.08 us
    ppermute x1, starting transfers between devices, local(): from_east = lax.ppermute(send_west, 'lon', westward)  3.36 us
    ppermute x3, waiting for transfers between devices, local(): lax.ppermute(weight, 'lon', [(i, i ^ bit * step) for i in range(strips)])  2.19 us
    pallas_call x1, Pallas kernels, local(): pl.pallas_call(functools.partial(prepare, sizes), out_shape=(packet, pack...  1.81 us
    pallas_call x2, Pallas kernels, bulk_of(): pl.pallas_call(functools.partial(observed_bulk, sizes, parity), out_shape...  1.66 us
    pallas_call x1, Pallas kernels, local(): pl.pallas_call(functools.partial(assemble, sizes), out_shape=shape(*whole...  1.58 us
    ppermute x1, starting transfers between devices, local(): lax.ppermute(bulk_weight, 'lon', [(i, i ^ 1) for i in range(strips)])  1.41 us
    ppermute x1, starting transfers between devices, local(): from_west = lax.ppermute(send_east, 'lon', eastward)  1.36 us
  transfers between devices with their start and end apart: 7, of which 3 were waited for; matrix products, arithmetic and copies ran while one was open for 0% of the time, Pallas kernels for 14%

profile of v15, /device:TPU:0, one launch (start us, length us, event | category | flops | bytes accessed | tf_op | source)
XLA Modules:
  0.0 21.8 jit_solution(2977163739224574923)
XLA Ops:
  0.6 1.8 %shard_map.104 = (f32[88,256]{1,0:T(8,128)S(1)}, f32[88,256]{1,0:T(8,128)S(1)}, f32[8,4,32,256]{3,2,1,0:T(8,128)S(1)}, bf16[2,8,4,32,256]{4,3,2,1,0:T(8,128)(2,1...) custom-call(f32[8,4,32,256]{3,2,1,0:T(8,128)} %state_hbm.1, ...), custom_call_target="tpu_custom_call" | custom-call | flops 1000000 | bytes 2000000 | tf_op jit(solution)/shard_map/pallas_call | solution.py:443
  2.4 1.7 %shard_map.105 = (f32[8,4,32,256]{3,2,1,0:T(8,128)S(1)}, f32[8,32,256]{2,1,0:T(8,128)S(1)}, f32[1,128]{1,0:T(1,128)S(1)}, f32[4,5,32,256]{3,2,1,0:T(8,128)S(1)}) custom-call(f32[8,4,32,256]{3,2,1,0:T(8,128)S(1)} %get-tuple-element.26.state, bf16[2,8,4,32,256]{4,3,2,1,0:T(8,128)(2,1)S(1)} %get-tuple-element.27.noise, ...), custom_call_target="tpu_custom_call" | custom-call | flops 20000000 | bytes 4000000 | tf_op jit(solution)/shard_map/pallas_call | solution.py:456
  4.1 1.4 %collective-permute-start = (f32[88,256]{1,0:T(8,128)S(1)}, f32[88,256]{1,0:T(8,128)S(1)}, u32[]{:S(2)}, u32[]{:S(2)}) collective-permute-start(f32[88,256]{1,0:T(8,128)S(1)} %get-tuple-element.41.own_east), channel_id=1, source_target_pairs={{0,2},{2,4},{4,6},{6,8},{8,10},{10,12},{12,14},{14,0},{1,3},{3,5},... | collective-permute-start | bytes 270344 | tf_op jit(solution)/shard_map/ppermute | solution.py:470
  5.5 3.4 %collective-permute-start.1 = (f32[88,256]{1,0:T(8,128)S(1)}, f32[88,256]{1,0:T(8,128)S(1)}, u32[]{:S(2)}, u32[]{:S(2)}) collective-permute-start(f32[88,256]{1,0:T(8,128)S(1)} %get-tuple-element.42.own_west), channel_id=1, source_target_pairs={{0,14},{2,0},{4,2},{6,4},{8,6},{10,8},{12,10},{14,12},{1,15},{3,1}... | collective-permute-start | bytes 270344 | tf_op jit(solution)/shard_map/ppermute | solution.py:471
  8.8 1.4 %collective-permute-start.2 = (f32[1,128]{1,0:T(1,128)S(1)}, f32[1,128]{1,0:T(1,128)S(1)}, u32[]{:S(2)}, u32[]{:S(2)}) collective-permute-start(f32[1,128]{1,0:T(1,128)S(1)} %get-tuple-element.43.bulk_weight), channel_id=1, source_target_pairs={{0,2},{2,0},{4,6},{6,4},{8,10},{10,8},{12,14},{14,12},{1,3},{3,1},... | collective-permute-start | bytes 1544 | tf_op jit(solution)/shard_map/ppermute | solution.py:473
  10.3 1.1 %shard_map.107.current = f32[8,4,32,256]{3,2,1,0:T(8,128)S(1)} custom-call(f32[8,4,32,256]{3,2,1,0:T(8,128)S(1)} %get-tuple-element.31.even_middle, f32[8,32,256]{2,1,0:T(8,128)S(1)} %get-tuple-element.32.even_observed, f32[4,5,32,256]{3,2,1,0:T(8,128)S(1)} %get-tuple-element.33.even_coefs, f32[8,4,32,256]{3,2,1,0:T(8,128)S(1)} %get-tuple-element.38.odd_middle, ...), custom_call_target="tpu_custom_call" | custom-call | tf_op jit(solution)/shard_map/pallas_call | solution.py:475
  11.4 0.5 %collective-permute-done.from_west = f32[88,256]{1,0:T(8,128)S(1)} collective-permute-done((f32[88,256]{1,0:T(8,128)S(1)}, f32[88,256]{1,0:T(8,128)S(1)}, u32[]{:S(2)}, u32[]{:S(2)}) %collective-permute-start) | collective-permute-done | bytes 90144 | tf_op jit(solution)/shard_map/ppermute | solution.py:470
  11.9 1.0 %collective-permute-done.1.from_east = f32[88,256]{1,0:T(8,128)S(1)} collective-permute-done((f32[88,256]{1,0:T(8,128)S(1)}, f32[88,256]{1,0:T(8,128)S(1)}, u32[]{:S(2)}, u32[]{:S(2)}) %collective-permute-start.1) | collective-permute-done | bytes 90144 | tf_op jit(solution)/shard_map/ppermute | solution.py:471
  12.9 0.2 shard_map.108
  13.1 0.2 shard_map.109.current
  13.2 0.0 collective-permute-done.2
  13.2 0.1 collective-permute-start.3
  13.3 0.0 copy-start
  13.3 2.5 %collective-permute-start.5 = (f32[1,128]{1,0:T(1,128)S(1)}, f32[1,128]{1,0:T(1,128)S(1)}, u32[]{:S(2)}, u32[]{:S(2)}) collective-permute-start(f32[1,128]{1,0:T(1,128)S(1)} %add.12), channel_id=1, source_target_pairs={{0,8},{2,10},{4,12},{6,14},{8,0},{10,2},{12,4},{14,6},{1,9},{3,11}... | collective-permute-start | bytes 1544 | tf_op jit(solution)/shard_map/ppermute | solution.py:512
  15.9 1.3 %collective-permute-start.4 = (f32[1,128]{1,0:T(1,128)S(1)}, f32[1,128]{1,0:T(1,128)S(1)}, u32[]{:S(2)}, u32[]{:S(2)}) collective-permute-start(f32[1,128]{1,0:T(1,128)S(1)} %add.12), channel_id=1, source_target_pairs={{0,12},{2,14},{4,8},{6,10},{8,4},{10,6},{12,0},{14,2},{1,13},{3,15... | collective-permute-start | bytes 1544 | tf_op jit(solution)/shard_map/ppermute | solution.py:512
  17.2 0.0 collective-permute-done.3.received
  17.2 0.2 collective-permute-start.6
  17.4 0.0 copy-done
  17.4 1.6 %shard_map.110 = f32[8,4,32,256]{3,2,1,0:T(8,128)} custom-call(s32[16]{0:T(128)S(1)} %copy-done, f32[8,4,32,256]{3,2,1,0:T(8,128)S(1)} %shard_map.109.current, f32[8,4,32,256]{3,2,1,0:T(8,128)S(1)} %collective-permute-done.3.received), custom_call_target="tpu_custom_call" | custom-call | bytes 2000000 | tf_op jit(solution)/shard_map/pallas_call | solution.py:516
  19.0 0.0 copy-start.1
  19.0 0.0 collective-permute-done.5
  19.0 2.2 %collective-permute-done.4 = f32[1,128]{1,0:T(1,128)S(1)} collective-permute-done((f32[1,128]{1,0:T(1,128)S(1)}, f32[1,128]{1,0:T(1,128)S(1)}, u32[]{:S(2)}, u32[]{:S(2)}) %collective-permute-start.4) | collective-permute-done | bytes 544 | tf_op jit(solution)/shard_map/ppermute | solution.py:512
  21.2 0.0 collective-permute-done.6
  21.2 0.0 copy-done.1
  21.2 0.5 %bitcast_subtract_fusion = f32[8]{0:T(128)} fusion(f32[8]{0:T(128)S(1)} %copy-done.1, f32[1,128]{1,0:T(1,128)S(1)} %add_add_fusion), kind=kLoop, calls=%fused_computation | loop fusion | flops 16 | bytes 96 | tf_op jit(solution)/shard_map/sub | solution.py:526
  (3 shorter events, 0.0 us)
Async XLA Ops:
  4.1 7.8 %collective-permute-start = (f32[88,256]{1,0:T(8,128)S(1)}, f32[88,256]{1,0:T(8,128)S(1)}, u32[]{:S(2)}, u32[]{:S(2)}) collective-permute-start(f32[88,256]{1,0:T(8,128)S(1)} %get-tuple-element.41.own_east), channel_id=1, source_target_pairs={{0,2},{2,4},{4,6},{6,8},{8,10},{10,12},{12,14},{14,0},{1,3},{3,5},... | collective-permute-start | bytes 270344 | tf_op jit(solution)/shard_map/ppermute | solution.py:470
  5.5 7.4 %collective-permute-start.1 = (f32[88,256]{1,0:T(8,128)S(1)}, f32[88,256]{1,0:T(8,128)S(1)}, u32[]{:S(2)}, u32[]{:S(2)}) collective-permute-start(f32[88,256]{1,0:T(8,128)S(1)} %get-tuple-element.42.own_west), channel_id=1, source_target_pairs={{0,14},{2,0},{4,2},{6,4},{8,6},{10,8},{12,10},{14,12},{1,15},{3,1}... | collective-permute-start | bytes 270344 | tf_op jit(solution)/shard_map/ppermute | solution.py:471
  8.8 4.4 %collective-permute-start.2 = (f32[1,128]{1,0:T(1,128)S(1)}, f32[1,128]{1,0:T(1,128)S(1)}, u32[]{:S(2)}, u32[]{:S(2)}) collective-permute-start(f32[1,128]{1,0:T(1,128)S(1)} %get-tuple-element.43.bulk_weight), channel_id=1, source_target_pairs={{0,2},{2,0},{4,6},{6,4},{8,10},{10,8},{12,14},{14,12},{1,3},{3,1},... | collective-permute-start | bytes 1544 | tf_op jit(solution)/shard_map/ppermute | solution.py:473
  13.2 4.0 %collective-permute-start.3 = (f32[8,4,32,256]{3,2,1,0:T(8,128)S(1)}, f32[8,4,32,256]{3,2,1,0:T(8,128)S(1)}, u32[]{:S(2)}, u32[]{:S(2)}) collective-permute-start(f32[8,4,32,256]{3,2,1,0:T(8,128)S(1)} %shard_map.109.current), channel_id=1, source_target_pairs={{0,1},{1,0},{2,3},{3,2},{4,5},{5,4},{6,7},{7,6},{8,9},{9,8},{10,11... | collective-permute-start | bytes 3145736 | tf_op jit(solution)/shard_map/ppermute | solution.py:504
  13.3 4.1 %copy-start = (s32[16]{0:T(128)S(1)}, s32[16]{0:T(128)}, u32[]{:S(2)}) copy-start(s32[16]{0:T(128)} %source.1) | copy-start | bytes 196
  13.3 5.7 %collective-permute-start.5 = (f32[1,128]{1,0:T(1,128)S(1)}, f32[1,128]{1,0:T(1,128)S(1)}, u32[]{:S(2)}, u32[]{:S(2)}) collective-permute-start(f32[1,128]{1,0:T(1,128)S(1)} %add.12), channel_id=1, source_target_pairs={{0,8},{2,10},{4,12},{6,14},{8,0},{10,2},{12,4},{14,6},{1,9},{3,11}... | collective-permute-start | bytes 1544 | tf_op jit(solution)/shard_map/ppermute | solution.py:512
  15.9 5.3 %collective-permute-start.4 = (f32[1,128]{1,0:T(1,128)S(1)}, f32[1,128]{1,0:T(1,128)S(1)}, u32[]{:S(2)}, u32[]{:S(2)}) collective-permute-start(f32[1,128]{1,0:T(1,128)S(1)} %add.12), channel_id=1, source_target_pairs={{0,12},{2,14},{4,8},{6,10},{8,4},{10,6},{12,0},{14,2},{1,13},{3,15... | collective-permute-start | bytes 1544 | tf_op jit(solution)/shard_map/ppermute | solution.py:512
  17.2 4.0 %collective-permute-start.6 = (f32[1,128]{1,0:T(1,128)S(1)}, f32[1,128]{1,0:T(1,128)S(1)}, u32[]{:S(2)}, u32[]{:S(2)}) collective-permute-start(f32[1,128]{1,0:T(1,128)S(1)} %add.12), channel_id=1, source_target_pairs={{0,4},{2,6},{4,0},{6,2},{8,12},{10,14},{12,8},{14,10},{1,5},{3,7},... | collective-permute-start | bytes 1544 | tf_op jit(solution)/shard_map/ppermute | solution.py:512
  19.0 2.2 %copy-start.1 = (f32[8]{0:T(128)S(1)}, f32[8]{0:T(128)}, u32[]{:S(2)}) copy-start(f32[8]{0:T(128)} %param.14) | copy-start | bytes 100

commit v16 on v15

--- a/solution.py
+++ b/solution.py
@@ -507,7 +507,7 @@
         steps = (3, 2, 1) if 2 * bit < strips else (1,)
         arrived = []
         for step in steps:
-            if step == 1 and bit * (len(steps) + 1) >= strips:
+            if step == steps[-2:][0] and bit * (len(steps) + 1) >= strips:
                 weight, received = lax.optimization_barrier((weight, received))
             arrived.append(lax.ppermute(weight, "lon", [(i, i ^ (bit * step)) for i in range(strips)]))
         weight = sum(arrived, weight)

time: 21.9 us -> 22.5 us (1.027)
  starting transfers between devices: 10.3 us -> 12 us
  waiting for transfers between devices: 3.71 us -> 2.61 us
    ppermute x3, starting transfers between devices: 4.08 us -> 5.81 us  [local(): lax.ppermute(weight, 'lon', [(i, i ^ bit * step) for i in range(strips)])]
    ppermute x3, waiting for transfers between devices: 2.19 us -> 1.08 us  [local(): lax.ppermute(weight, 'lon', [(i, i ^ bit * step) for i in range(strips)])]
  transfers between devices with their start and end apart: 7 -> 7, of which waited for: 3 -> 3; matrix products, arithmetic and copies ran while one was open for 0% -> 0% of each run, Pallas kernels for 14% -> 13%
where the time goes in v16:
time: 22.5 us; the launch traced here: 22.4 us
  starting transfers between devices  12 us (53%)
  Pallas kernels  6.49 us (29%)
  waiting for transfers between devices  2.61 us (12%)
  between operations  0.72 us (3%)
  other arithmetic  0.52 us (2%)
    ppermute x3, starting transfers between devices, local(): lax.ppermute(weight, 'lon', [(i, i ^ bit * step) for i in range(strips)])  5.81 us
    ppermute x1, starting transfers between devices, local(): from_east = lax.ppermute(send_west, 'lon', westward)  3.36 us
    pallas_call x1, Pallas kernels, local(): pl.pallas_call(functools.partial(prepare, sizes), out_shape=(packet, pack...  1.81 us
    pallas_call x2, Pallas kernels, bulk_of(): pl.pallas_call(functools.partial(observed_bulk, sizes, parity), out_shape...  1.66 us
    pallas_call x1, Pallas kernels, local(): pl.pallas_call(functools.partial(assemble, sizes), out_shape=shape(*whole...  1.58 us
    ppermute x1, starting transfers between devices, local(): lax.ppermute(bulk_weight, 'lon', [(i, i ^ 1) for i in range(strips)])  1.41 us
    ppermute x1, starting transfers between devices, local(): from_west = lax.ppermute(send_east, 'lon', eastward)  1.36 us
    pallas_call x1, Pallas kernels, local(): pl.pallas_call(functools.partial(other_bulk, sizes), out_shape=shape(*who...  1.09 us
  transfers between devices with their start and end apart: 7, of which 3 were waited for; matrix products, arithmetic and copies ran while one was open for 0% of the time, Pallas kernels for 13%

profile of v16, /device:TPU:0, one launch (start us, length us, event | category | flops | bytes accessed | tf_op | source)
XLA Modules:
  0.0 22.4 jit_solution(10455507045005579735)
XLA Ops:
  0.6 1.8 %shard_map.104 = (f32[88,256]{1,0:T(8,128)S(1)}, f32[88,256]{1,0:T(8,128)S(1)}, f32[8,4,32,256]{3,2,1,0:T(8,128)S(1)}, bf16[2,8,4,32,256]{4,3,2,1,0:T(8,128)(2,1...) custom-call(f32[8,4,32,256]{3,2,1,0:T(8,128)} %state_hbm.1, ...), custom_call_target="tpu_custom_call" | custom-call | flops 1000000 | bytes 2000000 | tf_op jit(solution)/shard_map/pallas_call | solution.py:443
  2.4 1.7 %shard_map.105 = (f32[8,4,32,256]{3,2,1,0:T(8,128)S(1)}, f32[8,32,256]{2,1,0:T(8,128)S(1)}, f32[1,128]{1,0:T(1,128)S(1)}, f32[4,5,32,256]{3,2,1,0:T(8,128)S(1)}) custom-call(f32[8,4,32,256]{3,2,1,0:T(8,128)S(1)} %get-tuple-element.26.state, bf16[2,8,4,32,256]{4,3,2,1,0:T(8,128)(2,1)S(1)} %get-tuple-element.27.noise, ...), custom_call_target="tpu_custom_call" | custom-call | flops 20000000 | bytes 4000000 | tf_op jit(solution)/shard_map/pallas_call | solution.py:456
  4.1 1.4 %collective-permute-start = (f32[88,256]{1,0:T(8,128)S(1)}, f32[88,256]{1,0:T(8,128)S(1)}, u32[]{:S(2)}, u32[]{:S(2)}) collective-permute-start(f32[88,256]{1,0:T(8,128)S(1)} %get-tuple-element.41.own_east), channel_id=1, source_target_pairs={{0,2},{2,4},{4,6},{6,8},{8,10},{10,12},{12,14},{14,0},{1,3},{3,5},... | collective-permute-start | bytes 270344 | tf_op jit(solution)/shard_map/ppermute | solution.py:470
  5.5 3.4 %collective-permute-start.1 = (f32[88,256]{1,0:T(8,128)S(1)}, f32[88,256]{1,0:T(8,128)S(1)}, u32[]{:S(2)}, u32[]{:S(2)}) collective-permute-start(f32[88,256]{1,0:T(8,128)S(1)} %get-tuple-element.42.own_west), channel_id=1, source_target_pairs={{0,14},{2,0},{4,2},{6,4},{8,6},{10,8},{12,10},{14,12},{1,15},{3,1}... | collective-permute-start | bytes 270344 | tf_op jit(solution)/shard_map/ppermute | solution.py:471
  8.8 1.4 %collective-permute-start.2 = (f32[1,128]{1,0:T(1,128)S(1)}, f32[1,128]{1,0:T(1,128)S(1)}, u32[]{:S(2)}, u32[]{:S(2)}) collective-permute-start(f32[1,128]{1,0:T(1,128)S(1)} %get-tuple-element.43.bulk_weight), channel_id=1, source_target_pairs={{0,2},{2,0},{4,6},{6,4},{8,10},{10,8},{12,14},{14,12},{1,3},{3,1},... | collective-permute-start | bytes 1544 | tf_op jit(solution)/shard_map/ppermute | solution.py:473
  10.3 1.1 %shard_map.107.current = f32[8,4,32,256]{3,2,1,0:T(8,128)S(1)} custom-call(f32[8,4,32,256]{3,2,1,0:T(8,128)S(1)} %get-tuple-element.31.even_middle, f32[8,32,256]{2,1,0:T(8,128)S(1)} %get-tuple-element.32.even_observed, f32[4,5,32,256]{3,2,1,0:T(8,128)S(1)} %get-tuple-element.33.even_coefs, f32[8,4,32,256]{3,2,1,0:T(8,128)S(1)} %get-tuple-element.38.odd_middle, ...), custom_call_target="tpu_custom_call" | custom-call | tf_op jit(solution)/shard_map/pallas_call | solution.py:475
  11.4 0.5 %collective-permute-done.from_west = f32[88,256]{1,0:T(8,128)S(1)} collective-permute-done((f32[88,256]{1,0:T(8,128)S(1)}, f32[88,256]{1,0:T(8,128)S(1)}, u32[]{:S(2)}, u32[]{:S(2)}) %collective-permute-start) | collective-permute-done | bytes 90144 | tf_op jit(solution)/shard_map/ppermute | solution.py:470
  11.9 1.0 %collective-permute-done.1.from_east = f32[88,256]{1,0:T(8,128)S(1)} collective-permute-done((f32[88,256]{1,0:T(8,128)S(1)}, f32[88,256]{1,0:T(8,128)S(1)}, u32[]{:S(2)}, u32[]{:S(2)}) %collective-permute-start.1) | collective-permute-done | bytes 90144 | tf_op jit(solution)/shard_map/ppermute | solution.py:471
  12.9 0.2 shard_map.108
  13.1 0.2 shard_map.109.current
  13.2 0.0 collective-permute-done.2
  13.2 0.1 collective-permute-start.3
  13.3 0.0 copy-start
  13.3 2.7 %collective-permute-start.4 = (f32[1,128]{1,0:T(1,128)S(1)}, f32[1,128]{1,0:T(1,128)S(1)}, u32[]{:S(2)}, u32[]{:S(2)}) collective-permute-start(f32[1,128]{1,0:T(1,128)S(1)} %add.12), channel_id=1, source_target_pairs={{0,12},{2,14},{4,8},{6,10},{8,4},{10,6},{12,0},{14,2},{1,13},{3,15... | collective-permute-start | bytes 1544 | tf_op jit(solution)/shard_map/ppermute | solution.py:512
  16.0 0.0 collective-permute-done.3.received
  16.0 1.4 %collective-permute-start.6 = (f32[1,128]{1,0:T(1,128)S(1)}, f32[1,128]{1,0:T(1,128)S(1)}, u32[]{:S(2)}, u32[]{:S(2)}) collective-permute-start(f32[1,128]{1,0:T(1,128)S(1)} %add.12), channel_id=1, source_target_pairs={{0,4},{2,6},{4,0},{6,2},{8,12},{10,14},{12,8},{14,10},{1,5},{3,7},... | collective-permute-start | bytes 1544 | tf_op jit(solution)/shard_map/ppermute | solution.py:512
  17.4 1.7 %collective-permute-start.5 = (f32[1,128]{1,0:T(1,128)S(1)}, f32[1,128]{1,0:T(1,128)S(1)}, u32[]{:S(2)}, u32[]{:S(2)}) collective-permute-start(f32[1,128]{1,0:T(1,128)S(1)} %add.12), channel_id=1, source_target_pairs={{0,8},{2,10},{4,12},{6,14},{8,0},{10,2},{12,4},{14,6},{1,9},{3,11}... | collective-permute-start | bytes 1544 | tf_op jit(solution)/shard_map/ppermute | solution.py:512
  19.2 0.0 copy-done
  19.2 1.6 %shard_map.110 = f32[8,4,32,256]{3,2,1,0:T(8,128)} custom-call(s32[16]{0:T(128)S(1)} %copy-done, f32[8,4,32,256]{3,2,1,0:T(8,128)S(1)} %shard_map.109.current, f32[8,4,32,256]{3,2,1,0:T(8,128)S(1)} %collective-permute-done.3.received), custom_call_target="tpu_custom_call" | custom-call | bytes 2000000 | tf_op jit(solution)/shard_map/pallas_call | solution.py:516
  20.7 0.0 copy-start.1
  20.8 0.0 collective-permute-done.4
  20.8 0.0 collective-permute-done.6
  20.8 1.1 %collective-permute-done.5 = f32[1,128]{1,0:T(1,128)S(1)} collective-permute-done((f32[1,128]{1,0:T(1,128)S(1)}, f32[1,128]{1,0:T(1,128)S(1)}, u32[]{:S(2)}, u32[]{:S(2)}) %collective-permute-start.5) | collective-permute-done | bytes 544 | tf_op jit(solution)/shard_map/ppermute | solution.py:512
  21.9 0.0 copy-done.1
  21.9 0.5 %bitcast_subtract_fusion = f32[8]{0:T(128)} fusion(f32[8]{0:T(128)S(1)} %copy-done.1, f32[1,128]{1,0:T(1,128)S(1)} %add_add_fusion), kind=kLoop, calls=%fused_computation | loop fusion | flops 16 | bytes 96 | tf_op jit(solution)/shard_map/sub | solution.py:526
  (3 shorter events, 0.0 us)
Async XLA Ops:
  4.1 7.8 %collective-permute-start = (f32[88,256]{1,0:T(8,128)S(1)}, f32[88,256]{1,0:T(8,128)S(1)}, u32[]{:S(2)}, u32[]{:S(2)}) collective-permute-start(f32[88,256]{1,0:T(8,128)S(1)} %get-tuple-element.41.own_east), channel_id=1, source_target_pairs={{0,2},{2,4},{4,6},{6,8},{8,10},{10,12},{12,14},{14,0},{1,3},{3,5},... | collective-permute-start | bytes 270344 | tf_op jit(solution)/shard_map/ppermute | solution.py:470
  5.5 7.4 %collective-permute-start.1 = (f32[88,256]{1,0:T(8,128)S(1)}, f32[88,256]{1,0:T(8,128)S(1)}, u32[]{:S(2)}, u32[]{:S(2)}) collective-permute-start(f32[88,256]{1,0:T(8,128)S(1)} %get-tuple-element.42.own_west), channel_id=1, source_target_pairs={{0,14},{2,0},{4,2},{6,4},{8,6},{10,8},{12,10},{14,12},{1,15},{3,1}... | collective-permute-start | bytes 270344 | tf_op jit(solution)/shard_map/ppermute | solution.py:471
  8.8 4.4 %collective-permute-start.2 = (f32[1,128]{1,0:T(1,128)S(1)}, f32[1,128]{1,0:T(1,128)S(1)}, u32[]{:S(2)}, u32[]{:S(2)}) collective-permute-start(f32[1,128]{1,0:T(1,128)S(1)} %get-tuple-element.43.bulk_weight), channel_id=1, source_target_pairs={{0,2},{2,0},{4,6},{6,4},{8,10},{10,8},{12,14},{14,12},{1,3},{3,1},... | collective-permute-start | bytes 1544 | tf_op jit(solution)/shard_map/ppermute | solution.py:473
  13.2 2.8 %collective-permute-start.3 = (f32[8,4,32,256]{3,2,1,0:T(8,128)S(1)}, f32[8,4,32,256]{3,2,1,0:T(8,128)S(1)}, u32[]{:S(2)}, u32[]{:S(2)}) collective-permute-start(f32[8,4,32,256]{3,2,1,0:T(8,128)S(1)} %shard_map.109.current), channel_id=1, source_target_pairs={{0,1},{1,0},{2,3},{3,2},{4,5},{5,4},{6,7},{7,6},{8,9},{9,8},{10,11... | collective-permute-start | bytes 3145736 | tf_op jit(solution)/shard_map/ppermute | solution.py:504
  13.3 5.8 %copy-start = (s32[16]{0:T(128)S(1)}, s32[16]{0:T(128)}, u32[]{:S(2)}) copy-start(s32[16]{0:T(128)} %source.1) | copy-start | bytes 196
  13.3 7.4 %collective-permute-start.4 = (f32[1,128]{1,0:T(1,128)S(1)}, f32[1,128]{1,0:T(1,128)S(1)}, u32[]{:S(2)}, u32[]{:S(2)}) collective-permute-start(f32[1,128]{1,0:T(1,128)S(1)} %add.12), channel_id=1, source_target_pairs={{0,12},{2,14},{4,8},{6,10},{8,4},{10,6},{12,0},{14,2},{1,13},{3,15... | collective-permute-start | bytes 1544 | tf_op jit(solution)/shard_map/ppermute | solution.py:512
  16.0 4.7 %collective-permute-start.6 = (f32[1,128]{1,0:T(1,128)S(1)}, f32[1,128]{1,0:T(1,128)S(1)}, u32[]{:S(2)}, u32[]{:S(2)}) collective-permute-start(f32[1,128]{1,0:T(1,128)S(1)} %add.12), channel_id=1, source_target_pairs={{0,4},{2,6},{4,0},{6,2},{8,12},{10,14},{12,8},{14,10},{1,5},{3,7},... | collective-permute-start | bytes 1544 | tf_op jit(solution)/shard_map/ppermute | solution.py:512
  17.4 4.4 %collective-permute-start.5 = (f32[1,128]{1,0:T(1,128)S(1)}, f32[1,128]{1,0:T(1,128)S(1)}, u32[]{:S(2)}, u32[]{:S(2)}) collective-permute-start(f32[1,128]{1,0:T(1,128)S(1)} %add.12), channel_id=1, source_target_pairs={{0,8},{2,10},{4,12},{6,14},{8,0},{10,2},{12,4},{14,6},{1,9},{3,11}... | collective-permute-start | bytes 1544 | tf_op jit(solution)/shard_map/ppermute | solution.py:512
  20.7 1.1 %copy-start.1 = (f32[8]{0:T(128)S(1)}, f32[8]{0:T(128)}, u32[]{:S(2)}) copy-start(f32[8]{0:T(128)} %param.14) | copy-start | bytes 100

commit v17 on v15

--- a/solution.py
+++ b/solution.py
@@ -504,7 +504,7 @@
     received = lax.ppermute(current, "dom", [(0, 1), (1, 0)])
     bit = 2
     while bit < strips:
-        steps = (3, 2, 1) if 2 * bit < strips else (1,)
+        steps = (2, 3, 1) if 2 * bit < strips else (1,)
         arrived = []
         for step in steps:
             if step == 1 and bit * (len(steps) + 1) >= strips:

time: 21.9 us -> 21.2 us (0.968)
  waiting for transfers between devices: 3.71 us -> 2.59 us
  starting transfers between devices: 10.3 us -> 10.7 us
    ppermute x3, waiting for transfers between devices: 2.19 us -> 1.07 us  [local(): lax.ppermute(weight, 'lon', [(i, i ^ bit * step) for i in range(strips)])]
    ppermute x3, starting transfers between devices: 4.08 us -> 4.45 us  [local(): lax.ppermute(weight, 'lon', [(i, i ^ bit * step) for i in range(strips)])]
where the time goes in v17:
time: 21.2 us; the launch traced here: 21 us
  starting transfers between devices  10.7 us (50%)
  Pallas kernels  6.49 us (31%)
  waiting for transfers between devices  2.59 us (12%)
  between operations  0.72 us (3%)
  other arithmetic  0.52 us (2%)
    ppermute x3, starting transfers between devices, local(): lax.ppermute(weight, 'lon', [(i, i ^ bit * step) for i in range(strips)])  4.45 us
    ppermute x1, starting transfers between devices, local(): from_east = lax.ppermute(send_west, 'lon', westward)  3.36 us
    pallas_call x1, Pallas kernels, local(): pl.pallas_call(functools.partial(prepare, sizes), out_shape=(packet, pack...  1.81 us
    pallas_call x2, Pallas kernels, bulk_of(): pl.pallas_call(functools.partial(observed_bulk, sizes, parity), out_shape...  1.66 us
    pallas_call x1, Pallas kernels, local(): pl.pallas_call(functools.partial(assemble, sizes), out_shape=shape(*whole...  1.58 us
    ppermute x1, starting transfers between devices, local(): lax.ppermute(bulk_weight, 'lon', [(i, i ^ 1) for i in range(strips)])  1.41 us
    ppermute x1, starting transfers between devices, local(): from_west = lax.ppermute(send_east, 'lon', eastward)  1.36 us
    pallas_call x1, Pallas kernels, local(): pl.pallas_call(functools.partial(other_bulk, sizes), out_shape=shape(*who...  1.09 us
  transfers between devices with their start and end apart: 7, of which 3 were waited for; matrix products, arithmetic and copies ran while one was open for 0% of the time, Pallas kernels for 14%

profile of v17, /device:TPU:0, one launch (start us, length us, event | category | flops | bytes accessed | tf_op | source)
XLA Modules:
  0.0 21.0 jit_solution(9943585468810376620)
XLA Ops:
  0.6 1.8 %shard_map.104 = (f32[88,256]{1,0:T(8,128)S(1)}, f32[88,256]{1,0:T(8,128)S(1)}, f32[8,4,32,256]{3,2,1,0:T(8,128)S(1)}, bf16[2,8,4,32,256]{4,3,2,1,0:T(8,128)(2,1...) custom-call(f32[8,4,32,256]{3,2,1,0:T(8,128)} %state_hbm.1, ...), custom_call_target="tpu_custom_call" | custom-call | flops 1000000 | bytes 2000000 | tf_op jit(solution)/shard_map/pallas_call | solution.py:443
  2.4 1.7 %shard_map.105 = (f32[8,4,32,256]{3,2,1,0:T(8,128)S(1)}, f32[8,32,256]{2,1,0:T(8,128)S(1)}, f32[1,128]{1,0:T(1,128)S(1)}, f32[4,5,32,256]{3,2,1,0:T(8,128)S(1)}) custom-call(f32[8,4,32,256]{3,2,1,0:T(8,128)S(1)} %get-tuple-element.26.state, bf16[2,8,4,32,256]{4,3,2,1,0:T(8,128)(2,1)S(1)} %get-tuple-element.27.noise, ...), custom_call_target="tpu_custom_call" | custom-call | flops 20000000 | bytes 4000000 | tf_op jit(solution)/shard_map/pallas_call | solution.py:456
  4.1 1.4 %collective-permute-start = (f32[88,256]{1,0:T(8,128)S(1)}, f32[88,256]{1,0:T(8,128)S(1)}, u32[]{:S(2)}, u32[]{:S(2)}) collective-permute-start(f32[88,256]{1,0:T(8,128)S(1)} %get-tuple-element.41.own_east), channel_id=1, source_target_pairs={{0,2},{2,4},{4,6},{6,8},{8,10},{10,12},{12,14},{14,0},{1,3},{3,5},... | collective-permute-start | bytes 270344 | tf_op jit(solution)/shard_map/ppermute | solution.py:470
  5.5 3.4 %collective-permute-start.1 = (f32[88,256]{1,0:T(8,128)S(1)}, f32[88,256]{1,0:T(8,128)S(1)}, u32[]{:S(2)}, u32[]{:S(2)}) collective-permute-start(f32[88,256]{1,0:T(8,128)S(1)} %get-tuple-element.42.own_west), channel_id=1, source_target_pairs={{0,14},{2,0},{4,2},{6,4},{8,6},{10,8},{12,10},{14,12},{1,15},{3,1}... | collective-permute-start | bytes 270344 | tf_op jit(solution)/shard_map/ppermute | solution.py:471
  8.8 1.4 %collective-permute-start.2 = (f32[1,128]{1,0:T(1,128)S(1)}, f32[1,128]{1,0:T(1,128)S(1)}, u32[]{:S(2)}, u32[]{:S(2)}) collective-permute-start(f32[1,128]{1,0:T(1,128)S(1)} %get-tuple-element.43.bulk_weight), channel_id=1, source_target_pairs={{0,2},{2,0},{4,6},{6,4},{8,10},{10,8},{12,14},{14,12},{1,3},{3,1},... | collective-permute-start | bytes 1544 | tf_op jit(solution)/shard_map/ppermute | solution.py:473
  10.3 1.1 %shard_map.107.current = f32[8,4,32,256]{3,2,1,0:T(8,128)S(1)} custom-call(f32[8,4,32,256]{3,2,1,0:T(8,128)S(1)} %get-tuple-element.31.even_middle, f32[8,32,256]{2,1,0:T(8,128)S(1)} %get-tuple-element.32.even_observed, f32[4,5,32,256]{3,2,1,0:T(8,128)S(1)} %get-tuple-element.33.even_coefs, f32[8,4,32,256]{3,2,1,0:T(8,128)S(1)} %get-tuple-element.38.odd_middle, ...), custom_call_target="tpu_custom_call" | custom-call | tf_op jit(solution)/shard_map/pallas_call | solution.py:475
  11.4 0.5 %collective-permute-done.from_west = f32[88,256]{1,0:T(8,128)S(1)} collective-permute-done((f32[88,256]{1,0:T(8,128)S(1)}, f32[88,256]{1,0:T(8,128)S(1)}, u32[]{:S(2)}, u32[]{:S(2)}) %collective-permute-start) | collective-permute-done | bytes 90144 | tf_op jit(solution)/shard_map/ppermute | solution.py:470
  11.9 1.0 %collective-permute-done.1.from_east = f32[88,256]{1,0:T(8,128)S(1)} collective-permute-done((f32[88,256]{1,0:T(8,128)S(1)}, f32[88,256]{1,0:T(8,128)S(1)}, u32[]{:S(2)}, u32[]{:S(2)}) %collective-permute-start.1) | collective-permute-done | bytes 90144 | tf_op jit(solution)/shard_map/ppermute | solution.py:471
  12.9 0.2 shard_map.108
  13.1 0.2 shard_map.109.current
  13.2 0.0 collective-permute-done.2
  13.2 0.1 collective-permute-start.3
  13.3 0.0 copy-start
  13.3 2.7 %collective-permute-start.5 = (f32[1,128]{1,0:T(1,128)S(1)}, f32[1,128]{1,0:T(1,128)S(1)}, u32[]{:S(2)}, u32[]{:S(2)}) collective-permute-start(f32[1,128]{1,0:T(1,128)S(1)} %add.12), channel_id=1, source_target_pairs={{0,12},{2,14},{4,8},{6,10},{8,4},{10,6},{12,0},{14,2},{1,13},{3,15... | collective-permute-start | bytes 1544 | tf_op jit(solution)/shard_map/ppermute | solution.py:512
  16.0 0.3 %collective-permute-start.4 = (f32[1,128]{1,0:T(1,128)S(1)}, f32[1,128]{1,0:T(1,128)S(1)}, u32[]{:S(2)}, u32[]{:S(2)}) collective-permute-start(f32[1,128]{1,0:T(1,128)S(1)} %add.12), channel_id=1, source_target_pairs={{0,8},{2,10},{4,12},{6,14},{8,0},{10,2},{12,4},{14,6},{1,9},{3,11}... | collective-permute-start | bytes 1544 | tf_op jit(solution)/shard_map/ppermute | solution.py:512
  16.3 0.0 collective-permute-done.3.received
  16.3 1.5 %collective-permute-start.6 = (f32[1,128]{1,0:T(1,128)S(1)}, f32[1,128]{1,0:T(1,128)S(1)}, u32[]{:S(2)}, u32[]{:S(2)}) collective-permute-start(f32[1,128]{1,0:T(1,128)S(1)} %add.12), channel_id=1, source_target_pairs={{0,4},{2,6},{4,0},{6,2},{8,12},{10,14},{12,8},{14,10},{1,5},{3,7},... | collective-permute-start | bytes 1544 | tf_op jit(solution)/shard_map/ppermute | solution.py:512
  17.8 0.0 copy-done
  17.8 1.6 %shard_map.110 = f32[8,4,32,256]{3,2,1,0:T(8,128)} custom-call(s32[16]{0:T(128)S(1)} %copy-done, f32[8,4,32,256]{3,2,1,0:T(8,128)S(1)} %shard_map.109.current, f32[8,4,32,256]{3,2,1,0:T(8,128)S(1)} %collective-permute-done.3.received), custom_call_target="tpu_custom_call" | custom-call | bytes 2000000 | tf_op jit(solution)/shard_map/pallas_call | solution.py:516
  19.4 0.0 copy-start.1
  19.4 0.0 collective-permute-done.5
  19.4 1.1 %collective-permute-done.4 = f32[1,128]{1,0:T(1,128)S(1)} collective-permute-done((f32[1,128]{1,0:T(1,128)S(1)}, f32[1,128]{1,0:T(1,128)S(1)}, u32[]{:S(2)}, u32[]{:S(2)}) %collective-permute-start.4) | collective-permute-done | bytes 544 | tf_op jit(solution)/shard_map/ppermute | solution.py:512
  20.5 0.0 collective-permute-done.6
  20.5 0.0 copy-done.1
  20.5 0.5 %bitcast_subtract_fusion = f32[8]{0:T(128)} fusion(f32[8]{0:T(128)S(1)} %copy-done.1, f32[1,128]{1,0:T(1,128)S(1)} %add_add_fusion), kind=kLoop, calls=%fused_computation | loop fusion | flops 16 | bytes 96 | tf_op jit(solution)/shard_map/sub | solution.py:526
  (3 shorter events, 0.0 us)
Async XLA Ops:
  4.1 7.8 %collective-permute-start = (f32[88,256]{1,0:T(8,128)S(1)}, f32[88,256]{1,0:T(8,128)S(1)}, u32[]{:S(2)}, u32[]{:S(2)}) collective-permute-start(f32[88,256]{1,0:T(8,128)S(1)} %get-tuple-element.41.own_east), channel_id=1, source_target_pairs={{0,2},{2,4},{4,6},{6,8},{8,10},{10,12},{12,14},{14,0},{1,3},{3,5},... | collective-permute-start | bytes 270344 | tf_op jit(solution)/shard_map/ppermute | solution.py:470
  5.5 7.4 %collective-permute-start.1 = (f32[88,256]{1,0:T(8,128)S(1)}, f32[88,256]{1,0:T(8,128)S(1)}, u32[]{:S(2)}, u32[]{:S(2)}) collective-permute-start(f32[88,256]{1,0:T(8,128)S(1)} %get-tuple-element.42.own_west), channel_id=1, source_target_pairs={{0,14},{2,0},{4,2},{6,4},{8,6},{10,8},{12,10},{14,12},{1,15},{3,1}... | collective-permute-start | bytes 270344 | tf_op jit(solution)/shard_map/ppermute | solution.py:471
  8.8 4.4 %collective-permute-start.2 = (f32[1,128]{1,0:T(1,128)S(1)}, f32[1,128]{1,0:T(1,128)S(1)}, u32[]{:S(2)}, u32[]{:S(2)}) collective-permute-start(f32[1,128]{1,0:T(1,128)S(1)} %get-tuple-element.43.bulk_weight), channel_id=1, source_target_pairs={{0,2},{2,0},{4,6},{6,4},{8,10},{10,8},{12,14},{14,12},{1,3},{3,1},... | collective-permute-start | bytes 1544 | tf_op jit(solution)/shard_map/ppermute | solution.py:473
  13.2 3.1 %collective-permute-start.3 = (f32[8,4,32,256]{3,2,1,0:T(8,128)S(1)}, f32[8,4,32,256]{3,2,1,0:T(8,128)S(1)}, u32[]{:S(2)}, u32[]{:S(2)}) collective-permute-start(f32[8,4,32,256]{3,2,1,0:T(8,128)S(1)} %shard_map.109.current), channel_id=1, source_target_pairs={{0,1},{1,0},{2,3},{3,2},{4,5},{5,4},{6,7},{7,6},{8,9},{9,8},{10,11... | collective-permute-start | bytes 3145736 | tf_op jit(solution)/shard_map/ppermute | solution.py:504
  13.3 4.5 %copy-start = (s32[16]{0:T(128)S(1)}, s32[16]{0:T(128)}, u32[]{:S(2)}) copy-start(s32[16]{0:T(128)} %source.1) | copy-start | bytes 196
  13.3 6.1 %collective-permute-start.5 = (f32[1,128]{1,0:T(1,128)S(1)}, f32[1,128]{1,0:T(1,128)S(1)}, u32[]{:S(2)}, u32[]{:S(2)}) collective-permute-start(f32[1,128]{1,0:T(1,128)S(1)} %add.12), channel_id=1, source_target_pairs={{0,12},{2,14},{4,8},{6,10},{8,4},{10,6},{12,0},{14,2},{1,13},{3,15... | collective-permute-start | bytes 1544 | tf_op jit(solution)/shard_map/ppermute | solution.py:512
  16.0 4.4 %collective-permute-start.4 = (f32[1,128]{1,0:T(1,128)S(1)}, f32[1,128]{1,0:T(1,128)S(1)}, u32[]{:S(2)}, u32[]{:S(2)}) collective-permute-start(f32[1,128]{1,0:T(1,128)S(1)} %add.12), channel_id=1, source_target_pairs={{0,8},{2,10},{4,12},{6,14},{8,0},{10,2},{12,4},{14,6},{1,9},{3,11}... | collective-permute-start | bytes 1544 | tf_op jit(solution)/shard_map/ppermute | solution.py:512
  16.3 4.1 %collective-permute-start.6 = (f32[1,128]{1,0:T(1,128)S(1)}, f32[1,128]{1,0:T(1,128)S(1)}, u32[]{:S(2)}, u32[]{:S(2)}) collective-permute-start(f32[1,128]{1,0:T(1,128)S(1)} %add.12), channel_id=1, source_target_pairs={{0,4},{2,6},{4,0},{6,2},{8,12},{10,14},{12,8},{14,10},{1,5},{3,7},... | collective-permute-start | bytes 1544 | tf_op jit(solution)/shard_map/ppermute | solution.py:512
  19.4 1.1 %copy-start.1 = (f32[8]{0:T(128)S(1)}, f32[8]{0:T(128)}, u32[]{:S(2)}) copy-start(f32[8]{0:T(128)} %param.14) | copy-start | bytes 100

commit v18 on v17

--- a/solution.py
+++ b/solution.py
@@ -18,11 +18,29 @@
 
 
 def north(v):
-    return pltpu.roll(v, v.shape[1] - 1, 1)
+    low, high = (pltpu.roll(v[:, at:at + 128], 127, 1) for at in (0, 128))
+    lane = lax.broadcasted_iota(jnp.int32, low.shape, 1)
+    return jnp.concatenate([jnp.where(lane == 127, high, low), high], 1)
 
 
 def south(v):
-    return pltpu.roll(v, 1, 1)
+    low, high = (pltpu.roll(v[:, at:at + 128], 1, 1) for at in (0, 128))
+    lane = lax.broadcasted_iota(jnp.int32, low.shape, 1)
+    return jnp.concatenate([low, jnp.where(lane == 0, low, high)], 1)
+
+
+def east_of(v):
+    tiles = [pltpu.roll(v[at:at + 8], 7, 0) for at in range(0, v.shape[0], 8)]
+    sub = lax.broadcasted_iota(jnp.int32, tiles[0].shape, 0)
+    mixed_tiles = [jnp.where(sub == 7, after, tile) for tile, after in zip(tiles[:-1], tiles[1:])]
+    return jnp.concatenate(mixed_tiles + tiles[-1:], 0)
+
+
+def west_of(v):
+    tiles = [pltpu.roll(v[at:at + 8], 1, 0) for at in range(0, v.shape[0], 8)]
+    sub = lax.broadcasted_iota(jnp.int32, tiles[0].shape, 0)
+    mixed_tiles = [jnp.where(sub == 0, before, tile) for before, tile in zip(tiles[:-1], tiles[1:])]
+    return jnp.concatenate(tiles[:1] + mixed_tiles, 0)
 
 
 def coefficients(zonal, merid, rate, self_mix):
@@ -260,7 +278,7 @@
 
     def moved(values, f):
         v = values[f]
-        return (coefs[f, 0] * v + coefs[f, 1] * pltpu.roll(v, strip - 1, 0) + coefs[f, 2] * pltpu.roll(v, 1, 0)
+        return (coefs[f, 0] * v + coefs[f, 1] * east_of(v) + coefs[f, 2] * west_of(v)
                 + coefs[f, 3] * north(v) + coefs[f, 4] * south(v) + mixed(mixing, f, values))
 
     return moved
@@ -291,9 +309,9 @@
         out[p] = new
         partial[pl.ds(p, 1), :] = wide(jnp.sum(total, axis=0, keepdims=True))
 
-    def body(pair, carry):
-        one(2 * pair)
-        one(2 * pair + 1)
+    def body(step, carry):
+        for k in range(4):
+            one(4 * step + k)
         return carry
 
     here = lax.axis_index("lon") % 2 == parity
@@ -301,7 +319,7 @@
     @pl.when(here)
     def _():
         zero_halo_coefs(sizes, courant, scalars, coefs)
-        lax.fori_loop(0, particles // 2, body, 0)
+        lax.fori_loop(0, particles // 4, body, 0)
         weight[...] = in_row(partial[...])
 
     @pl.when(jnp.logical_not(here))

time: 21.2 us -> 21.1 us (level)
  no operation moved by 1% of the time
where the time goes in v18:
time: 21.1 us; the launch traced here: 20.9 us
  starting transfers between devices  10.6 us (50%)
  Pallas kernels  6.33 us (30%)
  waiting for transfers between devices  2.75 us (13%)
  between operations  0.72 us (3%)
  other arithmetic  0.52 us (2%)
    ppermute x3, starting transfers between devices, local(): lax.ppermute(weight, 'lon', [(i, i ^ bit * step) for i in range(strips)])  4.45 us
    ppermute x1, starting transfers between devices, local(): from_east = lax.ppermute(send_west, 'lon', westward)  3.26 us
    pallas_call x1, Pallas kernels, local(): pl.pallas_call(functools.partial(prepare, sizes), out_shape=(packet, pack...  1.8 us
    pallas_call x1, Pallas kernels, local(): pl.pallas_call(functools.partial(assemble, sizes), out_shape=shape(*whole...  1.58 us
    pallas_call x2, Pallas kernels, bulk_of(): pl.pallas_call(functools.partial(observed_bulk, sizes, parity), out_shape...  1.56 us
    ppermute x1, starting transfers between devices, local(): from_west = lax.ppermute(send_east, 'lon', eastward)  1.47 us
    ppermute x1, starting transfers between devices, local(): lax.ppermute(bulk_weight, 'lon', [(i, i ^ 1) for i in range(strips)])  1.31 us
    ppermute x3, waiting for transfers between devices, local(): lax.ppermute(weight, 'lon', [(i, i ^ bit * step) for i in range(strips)])  1.06 us
  transfers between devices with their start and end apart: 7, of which 3 were waited for; matrix products, arithmetic and copies ran while one was open for 0% of the time, Pallas kernels for 14%

profile of v18, /device:TPU:0, one launch (start us, length us, event | category | flops | bytes accessed | tf_op | source)
XLA Modules:
  0.0 20.9 jit_solution(2202828423907318995)
XLA Ops:
  0.6 1.8 %shard_map.104 = (f32[88,256]{1,0:T(8,128)S(1)}, f32[88,256]{1,0:T(8,128)S(1)}, f32[8,4,32,256]{3,2,1,0:T(8,128)S(1)}, bf16[2,8,4,32,256]{4,3,2,1,0:T(8,128)(2,1...) custom-call(f32[8,4,32,256]{3,2,1,0:T(8,128)} %state_hbm.1, ...), custom_call_target="tpu_custom_call" | custom-call | flops 1000000 | bytes 2000000 | tf_op jit(solution)/shard_map/pallas_call | solution.py:461
  2.4 1.6 %shard_map.105 = (f32[8,4,32,256]{3,2,1,0:T(8,128)S(1)}, f32[8,32,256]{2,1,0:T(8,128)S(1)}, f32[1,128]{1,0:T(1,128)S(1)}, f32[4,5,32,256]{3,2,1,0:T(8,128)S(1)}) custom-call(f32[8,4,32,256]{3,2,1,0:T(8,128)S(1)} %get-tuple-element.26.state, bf16[2,8,4,32,256]{4,3,2,1,0:T(8,128)(2,1)S(1)} %get-tuple-element.27.noise, ...), custom_call_target="tpu_custom_call" | custom-call | flops 20000000 | bytes 4000000 | tf_op jit(solution)/shard_map/pallas_call | solution.py:474
  4.0 1.5 %collective-permute-start = (f32[88,256]{1,0:T(8,128)S(1)}, f32[88,256]{1,0:T(8,128)S(1)}, u32[]{:S(2)}, u32[]{:S(2)}) collective-permute-start(f32[88,256]{1,0:T(8,128)S(1)} %get-tuple-element.41.own_east), channel_id=1, source_target_pairs={{0,2},{2,4},{4,6},{6,8},{8,10},{10,12},{12,14},{14,0},{1,3},{3,5},... | collective-permute-start | bytes 270344 | tf_op jit(solution)/shard_map/ppermute | solution.py:488
  5.5 3.3 %collective-permute-start.1 = (f32[88,256]{1,0:T(8,128)S(1)}, f32[88,256]{1,0:T(8,128)S(1)}, u32[]{:S(2)}, u32[]{:S(2)}) collective-permute-start(f32[88,256]{1,0:T(8,128)S(1)} %get-tuple-element.42.own_west), channel_id=1, source_target_pairs={{0,14},{2,0},{4,2},{6,4},{8,6},{10,8},{12,10},{14,12},{1,15},{3,1}... | collective-permute-start | bytes 270344 | tf_op jit(solution)/shard_map/ppermute | solution.py:489
  8.7 1.3 %collective-permute-start.2 = (f32[1,128]{1,0:T(1,128)S(1)}, f32[1,128]{1,0:T(1,128)S(1)}, u32[]{:S(2)}, u32[]{:S(2)}) collective-permute-start(f32[1,128]{1,0:T(1,128)S(1)} %get-tuple-element.43.bulk_weight), channel_id=1, source_target_pairs={{0,2},{2,0},{4,6},{6,4},{8,10},{10,8},{12,14},{14,12},{1,3},{3,1},... | collective-permute-start | bytes 1544 | tf_op jit(solution)/shard_map/ppermute | solution.py:491
  10.0 1.0 %shard_map.107.current = f32[8,4,32,256]{3,2,1,0:T(8,128)S(1)} custom-call(f32[8,4,32,256]{3,2,1,0:T(8,128)S(1)} %get-tuple-element.31.even_middle, f32[8,32,256]{2,1,0:T(8,128)S(1)} %get-tuple-element.32.even_observed, f32[4,5,32,256]{3,2,1,0:T(8,128)S(1)} %get-tuple-element.33.even_coefs, f32[8,4,32,256]{3,2,1,0:T(8,128)S(1)} %get-tuple-element.38.odd_middle, ...), custom_call_target="tpu_custom_call" | custom-call | tf_op jit(solution)/shard_map/pallas_call | solution.py:493
  11.1 0.7 %collective-permute-done.from_west = f32[88,256]{1,0:T(8,128)S(1)} collective-permute-done((f32[88,256]{1,0:T(8,128)S(1)}, f32[88,256]{1,0:T(8,128)S(1)}, u32[]{:S(2)}, u32[]{:S(2)}) %collective-permute-start) | collective-permute-done | bytes 90144 | tf_op jit(solution)/shard_map/ppermute | solution.py:488
  11.8 1.0 %collective-permute-done.1.from_east = f32[88,256]{1,0:T(8,128)S(1)} collective-permute-done((f32[88,256]{1,0:T(8,128)S(1)}, f32[88,256]{1,0:T(8,128)S(1)}, u32[]{:S(2)}, u32[]{:S(2)}) %collective-permute-start.1) | collective-permute-done | bytes 90144 | tf_op jit(solution)/shard_map/ppermute | solution.py:489
  12.8 0.2 shard_map.108
  13.0 0.2 shard_map.109.current
  13.1 0.0 collective-permute-done.2
  13.1 0.1 collective-permute-start.3
  13.2 0.0 copy-start
  13.2 2.7 %collective-permute-start.5 = (f32[1,128]{1,0:T(1,128)S(1)}, f32[1,128]{1,0:T(1,128)S(1)}, u32[]{:S(2)}, u32[]{:S(2)}) collective-permute-start(f32[1,128]{1,0:T(1,128)S(1)} %add.12), channel_id=1, source_target_pairs={{0,12},{2,14},{4,8},{6,10},{8,4},{10,6},{12,0},{14,2},{1,13},{3,15... | collective-permute-start | bytes 1544 | tf_op jit(solution)/shard_map/ppermute | solution.py:530
  15.9 0.3 %collective-permute-start.4 = (f32[1,128]{1,0:T(1,128)S(1)}, f32[1,128]{1,0:T(1,128)S(1)}, u32[]{:S(2)}, u32[]{:S(2)}) collective-permute-start(f32[1,128]{1,0:T(1,128)S(1)} %add.12), channel_id=1, source_target_pairs={{0,8},{2,10},{4,12},{6,14},{8,0},{10,2},{12,4},{14,6},{1,9},{3,11}... | collective-permute-start | bytes 1544 | tf_op jit(solution)/shard_map/ppermute | solution.py:530
  16.2 0.0 collective-permute-done.3.received
  16.2 1.5 %collective-permute-start.6 = (f32[1,128]{1,0:T(1,128)S(1)}, f32[1,128]{1,0:T(1,128)S(1)}, u32[]{:S(2)}, u32[]{:S(2)}) collective-permute-start(f32[1,128]{1,0:T(1,128)S(1)} %add.12), channel_id=1, source_target_pairs={{0,4},{2,6},{4,0},{6,2},{8,12},{10,14},{12,8},{14,10},{1,5},{3,7},... | collective-permute-start | bytes 1544 | tf_op jit(solution)/shard_map/ppermute | solution.py:530
  17.7 0.0 copy-done
  17.7 1.6 %shard_map.110 = f32[8,4,32,256]{3,2,1,0:T(8,128)} custom-call(s32[16]{0:T(128)S(1)} %copy-done, f32[8,4,32,256]{3,2,1,0:T(8,128)S(1)} %shard_map.109.current, f32[8,4,32,256]{3,2,1,0:T(8,128)S(1)} %collective-permute-done.3.received), custom_call_target="tpu_custom_call" | custom-call | bytes 2000000 | tf_op jit(solution)/shard_map/pallas_call | solution.py:534
  19.3 0.0 copy-start.1
  19.3 0.0 collective-permute-done.5
  19.3 1.1 %collective-permute-done.4 = f32[1,128]{1,0:T(1,128)S(1)} collective-permute-done((f32[1,128]{1,0:T(1,128)S(1)}, f32[1,128]{1,0:T(1,128)S(1)}, u32[]{:S(2)}, u32[]{:S(2)}) %collective-permute-start.4) | collective-permute-done | bytes 544 | tf_op jit(solution)/shard_map/ppermute | solution.py:530
  20.4 0.0 collective-permute-done.6
  20.4 0.0 copy-done.1
  20.4 0.5 %bitcast_subtract_fusion = f32[8]{0:T(128)} fusion(f32[8]{0:T(128)S(1)} %copy-done.1, f32[1,128]{1,0:T(1,128)S(1)} %add_add_fusion), kind=kLoop, calls=%fused_computation | loop fusion | flops 16 | bytes 96 | tf_op jit(solution)/shard_map/sub | solution.py:544
  (3 shorter events, 0.0 us)
Async XLA Ops:
  4.0 7.8 %collective-permute-start = (f32[88,256]{1,0:T(8,128)S(1)}, f32[88,256]{1,0:T(8,128)S(1)}, u32[]{:S(2)}, u32[]{:S(2)}) collective-permute-start(f32[88,256]{1,0:T(8,128)S(1)} %get-tuple-element.41.own_east), channel_id=1, source_target_pairs={{0,2},{2,4},{4,6},{6,8},{8,10},{10,12},{12,14},{14,0},{1,3},{3,5},... | collective-permute-start | bytes 270344 | tf_op jit(solution)/shard_map/ppermute | solution.py:488
  5.5 7.3 %collective-permute-start.1 = (f32[88,256]{1,0:T(8,128)S(1)}, f32[88,256]{1,0:T(8,128)S(1)}, u32[]{:S(2)}, u32[]{:S(2)}) collective-permute-start(f32[88,256]{1,0:T(8,128)S(1)} %get-tuple-element.42.own_west), channel_id=1, source_target_pairs={{0,14},{2,0},{4,2},{6,4},{8,6},{10,8},{12,10},{14,12},{1,15},{3,1}... | collective-permute-start | bytes 270344 | tf_op jit(solution)/shard_map/ppermute | solution.py:489
  8.7 4.4 %collective-permute-start.2 = (f32[1,128]{1,0:T(1,128)S(1)}, f32[1,128]{1,0:T(1,128)S(1)}, u32[]{:S(2)}, u32[]{:S(2)}) collective-permute-start(f32[1,128]{1,0:T(1,128)S(1)} %get-tuple-element.43.bulk_weight), channel_id=1, source_target_pairs={{0,2},{2,0},{4,6},{6,4},{8,10},{10,8},{12,14},{14,12},{1,3},{3,1},... | collective-permute-start | bytes 1544 | tf_op jit(solution)/shard_map/ppermute | solution.py:491
  13.1 3.1 %collective-permute-start.3 = (f32[8,4,32,256]{3,2,1,0:T(8,128)S(1)}, f32[8,4,32,256]{3,2,1,0:T(8,128)S(1)}, u32[]{:S(2)}, u32[]{:S(2)}) collective-permute-start(f32[8,4,32,256]{3,2,1,0:T(8,128)S(1)} %shard_map.109.current), channel_id=1, source_target_pairs={{0,1},{1,0},{2,3},{3,2},{4,5},{5,4},{6,7},{7,6},{8,9},{9,8},{10,11... | collective-permute-start | bytes 3145736 | tf_op jit(solution)/shard_map/ppermute | solution.py:522
  13.2 4.5 %copy-start = (s32[16]{0:T(128)S(1)}, s32[16]{0:T(128)}, u32[]{:S(2)}) copy-start(s32[16]{0:T(128)} %source.1) | copy-start | bytes 196
  13.2 6.1 %collective-permute-start.5 = (f32[1,128]{1,0:T(1,128)S(1)}, f32[1,128]{1,0:T(1,128)S(1)}, u32[]{:S(2)}, u32[]{:S(2)}) collective-permute-start(f32[1,128]{1,0:T(1,128)S(1)} %add.12), channel_id=1, source_target_pairs={{0,12},{2,14},{4,8},{6,10},{8,4},{10,6},{12,0},{14,2},{1,13},{3,15... | collective-permute-start | bytes 1544 | tf_op jit(solution)/shard_map/ppermute | solution.py:530
  15.9 4.4 %collective-permute-start.4 = (f32[1,128]{1,0:T(1,128)S(1)}, f32[1,128]{1,0:T(1,128)S(1)}, u32[]{:S(2)}, u32[]{:S(2)}) collective-permute-start(f32[1,128]{1,0:T(1,128)S(1)} %add.12), channel_id=1, source_target_pairs={{0,8},{2,10},{4,12},{6,14},{8,0},{10,2},{12,4},{14,6},{1,9},{3,11}... | collective-permute-start | bytes 1544 | tf_op jit(solution)/shard_map/ppermute | solution.py:530
  16.2 4.1 %collective-permute-start.6 = (f32[1,128]{1,0:T(1,128)S(1)}, f32[1,128]{1,0:T(1,128)S(1)}, u32[]{:S(2)}, u32[]{:S(2)}) collective-permute-start(f32[1,128]{1,0:T(1,128)S(1)} %add.12), channel_id=1, source_target_pairs={{0,4},{2,6},{4,0},{6,2},{8,12},{10,14},{12,8},{14,10},{1,5},{3,7},... | collective-permute-start | bytes 1544 | tf_op jit(solution)/shard_map/ppermute | solution.py:530
  19.3 1.1 %copy-start.1 = (f32[8]{0:T(128)S(1)}, f32[8]{0:T(128)}, u32[]{:S(2)}) copy-start(f32[8]{0:T(128)} %param.14) | copy-start | bytes 100

commit v19 on v18

--- a/solution.py
+++ b/solution.py
@@ -131,16 +131,15 @@
 
 
 def prepare(sizes, state_hbm, noise_hbm, courant_hbm, diffusion_hbm, mixing_hbm, cell_hbm, value_hbm,
-            send_east, send_west, state, noise, maps, courant, scalars,
+            send_east, send_west, state, noise, late_noise, maps, courant, scalars,
             diffusion, mixing, cell, value, sems):
     particles, fields, strip, lats, strips = sizes
     n = fields * particles
     copies = [pltpu.make_async_copy(source, target, sems.at[k]) for k, (source, target) in enumerate((
         (cell_hbm, cell), (value_hbm, value), (courant_hbm, courant), (diffusion_hbm, diffusion),
         (mixing_hbm, mixing), (state_hbm.at[:, :, :8], state.at[:, :, :8]),
-        (state_hbm.at[:, :, strip - 8:], state.at[:, :, strip - 8:]), (noise_hbm.at[0], noise.at[0]),
-        (noise_hbm.at[1, :, 0], noise.at[1, :, 0]), (state_hbm.at[:, :, 8:strip - 8], state.at[:, :, 8:strip - 8]),
-        (noise_hbm.at[1, :, 1:], noise.at[1, :, 1:])))]
+        (state_hbm.at[:, :, strip - 8:], state.at[:, :, strip - 8:]), (noise_hbm.at[0], noise),
+        (noise_hbm.at[1, :, 0], late_noise), (state_hbm.at[:, :, 8:strip - 8], state.at[:, :, 8:strip - 8])))]
     for copy in copies:
         copy.start()
     copies[0].wait()
@@ -211,8 +210,8 @@
     started = [first_step(0, send_east), first_step(1, send_west)]
     copies[7].wait()
     copies[8].wait()
-    rows0 = jnp.dot(pick0, noise[0].reshape(n * strip, lats), preferred_element_type=F32)
-    rows1 = jnp.dot(pick1, noise[1, :, 0].reshape(particles * strip, lats), preferred_element_type=F32)
+    rows0 = jnp.dot(pick0, noise[...].reshape(n * strip, lats), preferred_element_type=F32)
+    rows1 = jnp.dot(pick1, late_noise[...].reshape(particles * strip, lats), preferred_element_type=F32)
 
     def edge(side, out):
         x, _, step = places[side]
@@ -255,7 +254,6 @@
     edge(0, send_east)
     edge(1, send_west)
     copies[9].wait()
-    copies[10].wait()
 
 
 def zero_halo_coefs(sizes, courant, scalars, coefs):
@@ -284,7 +282,7 @@
     return moved
 
 
-def observed_bulk(sizes, parity, state, noise, maps, courant, scalars, earlier, middle, out, weight, coefs, partial):
+def observed_bulk(sizes, parity, state, noise, late_noise, maps, courant, scalars, earlier, middle, out, weight, coefs, partial):
     particles, fields, strip, lats, strips = sizes
 
     def one(p):
@@ -293,7 +291,7 @@
         results = []
         for f in range(fields):
             new = moved(values, f)
-            add = noise[0, p, f].astype(F32)
+            add = noise[p, f].astype(F32)
             if f == 0:
                 push = maps[0] * (maps[1] - new)
                 new = new + push
@@ -301,7 +299,7 @@
             results.append(new + add)
             middle[p, f] = new + add
         new = moved(results, 0)
-        add = noise[1, p, 0].astype(F32)
+        add = late_noise[p].astype(F32)
         push = maps[0] * (maps[1] - new)
         new = new + push + add
         miss = maps[1] - new
@@ -328,17 +326,22 @@
 
 
 def other_bulk(sizes, even_middle, even_observed, even_coefs, odd_middle, odd_observed, odd_coefs,
-               noise, scalars, out):
-    particles, fields, strip, lats, strips = sizes
+               noise_hbm, scalars, out, noise, sem):
+    particles, fields, strip, lats, strips = sizes
+
+    fetch = pltpu.make_async_copy(noise_hbm.at[1, :, 1:], noise, sem)
+    fetch.start()
 
     def run(middle, observed, coefs):
         moved = zero_halo_step(sizes, scalars, coefs)
+        for p in range(particles):
+            out[p, 0] = observed[p]
+        fetch.wait()
 
         def body(p, carry):
             values = [middle[p, f] for f in range(fields)]
-            out[p, 0] = observed[p]
             for f in range(1, fields):
-                out[p, f] = moved(values, f) + noise[1, p, f].astype(F32)
+                out[p, f] = moved(values, f) + noise[p, f - 1].astype(F32)
             return carry
 
         lax.fori_loop(0, particles, body, 0)
@@ -458,14 +461,15 @@
         return pltpu.with_memory_space_constraint(array, pltpu.HBM)
 
     arrays = (ensemble_state, proposal_noise, courant, diffusion[None], mixing, cell, value)
-    send_east, send_west, state, noise, maps, courant, scalars = pl.pallas_call(
+    send_east, send_west, state, noise, late_noise, maps, courant, scalars = pl.pallas_call(
         functools.partial(prepare, sizes),
-        out_shape=(packet, packet, shape(*whole), jax.ShapeDtypeStruct((2,) + whole, BF16), shape(2, strip, lats),
+        out_shape=(packet, packet, shape(*whole), jax.ShapeDtypeStruct(whole, BF16),
+                   jax.ShapeDtypeStruct((particles, strip, lats), BF16), shape(2, strip, lats),
                    shape(*courant.shape), shape(fields * (fields + 2), lats)),
         in_specs=[HBM] * 7,
-        out_specs=(VMEM,) * 7,
+        out_specs=(VMEM,) * 8,
         scratch_shapes=[pltpu.VMEM(array.shape, array.dtype) for array in arrays[3:]]
-        + [pltpu.SemaphoreType.DMA((11,))],
+        + [pltpu.SemaphoreType.DMA((10,))],
         compiler_params=LIMIT,
         cost_estimate=pl.CostEstimate(flops=1000000, bytes_accessed=2000000, transcendentals=0),
     )(*[in_hbm(array) for array in arrays])
@@ -474,12 +478,12 @@
         return pl.pallas_call(
             functools.partial(observed_bulk, sizes, parity),
             out_shape=(shape(*whole), shape(particles, strip, lats), shape(1, 128), shape(fields, 5, strip, lats)),
-            in_specs=[VMEM] * 6,
+            in_specs=[VMEM] * 7,
             out_specs=(VMEM,) * 4,
             scratch_shapes=[pltpu.VMEM((particles, 128), F32)],
             compiler_params=LIMIT,
             cost_estimate=pl.CostEstimate(flops=20000000, bytes_accessed=4000000, transcendentals=0),
-        )(state, noise, maps, courant, scalars, earlier)
+        )(state, noise, late_noise, maps, courant, scalars, earlier)
 
     even_middle, even_observed, bulk_weight, even_coefs = bulk_of(0, scalars)
     send_east, send_west, bulk_weight = lax.optimization_barrier((send_east, send_west, bulk_weight))
@@ -493,11 +497,12 @@
     current = pl.pallas_call(
         functools.partial(other_bulk, sizes),
         out_shape=shape(*whole),
-        in_specs=[VMEM] * 8,
+        in_specs=[VMEM] * 6 + [HBM, VMEM],
+        scratch_shapes=[pltpu.VMEM((particles, fields - 1, strip, lats), BF16), pltpu.SemaphoreType.DMA],
         out_specs=VMEM,
         compiler_params=LIMIT,
         cost_estimate=FREE,
-    )(even_middle, even_observed, even_coefs, odd_middle, odd_observed, odd_coefs, noise, scalars)
+    )(even_middle, even_observed, even_coefs, odd_middle, odd_observed, odd_coefs, in_hbm(proposal_noise), scalars)
 
     weight, changes = pl.pallas_call(
         functools.partial(correct, sizes),

time: 21.1 us -> 21 us (level)
  waiting for transfers between devices: 2.75 us -> 1.76 us
  Pallas kernels: 6.33 us -> 7.3 us
    pallas_call x1, Pallas kernels: 1.04 us -> 2.05 us  [local(): pl.pallas_call(functools.partial(other_bulk, sizes), out_shape=shape(*who...]
    ppermute x1, waiting for transfers between devices: 0.7 us -> 0.01 us  [local(): from_west = lax.ppermute(send_east, 'lon', eastward)]
    ppermute x1, waiting for transfers between devices: 0.98 us -> 0.69 us  [local(): from_east = lax.ppermute(send_west, 'lon', westward)]
  transfers between devices with their start and end apart: 7 -> 7, of which waited for: 3 -> 2; matrix products, arithmetic and copies ran while one was open for 0% -> 0% of each run, Pallas kernels for 14% -> 19%
where the time goes in v19:
time: 21 us; the launch traced here: 20.9 us
  starting transfers between devices  10.5 us (50%)
  Pallas kernels  7.3 us (35%)
  waiting for transfers between devices  1.76 us (8%)
  between operations  0.73 us (3%)
  other arithmetic  0.52 us (2%)
    ppermute x3, starting transfers between devices, local(): lax.ppermute(weight, 'lon', [(i, i ^ bit * step) for i in range(strips)])  4.45 us
    ppermute x1, starting transfers between devices, local(): from_east = lax.ppermute(send_west, 'lon', westward)  3.23 us
    pallas_call x1, Pallas kernels, local(): pl.pallas_call(functools.partial(other_bulk, sizes), out_shape=shape(*who...  2.05 us
    pallas_call x1, Pallas kernels, local(): pl.pallas_call(functools.partial(prepare, sizes), out_shape=(packet, pack...  1.79 us
    pallas_call x1, Pallas kernels, local(): pl.pallas_call(functools.partial(assemble, sizes), out_shape=shape(*whole...  1.58 us
    pallas_call x2, Pallas kernels, bulk_of(): pl.pallas_call(functools.partial(observed_bulk, sizes, parity), out_shape...  1.53 us
    ppermute x1, starting transfers between devices, local(): from_west = lax.ppermute(send_east, 'lon', eastward)  1.5 us
    ppermute x1, starting transfers between devices, local(): lax.ppermute(bulk_weight, 'lon', [(i, i ^ 1) for i in range(strips)])  1.28 us
  transfers between devices with their start and end apart: 7, of which 2 were waited for; matrix products, arithmetic and copies ran while one was open for 0% of the time, Pallas kernels for 19%

profile of v19, /device:TPU:0, one launch (start us, length us, event | category | flops | bytes accessed | tf_op | source)
XLA Modules:
  0.0 20.9 jit_solution(11690950700663749410)
XLA Ops:
  0.6 1.8 %shard_map.104 = (f32[88,256]{1,0:T(8,128)S(1)}, f32[88,256]{1,0:T(8,128)S(1)}, f32[8,4,32,256]{3,2,1,0:T(8,128)S(1)}, bf16[8,4,32,256]{3,2,1,0:T(8,128)(2,1)S(1...) custom-call(f32[8,4,32,256]{3,2,1,0:T(8,128)} %state_hbm.1, ...), custom_call_target="tpu_custom_call" | custom-call | flops 1000000 | bytes 2000000 | tf_op jit(solution)/shard_map/pallas_call | solution.py:464
  2.4 1.5 %shard_map.105 = (f32[8,4,32,256]{3,2,1,0:T(8,128)S(1)}, f32[8,32,256]{2,1,0:T(8,128)S(1)}, f32[1,128]{1,0:T(1,128)S(1)}, f32[4,5,32,256]{3,2,1,0:T(8,128)S(1)}) custom-call(f32[8,4,32,256]{3,2,1,0:T(8,128)S(1)} %get-tuple-element.27.state, bf16[8,4,32,256]{3,2,1,0:T(8,128)(2,1)S(1)} %get-tuple-element.28.noise, ...), custom_call_target="tpu_custom_call" | custom-call | flops 20000000 | bytes 4000000 | tf_op jit(solution)/shard_map/pallas_call | solution.py:478
  4.0 1.5 %collective-permute-start = (f32[88,256]{1,0:T(8,128)S(1)}, f32[88,256]{1,0:T(8,128)S(1)}, u32[]{:S(2)}, u32[]{:S(2)}) collective-permute-start(f32[88,256]{1,0:T(8,128)S(1)} %get-tuple-element.43.own_east), channel_id=1, source_target_pairs={{0,2},{2,4},{4,6},{6,8},{8,10},{10,12},{12,14},{14,0},{1,3},{3,5},... | collective-permute-start | bytes 270344 | tf_op jit(solution)/shard_map/ppermute | solution.py:492
  5.5 3.2 %collective-permute-start.1 = (f32[88,256]{1,0:T(8,128)S(1)}, f32[88,256]{1,0:T(8,128)S(1)}, u32[]{:S(2)}, u32[]{:S(2)}) collective-permute-start(f32[88,256]{1,0:T(8,128)S(1)} %get-tuple-element.44.own_west), channel_id=1, source_target_pairs={{0,14},{2,0},{4,2},{6,4},{8,6},{10,8},{12,10},{14,12},{1,15},{3,1}... | collective-permute-start | bytes 270344 | tf_op jit(solution)/shard_map/ppermute | solution.py:493
  8.7 1.3 %collective-permute-start.2 = (f32[1,128]{1,0:T(1,128)S(1)}, f32[1,128]{1,0:T(1,128)S(1)}, u32[]{:S(2)}, u32[]{:S(2)}) collective-permute-start(f32[1,128]{1,0:T(1,128)S(1)} %get-tuple-element.45.bulk_weight), channel_id=1, source_target_pairs={{0,2},{2,0},{4,6},{6,4},{8,10},{10,8},{12,14},{14,12},{1,3},{3,1},... | collective-permute-start | bytes 1544 | tf_op jit(solution)/shard_map/ppermute | solution.py:495
  10.0 2.0 %shard_map.107.current = f32[8,4,32,256]{3,2,1,0:T(8,128)S(1)} custom-call(f32[8,4,32,256]{3,2,1,0:T(8,128)S(1)} %get-tuple-element.33.even_middle, f32[8,32,256]{2,1,0:T(8,128)S(1)} %get-tuple-element.34.even_observed, f32[4,5,32,256]{3,2,1,0:T(8,128)S(1)} %get-tuple-element.35.even_coefs, f32[8,4,32,256]{3,2,1,0:T(8,128)S(1)} %get-tuple-element.40.odd_middle, ...), custom_call_target="tpu_custom_call" | custom-call | tf_op jit(solution)/shard_map/pallas_call | solution.py:497
  12.0 0.0 collective-permute-done.from_west
  12.0 0.7 %collective-permute-done.1.from_east = f32[88,256]{1,0:T(8,128)S(1)} collective-permute-done((f32[88,256]{1,0:T(8,128)S(1)}, f32[88,256]{1,0:T(8,128)S(1)}, u32[]{:S(2)}, u32[]{:S(2)}) %collective-permute-start.1) | collective-permute-done | bytes 90144 | tf_op jit(solution)/shard_map/ppermute | solution.py:493
  12.7 0.2 shard_map.108
  12.9 0.2 shard_map.109.current
  13.1 0.0 collective-permute-done.2
  13.1 0.1 collective-permute-start.3
  13.2 0.0 copy-start
  13.2 2.7 %collective-permute-start.5 = (f32[1,128]{1,0:T(1,128)S(1)}, f32[1,128]{1,0:T(1,128)S(1)}, u32[]{:S(2)}, u32[]{:S(2)}) collective-permute-start(f32[1,128]{1,0:T(1,128)S(1)} %add.12), channel_id=1, source_target_pairs={{0,12},{2,14},{4,8},{6,10},{8,4},{10,6},{12,0},{14,2},{1,13},{3,15... | collective-permute-start | bytes 1544 | tf_op jit(solution)/shard_map/ppermute | solution.py:535
  15.9 0.3 %collective-permute-start.4 = (f32[1,128]{1,0:T(1,128)S(1)}, f32[1,128]{1,0:T(1,128)S(1)}, u32[]{:S(2)}, u32[]{:S(2)}) collective-permute-start(f32[1,128]{1,0:T(1,128)S(1)} %add.12), channel_id=1, source_target_pairs={{0,8},{2,10},{4,12},{6,14},{8,0},{10,2},{12,4},{14,6},{1,9},{3,11}... | collective-permute-start | bytes 1544 | tf_op jit(solution)/shard_map/ppermute | solution.py:535
  16.2 0.0 collective-permute-done.3.received
  16.2 1.5 %collective-permute-start.6 = (f32[1,128]{1,0:T(1,128)S(1)}, f32[1,128]{1,0:T(1,128)S(1)}, u32[]{:S(2)}, u32[]{:S(2)}) collective-permute-start(f32[1,128]{1,0:T(1,128)S(1)} %add.12), channel_id=1, source_target_pairs={{0,4},{2,6},{4,0},{6,2},{8,12},{10,14},{12,8},{14,10},{1,5},{3,7},... | collective-permute-start | bytes 1544 | tf_op jit(solution)/shard_map/ppermute | solution.py:535
  17.6 0.0 copy-done
  17.6 1.6 %shard_map.110 = f32[8,4,32,256]{3,2,1,0:T(8,128)} custom-call(s32[16]{0:T(128)S(1)} %copy-done, f32[8,4,32,256]{3,2,1,0:T(8,128)S(1)} %shard_map.109.current, f32[8,4,32,256]{3,2,1,0:T(8,128)S(1)} %collective-permute-done.3.received), custom_call_target="tpu_custom_call" | custom-call | bytes 2000000 | tf_op jit(solution)/shard_map/pallas_call | solution.py:539
  19.2 0.0 copy-start.1
  19.2 0.0 collective-permute-done.5
  19.3 1.1 %collective-permute-done.4 = f32[1,128]{1,0:T(1,128)S(1)} collective-permute-done((f32[1,128]{1,0:T(1,128)S(1)}, f32[1,128]{1,0:T(1,128)S(1)}, u32[]{:S(2)}, u32[]{:S(2)}) %collective-permute-start.4) | collective-permute-done | bytes 544 | tf_op jit(solution)/shard_map/ppermute | solution.py:535
  20.3 0.0 collective-permute-done.6
  20.3 0.0 copy-done.1
  20.3 0.5 %bitcast_subtract_fusion = f32[8]{0:T(128)} fusion(f32[8]{0:T(128)S(1)} %copy-done.1, f32[1,128]{1,0:T(1,128)S(1)} %add_add_fusion), kind=kLoop, calls=%fused_computation | loop fusion | flops 16 | bytes 96 | tf_op jit(solution)/shard_map/sub | solution.py:549
  (3 shorter events, 0.0 us)
Async XLA Ops:
  4.0 8.1 %collective-permute-start = (f32[88,256]{1,0:T(8,128)S(1)}, f32[88,256]{1,0:T(8,128)S(1)}, u32[]{:S(2)}, u32[]{:S(2)}) collective-permute-start(f32[88,256]{1,0:T(8,128)S(1)} %get-tuple-element.43.own_east), channel_id=1, source_target_pairs={{0,2},{2,4},{4,6},{6,8},{8,10},{10,12},{12,14},{14,0},{1,3},{3,5},... | collective-permute-start | bytes 270344 | tf_op jit(solution)/shard_map/ppermute | solution.py:492
  5.5 7.3 %collective-permute-start.1 = (f32[88,256]{1,0:T(8,128)S(1)}, f32[88,256]{1,0:T(8,128)S(1)}, u32[]{:S(2)}, u32[]{:S(2)}) collective-permute-start(f32[88,256]{1,0:T(8,128)S(1)} %get-tuple-element.44.own_west), channel_id=1, source_target_pairs={{0,14},{2,0},{4,2},{6,4},{8,6},{10,8},{12,10},{14,12},{1,15},{3,1}... | collective-permute-start | bytes 270344 | tf_op jit(solution)/shard_map/ppermute | solution.py:493
  8.7 4.4 %collective-permute-start.2 = (f32[1,128]{1,0:T(1,128)S(1)}, f32[1,128]{1,0:T(1,128)S(1)}, u32[]{:S(2)}, u32[]{:S(2)}) collective-permute-start(f32[1,128]{1,0:T(1,128)S(1)} %get-tuple-element.45.bulk_weight), channel_id=1, source_target_pairs={{0,2},{2,0},{4,6},{6,4},{8,10},{10,8},{12,14},{14,12},{1,3},{3,1},... | collective-permute-start | bytes 1544 | tf_op jit(solution)/shard_map/ppermute | solution.py:495
  13.1 3.1 %collective-permute-start.3 = (f32[8,4,32,256]{3,2,1,0:T(8,128)S(1)}, f32[8,4,32,256]{3,2,1,0:T(8,128)S(1)}, u32[]{:S(2)}, u32[]{:S(2)}) collective-permute-start(f32[8,4,32,256]{3,2,1,0:T(8,128)S(1)} %shard_map.109.current), channel_id=1, source_target_pairs={{0,1},{1,0},{2,3},{3,2},{4,5},{5,4},{6,7},{7,6},{8,9},{9,8},{10,11... | collective-permute-start | bytes 3145736 | tf_op jit(solution)/shard_map/ppermute | solution.py:527
  13.2 4.5 %copy-start = (s32[16]{0:T(128)S(1)}, s32[16]{0:T(128)}, u32[]{:S(2)}) copy-start(s32[16]{0:T(128)} %source.1) | copy-start | bytes 196
  13.2 6.1 %collective-permute-start.5 = (f32[1,128]{1,0:T(1,128)S(1)}, f32[1,128]{1,0:T(1,128)S(1)}, u32[]{:S(2)}, u32[]{:S(2)}) collective-permute-start(f32[1,128]{1,0:T(1,128)S(1)} %add.12), channel_id=1, source_target_pairs={{0,12},{2,14},{4,8},{6,10},{8,4},{10,6},{12,0},{14,2},{1,13},{3,15... | collective-permute-start | bytes 1544 | tf_op jit(solution)/shard_map/ppermute | solution.py:535
  15.9 4.4 %collective-permute-start.4 = (f32[1,128]{1,0:T(1,128)S(1)}, f32[1,128]{1,0:T(1,128)S(1)}, u32[]{:S(2)}, u32[]{:S(2)}) collective-permute-start(f32[1,128]{1,0:T(1,128)S(1)} %add.12), channel_id=1, source_target_pairs={{0,8},{2,10},{4,12},{6,14},{8,0},{10,2},{12,4},{14,6},{1,9},{3,11}... | collective-permute-start | bytes 1544 | tf_op jit(solution)/shard_map/ppermute | solution.py:535
  16.2 4.1 %collective-permute-start.6 = (f32[1,128]{1,0:T(1,128)S(1)}, f32[1,128]{1,0:T(1,128)S(1)}, u32[]{:S(2)}, u32[]{:S(2)}) collective-permute-start(f32[1,128]{1,0:T(1,128)S(1)} %add.12), channel_id=1, source_target_pairs={{0,4},{2,6},{4,0},{6,2},{8,12},{10,14},{12,8},{14,10},{1,5},{3,7},... | collective-permute-start | bytes 1544 | tf_op jit(solution)/shard_map/ppermute | solution.py:535
  19.2 1.1 %copy-start.1 = (f32[8]{0:T(128)S(1)}, f32[8]{0:T(128)}, u32[]{:S(2)}) copy-start(f32[8]{0:T(128)} %param.14) | copy-start | bytes 100

commit v20 on v19

--- a/solution.py
+++ b/solution.py
@@ -135,10 +135,13 @@
             diffusion, mixing, cell, value, sems):
     particles, fields, strip, lats, strips = sizes
     n = fields * particles
+    quarter = particles // 4
+    noise_parts = [(noise_hbm.at[0, at:at + quarter], noise.at[at:at + quarter])
+                   for at in range(0, particles, quarter)]
     copies = [pltpu.make_async_copy(source, target, sems.at[k]) for k, (source, target) in enumerate((
         (cell_hbm, cell), (value_hbm, value), (courant_hbm, courant), (diffusion_hbm, diffusion),
         (mixing_hbm, mixing), (state_hbm.at[:, :, :8], state.at[:, :, :8]),
-        (state_hbm.at[:, :, strip - 8:], state.at[:, :, strip - 8:]), (noise_hbm.at[0], noise),
+        (state_hbm.at[:, :, strip - 8:], state.at[:, :, strip - 8:]), *noise_parts,
         (noise_hbm.at[1, :, 0], late_noise), (state_hbm.at[:, :, 8:strip - 8], state.at[:, :, 8:strip - 8])))]
     for copy in copies:
         copy.start()
@@ -208,8 +211,8 @@
     copies[5].wait()
     copies[6].wait()
     started = [first_step(0, send_east), first_step(1, send_west)]
-    copies[7].wait()
-    copies[8].wait()
+    for copy in copies[7:12]:
+        copy.wait()
     rows0 = jnp.dot(pick0, noise[...].reshape(n * strip, lats), preferred_element_type=F32)
     rows1 = jnp.dot(pick1, late_noise[...].reshape(particles * strip, lats), preferred_element_type=F32)
 
@@ -253,7 +256,7 @@
 
     edge(0, send_east)
     edge(1, send_west)
-    copies[9].wait()
+    copies[12].wait()
 
 
 def zero_halo_coefs(sizes, courant, scalars, coefs):
@@ -469,7 +472,7 @@
         in_specs=[HBM] * 7,
         out_specs=(VMEM,) * 8,
         scratch_shapes=[pltpu.VMEM(array.shape, array.dtype) for array in arrays[3:]]
-        + [pltpu.SemaphoreType.DMA((10,))],
+        + [pltpu.SemaphoreType.DMA((13,))],
         compiler_params=LIMIT,
         cost_estimate=pl.CostEstimate(flops=1000000, bytes_accessed=2000000, transcendentals=0),
     )(*[in_hbm(array) for array in arrays])

time: 21 us -> 21.1 us (level)
  no operation moved by 1% of the time
where the time goes in v20:
time: 21.1 us; the launch traced here: 20.9 us
  starting transfers between devices  10.5 us (50%)
  Pallas kernels  7.33 us (35%)
  waiting for transfers between devices  1.76 us (8%)
  between operations  0.73 us (3%)
  other arithmetic  0.52 us (2%)
    ppermute x3, starting transfers between devices, local(): lax.ppermute(weight, 'lon', [(i, i ^ bit * step) for i in range(strips)])  4.45 us
    ppermute x1, starting transfers between devices, local(): from_east = lax.ppermute(send_west, 'lon', westward)  3.23 us
    pallas_call x1, Pallas kernels, local(): pl.pallas_call(functools.partial(other_bulk, sizes), out_shape=shape(*who...  2.05 us
    pallas_call x1, Pallas kernels, local(): pl.pallas_call(functools.partial(prepare, sizes), out_shape=(packet, pack...  1.83 us
    pallas_call x1, Pallas kernels, local(): pl.pallas_call(functools.partial(assemble, sizes), out_shape=shape(*whole...  1.58 us
    pallas_call x2, Pallas kernels, bulk_of(): pl.pallas_call(functools.partial(observed_bulk, sizes, parity), out_shape...  1.53 us
    ppermute x1, starting transfers between devices, local(): from_west = lax.ppermute(send_east, 'lon', eastward)  1.5 us
    ppermute x1, starting transfers between devices, local(): lax.ppermute(bulk_weight, 'lon', [(i, i ^ 1) for i in range(strips)])  1.28 us
  transfers between devices with their start and end apart: 7, of which 2 were waited for; matrix products, arithmetic and copies ran while one was open for 0% of the time, Pallas kernels for 19%

profile of v20, /device:TPU:0, one launch (start us, length us, event | category | flops | bytes accessed | tf_op | source)
XLA Modules:
  0.0 20.9 jit_solution(12639589964555908262)
XLA Ops:
  0.6 1.8 %shard_map.104 = (f32[88,256]{1,0:T(8,128)S(1)}, f32[88,256]{1,0:T(8,128)S(1)}, f32[8,4,32,256]{3,2,1,0:T(8,128)S(1)}, bf16[8,4,32,256]{3,2,1,0:T(8,128)(2,1)S(1...) custom-call(f32[8,4,32,256]{3,2,1,0:T(8,128)} %state_hbm.1, ...), custom_call_target="tpu_custom_call" | custom-call | flops 1000000 | bytes 2000000 | tf_op jit(solution)/shard_map/pallas_call | solution.py:467
  2.5 1.5 %shard_map.105 = (f32[8,4,32,256]{3,2,1,0:T(8,128)S(1)}, f32[8,32,256]{2,1,0:T(8,128)S(1)}, f32[1,128]{1,0:T(1,128)S(1)}, f32[4,5,32,256]{3,2,1,0:T(8,128)S(1)}) custom-call(f32[8,4,32,256]{3,2,1,0:T(8,128)S(1)} %get-tuple-element.27.state, bf16[8,4,32,256]{3,2,1,0:T(8,128)(2,1)S(1)} %get-tuple-element.28.noise, ...), custom_call_target="tpu_custom_call" | custom-call | flops 20000000 | bytes 4000000 | tf_op jit(solution)/shard_map/pallas_call | solution.py:481
  4.0 1.5 %collective-permute-start = (f32[88,256]{1,0:T(8,128)S(1)}, f32[88,256]{1,0:T(8,128)S(1)}, u32[]{:S(2)}, u32[]{:S(2)}) collective-permute-start(f32[88,256]{1,0:T(8,128)S(1)} %get-tuple-element.43.own_east), channel_id=1, source_target_pairs={{0,2},{2,4},{4,6},{6,8},{8,10},{10,12},{12,14},{14,0},{1,3},{3,5},... | collective-permute-start | bytes 270344 | tf_op jit(solution)/shard_map/ppermute | solution.py:495
  5.5 3.2 %collective-permute-start.1 = (f32[88,256]{1,0:T(8,128)S(1)}, f32[88,256]{1,0:T(8,128)S(1)}, u32[]{:S(2)}, u32[]{:S(2)}) collective-permute-start(f32[88,256]{1,0:T(8,128)S(1)} %get-tuple-element.44.own_west), channel_id=1, source_target_pairs={{0,14},{2,0},{4,2},{6,4},{8,6},{10,8},{12,10},{14,12},{1,15},{3,1}... | collective-permute-start | bytes 270344 | tf_op jit(solution)/shard_map/ppermute | solution.py:496
  8.7 1.3 %collective-permute-start.2 = (f32[1,128]{1,0:T(1,128)S(1)}, f32[1,128]{1,0:T(1,128)S(1)}, u32[]{:S(2)}, u32[]{:S(2)}) collective-permute-start(f32[1,128]{1,0:T(1,128)S(1)} %get-tuple-element.45.bulk_weight), channel_id=1, source_target_pairs={{0,2},{2,0},{4,6},{6,4},{8,10},{10,8},{12,14},{14,12},{1,3},{3,1},... | collective-permute-start | bytes 1544 | tf_op jit(solution)/shard_map/ppermute | solution.py:498
  10.0 2.0 %shard_map.107.current = f32[8,4,32,256]{3,2,1,0:T(8,128)S(1)} custom-call(f32[8,4,32,256]{3,2,1,0:T(8,128)S(1)} %get-tuple-element.33.even_middle, f32[8,32,256]{2,1,0:T(8,128)S(1)} %get-tuple-element.34.even_observed, f32[4,5,32,256]{3,2,1,0:T(8,128)S(1)} %get-tuple-element.35.even_coefs, f32[8,4,32,256]{3,2,1,0:T(8,128)S(1)} %get-tuple-element.40.odd_middle, ...), custom_call_target="tpu_custom_call" | custom-call | tf_op jit(solution)/shard_map/pallas_call | solution.py:500
  12.1 0.0 collective-permute-done.from_west
  12.1 0.7 %collective-permute-done.1.from_east = f32[88,256]{1,0:T(8,128)S(1)} collective-permute-done((f32[88,256]{1,0:T(8,128)S(1)}, f32[88,256]{1,0:T(8,128)S(1)}, u32[]{:S(2)}, u32[]{:S(2)}) %collective-permute-start.1) | collective-permute-done | bytes 90144 | tf_op jit(solution)/shard_map/ppermute | solution.py:496
  12.8 0.2 shard_map.108
  12.9 0.2 shard_map.109.current
  13.1 0.0 collective-permute-done.2
  13.1 0.1 collective-permute-start.3
  13.2 0.0 copy-start
  13.2 2.7 %collective-permute-start.5 = (f32[1,128]{1,0:T(1,128)S(1)}, f32[1,128]{1,0:T(1,128)S(1)}, u32[]{:S(2)}, u32[]{:S(2)}) collective-permute-start(f32[1,128]{1,0:T(1,128)S(1)} %add.12), channel_id=1, source_target_pairs={{0,12},{2,14},{4,8},{6,10},{8,4},{10,6},{12,0},{14,2},{1,13},{3,15... | collective-permute-start | bytes 1544 | tf_op jit(solution)/shard_map/ppermute | solution.py:538
  15.9 0.3 %collective-permute-start.4 = (f32[1,128]{1,0:T(1,128)S(1)}, f32[1,128]{1,0:T(1,128)S(1)}, u32[]{:S(2)}, u32[]{:S(2)}) collective-permute-start(f32[1,128]{1,0:T(1,128)S(1)} %add.12), channel_id=1, source_target_pairs={{0,8},{2,10},{4,12},{6,14},{8,0},{10,2},{12,4},{14,6},{1,9},{3,11}... | collective-permute-start | bytes 1544 | tf_op jit(solution)/shard_map/ppermute | solution.py:538
  16.2 0.0 collective-permute-done.3.received
  16.2 1.5 %collective-permute-start.6 = (f32[1,128]{1,0:T(1,128)S(1)}, f32[1,128]{1,0:T(1,128)S(1)}, u32[]{:S(2)}, u32[]{:S(2)}) collective-permute-start(f32[1,128]{1,0:T(1,128)S(1)} %add.12), channel_id=1, source_target_pairs={{0,4},{2,6},{4,0},{6,2},{8,12},{10,14},{12,8},{14,10},{1,5},{3,7},... | collective-permute-start | bytes 1544 | tf_op jit(solution)/shard_map/ppermute | solution.py:538
  17.7 0.0 copy-done
  17.7 1.6 %shard_map.110 = f32[8,4,32,256]{3,2,1,0:T(8,128)} custom-call(s32[16]{0:T(128)S(1)} %copy-done, f32[8,4,32,256]{3,2,1,0:T(8,128)S(1)} %shard_map.109.current, f32[8,4,32,256]{3,2,1,0:T(8,128)S(1)} %collective-permute-done.3.received), custom_call_target="tpu_custom_call" | custom-call | bytes 2000000 | tf_op jit(solution)/shard_map/pallas_call | solution.py:542
  19.3 0.0 copy-start.1
  19.3 0.0 collective-permute-done.5
  19.3 1.1 %collective-permute-done.4 = f32[1,128]{1,0:T(1,128)S(1)} collective-permute-done((f32[1,128]{1,0:T(1,128)S(1)}, f32[1,128]{1,0:T(1,128)S(1)}, u32[]{:S(2)}, u32[]{:S(2)}) %collective-permute-start.4) | collective-permute-done | bytes 544 | tf_op jit(solution)/shard_map/ppermute | solution.py:538
  20.4 0.0 collective-permute-done.6
  20.4 0.0 copy-done.1
  20.4 0.5 %bitcast_subtract_fusion = f32[8]{0:T(128)} fusion(f32[8]{0:T(128)S(1)} %copy-done.1, f32[1,128]{1,0:T(1,128)S(1)} %add_add_fusion), kind=kLoop, calls=%fused_computation | loop fusion | flops 16 | bytes 96 | tf_op jit(solution)/shard_map/sub | solution.py:552
  (3 shorter events, 0.0 us)
Async XLA Ops:
  4.0 8.1 %collective-permute-start = (f32[88,256]{1,0:T(8,128)S(1)}, f32[88,256]{1,0:T(8,128)S(1)}, u32[]{:S(2)}, u32[]{:S(2)}) collective-permute-start(f32[88,256]{1,0:T(8,128)S(1)} %get-tuple-element.43.own_east), channel_id=1, source_target_pairs={{0,2},{2,4},{4,6},{6,8},{8,10},{10,12},{12,14},{14,0},{1,3},{3,5},... | collective-permute-start | bytes 270344 | tf_op jit(solution)/shard_map/ppermute | solution.py:495
  5.5 7.3 %collective-permute-start.1 = (f32[88,256]{1,0:T(8,128)S(1)}, f32[88,256]{1,0:T(8,128)S(1)}, u32[]{:S(2)}, u32[]{:S(2)}) collective-permute-start(f32[88,256]{1,0:T(8,128)S(1)} %get-tuple-element.44.own_west), channel_id=1, source_target_pairs={{0,14},{2,0},{4,2},{6,4},{8,6},{10,8},{12,10},{14,12},{1,15},{3,1}... | collective-permute-start | bytes 270344 | tf_op jit(solution)/shard_map/ppermute | solution.py:496
  8.7 4.4 %collective-permute-start.2 = (f32[1,128]{1,0:T(1,128)S(1)}, f32[1,128]{1,0:T(1,128)S(1)}, u32[]{:S(2)}, u32[]{:S(2)}) collective-permute-start(f32[1,128]{1,0:T(1,128)S(1)} %get-tuple-element.45.bulk_weight), channel_id=1, source_target_pairs={{0,2},{2,0},{4,6},{6,4},{8,10},{10,8},{12,14},{14,12},{1,3},{3,1},... | collective-permute-start | bytes 1544 | tf_op jit(solution)/shard_map/ppermute | solution.py:498
  13.1 3.1 %collective-permute-start.3 = (f32[8,4,32,256]{3,2,1,0:T(8,128)S(1)}, f32[8,4,32,256]{3,2,1,0:T(8,128)S(1)}, u32[]{:S(2)}, u32[]{:S(2)}) collective-permute-start(f32[8,4,32,256]{3,2,1,0:T(8,128)S(1)} %shard_map.109.current), channel_id=1, source_target_pairs={{0,1},{1,0},{2,3},{3,2},{4,5},{5,4},{6,7},{7,6},{8,9},{9,8},{10,11... | collective-permute-start | bytes 3145736 | tf_op jit(solution)/shard_map/ppermute | solution.py:530
  13.2 4.5 %copy-start = (s32[16]{0:T(128)S(1)}, s32[16]{0:T(128)}, u32[]{:S(2)}) copy-start(s32[16]{0:T(128)} %source.1) | copy-start | bytes 196
  13.2 6.1 %collective-permute-start.5 = (f32[1,128]{1,0:T(1,128)S(1)}, f32[1,128]{1,0:T(1,128)S(1)}, u32[]{:S(2)}, u32[]{:S(2)}) collective-permute-start(f32[1,128]{1,0:T(1,128)S(1)} %add.12), channel_id=1, source_target_pairs={{0,12},{2,14},{4,8},{6,10},{8,4},{10,6},{12,0},{14,2},{1,13},{3,15... | collective-permute-start | bytes 1544 | tf_op jit(solution)/shard_map/ppermute | solution.py:538
  15.9 4.4 %collective-permute-start.4 = (f32[1,128]{1,0:T(1,128)S(1)}, f32[1,128]{1,0:T(1,128)S(1)}, u32[]{:S(2)}, u32[]{:S(2)}) collective-permute-start(f32[1,128]{1,0:T(1,128)S(1)} %add.12), channel_id=1, source_target_pairs={{0,8},{2,10},{4,12},{6,14},{8,0},{10,2},{12,4},{14,6},{1,9},{3,11}... | collective-permute-start | bytes 1544 | tf_op jit(solution)/shard_map/ppermute | solution.py:538
  16.2 4.1 %collective-permute-start.6 = (f32[1,128]{1,0:T(1,128)S(1)}, f32[1,128]{1,0:T(1,128)S(1)}, u32[]{:S(2)}, u32[]{:S(2)}) collective-permute-start(f32[1,128]{1,0:T(1,128)S(1)} %add.12), channel_id=1, source_target_pairs={{0,4},{2,6},{4,0},{6,2},{8,12},{10,14},{12,8},{14,10},{1,5},{3,7},... | collective-permute-start | bytes 1544 | tf_op jit(solution)/shard_map/ppermute | solution.py:538
  19.3 1.1 %copy-start.1 = (f32[8]{0:T(128)S(1)}, f32[8]{0:T(128)}, u32[]{:S(2)}) copy-start(f32[8]{0:T(128)} %param.14) | copy-start | bytes 100

commit v21 on v19

--- a/solution.py
+++ b/solution.py
@@ -307,17 +307,13 @@
         out[p] = new
         partial[pl.ds(p, 1), :] = wide(jnp.sum(total, axis=0, keepdims=True))
 
-    def body(step, carry):
-        for k in range(4):
-            one(4 * step + k)
-        return carry
-
     here = lax.axis_index("lon") % 2 == parity
 
     @pl.when(here)
     def _():
         zero_halo_coefs(sizes, courant, scalars, coefs)
-        lax.fori_loop(0, particles // 4, body, 0)
+        for p in range(particles):
+            one(p)
         weight[...] = in_row(partial[...])
 
     @pl.when(jnp.logical_not(here))

time: 21 us -> 20.9 us (level)
  no operation moved by 1% of the time
where the time goes in v21:
time: 20.9 us; the launch traced here: 20.8 us
  starting transfers between devices  10.4 us (50%)
  Pallas kernels  7.2 us (34%)
  waiting for transfers between devices  1.84 us (9%)
  between operations  0.73 us (3%)
  other arithmetic  0.52 us (2%)
    ppermute x3, starting transfers between devices, local(): lax.ppermute(weight, 'lon', [(i, i ^ bit * step) for i in range(strips)])  4.45 us
    ppermute x1, starting transfers between devices, local(): from_east = lax.ppermute(send_west, 'lon', westward)  3.13 us
    pallas_call x1, Pallas kernels, local(): pl.pallas_call(functools.partial(other_bulk, sizes), out_shape=shape(*who...  2.05 us
    pallas_call x1, Pallas kernels, local(): pl.pallas_call(functools.partial(prepare, sizes), out_shape=(packet, pack...  1.79 us
    ppermute x1, starting transfers between devices, local(): from_west = lax.ppermute(send_east, 'lon', eastward)  1.59 us
    pallas_call x1, Pallas kernels, local(): pl.pallas_call(functools.partial(assemble, sizes), out_shape=shape(*whole...  1.58 us
    pallas_call x2, Pallas kernels, bulk_of(): pl.pallas_call(functools.partial(observed_bulk, sizes, parity), out_shape...  1.44 us
    ppermute x1, starting transfers between devices, local(): lax.ppermute(bulk_weight, 'lon', [(i, i ^ 1) for i in range(strips)])  1.2 us
  transfers between devices with their start and end apart: 7, of which 2 were waited for; matrix products, arithmetic and copies ran while one was open for 0% of the time, Pallas kernels for 19%

profile of v21, /device:TPU:0, one launch (start us, length us, event | category | flops | bytes accessed | tf_op | source)
XLA Modules:
  0.0 20.8 jit_solution(6911562785299673484)
XLA Ops:
  0.6 1.8 %shard_map.104 = (f32[88,256]{1,0:T(8,128)S(1)}, f32[88,256]{1,0:T(8,128)S(1)}, f32[8,4,32,256]{3,2,1,0:T(8,128)S(1)}, bf16[8,4,32,256]{3,2,1,0:T(8,128)(2,1)S(1...) custom-call(f32[8,4,32,256]{3,2,1,0:T(8,128)} %state_hbm.1, ...), custom_call_target="tpu_custom_call" | custom-call | flops 1000000 | bytes 2000000 | tf_op jit(solution)/shard_map/pallas_call | solution.py:460
  2.4 1.4 %shard_map.105 = (f32[8,4,32,256]{3,2,1,0:T(8,128)S(1)}, f32[8,32,256]{2,1,0:T(8,128)S(1)}, f32[1,128]{1,0:T(1,128)S(1)}, f32[4,5,32,256]{3,2,1,0:T(8,128)S(1)}) custom-call(f32[8,4,32,256]{3,2,1,0:T(8,128)S(1)} %get-tuple-element.27.state, bf16[8,4,32,256]{3,2,1,0:T(8,128)(2,1)S(1)} %get-tuple-element.28.noise, ...), custom_call_target="tpu_custom_call" | custom-call | flops 20000000 | bytes 4000000 | tf_op jit(solution)/shard_map/pallas_call | solution.py:474
  3.9 1.6 %collective-permute-start = (f32[88,256]{1,0:T(8,128)S(1)}, f32[88,256]{1,0:T(8,128)S(1)}, u32[]{:S(2)}, u32[]{:S(2)}) collective-permute-start(f32[88,256]{1,0:T(8,128)S(1)} %get-tuple-element.43.own_east), channel_id=1, source_target_pairs={{0,2},{2,4},{4,6},{6,8},{8,10},{10,12},{12,14},{14,0},{1,3},{3,5},... | collective-permute-start | bytes 270344 | tf_op jit(solution)/shard_map/ppermute | solution.py:488
  5.5 3.1 %collective-permute-start.1 = (f32[88,256]{1,0:T(8,128)S(1)}, f32[88,256]{1,0:T(8,128)S(1)}, u32[]{:S(2)}, u32[]{:S(2)}) collective-permute-start(f32[88,256]{1,0:T(8,128)S(1)} %get-tuple-element.44.own_west), channel_id=1, source_target_pairs={{0,14},{2,0},{4,2},{6,4},{8,6},{10,8},{12,10},{14,12},{1,15},{3,1}... | collective-permute-start | bytes 270344 | tf_op jit(solution)/shard_map/ppermute | solution.py:489
  8.6 1.2 %collective-permute-start.2 = (f32[1,128]{1,0:T(1,128)S(1)}, f32[1,128]{1,0:T(1,128)S(1)}, u32[]{:S(2)}, u32[]{:S(2)}) collective-permute-start(f32[1,128]{1,0:T(1,128)S(1)} %get-tuple-element.45.bulk_weight), channel_id=1, source_target_pairs={{0,2},{2,0},{4,6},{6,4},{8,10},{10,8},{12,14},{14,12},{1,3},{3,1},... | collective-permute-start | bytes 1544 | tf_op jit(solution)/shard_map/ppermute | solution.py:491
  9.8 2.0 %shard_map.107.current = f32[8,4,32,256]{3,2,1,0:T(8,128)S(1)} custom-call(f32[8,4,32,256]{3,2,1,0:T(8,128)S(1)} %get-tuple-element.33.even_middle, f32[8,32,256]{2,1,0:T(8,128)S(1)} %get-tuple-element.34.even_observed, f32[4,5,32,256]{3,2,1,0:T(8,128)S(1)} %get-tuple-element.35.even_coefs, f32[8,4,32,256]{3,2,1,0:T(8,128)S(1)} %get-tuple-element.40.odd_middle, ...), custom_call_target="tpu_custom_call" | custom-call | tf_op jit(solution)/shard_map/pallas_call | solution.py:493
  11.8 0.0 collective-permute-done.from_west
  11.9 0.8 %collective-permute-done.1.from_east = f32[88,256]{1,0:T(8,128)S(1)} collective-permute-done((f32[88,256]{1,0:T(8,128)S(1)}, f32[88,256]{1,0:T(8,128)S(1)}, u32[]{:S(2)}, u32[]{:S(2)}) %collective-permute-start.1) | collective-permute-done | bytes 90144 | tf_op jit(solution)/shard_map/ppermute | solution.py:489
  12.6 0.2 shard_map.108
  12.8 0.2 shard_map.109.current
  13.0 0.0 collective-permute-done.2
  13.0 0.1 collective-permute-start.3
  13.1 0.0 copy-start
  13.1 2.7 %collective-permute-start.5 = (f32[1,128]{1,0:T(1,128)S(1)}, f32[1,128]{1,0:T(1,128)S(1)}, u32[]{:S(2)}, u32[]{:S(2)}) collective-permute-start(f32[1,128]{1,0:T(1,128)S(1)} %add.12), channel_id=1, source_target_pairs={{0,12},{2,14},{4,8},{6,10},{8,4},{10,6},{12,0},{14,2},{1,13},{3,15... | collective-permute-start | bytes 1544 | tf_op jit(solution)/shard_map/ppermute | solution.py:531
  15.8 0.3 %collective-permute-start.4 = (f32[1,128]{1,0:T(1,128)S(1)}, f32[1,128]{1,0:T(1,128)S(1)}, u32[]{:S(2)}, u32[]{:S(2)}) collective-permute-start(f32[1,128]{1,0:T(1,128)S(1)} %add.12), channel_id=1, source_target_pairs={{0,8},{2,10},{4,12},{6,14},{8,0},{10,2},{12,4},{14,6},{1,9},{3,11}... | collective-permute-start | bytes 1544 | tf_op jit(solution)/shard_map/ppermute | solution.py:531
  16.1 0.0 collective-permute-done.3.received
  16.1 1.5 %collective-permute-start.6 = (f32[1,128]{1,0:T(1,128)S(1)}, f32[1,128]{1,0:T(1,128)S(1)}, u32[]{:S(2)}, u32[]{:S(2)}) collective-permute-start(f32[1,128]{1,0:T(1,128)S(1)} %add.12), channel_id=1, source_target_pairs={{0,4},{2,6},{4,0},{6,2},{8,12},{10,14},{12,8},{14,10},{1,5},{3,7},... | collective-permute-start | bytes 1544 | tf_op jit(solution)/shard_map/ppermute | solution.py:531
  17.5 0.0 copy-done
  17.6 1.6 %shard_map.110 = f32[8,4,32,256]{3,2,1,0:T(8,128)} custom-call(s32[16]{0:T(128)S(1)} %copy-done, f32[8,4,32,256]{3,2,1,0:T(8,128)S(1)} %shard_map.109.current, f32[8,4,32,256]{3,2,1,0:T(8,128)S(1)} %collective-permute-done.3.received), custom_call_target="tpu_custom_call" | custom-call | bytes 2000000 | tf_op jit(solution)/shard_map/pallas_call | solution.py:535
  19.1 0.0 copy-start.1
  19.2 0.0 collective-permute-done.5
  19.2 1.1 %collective-permute-done.4 = f32[1,128]{1,0:T(1,128)S(1)} collective-permute-done((f32[1,128]{1,0:T(1,128)S(1)}, f32[1,128]{1,0:T(1,128)S(1)}, u32[]{:S(2)}, u32[]{:S(2)}) %collective-permute-start.4) | collective-permute-done | bytes 544 | tf_op jit(solution)/shard_map/ppermute | solution.py:531
  20.2 0.0 collective-permute-done.6
  20.2 0.0 copy-done.1
  20.2 0.5 %bitcast_subtract_fusion = f32[8]{0:T(128)} fusion(f32[8]{0:T(128)S(1)} %copy-done.1, f32[1,128]{1,0:T(1,128)S(1)} %add_add_fusion), kind=kLoop, calls=%fused_computation | loop fusion | flops 16 | bytes 96 | tf_op jit(solution)/shard_map/sub | solution.py:545
  (3 shorter events, 0.0 us)
Async XLA Ops:
  3.9 8.0 %collective-permute-start = (f32[88,256]{1,0:T(8,128)S(1)}, f32[88,256]{1,0:T(8,128)S(1)}, u32[]{:S(2)}, u32[]{:S(2)}) collective-permute-start(f32[88,256]{1,0:T(8,128)S(1)} %get-tuple-element.43.own_east), channel_id=1, source_target_pairs={{0,2},{2,4},{4,6},{6,8},{8,10},{10,12},{12,14},{14,0},{1,3},{3,5},... | collective-permute-start | bytes 270344 | tf_op jit(solution)/shard_map/ppermute | solution.py:488
  5.5 7.2 %collective-permute-start.1 = (f32[88,256]{1,0:T(8,128)S(1)}, f32[88,256]{1,0:T(8,128)S(1)}, u32[]{:S(2)}, u32[]{:S(2)}) collective-permute-start(f32[88,256]{1,0:T(8,128)S(1)} %get-tuple-element.44.own_west), channel_id=1, source_target_pairs={{0,14},{2,0},{4,2},{6,4},{8,6},{10,8},{12,10},{14,12},{1,15},{3,1}... | collective-permute-start | bytes 270344 | tf_op jit(solution)/shard_map/ppermute | solution.py:489
  8.6 4.4 %collective-permute-start.2 = (f32[1,128]{1,0:T(1,128)S(1)}, f32[1,128]{1,0:T(1,128)S(1)}, u32[]{:S(2)}, u32[]{:S(2)}) collective-permute-start(f32[1,128]{1,0:T(1,128)S(1)} %get-tuple-element.45.bulk_weight), channel_id=1, source_target_pairs={{0,2},{2,0},{4,6},{6,4},{8,10},{10,8},{12,14},{14,12},{1,3},{3,1},... | collective-permute-start | bytes 1544 | tf_op jit(solution)/shard_map/ppermute | solution.py:491
  13.0 3.1 %collective-permute-start.3 = (f32[8,4,32,256]{3,2,1,0:T(8,128)S(1)}, f32[8,4,32,256]{3,2,1,0:T(8,128)S(1)}, u32[]{:S(2)}, u32[]{:S(2)}) collective-permute-start(f32[8,4,32,256]{3,2,1,0:T(8,128)S(1)} %shard_map.109.current), channel_id=1, source_target_pairs={{0,1},{1,0},{2,3},{3,2},{4,5},{5,4},{6,7},{7,6},{8,9},{9,8},{10,11... | collective-permute-start | bytes 3145736 | tf_op jit(solution)/shard_map/ppermute | solution.py:523
  13.1 4.5 %copy-start = (s32[16]{0:T(128)S(1)}, s32[16]{0:T(128)}, u32[]{:S(2)}) copy-start(s32[16]{0:T(128)} %source.1) | copy-start | bytes 196
  13.1 6.1 %collective-permute-start.5 = (f32[1,128]{1,0:T(1,128)S(1)}, f32[1,128]{1,0:T(1,128)S(1)}, u32[]{:S(2)}, u32[]{:S(2)}) collective-permute-start(f32[1,128]{1,0:T(1,128)S(1)} %add.12), channel_id=1, source_target_pairs={{0,12},{2,14},{4,8},{6,10},{8,4},{10,6},{12,0},{14,2},{1,13},{3,15... | collective-permute-start | bytes 1544 | tf_op jit(solution)/shard_map/ppermute | solution.py:531
  15.8 4.4 %collective-permute-start.4 = (f32[1,128]{1,0:T(1,128)S(1)}, f32[1,128]{1,0:T(1,128)S(1)}, u32[]{:S(2)}, u32[]{:S(2)}) collective-permute-start(f32[1,128]{1,0:T(1,128)S(1)} %add.12), channel_id=1, source_target_pairs={{0,8},{2,10},{4,12},{6,14},{8,0},{10,2},{12,4},{14,6},{1,9},{3,11}... | collective-permute-start | bytes 1544 | tf_op jit(solution)/shard_map/ppermute | solution.py:531
  16.1 4.1 %collective-permute-start.6 = (f32[1,128]{1,0:T(1,128)S(1)}, f32[1,128]{1,0:T(1,128)S(1)}, u32[]{:S(2)}, u32[]{:S(2)}) collective-permute-start(f32[1,128]{1,0:T(1,128)S(1)} %add.12), channel_id=1, source_target_pairs={{0,4},{2,6},{4,0},{6,2},{8,12},{10,14},{12,8},{14,10},{1,5},{3,7},... | collective-permute-start | bytes 1544 | tf_op jit(solution)/shard_map/ppermute | solution.py:531
  19.1 1.1 %copy-start.1 = (f32[8]{0:T(128)S(1)}, f32[8]{0:T(128)}, u32[]{:S(2)}) copy-start(f32[8]{0:T(128)} %param.14) | copy-start | bytes 100

commit v22 on v19

--- a/solution.py
+++ b/solution.py
@@ -140,7 +140,7 @@
         (mixing_hbm, mixing), (state_hbm.at[:, :, :8], state.at[:, :, :8]),
         (state_hbm.at[:, :, strip - 8:], state.at[:, :, strip - 8:]), (noise_hbm.at[0], noise),
         (noise_hbm.at[1, :, 0], late_noise), (state_hbm.at[:, :, 8:strip - 8], state.at[:, :, 8:strip - 8])))]
-    for copy in copies:
+    for copy in copies[:5] + copies[7:8] + copies[5:7] + copies[8:]:
         copy.start()
     copies[0].wait()
     copies[1].wait()

time: 21 us -> 21.2 us (level)
  no operation moved by 1% of the time
where the time goes in v22:
time: 21.2 us; the launch traced here: 21 us
  starting transfers between devices  10.5 us (50%)
  Pallas kernels  7.46 us (35%)
  waiting for transfers between devices  1.76 us (8%)
  between operations  0.73 us (3%)
  other arithmetic  0.52 us (2%)
    ppermute x3, starting transfers between devices, local(): lax.ppermute(weight, 'lon', [(i, i ^ bit * step) for i in range(strips)])  4.45 us
    ppermute x1, starting transfers between devices, local(): from_east = lax.ppermute(send_west, 'lon', westward)  3.23 us
    pallas_call x1, Pallas kernels, local(): pl.pallas_call(functools.partial(other_bulk, sizes), out_shape=shape(*who...  2.05 us
    pallas_call x1, Pallas kernels, local(): pl.pallas_call(functools.partial(prepare, sizes), out_shape=(packet, pack...  1.95 us
    pallas_call x1, Pallas kernels, local(): pl.pallas_call(functools.partial(assemble, sizes), out_shape=shape(*whole...  1.58 us
    pallas_call x2, Pallas kernels, bulk_of(): pl.pallas_call(functools.partial(observed_bulk, sizes, parity), out_shape...  1.53 us
    ppermute x1, starting transfers between devices, local(): from_west = lax.ppermute(send_east, 'lon', eastward)  1.5 us
    ppermute x1, starting transfers between devices, local(): lax.ppermute(bulk_weight, 'lon', [(i, i ^ 1) for i in range(strips)])  1.28 us
  transfers between devices with their start and end apart: 7, of which 2 were waited for; matrix products, arithmetic and copies ran while one was open for 0% of the time, Pallas kernels for 19%

profile of v22, /device:TPU:0, one launch (start us, length us, event | category | flops | bytes accessed | tf_op | source)
XLA Modules:
  0.0 21.0 jit_solution(8541714167933385210)
XLA Ops:
  0.6 2.0 %shard_map.104 = (f32[88,256]{1,0:T(8,128)S(1)}, f32[88,256]{1,0:T(8,128)S(1)}, f32[8,4,32,256]{3,2,1,0:T(8,128)S(1)}, bf16[8,4,32,256]{3,2,1,0:T(8,128)(2,1)S(1...) custom-call(f32[8,4,32,256]{3,2,1,0:T(8,128)} %state_hbm.1, ...), custom_call_target="tpu_custom_call" | custom-call | flops 1000000 | bytes 2000000 | tf_op jit(solution)/shard_map/pallas_call | solution.py:464
  2.6 1.5 %shard_map.105 = (f32[8,4,32,256]{3,2,1,0:T(8,128)S(1)}, f32[8,32,256]{2,1,0:T(8,128)S(1)}, f32[1,128]{1,0:T(1,128)S(1)}, f32[4,5,32,256]{3,2,1,0:T(8,128)S(1)}) custom-call(f32[8,4,32,256]{3,2,1,0:T(8,128)S(1)} %get-tuple-element.27.state, bf16[8,4,32,256]{3,2,1,0:T(8,128)(2,1)S(1)} %get-tuple-element.28.noise, ...), custom_call_target="tpu_custom_call" | custom-call | flops 20000000 | bytes 4000000 | tf_op jit(solution)/shard_map/pallas_call | solution.py:478
  4.1 1.5 %collective-permute-start = (f32[88,256]{1,0:T(8,128)S(1)}, f32[88,256]{1,0:T(8,128)S(1)}, u32[]{:S(2)}, u32[]{:S(2)}) collective-permute-start(f32[88,256]{1,0:T(8,128)S(1)} %get-tuple-element.43.own_east), channel_id=1, source_target_pairs={{0,2},{2,4},{4,6},{6,8},{8,10},{10,12},{12,14},{14,0},{1,3},{3,5},... | collective-permute-start | bytes 270344 | tf_op jit(solution)/shard_map/ppermute | solution.py:492
  5.6 3.2 %collective-permute-start.1 = (f32[88,256]{1,0:T(8,128)S(1)}, f32[88,256]{1,0:T(8,128)S(1)}, u32[]{:S(2)}, u32[]{:S(2)}) collective-permute-start(f32[88,256]{1,0:T(8,128)S(1)} %get-tuple-element.44.own_west), channel_id=1, source_target_pairs={{0,14},{2,0},{4,2},{6,4},{8,6},{10,8},{12,10},{14,12},{1,15},{3,1}... | collective-permute-start | bytes 270344 | tf_op jit(solution)/shard_map/ppermute | solution.py:493
  8.8 1.3 %collective-permute-start.2 = (f32[1,128]{1,0:T(1,128)S(1)}, f32[1,128]{1,0:T(1,128)S(1)}, u32[]{:S(2)}, u32[]{:S(2)}) collective-permute-start(f32[1,128]{1,0:T(1,128)S(1)} %get-tuple-element.45.bulk_weight), channel_id=1, source_target_pairs={{0,2},{2,0},{4,6},{6,4},{8,10},{10,8},{12,14},{14,12},{1,3},{3,1},... | collective-permute-start | bytes 1544 | tf_op jit(solution)/shard_map/ppermute | solution.py:495
  10.1 2.0 %shard_map.107.current = f32[8,4,32,256]{3,2,1,0:T(8,128)S(1)} custom-call(f32[8,4,32,256]{3,2,1,0:T(8,128)S(1)} %get-tuple-element.33.even_middle, f32[8,32,256]{2,1,0:T(8,128)S(1)} %get-tuple-element.34.even_observed, f32[4,5,32,256]{3,2,1,0:T(8,128)S(1)} %get-tuple-element.35.even_coefs, f32[8,4,32,256]{3,2,1,0:T(8,128)S(1)} %get-tuple-element.40.odd_middle, ...), custom_call_target="tpu_custom_call" | custom-call | tf_op jit(solution)/shard_map/pallas_call | solution.py:497
  12.2 0.0 collective-permute-done.from_west
  12.2 0.7 %collective-permute-done.1.from_east = f32[88,256]{1,0:T(8,128)S(1)} collective-permute-done((f32[88,256]{1,0:T(8,128)S(1)}, f32[88,256]{1,0:T(8,128)S(1)}, u32[]{:S(2)}, u32[]{:S(2)}) %collective-permute-start.1) | collective-permute-done | bytes 90144 | tf_op jit(solution)/shard_map/ppermute | solution.py:493
  12.9 0.2 shard_map.108
  13.1 0.2 shard_map.109.current
  13.2 0.0 collective-permute-done.2
  13.2 0.1 collective-permute-start.3
  13.3 0.0 copy-start
  13.3 2.7 %collective-permute-start.5 = (f32[1,128]{1,0:T(1,128)S(1)}, f32[1,128]{1,0:T(1,128)S(1)}, u32[]{:S(2)}, u32[]{:S(2)}) collective-permute-start(f32[1,128]{1,0:T(1,128)S(1)} %add.12), channel_id=1, source_target_pairs={{0,12},{2,14},{4,8},{6,10},{8,4},{10,6},{12,0},{14,2},{1,13},{3,15... | collective-permute-start | bytes 1544 | tf_op jit(solution)/shard_map/ppermute | solution.py:535
  16.0 0.3 %collective-permute-start.4 = (f32[1,128]{1,0:T(1,128)S(1)}, f32[1,128]{1,0:T(1,128)S(1)}, u32[]{:S(2)}, u32[]{:S(2)}) collective-permute-start(f32[1,128]{1,0:T(1,128)S(1)} %add.12), channel_id=1, source_target_pairs={{0,8},{2,10},{4,12},{6,14},{8,0},{10,2},{12,4},{14,6},{1,9},{3,11}... | collective-permute-start | bytes 1544 | tf_op jit(solution)/shard_map/ppermute | solution.py:535
  16.3 0.0 collective-permute-done.3.received
  16.3 1.5 %collective-permute-start.6 = (f32[1,128]{1,0:T(1,128)S(1)}, f32[1,128]{1,0:T(1,128)S(1)}, u32[]{:S(2)}, u32[]{:S(2)}) collective-permute-start(f32[1,128]{1,0:T(1,128)S(1)} %add.12), channel_id=1, source_target_pairs={{0,4},{2,6},{4,0},{6,2},{8,12},{10,14},{12,8},{14,10},{1,5},{3,7},... | collective-permute-start | bytes 1544 | tf_op jit(solution)/shard_map/ppermute | solution.py:535
  17.8 0.0 copy-done
  17.8 1.6 %shard_map.110 = f32[8,4,32,256]{3,2,1,0:T(8,128)} custom-call(s32[16]{0:T(128)S(1)} %copy-done, f32[8,4,32,256]{3,2,1,0:T(8,128)S(1)} %shard_map.109.current, f32[8,4,32,256]{3,2,1,0:T(8,128)S(1)} %collective-permute-done.3.received), custom_call_target="tpu_custom_call" | custom-call | bytes 2000000 | tf_op jit(solution)/shard_map/pallas_call | solution.py:539
  19.4 0.0 copy-start.1
  19.4 0.0 collective-permute-done.5
  19.4 1.1 %collective-permute-done.4 = f32[1,128]{1,0:T(1,128)S(1)} collective-permute-done((f32[1,128]{1,0:T(1,128)S(1)}, f32[1,128]{1,0:T(1,128)S(1)}, u32[]{:S(2)}, u32[]{:S(2)}) %collective-permute-start.4) | collective-permute-done | bytes 544 | tf_op jit(solution)/shard_map/ppermute | solution.py:535
  20.5 0.0 collective-permute-done.6
  20.5 0.0 copy-done.1
  20.5 0.5 %bitcast_subtract_fusion = f32[8]{0:T(128)} fusion(f32[8]{0:T(128)S(1)} %copy-done.1, f32[1,128]{1,0:T(1,128)S(1)} %add_add_fusion), kind=kLoop, calls=%fused_computation | loop fusion | flops 16 | bytes 96 | tf_op jit(solution)/shard_map/sub | solution.py:549
  (3 shorter events, 0.0 us)
Async XLA Ops:
  4.1 8.1 %collective-permute-start = (f32[88,256]{1,0:T(8,128)S(1)}, f32[88,256]{1,0:T(8,128)S(1)}, u32[]{:S(2)}, u32[]{:S(2)}) collective-permute-start(f32[88,256]{1,0:T(8,128)S(1)} %get-tuple-element.43.own_east), channel_id=1, source_target_pairs={{0,2},{2,4},{4,6},{6,8},{8,10},{10,12},{12,14},{14,0},{1,3},{3,5},... | collective-permute-start | bytes 270344 | tf_op jit(solution)/shard_map/ppermute | solution.py:492
  5.6 7.3 %collective-permute-start.1 = (f32[88,256]{1,0:T(8,128)S(1)}, f32[88,256]{1,0:T(8,128)S(1)}, u32[]{:S(2)}, u32[]{:S(2)}) collective-permute-start(f32[88,256]{1,0:T(8,128)S(1)} %get-tuple-element.44.own_west), channel_id=1, source_target_pairs={{0,14},{2,0},{4,2},{6,4},{8,6},{10,8},{12,10},{14,12},{1,15},{3,1}... | collective-permute-start | bytes 270344 | tf_op jit(solution)/shard_map/ppermute | solution.py:493
  8.8 4.4 %collective-permute-start.2 = (f32[1,128]{1,0:T(1,128)S(1)}, f32[1,128]{1,0:T(1,128)S(1)}, u32[]{:S(2)}, u32[]{:S(2)}) collective-permute-start(f32[1,128]{1,0:T(1,128)S(1)} %get-tuple-element.45.bulk_weight), channel_id=1, source_target_pairs={{0,2},{2,0},{4,6},{6,4},{8,10},{10,8},{12,14},{14,12},{1,3},{3,1},... | collective-permute-start | bytes 1544 | tf_op jit(solution)/shard_map/ppermute | solution.py:495
  13.2 3.1 %collective-permute-start.3 = (f32[8,4,32,256]{3,2,1,0:T(8,128)S(1)}, f32[8,4,32,256]{3,2,1,0:T(8,128)S(1)}, u32[]{:S(2)}, u32[]{:S(2)}) collective-permute-start(f32[8,4,32,256]{3,2,1,0:T(8,128)S(1)} %shard_map.109.current), channel_id=1, source_target_pairs={{0,1},{1,0},{2,3},{3,2},{4,5},{5,4},{6,7},{7,6},{8,9},{9,8},{10,11... | collective-permute-start | bytes 3145736 | tf_op jit(solution)/shard_map/ppermute | solution.py:527
  13.3 4.5 %copy-start = (s32[16]{0:T(128)S(1)}, s32[16]{0:T(128)}, u32[]{:S(2)}) copy-start(s32[16]{0:T(128)} %source.1) | copy-start | bytes 196
  13.3 6.1 %collective-permute-start.5 = (f32[1,128]{1,0:T(1,128)S(1)}, f32[1,128]{1,0:T(1,128)S(1)}, u32[]{:S(2)}, u32[]{:S(2)}) collective-permute-start(f32[1,128]{1,0:T(1,128)S(1)} %add.12), channel_id=1, source_target_pairs={{0,12},{2,14},{4,8},{6,10},{8,4},{10,6},{12,0},{14,2},{1,13},{3,15... | collective-permute-start | bytes 1544 | tf_op jit(solution)/shard_map/ppermute | solution.py:535
  16.0 4.4 %collective-permute-start.4 = (f32[1,128]{1,0:T(1,128)S(1)}, f32[1,128]{1,0:T(1,128)S(1)}, u32[]{:S(2)}, u32[]{:S(2)}) collective-permute-start(f32[1,128]{1,0:T(1,128)S(1)} %add.12), channel_id=1, source_target_pairs={{0,8},{2,10},{4,12},{6,14},{8,0},{10,2},{12,4},{14,6},{1,9},{3,11}... | collective-permute-start | bytes 1544 | tf_op jit(solution)/shard_map/ppermute | solution.py:535
  16.3 4.1 %collective-permute-start.6 = (f32[1,128]{1,0:T(1,128)S(1)}, f32[1,128]{1,0:T(1,128)S(1)}, u32[]{:S(2)}, u32[]{:S(2)}) collective-permute-start(f32[1,128]{1,0:T(1,128)S(1)} %add.12), channel_id=1, source_target_pairs={{0,4},{2,6},{4,0},{6,2},{8,12},{10,14},{12,8},{14,10},{1,5},{3,7},... | collective-permute-start | bytes 1544 | tf_op jit(solution)/shard_map/ppermute | solution.py:535
  19.4 1.1 %copy-start.1 = (f32[8]{0:T(128)S(1)}, f32[8]{0:T(128)}, u32[]{:S(2)}) copy-start(f32[8]{0:T(128)} %param.14) | copy-start | bytes 100
